TPU v7x, 32 devices: a whole 2x2x4 slice. The times are simulated.
32 devices in a mesh: seq: 8 (over z, y), mp: 4 (over x, core).
Axes of the slice: x: 2, y: 2, z: 4, core: 2. Of those that a mesh axis runs over, the one named last changes fastest.
Arguments:
- hidden_rows: bfloat16 [2048, 1536], P('seq', 'mp'), may hold values from -6 to 6
- norm_gain: bfloat16 [1536], P('mp'), may hold values from 0.099609375 to 1.8984375
- encodings: bfloat16 [16, 128, 1536], P('seq', None, 'mp'), may hold values from -56 to 56
- w_query: bfloat16 [1536, 1536], P('seq', 'mp'), may hold values from -0.15625 to 0.15625
- w_key: bfloat16 [1536, 1536], P('seq', 'mp'), may hold values from -0.15625 to 0.15625
- w_value: bfloat16 [1536, 1536], P('seq', 'mp'), may hold values from -0.625 to 0.625
- w_out: bfloat16 [1536, 1536], P('mp', 'seq'), may hold values from -0.4375 to 0.4375
- neighbours: int32 [32, 2], P('seq'), may hold values from 0 to 15, as said below
- grad_out: bfloat16 [2048, 1536], P('seq', 'mp'), may hold values from -6 to 6
Outputs:
- branch_out: bfloat16 [2048, 1536], P('seq', 'mp')
- grad_rows: bfloat16 [2048, 1536], P('seq', 'mp')
- grad_encodings: bfloat16 [16, 128, 1536], P('seq', None, 'mp')
Inputs may be any that keep to these rules, and one draw needn't show every extreme that they name: `neighbours`: A stretch of seq device d names only encoded stretches whose owner, id // 2, is one of the devices d - 2 to d + 2 along seq, counted around the axis. On every device the first stretch names an encoded stretch of owner d - 2 first and, second, the last encoded stretch (local index 1) of owner d + 2.
All inputs are finite; a program needn't handle non-finite values.
Results may differ from a plain program's by a relative error of at most 0.023.
The roundings to bfloat16 on the way count: a program that leaves them out, or rounds other values in their place, can miss the bound.
Values may be sent and summed in bfloat16 or wider, within the bound.
No kernel may reach another device: no remote copies, remote signals or barrier semaphores. Data moves between devices by JAX's collectives and lax.ppermute only.
A program may use at most 64 MiB of HBM per device.

v0:
```python
import jax
import jax.numpy as jnp
from jax import lax
from jax.sharding import PartitionSpec as P

HD = 128
STRETCH = 64
NBR = 2
RET = 128
SPAN = 2
OWN_DEV = 2


epsilon = 1e-05


def from_behind(value, axis, by):
    devices = lax.axis_size(axis)
    return lax.ppermute(value, axis, [(i, (i + by) % devices) for i in range(devices)])


def fetch_direct(packed, offset):
    return from_behind(packed, "seq", -offset)


def return_direct(block, offset):
    return from_behind(block.astype(jnp.bfloat16), "seq", offset).astype(block.dtype)


def shards(hidden_rows, norm_gain, encodings, w_query, w_key, w_value, w_out, neighbours, grad_out):
    full_rows, full_gain, full_grad, own_encodings = (
        lax.all_gather(hidden_rows, "mp", axis=1, tiled=True),
        lax.all_gather(norm_gain, "mp", axis=0, tiled=True),
        lax.all_gather(grad_out, "mp", axis=1, tiled=True),
        lax.all_gather(encodings, "mp", axis=2, tiled=True),
    )
    panel_query, panel_key, panel_value, panel_out = (
        lax.all_gather(w_query, "seq", axis=0, tiled=True),
        lax.all_gather(w_key, "seq", axis=0, tiled=True),
        lax.all_gather(w_value, "seq", axis=0, tiled=True),
        lax.all_gather(w_out, "seq", axis=1, tiled=True),
    )
    token_count = hidden_rows.shape[0]
    full_width = full_rows.shape[1]
    local_width = w_query.shape[1]
    heads_local = local_width // HD
    stretch_count = token_count // STRETCH
    score_scale = HD ** (-0.5)
    contract = (((1,), (1,)), ((), ()))
    rows_float = full_rows.astype(jnp.float32)
    gain_float = full_gain.astype(jnp.float32)
    inv_rms = lax.rsqrt(jnp.mean(rows_float * rows_float, axis=1, keepdims=True) + epsilon)
    normed = (rows_float * inv_rms * gain_float).astype(jnp.bfloat16)
    queries = jnp.dot(normed, panel_query, preferred_element_type=jnp.float32).astype(jnp.bfloat16)
    enc_flat = own_encodings.reshape(OWN_DEV * RET, full_width)
    own_keys = jnp.dot(enc_flat, panel_key, preferred_element_type=jnp.float32).astype(jnp.bfloat16)
    own_values = jnp.dot(enc_flat, panel_value, preferred_element_type=jnp.float32).astype(
        jnp.bfloat16
    )
    own_packed = jnp.concatenate([own_keys, own_values], axis=1).reshape(
        OWN_DEV, RET, 2 * local_width
    )
    window_parts = []
    for offset in range(-SPAN, SPAN + 1):
        if offset == 0:
            window_parts.append(own_packed)
        else:
            window_parts.append(fetch_direct(own_packed, offset))
    slot_total = (2 * SPAN + 1) * OWN_DEV
    window = jnp.stack(window_parts, axis=0).reshape(slot_total, RET, 2 * local_width)
    device = lax.axis_index("seq")
    seq_count = lax.axis_size("seq")
    owners = neighbours // OWN_DEV
    offsets = (owners - device + SPAN) % seq_count - SPAN
    slot_index = ((offsets + SPAN) * OWN_DEV + neighbours % OWN_DEV).reshape(-1)
    picked = jnp.take(window, slot_index, axis=0).reshape(stretch_count, NBR * RET, 2 * local_width)
    key_rows = picked[:, :, :local_width].reshape(stretch_count, NBR * RET, heads_local, HD)
    value_rows = picked[:, :, local_width:].reshape(stretch_count, NBR * RET, heads_local, HD)
    query_rows = queries.reshape(stretch_count, STRETCH, heads_local, HD)
    scores = (
        jnp.einsum("cmhe,cshe->chms", query_rows, key_rows, preferred_element_type=jnp.float32)
        * score_scale
    )
    row_peak = jnp.max(scores, axis=3, keepdims=True)
    exponent = jnp.exp(scores - row_peak)
    weights = exponent / jnp.sum(exponent, axis=3, keepdims=True)
    weights_low = weights.astype(jnp.bfloat16)
    attended = jnp.einsum(
        "chms,cshe->cmhe", weights_low, value_rows, preferred_element_type=jnp.float32
    )
    attended = attended.astype(jnp.bfloat16).reshape(token_count, local_width)
    partial_out = jnp.dot(attended, panel_out, preferred_element_type=jnp.float32)
    branch_out = lax.psum_scatter(
        partial_out.astype(jnp.bfloat16), "mp", scatter_dimension=1, tiled=True
    )
    d_attended = lax.dot_general(
        full_grad, panel_out, contract, preferred_element_type=jnp.float32
    ).astype(jnp.bfloat16)
    grad_attn = d_attended.reshape(stretch_count, STRETCH, heads_local, HD)
    d_weights = jnp.einsum(
        "cmhe,cshe->chms", grad_attn, value_rows, preferred_element_type=jnp.float32
    )
    d_scores = (
        weights * (d_weights - jnp.sum(d_weights * weights, axis=3, keepdims=True)) * score_scale
    ).astype(jnp.bfloat16)
    d_queries = jnp.einsum(
        "chms,cshe->cmhe", d_scores, key_rows, preferred_element_type=jnp.float32
    )
    d_queries = d_queries.astype(jnp.bfloat16).reshape(token_count, local_width)
    d_keys = jnp.einsum("chms,cmhe->cshe", d_scores, query_rows, preferred_element_type=jnp.float32)
    d_values = jnp.einsum(
        "chms,cmhe->cshe", weights_low, grad_attn, preferred_element_type=jnp.float32
    )
    d_packed = jnp.concatenate(
        [
            d_keys.reshape(stretch_count * NBR, RET, local_width),
            d_values.reshape(stretch_count * NBR, RET, local_width),
        ],
        axis=2,
    )
    selector = (jnp.arange(slot_total, dtype=jnp.int32)[:, None] == slot_index[None, :]).astype(
        jnp.float32
    )
    d_window = jnp.einsum("sr,rtf->stf", selector, d_packed, precision=lax.Precision.HIGHEST)
    d_window = d_window.reshape(2 * SPAN + 1, OWN_DEV, RET, 2 * local_width)
    own_grads = d_window[SPAN]
    for offset in range(-SPAN, SPAN + 1):
        if offset != 0:
            own_grads = own_grads + return_direct(d_window[offset + SPAN], offset)
    own_low = own_grads.astype(jnp.bfloat16).reshape(OWN_DEV * RET, 2 * local_width)
    enc_partial = lax.dot_general(
        own_low[:, :local_width], panel_key, contract, preferred_element_type=jnp.float32
    )
    enc_partial = enc_partial + lax.dot_general(
        own_low[:, local_width:], panel_value, contract, preferred_element_type=jnp.float32
    )
    grad_encodings = lax.psum_scatter(
        enc_partial.reshape(OWN_DEV, RET, full_width).astype(jnp.bfloat16),
        "mp",
        scatter_dimension=2,
        tiled=True,
    )
    d_normed = lax.dot_general(d_queries, panel_query, contract, preferred_element_type=jnp.float32)
    normed_grad = lax.psum(d_normed.astype(jnp.bfloat16), "mp").astype(jnp.float32)
    statistic = jnp.sum(rows_float * gain_float * normed_grad, axis=1, keepdims=True) / full_width
    full_change = inv_rms * gain_float * normed_grad - rows_float * inv_rms**3 * statistic
    column_start = lax.axis_index("mp") * local_width
    grad_rows = lax.dynamic_slice_in_dim(full_change, column_start, local_width, 1).astype(
        jnp.bfloat16
    )
    return (branch_out, grad_rows, grad_encodings)


def solution(mesh):
    placed = (
        P("seq", "mp"),
        P("mp"),
        P("seq", None, "mp"),
        P("seq", "mp"),
        P("seq", "mp"),
        P("seq", "mp"),
        P("mp", "seq"),
        P("seq", None),
        P("seq", "mp"),
    )
    return jax.shard_map(
        shards,
        mesh=mesh,
        in_specs=placed,
        out_specs=(P("seq", "mp"), P("seq", "mp"), P("seq", None, "mp")),
        check_vma=False,
    )
```

profile of v0, /device:TPU:1, one launch (start us, length us, event | category | flops | bytes accessed | tf_op | source)
XLA Modules:
  0.0 320.6 jit_solution(12744074891664399670)
XLA Ops:
  12.2 5.9 %all-gather = bf16[4,1,384]{2,1,0:T(2,128)(2,1)S(1)} all-gather(bf16[1,1,384]{2,1,0:T(2,128)(2,1)S(1)} %reshape.144), channel_id=1, replica_groups=mesh['seq'=8,'mp'=4] {'mp'}, dimensions={0}, use_global_device_ids=true | all-gather | bytes 3840 | tf_op jit(solution)/shard_map/all_gather | solution.py:33
  18.2 9.4 %all_gather.27 = bf16[256,1536]{1,0:T(8,128)(2,1)S(1)} all-gather(bf16[256,384]{1,0:T(8,128)(2,1)} %param.9), channel_id=1, replica_groups=mesh['seq'=8,'mp'=4] {'mp'}, dimensions={1}, use_global_device_ids=true | all-gather | bytes 983040 | tf_op jit(solution)/shard_map/all_gather | solution.py:32
  27.9 8.7 %all_gather.24 = bf16[2,128,1536]{2,1,0:T(8,128)(2,1)S(1)} all-gather(bf16[2,128,384]{2,1,0:T(8,128)(2,1)S(1)} %copy-done.7), channel_id=1, replica_groups=mesh['seq'=8,'mp'=4] {'mp'}, dimensions={2}, use_global_device_ids=true | all-gather | bytes 983040 | tf_op jit(solution)/shard_map/all_gather | solution.py:35
  36.6 8.7 %all_gather.31 = bf16[256,1536]{1,0:T(8,128)(2,1)S(1)} all-gather(bf16[256,384]{1,0:T(8,128)(2,1)S(1)} %copy-done.8), channel_id=1, replica_groups=mesh['seq'=8,'mp'=4] {'mp'}, dimensions={1}, use_global_device_ids=true | all-gather | bytes 983040 | tf_op jit(solution)/shard_map/all_gather | solution.py:34
  45.3 6.8 %all-gather.8.cloned.1.call-done = bf16[1536,384]{1,0:T(8,128)(2,1)} async-done(((bf16[192,384]{1,0:T(8,128)(2,1)}), bf16[1536,384]{1,0:T(8,128)(2,1)}) %all-gather.8.cloned.1.call-update) | async-done | bytes 1179664 | tf_op jit(solution)/shard_map/all_gather | solution.py:40
  52.1 1.8 convolution_convert_fusion.4
  53.9 40.2 %all-gather.6.cloned.1.call-done = bf16[1536,384]{1,0:T(8,128)(2,1)} async-done(((bf16[192,384]{1,0:T(8,128)(2,1)}), bf16[1536,384]{1,0:T(8,128)(2,1)}) %all-gather.6.cloned.1.call-update) | async-done | bytes 1179664 | tf_op jit(solution)/shard_map/all_gather | solution.py:39
  94.1 1.8 convolution_convert_fusion.5
  96.0 1.8 collective-permute-start.3
  99.4 44.2 %all-gather.10.cloned.1.call-done = bf16[1536,384]{1,0:T(8,128)(2,1)} async-done(((bf16[192,384]{1,0:T(8,128)(2,1)}), bf16[1536,384]{1,0:T(8,128)(2,1)}) %all-gather.10.cloned.1.call-update) | async-done | bytes 1179664 | tf_op jit(solution)/shard_map/all_gather | solution.py:38
  143.6 2.6 convolution_convert_fusion.3
  146.1 1.0 reshape.127
  147.1 38.3 %all-gather.12.cloned.1.call-done = bf16[384,1536]{0,1:T(8,128)(2,1)} async-done(((bf16[384,192]{0,1:T(8,128)(2,1)}), bf16[384,1536]{0,1:T(8,128)(2,1)}) %all-gather.12.cloned.1.call-update) | async-done | bytes 1179664 | tf_op jit(solution)/shard_map/all_gather | solution.py:41
  185.5 2.5 convolution_convert_fusion.2
  188.0 1.7 reshape.130
  189.7 1.0 bitcast_dynamic-update-slice_fusion.3
  190.9 1.3 copy-done.1
  192.2 2.2 gather_fusion
  195.6 1.1 fusion.60
  196.7 1.1 fusion.40
  197.9 2.1 fusion.13
  200.0 6.5 %fusion.14 = bf16[4,64,3,128]{3,1,2,0:T(8,128)(2,1)} fusion(bf16[4,256,3,128]{1,3,2,0:T(8,128)(2,1)S(1)} %bitcast.76, f32[4,3,64,256]{3,2,1,0:T(8,128)} %fusion.40, f32[4,3,64,256]{3,2,1,0:T(8,128)} %get-tuple-element.16, f32[4,3,64]{2,1,0:T(4,128)S(1)} %get-tuple-element.15), kind=kOutput, calls=%fused_computation.31 | convolution fusion | flops 51807232 | bytes 2558976 | tf_op jit(solution)/shard_map/chms,cshe->cmhe/dot_general | solution.py:106
  206.4 7.2 %convolution_bitcast_fusion.1 = f32[4,256,3,128]{1,3,2,0:T(8,128)} fusion(f32[4,3,64,256]{3,2,1,0:T(8,128)} %fusion.40, bf16[4,64,3,128]{3,2,1,0:T(4,128)(2,1)S(1)} %reshape.127, f32[4,3,64,256]{3,2,1,0:T(8,128)} %get-tuple-element.16, f32[4,3,64]{2,1,0:T(4,128)S(1)} %get-tuple-element.15), kind=kOutput, calls=%fused_computation.16 | convolution fusion | flops 51708928 | bytes 3345408 | tf_op jit(solution)/shard_map/chms,cmhe->cshe/dot_general | solution.py:110
  213.7 2.7 convolution_bitcast_fusion
  216.4 2.4 copy.87
  218.9 1.8 reshape.133
  220.6 2.1 copy.90
  222.7 1.1 copy.84
  223.8 1.5 convolution_convert_fusion
  225.7 1.1 copy.80
  226.8 1.9 convolution_convert_fusion.1
  228.7 1.2 copy.98
  229.8 3.6 %copy.89 = f32[4,256,3,128]{1,0,3,2:T(4,128)} copy(f32[4,256,3,128]{1,3,2,0:T(8,128)} %convolution_bitcast_fusion) | data formatting | bytes 3145728 | tf_op jit(solution)/shard_map/chms,cmhe->cshe/transpose | solution.py:111
  233.4 2.8 reshape.134
  236.2 3.1 copy.91
  239.3 4.3 %fusion.2 = f32[10,128,768]{2,0,1:T(8,128)S(1)} fusion(f32[8,128,384]{2,0,1:T(8,128)} %copy.91, f32[8,128,384]{2,0,1:T(8,128)S(1)} %copy.90, s32[8]{0:T(128)S(1)} %copy-done.9), kind=kOutput, calls=%fused_computation.3 | convolution fusion | flops 95158352 | bytes 7077920 | tf_op jit(solution)/shard_map/sr,rtf->stf/dot_general | solution.py:124
  243.6 4.2 %fusion.56 = (bf16[10,128,768]{2,1,0:T(8,128)(2,1)S(1)}, f32[10,128,768]{2,1,0:T(8,128)}) fusion(f32[10,128,768]{2,0,1:T(8,128)S(1)} %fusion.2), kind=kLoop, calls=%fused_computation.100 | loop fusion | flops 983040 | bytes 9830400 | tf_op jit(solution)/shard_map/convert.3
  248.0 1.8 collective-permute-start.4
  250.2 3.8 %collective-permute-start.5 = (bf16[2,128,768]{2,1,0:T(8,128)(2,1)S(1)}, bf16[2,128,768]{2,1,0:T(8,128)(2,1)S(1)}, u32[]{:S(2)}, u32[]{:S(2)}) collective-permute-start(bf16[2,128,768]{2,1,0:T(8,128)(2,1)S(1)} %get-tuple-element.10), channel_id=1, source_target_pairs={{0,28},{4,0},{8,4},{12,8},{16,12},{20,16},{24,20},{28,24},{1,29},{... | collective-permute-start | bytes 1179656 | tf_op jit(solution)/shard_map/ppermute | solution.py:19
  254.0 2.7 collective-permute-done.4
  256.7 10.5 %collective-permute-done.7 = bf16[2,128,768]{2,1,0:T(8,128)(2,1)S(1)} collective-permute-done((bf16[2,128,768]{2,1,0:T(8,128)(2,1)S(1)}, bf16[2,128,768]{2,1,0:T(8,128)(2,1)S(1)}, u32[]{:S(2)}, u32[]{:S(2)}) %collective-permute-start.7) | collective-permute-done | bytes 393248 | tf_op jit(solution)/shard_map/ppermute | solution.py:19
  267.2 8.3 %collective-permute-done.6 = bf16[2,128,768]{2,1,0:T(8,128)(2,1)S(1)} collective-permute-done((bf16[2,128,768]{2,1,0:T(8,128)(2,1)S(1)}, bf16[2,128,768]{2,1,0:T(8,128)(2,1)S(1)}, u32[]{:S(2)}, u32[]{:S(2)}) %collective-permute-start.6) | collective-permute-done | bytes 393248 | tf_op jit(solution)/shard_map/ppermute | solution.py:19
  275.5 1.4 fusion.22
  279.4 1.0 copy.123
  280.7 1.4 convert_element_type.92
  283.3 2.7 reduce-scatter.7.cloned.1.call-done
  286.0 1.7 copy.99
  287.7 24.3 %reduce-scatter.9.cloned.1.call-done = bf16[384,256]{1,0:T(8,128)(2,1)} async-done(((bf16[1536,256]{1,0:T(8,128)(2,1)}), bf16[384,256]{1,0:T(8,128)(2,1)}) %reduce-scatter.9.cloned.1.call-update) | async-done | bytes 196624
  (77 shorter events, 14.8 us)
Async XLA Ops:
  7.2 20.7 %copy-start.7 = (bf16[2,128,384]{2,1,0:T(8,128)(2,1)S(1)}, bf16[2,128,384]{2,1,0:T(8,128)(2,1)}, u32[]{:S(2)}) copy-start(bf16[2,128,384]{2,1,0:T(8,128)(2,1)} %param.11) | copy-start | bytes 589828
  7.2 44.9 %all-gather.8.cloned.1.call-start = ((), (), s32[]{:S(2)}) async-start(), calls=%async_computation.3 | async-start | bytes 1327104 | tf_op jit(solution)/shard_map/all_gather | solution.py:40
  7.9 86.2 %all-gather.6.cloned.1.call-start = ((), (), s32[]{:S(2)}) async-start(), calls=%async_computation.2 | async-start | bytes 1327104 | tf_op jit(solution)/shard_map/all_gather | solution.py:39
  8.7 27.9 %copy-start.8 = (bf16[256,384]{1,0:T(8,128)(2,1)S(1)}, bf16[256,384]{1,0:T(8,128)(2,1)}, u32[]{:S(2)}) copy-start(bf16[256,384]{1,0:T(8,128)(2,1)} %param.17) | copy-start | bytes 589828
  8.7 134.9 %all-gather.10.cloned.1.call-start = ((), (), s32[]{:S(2)}) async-start(), calls=%async_computation.4 | async-start | bytes 1327104 | tf_op jit(solution)/shard_map/all_gather | solution.py:38
  9.4 176.1 %all-gather.12.cloned.1.call-start = ((), (), s32[]{:S(2)}) async-start(), calls=%async_computation.5 | async-start | bytes 1327104 | tf_op jit(solution)/shard_map/all_gather | solution.py:41
  10.0 270.7 %all-reduce.2.cloned.1.call-start = ((), (), s32[]{:S(2)}) async-start(), calls=%async_computation.6 | async-start | bytes 1572864 | tf_op jit(solution)/shard_map/psum | solution.py:144
  96.0 94.8 %collective-permute-start.3 = (bf16[2,128,768]{2,1,0:T(8,128)(2,1)S(1)}, bf16[2,128,768]{2,1,0:T(8,128)(2,1)S(1)}, u32[]{:S(2)}, u32[]{:S(2)}) collective-permute-start(bf16[2,128,768]{2,1,0:T(8,128)(2,1)S(1)} %bitcast.86), channel_id=1, source_target_pairs={{0,24},{4,28},{8,0},{12,4},{16,8},{20,12},{24,16},{28,20},{1,25},{... | collective-permute-start | bytes 1179656 | tf_op jit(solution)/shard_map/ppermute | solution.py:19
  97.8 93.0 %collective-permute-start.2 = (bf16[2,128,768]{2,1,0:T(8,128)(2,1)S(1)}, bf16[2,128,768]{2,1,0:T(8,128)(2,1)S(1)}, u32[]{:S(2)}, u32[]{:S(2)}) collective-permute-start(bf16[2,128,768]{2,1,0:T(8,128)(2,1)S(1)} %bitcast.87), channel_id=1, source_target_pairs={{0,28},{4,0},{8,4},{12,8},{16,12},{20,16},{24,20},{28,24},{1,29},{... | collective-permute-start | bytes 1179656 | tf_op jit(solution)/shard_map/ppermute | solution.py:19
  98.8 91.9 %collective-permute-start.1 = (bf16[2,128,768]{2,1,0:T(8,128)(2,1)S(1)}, bf16[2,128,768]{2,1,0:T(8,128)(2,1)S(1)}, u32[]{:S(2)}, u32[]{:S(2)}) collective-permute-start(bf16[2,128,768]{2,1,0:T(8,128)(2,1)S(1)} %bitcast.88), channel_id=1, source_target_pairs={{0,4},{4,8},{8,12},{12,16},{16,20},{20,24},{24,28},{28,0},{1,5},{5... | collective-permute-start | bytes 1179656 | tf_op jit(solution)/shard_map/ppermute | solution.py:19
  99.3 90.4 %collective-permute-start = (bf16[2,128,768]{2,1,0:T(8,128)(2,1)S(1)}, bf16[2,128,768]{2,1,0:T(8,128)(2,1)}, u32[]{:S(2)}, u32[]{:S(2)}) collective-permute-start(bf16[2,128,768]{2,1,0:T(8,128)(2,1)S(1)} %bitcast.89), channel_id=1, source_target_pairs={{0,8},{4,12},{8,16},{12,20},{16,24},{20,28},{24,0},{28,4},{1,9},{5... | collective-permute-start | bytes 1179656 | tf_op jit(solution)/shard_map/ppermute | solution.py:19
  190.9 1.3 copy-start.1
  195.4 1.4 copy-start.5
  206.4 7.3 %copy-start.6 = (bf16[4,64,3,128]{3,2,1,0:T(4,128)(2,1)S(1)}, bf16[4,64,3,128]{3,2,1,0:T(4,128)(2,1)}, u32[]{:S(2)}) copy-start(bf16[4,64,3,128]{3,2,1,0:T(4,128)(2,1)} %reshape.130) | copy-start | bytes 589828
  220.6 3.2 copy-start.3
  225.4 60.5 %reduce-scatter.7.cloned.1.call-start = ((), (), s32[]{:S(2)}) async-start(), calls=%async_computation.7 | async-start | bytes 983040
  236.2 3.1 copy-start.9
  247.8 64.1 %reduce-scatter.9.cloned.1.call-start = ((), (), s32[]{:S(2)}) async-start(), calls=%async_computation.8 | async-start | bytes 983040
  248.0 28.9 %copy-start.4 = (bf16[1536,384]{1,0:T(8,128)(2,1)S(1)}, bf16[1536,384]{1,0:T(8,128)(2,1)}, u32[]{:S(2)}) copy-start(bf16[1536,384]{1,0:T(8,128)(2,1)} %all-gather.6.cloned.1.call-done) | copy-start | bytes 3538948
  248.0 8.7 %collective-permute-start.4 = (bf16[2,128,768]{2,1,0:T(8,128)(2,1)S(1)}, bf16[2,128,768]{2,1,0:T(8,128)(2,1)S(1)}, u32[]{:S(2)}, u32[]{:S(2)}) collective-permute-start(bf16[2,128,768]{2,1,0:T(8,128)(2,1)S(1)} %get-tuple-element.7), channel_id=1, source_target_pairs={{0,24},{4,28},{8,0},{12,4},{16,8},{20,12},{24,16},{28,20},{1,25},{... | collective-permute-start | bytes 1179656 | tf_op jit(solution)/shard_map/ppermute | solution.py:19
  249.8 17.4 %collective-permute-start.7 = (bf16[2,128,768]{2,1,0:T(8,128)(2,1)S(1)}, bf16[2,128,768]{2,1,0:T(8,128)(2,1)S(1)}, u32[]{:S(2)}, u32[]{:S(2)}) collective-permute-start(bf16[2,128,768]{2,1,0:T(8,128)(2,1)S(1)} %get-tuple-element.8), channel_id=1, source_target_pairs={{0,8},{4,12},{8,16},{12,20},{16,24},{20,28},{24,0},{28,4},{1,9},{5... | collective-permute-start | bytes 1179656 | tf_op jit(solution)/shard_map/ppermute | solution.py:19
  249.8 25.7 %collective-permute-start.6 = (bf16[2,128,768]{2,1,0:T(8,128)(2,1)S(1)}, bf16[2,128,768]{2,1,0:T(8,128)(2,1)S(1)}, u32[]{:S(2)}, u32[]{:S(2)}) collective-permute-start(bf16[2,128,768]{2,1,0:T(8,128)(2,1)S(1)} %get-tuple-element.9), channel_id=1, source_target_pairs={{0,4},{4,8},{8,12},{12,16},{16,20},{20,24},{24,28},{28,0},{1,5},{5... | collective-permute-start | bytes 1179656 | tf_op jit(solution)/shard_map/ppermute | solution.py:19
  250.2 25.4 %collective-permute-start.5 = (bf16[2,128,768]{2,1,0:T(8,128)(2,1)S(1)}, bf16[2,128,768]{2,1,0:T(8,128)(2,1)S(1)}, u32[]{:S(2)}, u32[]{:S(2)}) collective-permute-start(bf16[2,128,768]{2,1,0:T(8,128)(2,1)S(1)} %get-tuple-element.10), channel_id=1, source_target_pairs={{0,28},{4,0},{8,4},{12,8},{16,12},{20,16},{24,20},{28,24},{1,29},{... | collective-permute-start | bytes 1179656 | tf_op jit(solution)/shard_map/ppermute | solution.py:19
  276.9 1.3 copy-start.2
  280.7 1.4 copy-start
Sparse Core Ops, SparseCore 0:
  10.2 41.8 all-gather.7
  54.3 39.8 all-gather.5
  96.3 47.2 all-gather.9
  145.6 39.8 all-gather.11
  225.5 33.4 all-reduce.1
  261.4 24.5 reduce-scatter.6
  288.6 23.2 reduce-scatter.8
where the time goes:
time: 322 us; the launch traced here: 321 us
  waiting for transfers between devices  181 us (56%)
  matrix products  37.6 us (12%)
  local copies, waits for them, and re-layouts  34.7 us (11%)
  blocking collectives  32.7 us (10%)
  between operations  14.5 us (5%)
  other arithmetic  10.6 us (3%)
  starting transfers between devices  9.83 us (3%)
    all_gather x1, waiting for transfers between devices, shards(): lax.all_gather(w_query, 'seq', axis=0, tiled=True)  44.2 us
    all_gather x1, waiting for transfers between devices, shards(): lax.all_gather(w_key, 'seq', axis=0, tiled=True)  40.2 us
    all_gather x1, waiting for transfers between devices, shards(): lax.all_gather(w_out, 'seq', axis=1, tiled=True)  38.3 us
    unnamed x9, waiting for transfers between devices  29.5 us
    ppermute x8, waiting for transfers between devices, from_behind(): lax.ppermute(value, axis, [(i, (i + by) % devices) for i in range(devices)])  21.6 us
    unnamed x31, local copies, waits for them, and re-layouts  10.1 us
    all_gather x1, blocking collectives, shards(): lax.all_gather(hidden_rows, 'mp', axis=1, tiled=True)  9.36 us
    ppermute x8, starting transfers between devices, from_behind(): lax.ppermute(value, axis, [(i, (i + by) % devices) for i in range(devices)])  9.34 us
  transfers between devices with their start and end apart: 15, of which 9 were waited for; matrix products, arithmetic and copies ran while one was open for 14% of the time, Pallas kernels for 0%

commit v1 on v0

v1 whole, which is shorter than its diff:
```python
import jax
import jax.numpy as jnp
from jax import lax
from jax.experimental import pallas as pl
from jax.experimental.pallas import tpu as pltpu
from jax.sharding import PartitionSpec as P

HD = 128
STRETCH = 64
NBR = 2
RET = 128
OWN_DEV = 2
OWN_ROWS = OWN_DEV * RET
GAIN_ROWS = 16
LOW = jnp.bfloat16
F32 = jnp.float32
epsilon = 1e-05


def joint(step):
    seq_count, mp_count = lax.axis_size("seq"), lax.axis_size("mp")
    pairs = []
    for d in range(seq_count):
        for m in range(mp_count):
            target = step(d // 2, d % 2, m // 2, m % 2)
            if target is not None:
                z, y, x, c = target
                pairs.append((d * mp_count + m, ((z % (seq_count // 2)) * 2 + y) * mp_count + 2 * x + c))
    return pairs


def move(value, step):
    return lax.ppermute(value, ("seq", "mp"), joint(step))


def swap(z, y, x, c):
    return (z, c, x, y)


def cross(z, y, x, c):
    return (z, c, x, 1 - y)


def flip_x(z, y, x, c):
    return (z, y, 1 - x, c)


def flip_y(z, y, x, c):
    return (z, 1 - y, x, c)


def flip_core(z, y, x, c):
    return (z, y, x, 1 - c)


def ring_up(z, y, x, c):
    return (z + 1, y, x, c)


def ring_down(z, y, x, c):
    return (z - 1, y, x, c)


def place():
    d, m = lax.axis_index("seq"), lax.axis_index("mp")
    return d // 2, d % 2, m // 2, m % 2


def spread(value, x_first):
    first, second = (flip_x, flip_y) if x_first else (flip_y, flip_x)
    near = move(value, first)
    other = move(value, second)
    far = move(near, second)
    if x_first:
        return [value, other, near, far]
    return [value, near, other, far]


def line_pieces(own, z):
    from_below = move(own, lambda z, y, x, c: (z + 1, y, x, c) if z < 3 else None)
    from_above = move(own, lambda z, y, x, c: (z - 1, y, x, c) if z > 0 else None)
    below_two = move(from_below, lambda z, y, x, c: (z + 1, y, x, c) if z in (1, 2) else None)
    above_two = move(from_above, lambda z, y, x, c: (z - 1, y, x, c) if z in (1, 2) else None)
    two = jnp.where(z <= 1, above_two, below_two)
    three = move(two, lambda z, y, x, c: {1: (0, y, x, c), 2: (3, y, x, c)}.get(z))
    pieces = [own, from_below, from_above, two, three]
    return pieces + [move(piece, flip_core) for piece in pieces]


def any_pieces(own, z, y, g):
    seq_count = lax.axis_size("seq")
    z_count = seq_count // 2
    groups = [[2 * i + j for i in range(z_count)] for j in range(2)]
    mine = lax.all_gather(own, "seq", axis=0, axis_index_groups=groups)
    theirs = move(mine, flip_core)
    c = lax.axis_index("mp") % 2
    both = jnp.stack([jnp.where(c == 0, mine, theirs), jnp.where(c == 0, theirs, mine)], axis=1)
    rows = own.shape[0] // 2
    both = both.reshape(seq_count, 2, rows, -1)
    both = jnp.moveaxis(both, 1, 2).reshape(4, seq_count * rows // 4, 2, -1)
    ordered = jnp.take(both, g ^ jnp.arange(4), axis=0)
    width = ordered.shape[-1]
    return [ordered.reshape(seq_count * rows, 2 * width)]


def assemble(pieces, whole, z, c, g):
    if len(pieces) == 1:
        whole[...] = pieces[0][...]
        return
    rows = pieces[0].shape[0] // 2
    width = pieces[0].shape[1]
    half = len(pieces) // 2

    def put(piece, from_z, from_c):
        start = pl.multiple_of(((from_z ^ g) * 2 + from_c) * rows, 64)
        whole[pl.ds(start, rows), 0:width] = piece[0:rows, :]
        whole[pl.ds(start, rows), width : 2 * width] = piece[rows : 2 * rows, :]

    for side in range(2):
        own, below, above, two, three = pieces[side * half : (side + 1) * half]
        side_c = c if side == 0 else 1 - c
        put(own, z, side_c)
        put(two, (z + 2) % 4, side_c)

        @pl.when(z > 0)
        def _():
            put(below, z - 1, side_c)

        @pl.when(z < 3)
        def _():
            put(above, z + 1, side_c)

        @pl.when(jnp.logical_or(z == 0, z == 3))
        def _():
            put(three, 3 - z, side_c)


def table_kernel(piece_count, token_count, *refs):
    z, y, x, c = place()
    g = 2 * x + y
    rows_refs, refs = refs[:4], refs[4:]
    enc_refs, refs = refs[:12], refs[12:]
    pieces, refs = refs[:piece_count], refs[piece_count:]
    normed_out, inv_out, whole, tables, shared = refs
    full_width = 4 * rows_refs[0].shape[1]
    total = None
    for ref in rows_refs:
        rows = ref[0:token_count, :].astype(F32)
        part = jnp.sum(rows * rows, axis=1, keepdims=True)
        total = part if total is None else total + part
    inv_rms = lax.rsqrt(total / full_width + epsilon)
    inv_out[...] = inv_rms
    for k, ref in enumerate(rows_refs):
        width = ref.shape[1]
        rows = ref[0:token_count, :].astype(F32)
        gain = ref[token_count : token_count + 1, :].astype(F32)
        normed_out[:, k * width : (k + 1) * width] = (rows * inv_rms * gain).astype(LOW)
    assemble(pieces, whole, z, c, g)
    for i in range(3):
        enc = jnp.concatenate([ref[...] for ref in enc_refs[4 * i : 4 * i + 4]], axis=1)
        tables[i * OWN_ROWS : (i + 1) * OWN_ROWS, :] = jnp.dot(
            enc, whole[...], preferred_element_type=F32
        ).astype(LOW)
    shared[0:OWN_ROWS, :] = tables[OWN_ROWS : 2 * OWN_ROWS, :]
    start = pl.multiple_of(jnp.where(c == 1, 0, 2 * OWN_ROWS), OWN_ROWS)
    shared[OWN_ROWS : 2 * OWN_ROWS, :] = tables[pl.ds(start, OWN_ROWS), :]


def attention_kernel(piece_count, seq_count, *refs):
    z, y, x, c = place()
    g = 2 * x + y
    chosen, normed, refs = refs[0], refs[1], refs[2:]
    grad_refs, refs = refs[:4], refs[4:]
    pieces, refs = refs[:piece_count], refs[piece_count:]
    tables, shared, attended, d_queries, whole, d_own, d_shared, queries, d_attended, window, d_window = refs
    token_count = normed.shape[0]
    width = attended.shape[1]
    assemble(pieces, whole, z, c, g)
    queries[...] = jnp.dot(normed[...], whole[:, 0:width], preferred_element_type=F32).astype(LOW)
    grads = jnp.concatenate([ref[...] for ref in grad_refs], axis=1)
    d_attended[...] = jnp.dot(grads, whole[:, width:], preferred_element_type=F32).astype(LOW)
    window[0 : 3 * OWN_ROWS, :] = tables[...]
    window[3 * OWN_ROWS : 5 * OWN_ROWS, :] = shared[...]
    d_window[...] = jnp.zeros_like(d_window)
    scale = HD ** (-0.5)
    t = 2 * z + c
    across = (((1,), (1,)), ((), ()))
    down = (((0,), (0,)), ((), ()))
    for s in range(token_count // STRETCH):
        starts = []
        for j in range(NBR):
            name = chosen[s, j]
            away = (name // OWN_DEV - t + 2 + seq_count) % seq_count
            odd = 3 + jnp.where(away == 1, 1 - c, c)
            index = jnp.where(away % 2 == 0, away // 2, odd)
            starts.append(pl.multiple_of(index * OWN_ROWS + (name % OWN_DEV) * RET, RET))
        tokens = slice(s * STRETCH, (s + 1) * STRETCH)
        for h in range(width // HD):
            left = slice(h * HD, (h + 1) * HD)
            right = slice(width + h * HD, width + (h + 1) * HD)
            keys = jnp.concatenate([window[pl.ds(a, RET), left] for a in starts], axis=0)
            values = jnp.concatenate([window[pl.ds(a, RET), right] for a in starts], axis=0)
            query = queries[tokens, left]
            d_att = d_attended[tokens, left]
            scores = lax.dot_general(query, keys, across, preferred_element_type=F32) * scale
            exponent = jnp.exp(scores - jnp.max(scores, axis=1, keepdims=True))
            weights = exponent / jnp.sum(exponent, axis=1, keepdims=True)
            weights_low = weights.astype(LOW)
            attended[tokens, left] = jnp.dot(
                weights_low, values, preferred_element_type=F32
            ).astype(LOW)
            d_weights = lax.dot_general(d_att, values, across, preferred_element_type=F32)
            inner = jnp.sum(d_weights * weights, axis=1, keepdims=True)
            d_scores = (weights * (d_weights - inner) * scale).astype(LOW)
            d_queries[tokens, left] = jnp.dot(d_scores, keys, preferred_element_type=F32).astype(LOW)
            d_keys = lax.dot_general(d_scores, query, down, preferred_element_type=F32)
            d_values = lax.dot_general(weights_low, d_att, down, preferred_element_type=F32)
            for j, a in enumerate(starts):
                d_window[pl.ds(a, RET), left] += d_keys[j * RET : (j + 1) * RET, :]
                d_window[pl.ds(a, RET), right] += d_values[j * RET : (j + 1) * RET, :]
    d_own[...] = d_window[0 : 3 * OWN_ROWS, :]
    d_shared[...] = d_window[3 * OWN_ROWS : 5 * OWN_ROWS, :].astype(LOW)


def product_kernel(*refs):
    attended, d_queries, whole = refs[:3]
    rows_refs = refs[3:7]
    near, far, partial = refs[7:]
    token_count, width = attended.shape
    across = (((1,), (1,)), ((), ()))
    total = None
    for k in range(4):
        block = slice(k * width, (k + 1) * width)
        out = lax.dot_general(
            attended[...], whole[block, width:], across, preferred_element_type=F32
        ).astype(LOW)
        back = lax.dot_general(
            d_queries[...], whole[block, 0:width], across, preferred_element_type=F32
        ).astype(LOW)
        target = near if k < 2 else far
        target[0, k % 2] = out
        target[1, k % 2] = back
        rows = rows_refs[k][0:token_count, :].astype(F32)
        gain = rows_refs[k][token_count : token_count + 1, :].astype(F32)
        part = jnp.sum(rows * gain * back.astype(F32), axis=1, keepdims=True)
        total = part if total is None else total + part
    partial[...] = total


def encoding_kernel(own, up, down, whole, near, far):
    width = whole.shape[1] // 2
    own_low = (own[...] + up[...].astype(F32) + down[...].astype(F32)).astype(LOW)
    across = (((1,), (1,)), ((), ()))
    for k in range(4):
        target = near if k < 2 else far
        target[k % 2] = lax.dot_general(
            own_low, whole[k * width : (k + 1) * width, :], across, preferred_element_type=F32
        ).astype(LOW)


def call(kernel, operands, outs, scratch=(), first_small=False):
    in_vmem = pl.BlockSpec(memory_space=pltpu.VMEM)
    specs = [in_vmem] * len(operands)
    if first_small:
        specs[0] = pl.BlockSpec(memory_space=pltpu.SMEM)
    return pl.pallas_call(
        kernel,
        out_shape=[jax.ShapeDtypeStruct(shape, dtype) for shape, dtype in outs],
        in_specs=specs,
        out_specs=[in_vmem] * len(outs),
        scratch_shapes=list(scratch),
        compiler_params=pltpu.CompilerParams(vmem_limit_bytes=40 * 1024 * 1024),
    )(*operands)


def reduce_blocks(near, far):
    arrived = move(far, flip_x)
    both = (near.astype(F32) + arrived.astype(F32)).astype(LOW)
    first = move(both[..., 0, :, :], swap)
    second = move(both[..., 1, :, :], cross)
    return first.astype(F32) + second.astype(F32)


def shards(hidden_rows, norm_gain, encodings, w_query, w_key, w_value, w_out, neighbours, grad_out):
    seq_count = lax.axis_size("seq")
    z, y, x, c = place()
    g = 2 * x + y
    token_count, width = hidden_rows.shape
    full_width = 4 * width

    key_value = move(jnp.concatenate([w_key, w_value], axis=0), swap)
    own_enc = move(encodings.reshape(OWN_ROWS, width), swap)
    query_out = move(jnp.concatenate([w_query, w_out.T], axis=0), swap)
    gain_rows = jnp.broadcast_to(norm_gain[None, :], (GAIN_ROWS, width))
    tokens = move(jnp.concatenate([hidden_rows, gain_rows], axis=0), swap)
    grads = move(grad_out, swap)
    chosen = move(neighbours, swap)

    enc_below = move(own_enc, ring_up)
    enc_above = move(own_enc, ring_down)
    if seq_count == 8:
        kv_pieces = line_pieces(key_value, z)
        qo_pieces = line_pieces(query_out, z)
    else:
        kv_pieces = any_pieces(key_value, z, y, g)
        qo_pieces = any_pieces(query_out, z, y, g)
    enc_blocks = spread(enc_below, True) + spread(own_enc, False) + spread(enc_above, True)
    token_blocks = spread(tokens, False)
    grad_blocks = spread(grads, False)

    normed, inv_rms, whole_kv, tables, shared = call(
        lambda *refs: table_kernel(len(kv_pieces), token_count, *refs),
        token_blocks + enc_blocks + kv_pieces,
        [
            ((token_count, full_width), LOW),
            ((token_count, 1), F32),
            ((full_width, 2 * width), LOW),
            ((3 * OWN_ROWS, 2 * width), LOW),
            ((2 * OWN_ROWS, 2 * width), LOW),
        ],
    )
    shared = move(shared, flip_core)
    inv_rms = inv_rms.reshape(token_count // 128, 128)
    inv_rms = jnp.where(c == y, inv_rms, move(inv_rms, flip_core)).reshape(token_count, 1)
    attended, d_queries, whole_qo, d_own, d_shared = call(
        lambda *refs: attention_kernel(len(qo_pieces), seq_count, *refs),
        [chosen, normed] + grad_blocks + qo_pieces + [tables, shared],
        [
            ((token_count, width), LOW),
            ((token_count, width), LOW),
            ((full_width, 2 * width), LOW),
            ((3 * OWN_ROWS, 2 * width), F32),
            ((2 * OWN_ROWS, 2 * width), LOW),
        ],
        [
            pltpu.VMEM((token_count, width), LOW),
            pltpu.VMEM((token_count, width), LOW),
            pltpu.VMEM((5 * OWN_ROWS, 2 * width), LOW),
            pltpu.VMEM((5 * OWN_ROWS, 2 * width), F32),
        ],
        first_small=True,
    )
    from_core = move(d_shared, flip_core)
    outer = from_core[OWN_ROWS:].astype(F32)
    to_below = (d_own[:OWN_ROWS] + jnp.where(c == 1, outer, 0.0)).astype(LOW)
    to_above = (d_own[2 * OWN_ROWS :] + jnp.where(c == 0, outer, 0.0)).astype(LOW)
    kept = d_own[OWN_ROWS : 2 * OWN_ROWS] + from_core[:OWN_ROWS].astype(F32)
    up = move(to_above, ring_up)
    down = move(to_below, ring_down)

    near, far, partial = call(
        product_kernel,
        [attended, d_queries, whole_qo] + token_blocks,
        [
            ((2, 2, token_count, width), LOW),
            ((2, 2, token_count, width), LOW),
            ((token_count, 1), F32),
        ],
    )
    sums = reduce_blocks(near, far)
    branch_out = sums[0].astype(LOW)
    partial = partial.reshape(token_count // 128, 128)
    partial = partial + move(partial, flip_x)
    partial = move(partial, swap) + move(partial, cross)
    statistic = partial.reshape(token_count, 1) / full_width
    gain = norm_gain.astype(F32)[None, :]
    grad_rows = (
        inv_rms * gain * sums[1] - hidden_rows.astype(F32) * inv_rms**3 * statistic
    ).astype(LOW)

    near_enc, far_enc = call(
        encoding_kernel,
        [kept, up, down, whole_kv],
        [((2, OWN_ROWS, width), LOW), ((2, OWN_ROWS, width), LOW)],
    )
    grad_encodings = reduce_blocks(near_enc, far_enc).astype(LOW).reshape(encodings.shape)
    return (branch_out, grad_rows, grad_encodings)


def solution(mesh):
    placed = (
        P("seq", "mp"),
        P("mp"),
        P("seq", None, "mp"),
        P("seq", "mp"),
        P("seq", "mp"),
        P("seq", "mp"),
        P("mp", "seq"),
        P("seq", None),
        P("seq", "mp"),
    )
    return jax.shard_map(
        shards,
        mesh=mesh,
        in_specs=placed,
        out_specs=(P("seq", "mp"), P("seq", "mp"), P("seq", None, "mp")),
        check_vma=False,
    )
```

time: 322 us -> 210 us (0.65)
  waiting for transfers between devices: 181 us -> 72.8 us
  starting transfers between devices: 9.83 us -> 86 us
  matrix products: 37.6 us -> 0 us
  blocking collectives: 32.7 us -> 0 us
  Pallas kernels: 0 us -> 17.2 us
  between operations: 14.5 us -> 1.1 us
  local copies, waits for them, and re-layouts: 34.7 us -> 22.2 us
    all_gather x4 -> x0, waiting for transfers between devices: 130 us -> none  [the longest x1 44.2 us: shards(): lax.all_gather(w_query, 'seq', axis=0, tiled=True)]
    ppermute x8 -> x57, starting transfers between devices: 9.34 us -> 86 us  [move(): return lax.ppermute(value, ('seq', 'mp'), joint(step))]
    ppermute x8 -> x57, waiting for transfers between devices: 21.6 us -> 72.8 us  [move(): return lax.ppermute(value, ('seq', 'mp'), joint(step))]
    dot_general x15 -> x0, matrix products: 37.6 us -> none  [the longest x1 7.25 us: shards(): jnp.einsum('chms,cmhe->cshe', d_scores, query_rows, preferred_element_typ...]
    all_gather x4 -> x0, blocking collectives: 32.7 us -> none  [the longest x1 9.36 us: shards(): lax.all_gather(hidden_rows, 'mp', axis=1, tiled=True)]
    unnamed x9 -> x0, waiting for transfers between devices: 29.5 us -> none
    pallas_call x0 -> x4, Pallas kernels: none -> 17.2 us  [call(): pl.pallas_call(kernel, out_shape=[jax.ShapeDtypeStruct(shape, dtype) for...]
    reshape x8 -> x0, local copies, waits for them, and re-layouts: 13.1 us -> none  [the longest x2 5.9 us: shards(): d_values.reshape(stretch_count * NBR, RET, local_width)]
  transfers between devices with their start and end apart: 15 -> 57, of which waited for: 9 -> 18; matrix products, arithmetic and copies ran while one was open for 14% -> 4% of each run, Pallas kernels for 0% -> 3%
where the time goes in v1:
time: 210 us; the launch traced here: 207 us
  starting transfers between devices  86 us (41%)
  waiting for transfers between devices  72.8 us (35%)
  local copies, waits for them, and re-layouts  22.2 us (11%)
  Pallas kernels  17.2 us (8%)
  other arithmetic  7.79 us (4%)
    ppermute x57, starting transfers between devices, move(): return lax.ppermute(value, ('seq', 'mp'), joint(step))  86 us
    ppermute x57, waiting for transfers between devices, move(): return lax.ppermute(value, ('seq', 'mp'), joint(step))  72.8 us
    unnamed x65, local copies, waits for them, and re-layouts  20.7 us
    pallas_call x4, Pallas kernels, call(): pl.pallas_call(kernel, out_shape=[jax.ShapeDtypeStruct(shape, dtype) for...  17.2 us
  transfers between devices with their start and end apart: 57, of which 18 were waited for; matrix products, arithmetic and copies ran while one was open for 4% of the time, Pallas kernels for 3%

profile of v1, /device:TPU:1, one launch (start us, length us, event | category | flops | bytes accessed | tf_op | source)
XLA Modules:
  0.0 207.1 jit_solution(10359962882037489152)
XLA Ops:
  1.6 4.5 %collective-permute-start.17 = (bf16[384,384]{1,0:T(8,128)(2,1)S(1)}, bf16[384,384]{1,0:T(8,128)(2,1)S(1)}, u32[]{:S(2)}, u32[]{:S(2)}) collective-permute-start(bf16[384,384]{1,0:T(8,128)(2,1)S(1)} %pad_maximum_fusion), channel_id=1, source_target_pairs={{0,0},{1,4},{2,2},{3,6},{4,1},{5,5},{6,3},{7,7},{8,8},{9,12},{10,1... | collective-permute-start | bytes 884744 | tf_op jit(solution)/shard_map/ppermute | solution.py:33
  7.2 1.9 collective-permute-start.32
  10.8 3.6 %collective-permute-start.1 = (bf16[272,384]{1,0:T(8,128)(2,1)S(1)}, bf16[272,384]{1,0:T(8,128)(2,1)S(1)}, u32[]{:S(2)}, u32[]{:S(2)}) collective-permute-start(bf16[272,384]{1,0:T(8,128)(2,1)S(1)} %pad_maximum_fusion.2), channel_id=1, source_target_pairs={{0,0},{1,4},{2,2},{3,6},{4,1},{5,5},{6,3},{7,7},{8,8},{9,12},{10,1... | collective-permute-start | bytes 626696 | tf_op jit(solution)/shard_map/ppermute | solution.py:33
  14.4 1.9 collective-permute-start.5
  16.4 3.6 %collective-permute-start.28 = (bf16[256,384]{1,0:T(8,128)(2,1)}, bf16[256,384]{1,0:T(8,128)(2,1)}, u32[]{:S(2)}, u32[]{:S(2)}) collective-permute-start(bf16[256,384]{1,0:T(8,128)(2,1)} %param.17), channel_id=1, source_target_pairs={{0,0},{1,4},{2,2},{3,6},{4,1},{5,5},{6,3},{7,7},{8,8},{9,12},{10,1... | collective-permute-start | bytes 589832 | tf_op jit(solution)/shard_map/ppermute | solution.py:33
  20.0 1.6 collective-permute-done.5.refs_8_
  21.6 3.3 %collective-permute-start.13 = (bf16[256,384]{1,0:T(8,128)(2,1)S(1)}, bf16[256,384]{1,0:T(8,128)(2,1)S(1)}, u32[]{:S(2)}, u32[]{:S(2)}) collective-permute-start(bf16[256,384]{1,0:T(8,128)(2,1)S(1)} %collective-permute-done.5.refs_8_), channel_id=1, source_target_pairs={{0,24},{1,25},{2,26},{3,27},{4,28},{5,29},{6,30},{7,31},{8,0},{9,1... | collective-permute-start | bytes 589832 | tf_op jit(solution)/shard_map/ppermute | solution.py:33
  25.0 1.2 collective-permute-start.11
  26.2 1.3 collective-permute-start.19
  27.5 4.0 %collective-permute-start.18 = (bf16[384,384]{1,0:T(8,128)(2,1)S(1)}, bf16[384,384]{1,0:T(8,128)(2,1)S(1)}, u32[]{:S(2)}, u32[]{:S(2)}) collective-permute-start(bf16[384,384]{1,0:T(8,128)(2,1)S(1)} %collective-permute-done.17.refs_16_), channel_id=1, source_target_pairs={{0,8},{1,9},{2,10},{3,11},{4,12},{5,13},{6,14},{7,15},{8,16},{9,17... | collective-permute-start | bytes 884744 | tf_op jit(solution)/shard_map/ppermute | solution.py:33
  31.9 1.5 collective-permute-start.2
  33.5 2.0 collective-permute-done.19.refs_18_
  35.5 1.3 collective-permute-start.20
  36.8 1.4 collective-permute-start.21
  38.2 3.3 %collective-permute-done.6.refs_4_ = bf16[256,384]{1,0:T(8,128)(2,1)S(1)} collective-permute-done((bf16[256,384]{1,0:T(8,128)(2,1)S(1)}, bf16[256,384]{1,0:T(8,128)(2,1)S(1)}, u32[]{:S(2)}, u32[]{:S(2)}) %collective-permute-start.6) | collective-permute-done | bytes 196640 | tf_op jit(solution)/shard_map/ppermute | solution.py:33
  42.3 1.8 collective-permute-start.14
  46.5 4.0 %collective-permute-start.23 = (bf16[384,384]{1,0:T(8,128)(2,1)S(1)}, bf16[384,384]{1,0:T(8,128)(2,1)S(1)}, u32[]{:S(2)}, u32[]{:S(2)}) collective-permute-start(bf16[384,384]{1,0:T(8,128)(2,1)S(1)} %collective-permute-done.17.refs_16_), channel_id=1, source_target_pairs={{0,1},{1,0},{2,3},{3,2},{4,5},{5,4},{6,7},{7,6},{8,9},{9,8},{10,11... | collective-permute-start | bytes 884744 | tf_op jit(solution)/shard_map/ppermute | solution.py:33
  51.1 1.3 collective-permute-start.34
  52.4 5.9 %collective-permute-start.33 = (bf16[384,384]{1,0:T(8,128)(2,1)S(1)}, bf16[384,384]{1,0:T(8,128)(2,1)S(1)}, u32[]{:S(2)}, u32[]{:S(2)}) collective-permute-start(bf16[384,384]{1,0:T(8,128)(2,1)S(1)} %collective-permute-done.32.refs_6_), channel_id=1, source_target_pairs={{0,8},{1,9},{2,10},{3,11},{4,12},{5,13},{6,14},{7,15},{8,16},{9,17... | collective-permute-start | bytes 884744 | tf_op jit(solution)/shard_map/ppermute | solution.py:33
  61.2 3.5 %collective-permute-done.8.refs_6_ = bf16[256,384]{1,0:T(8,128)(2,1)S(1)} collective-permute-done((bf16[256,384]{1,0:T(8,128)(2,1)S(1)}, bf16[256,384]{1,0:T(8,128)(2,1)S(1)}, u32[]{:S(2)}, u32[]{:S(2)}) %collective-permute-start.8) | collective-permute-done | bytes 196640 | tf_op jit(solution)/shard_map/ppermute | solution.py:33
  64.7 1.3 collective-permute-start.22
  68.7 5.2 %collective-permute-done.4.refs_3_.refs_6_ = bf16[272,384]{1,0:T(8,128)(2,1)S(1)} collective-permute-done((bf16[272,384]{1,0:T(8,128)(2,1)S(1)}, bf16[272,384]{1,0:T(8,128)(2,1)S(1)}, u32[]{:S(2)}, u32[]{:S(2)}) %collective-permute-start.4) | collective-permute-done | bytes 208928 | tf_op jit(solution)/shard_map/ppermute | solution.py:33
  76.0 1.9 collective-permute-done.9.refs_7_
  77.9 1.3 collective-permute-start.35
  80.8 1.5 collective-permute-start.38
  86.9 4.7 %shard_map.112 = (bf16[256,1536]{1,0:T(8,128)(2,1)S(1)}, f32[256,1]{1,0:T(8,128)S(1)}, bf16[1536,768]{1,0:T(8,128)(2,1)S(1)}, bf16[768,768]{1,0:T(8,128)(2,1)S(1)}, bf16[512,768]{1,0:T(8,128)(2,1)}) custom-call(bf16[272,384]{1,0:T(8,128)(2,1)S(1)} %collective-permute-done.1.refs_0_.refs_3_, bf16[272,384]{1,0:T(8,128)(2,1)S(1)} %collective-permute-done.2.refs_1_.refs_4_, ...), custom_call_target="tpu_custom_call" | custom-call | tf_op jit(solution)/shard_map/pallas_call | solution.py:266
  91.6 1.4 copy-done
  95.6 1.3 collective-permute-start.37
  97.0 2.8 %collective-permute-start = (s32[4,2]{1,0:T(4,128)S(1)}, s32[4,2]{1,0:T(4,128)S(1)}, u32[]{:S(2)}, u32[]{:S(2)}) collective-permute-start(s32[4,2]{1,0:T(4,128)S(1)} %copy.14), channel_id=1, source_target_pairs={{0,0},{1,4},{2,2},{3,6},{4,1},{5,5},{6,3},{7,7},{8,8},{9,12},{10,1... | collective-permute-start | bytes 104 | tf_op jit(solution)/shard_map/ppermute | solution.py:33
  99.8 2.4 %collective-permute-done.refs_0_ = s32[4,2]{1,0:T(4,128)S(1)} collective-permute-done((s32[4,2]{1,0:T(4,128)S(1)}, s32[4,2]{1,0:T(4,128)S(1)}, u32[]{:S(2)}, u32[]{:S(2)}) %collective-permute-start) | collective-permute-done | bytes 64 | tf_op jit(solution)/shard_map/ppermute | solution.py:33
  102.2 1.2 collective-permute-start.30
  103.7 4.3 %collective-permute-done.30.refs_4_ = bf16[256,384]{1,0:T(8,128)(2,1)S(1)} collective-permute-done((bf16[256,384]{1,0:T(8,128)(2,1)}, bf16[256,384]{1,0:T(8,128)(2,1)S(1)}, u32[]{:S(2)}, u32[]{:S(2)}) %collective-permute-start.30) | collective-permute-done | bytes 196640 | tf_op jit(solution)/shard_map/ppermute | solution.py:33
  108.0 2.1 %collective-permute-done.31.refs_5_ = bf16[256,384]{1,0:T(8,128)(2,1)S(1)} collective-permute-done((bf16[256,384]{1,0:T(8,128)(2,1)}, bf16[256,384]{1,0:T(8,128)(2,1)S(1)}, u32[]{:S(2)}, u32[]{:S(2)}) %collective-permute-start.31) | collective-permute-done | bytes 196640 | tf_op jit(solution)/shard_map/ppermute | solution.py:33
  113.4 1.3 copy-done.3
  120.8 9.4 %shard_map.113 = (bf16[256,384]{1,0:T(8,128)(2,1)S(1)}, bf16[256,384]{1,0:T(8,128)(2,1)S(1)}, bf16[1536,768]{1,0:T(8,128)(2,1)S(1)}, f32[768,768]{1,0:T(8,128)S(1)}, bf16[512,768]{1,0:T(8,128)(2,1)}) custom-call(s32[4,2]{1,0:T(4,128)S(1)} %collective-permute-done.refs_0_, bf16[256,1536]{1,0:T(8,128)(2,1)S(1)} %copy-done.5, ...), custom_call_target="tpu_custom_call" | custom-call | tf_op jit(solution)/shard_map/pallas_call | solution.py:266
  130.2 2.1 %shard_map.114 = (bf16[2,2,256,384]{3,2,1,0:T(8,128)(2,1)S(1)}, bf16[2,2,256,384]{3,2,1,0:T(8,128)(2,1)}, f32[256,1]{1,0:T(8,128)S(1)}) custom-call(bf16[256,384]{1,0:T(8,128)(2,1)S(1)} %get-tuple-element.21.refs_0_, bf16[256,384]{1,0:T(8,128)(2,1)S(1)} %get-tuple-element.22.refs_1_, bf16[1536,768]{1,0:T(8,128)(2,1)S(1)} %get-tuple-element.23.refs_2_, ...), custom_call_target="tpu_custom_call" | custom-call | tf_op jit(solution)/shard_map/pallas_call | solution.py:266
  135.8 16.7 %collective-permute-done.48 = f32[2,128]{1,0:T(2,128)S(1)} collective-permute-done((f32[2,128]{1,0:T(2,128)S(1)}, f32[2,128]{1,0:T(2,128)S(1)}, u32[]{:S(2)}, u32[]{:S(2)}) %collective-permute-start.48) | collective-permute-done | bytes 1056 | tf_op jit(solution)/shard_map/ppermute | solution.py:33
  152.8 4.2 %collective-permute-start.49 = (f32[2,128]{1,0:T(2,128)S(1)}, f32[2,128]{1,0:T(2,128)S(1)}, u32[]{:S(2)}, u32[]{:S(2)}) collective-permute-start(f32[2,128]{1,0:T(2,128)S(1)} %bitcast_add_fusion), channel_id=1, source_target_pairs={{0,0},{1,4},{2,2},{3,6},{4,1},{5,5},{6,3},{7,7},{8,8},{9,12},{10,1... | collective-permute-start | bytes 3080 | tf_op jit(solution)/shard_map/ppermute | solution.py:33
  157.0 1.6 add_convert_fusion
  158.7 1.9 collective-permute-start.45
  161.4 5.6 %collective-permute-start.52 = (bf16[256,768]{1,0:T(8,128)(2,1)S(1)}, bf16[256,768]{1,0:T(8,128)(2,1)S(1)}, u32[]{:S(2)}, u32[]{:S(2)}) collective-permute-start(bf16[256,768]{1,0:T(8,128)(2,1)S(1)} %get-tuple-element.36), channel_id=1, source_target_pairs={{0,8},{1,9},{2,10},{3,11},{4,12},{5,13},{6,14},{7,15},{8,16},{9,17... | collective-permute-start | bytes 1179656 | tf_op jit(solution)/shard_map/ppermute | solution.py:33
  167.0 9.0 %collective-permute-done.53.down = bf16[256,768]{1,0:T(8,128)(2,1)S(1)} collective-permute-done((bf16[256,768]{1,0:T(8,128)(2,1)S(1)}, bf16[256,768]{1,0:T(8,128)(2,1)S(1)}, u32[]{:S(2)}, u32[]{:S(2)}) %collective-permute-start.53) | collective-permute-done | bytes 393248 | tf_op jit(solution)/shard_map/ppermute | solution.py:33
  176.0 8.8 %collective-permute-done.52.up = bf16[256,768]{1,0:T(8,128)(2,1)S(1)} collective-permute-done((bf16[256,768]{1,0:T(8,128)(2,1)S(1)}, bf16[256,768]{1,0:T(8,128)(2,1)S(1)}, u32[]{:S(2)}, u32[]{:S(2)}) %collective-permute-start.52) | collective-permute-done | bytes 393248 | tf_op jit(solution)/shard_map/ppermute | solution.py:33
  185.8 1.3 collective-permute-start.54
  188.0 7.1 %collective-permute-done.54 = bf16[2,256,384]{2,1,0:T(8,128)(2,1)S(1)} collective-permute-done((bf16[2,256,384]{2,1,0:T(8,128)(2,1)S(1)}, bf16[2,256,384]{2,1,0:T(8,128)(2,1)S(1)}, u32[]{:S(2)}, u32[]{:S(2)}) %collective-permute-start.54) | collective-permute-done | bytes 393248 | tf_op jit(solution)/shard_map/ppermute | solution.py:33
  195.2 6.4 %collective-permute-start.55 = (bf16[256,384]{1,0:T(8,128)(2,1)S(1)}, bf16[256,384]{1,0:T(8,128)(2,1)S(1)}, u32[]{:S(2)}, u32[]{:S(2)}) collective-permute-start(bf16[256,384]{1,0:T(8,128)(2,1)S(1)} %get-tuple-element.40), channel_id=1, source_target_pairs={{0,0},{1,4},{2,2},{3,6},{4,1},{5,5},{6,3},{7,7},{8,8},{9,12},{10,1... | collective-permute-start | bytes 589832 | tf_op jit(solution)/shard_map/ppermute | solution.py:33
  202.4 2.6 %collective-permute-done.55 = bf16[256,384]{1,0:T(8,128)(2,1)S(1)} collective-permute-done((bf16[256,384]{1,0:T(8,128)(2,1)S(1)}, bf16[256,384]{1,0:T(8,128)(2,1)S(1)}, u32[]{:S(2)}, u32[]{:S(2)}) %collective-permute-start.55) | collective-permute-done | bytes 196640 | tf_op jit(solution)/shard_map/ppermute | solution.py:33
  205.0 1.4 collective-permute-done.56
  (156 shorter events, 42.6 us)
Async XLA Ops:
  1.6 24.5 %collective-permute-start.17 = (bf16[384,384]{1,0:T(8,128)(2,1)S(1)}, bf16[384,384]{1,0:T(8,128)(2,1)S(1)}, u32[]{:S(2)}, u32[]{:S(2)}) collective-permute-start(bf16[384,384]{1,0:T(8,128)(2,1)S(1)} %pad_maximum_fusion), channel_id=1, source_target_pairs={{0,0},{1,4},{2,2},{3,6},{4,1},{5,5},{6,3},{7,7},{8,8},{9,12},{10,1... | collective-permute-start | bytes 884744 | tf_op jit(solution)/shard_map/ppermute | solution.py:33
  7.2 20.3 %collective-permute-start.32 = (bf16[384,384]{1,0:T(8,128)(2,1)S(1)}, bf16[384,384]{1,0:T(8,128)(2,1)S(1)}, u32[]{:S(2)}, u32[]{:S(2)}) collective-permute-start(bf16[384,384]{1,0:T(8,128)(2,1)S(1)} %pad_maximum_fusion.1), channel_id=1, source_target_pairs={{0,0},{1,4},{2,2},{3,6},{4,1},{5,5},{6,3},{7,7},{8,8},{9,12},{10,1... | collective-permute-start | bytes 884744 | tf_op jit(solution)/shard_map/ppermute | solution.py:33
  10.8 15.4 %collective-permute-start.1 = (bf16[272,384]{1,0:T(8,128)(2,1)S(1)}, bf16[272,384]{1,0:T(8,128)(2,1)S(1)}, u32[]{:S(2)}, u32[]{:S(2)}) collective-permute-start(bf16[272,384]{1,0:T(8,128)(2,1)S(1)} %pad_maximum_fusion.2), channel_id=1, source_target_pairs={{0,0},{1,4},{2,2},{3,6},{4,1},{5,5},{6,3},{7,7},{8,8},{9,12},{10,1... | collective-permute-start | bytes 626696 | tf_op jit(solution)/shard_map/ppermute | solution.py:33
  14.4 7.2 %collective-permute-start.5 = (bf16[256,384]{1,0:T(8,128)(2,1)}, bf16[256,384]{1,0:T(8,128)(2,1)S(1)}, u32[]{:S(2)}, u32[]{:S(2)}) collective-permute-start(bf16[256,384]{1,0:T(8,128)(2,1)} %bitcast.37), channel_id=1, source_target_pairs={{0,0},{1,4},{2,2},{3,6},{4,1},{5,5},{6,3},{7,7},{8,8},{9,12},{10,1... | collective-permute-start | bytes 589832 | tf_op jit(solution)/shard_map/ppermute | solution.py:33
  16.4 8.6 %collective-permute-start.28 = (bf16[256,384]{1,0:T(8,128)(2,1)}, bf16[256,384]{1,0:T(8,128)(2,1)}, u32[]{:S(2)}, u32[]{:S(2)}) collective-permute-start(bf16[256,384]{1,0:T(8,128)(2,1)} %param.17), channel_id=1, source_target_pairs={{0,0},{1,4},{2,2},{3,6},{4,1},{5,5},{6,3},{7,7},{8,8},{9,12},{10,1... | collective-permute-start | bytes 589832 | tf_op jit(solution)/shard_map/ppermute | solution.py:33
  21.6 9.9 %collective-permute-start.13 = (bf16[256,384]{1,0:T(8,128)(2,1)S(1)}, bf16[256,384]{1,0:T(8,128)(2,1)S(1)}, u32[]{:S(2)}, u32[]{:S(2)}) collective-permute-start(bf16[256,384]{1,0:T(8,128)(2,1)S(1)} %collective-permute-done.5.refs_8_), channel_id=1, source_target_pairs={{0,24},{1,25},{2,26},{3,27},{4,28},{5,29},{6,30},{7,31},{8,0},{9,1... | collective-permute-start | bytes 589832 | tf_op jit(solution)/shard_map/ppermute | solution.py:33
  25.0 6.9 %collective-permute-start.11 = (bf16[256,384]{1,0:T(8,128)(2,1)S(1)}, bf16[256,384]{1,0:T(8,128)(2,1)S(1)}, u32[]{:S(2)}, u32[]{:S(2)}) collective-permute-start(bf16[256,384]{1,0:T(8,128)(2,1)S(1)} %collective-permute-done.5.refs_8_), channel_id=1, source_target_pairs={{0,2},{1,3},{2,0},{3,1},{4,6},{5,7},{6,4},{7,5},{8,10},{9,11},{10,... | collective-permute-start | bytes 589832 | tf_op jit(solution)/shard_map/ppermute | solution.py:33
  26.2 7.1 %collective-permute-start.10 = (bf16[256,384]{1,0:T(8,128)(2,1)S(1)}, bf16[256,384]{1,0:T(8,128)(2,1)S(1)}, u32[]{:S(2)}, u32[]{:S(2)}) collective-permute-start(bf16[256,384]{1,0:T(8,128)(2,1)S(1)} %collective-permute-done.5.refs_8_), channel_id=1, source_target_pairs={{0,4},{1,5},{2,6},{3,7},{4,0},{5,1},{6,2},{7,3},{8,12},{9,13},{10,... | collective-permute-start | bytes 589832 | tf_op jit(solution)/shard_map/ppermute | solution.py:33
  26.2 9.3 %collective-permute-start.19 = (bf16[384,384]{1,0:T(8,128)(2,1)S(1)}, bf16[384,384]{1,0:T(8,128)(2,1)S(1)}, u32[]{:S(2)}, u32[]{:S(2)}) collective-permute-start(bf16[384,384]{1,0:T(8,128)(2,1)S(1)} %collective-permute-done.17.refs_16_), channel_id=1, source_target_pairs={{8,0},{9,1},{10,2},{11,3},{12,4},{13,5},{14,6},{15,7},{16,8},{17,9... | collective-permute-start | bytes 884744 | tf_op jit(solution)/shard_map/ppermute | solution.py:33
  27.5 9.3 %collective-permute-start.18 = (bf16[384,384]{1,0:T(8,128)(2,1)S(1)}, bf16[384,384]{1,0:T(8,128)(2,1)S(1)}, u32[]{:S(2)}, u32[]{:S(2)}) collective-permute-start(bf16[384,384]{1,0:T(8,128)(2,1)S(1)} %collective-permute-done.17.refs_16_), channel_id=1, source_target_pairs={{0,8},{1,9},{2,10},{3,11},{4,12},{5,13},{6,14},{7,15},{8,16},{9,17... | collective-permute-start | bytes 884744 | tf_op jit(solution)/shard_map/ppermute | solution.py:33
  31.5 10.7 %collective-permute-start.3 = (bf16[272,384]{1,0:T(8,128)(2,1)S(1)}, bf16[272,384]{1,0:T(8,128)(2,1)S(1)}, u32[]{:S(2)}, u32[]{:S(2)}) collective-permute-start(bf16[272,384]{1,0:T(8,128)(2,1)S(1)} %collective-permute-done.1.refs_0_.refs_3_), channel_id=1, source_target_pairs={{0,2},{1,3},{2,0},{3,1},{4,6},{5,7},{6,4},{7,5},{8,10},{9,11},{10,... | collective-permute-start | bytes 626696 | tf_op jit(solution)/shard_map/ppermute | solution.py:33
  31.9 12.2 %collective-permute-start.2 = (bf16[272,384]{1,0:T(8,128)(2,1)S(1)}, bf16[272,384]{1,0:T(8,128)(2,1)S(1)}, u32[]{:S(2)}, u32[]{:S(2)}) collective-permute-start(bf16[272,384]{1,0:T(8,128)(2,1)S(1)} %collective-permute-done.1.refs_0_.refs_3_), channel_id=1, source_target_pairs={{0,4},{1,5},{2,6},{3,7},{4,0},{5,1},{6,2},{7,3},{8,12},{9,13},{10,... | collective-permute-start | bytes 626696 | tf_op jit(solution)/shard_map/ppermute | solution.py:33
  33.3 8.1 %collective-permute-start.6 = (bf16[256,384]{1,0:T(8,128)(2,1)S(1)}, bf16[256,384]{1,0:T(8,128)(2,1)S(1)}, u32[]{:S(2)}, u32[]{:S(2)}) collective-permute-start(bf16[256,384]{1,0:T(8,128)(2,1)S(1)} %collective-permute-done.5.refs_8_), channel_id=1, source_target_pairs={{0,8},{1,9},{2,10},{3,11},{4,12},{5,13},{6,14},{7,15},{8,16},{9,17... | collective-permute-start | bytes 589832 | tf_op jit(solution)/shard_map/ppermute | solution.py:33
  35.5 22.9 %collective-permute-start.20 = (bf16[384,384]{1,0:T(8,128)(2,1)S(1)}, bf16[384,384]{1,0:T(8,128)(2,1)}, u32[]{:S(2)}, u32[]{:S(2)}) collective-permute-start(bf16[384,384]{1,0:T(8,128)(2,1)S(1)} %collective-permute-done.19.refs_18_), channel_id=1, source_target_pairs={{8,0},{9,1},{10,2},{11,3},{12,4},{13,5},{14,6},{15,7},{16,8},{17,9... | collective-permute-start | bytes 884744 | tf_op jit(solution)/shard_map/ppermute | solution.py:33
  36.8 21.7 %collective-permute-start.21 = (bf16[384,384]{1,0:T(8,128)(2,1)S(1)}, bf16[384,384]{1,0:T(8,128)(2,1)}, u32[]{:S(2)}, u32[]{:S(2)}) collective-permute-start(bf16[384,384]{1,0:T(8,128)(2,1)S(1)} %collective-permute-done.18.refs_17_), channel_id=1, source_target_pairs={{8,16},{9,17},{10,18},{11,19},{12,20},{13,21},{14,22},{15,23},{16,... | collective-permute-start | bytes 884744 | tf_op jit(solution)/shard_map/ppermute | solution.py:33
  42.3 8.2 %collective-permute-start.14 = (bf16[256,384]{1,0:T(8,128)(2,1)S(1)}, bf16[256,384]{1,0:T(8,128)(2,1)S(1)}, u32[]{:S(2)}, u32[]{:S(2)}) collective-permute-start(bf16[256,384]{1,0:T(8,128)(2,1)S(1)} %collective-permute-done.13.refs_12_), channel_id=1, source_target_pairs={{0,4},{1,5},{2,6},{3,7},{4,0},{5,1},{6,2},{7,3},{8,12},{9,13},{10,... | collective-permute-start | bytes 589832 | tf_op jit(solution)/shard_map/ppermute | solution.py:33
  44.1 8.3 %collective-permute-start.12 = (bf16[256,384]{1,0:T(8,128)(2,1)S(1)}, bf16[256,384]{1,0:T(8,128)(2,1)}, u32[]{:S(2)}, u32[]{:S(2)}) collective-permute-start(bf16[256,384]{1,0:T(8,128)(2,1)S(1)} %collective-permute-done.10.refs_9_), channel_id=1, source_target_pairs={{0,2},{1,3},{2,0},{3,1},{4,6},{5,7},{6,4},{7,5},{8,10},{9,11},{10,... | collective-permute-start | bytes 589832 | tf_op jit(solution)/shard_map/ppermute | solution.py:33
  46.5 20.7 %collective-permute-start.23 = (bf16[384,384]{1,0:T(8,128)(2,1)S(1)}, bf16[384,384]{1,0:T(8,128)(2,1)S(1)}, u32[]{:S(2)}, u32[]{:S(2)}) collective-permute-start(bf16[384,384]{1,0:T(8,128)(2,1)S(1)} %collective-permute-done.17.refs_16_), channel_id=1, source_target_pairs={{0,1},{1,0},{2,3},{3,2},{4,5},{5,4},{6,7},{7,6},{8,9},{9,8},{10,11... | collective-permute-start | bytes 884744 | tf_op jit(solution)/shard_map/ppermute | solution.py:33
  51.1 16.1 %collective-permute-start.34 = (bf16[384,384]{1,0:T(8,128)(2,1)S(1)}, bf16[384,384]{1,0:T(8,128)(2,1)S(1)}, u32[]{:S(2)}, u32[]{:S(2)}) collective-permute-start(bf16[384,384]{1,0:T(8,128)(2,1)S(1)} %collective-permute-done.32.refs_6_), channel_id=1, source_target_pairs={{8,0},{9,1},{10,2},{11,3},{12,4},{13,5},{14,6},{15,7},{16,8},{17,9... | collective-permute-start | bytes 884744 | tf_op jit(solution)/shard_map/ppermute | solution.py:33
  52.4 15.8 %collective-permute-start.33 = (bf16[384,384]{1,0:T(8,128)(2,1)S(1)}, bf16[384,384]{1,0:T(8,128)(2,1)S(1)}, u32[]{:S(2)}, u32[]{:S(2)}) collective-permute-start(bf16[384,384]{1,0:T(8,128)(2,1)S(1)} %collective-permute-done.32.refs_6_), channel_id=1, source_target_pairs={{0,8},{1,9},{2,10},{3,11},{4,12},{5,13},{6,14},{7,15},{8,16},{9,17... | collective-permute-start | bytes 884744 | tf_op jit(solution)/shard_map/ppermute | solution.py:33
  58.4 6.3 %collective-permute-start.8 = (bf16[256,384]{1,0:T(8,128)(2,1)S(1)}, bf16[256,384]{1,0:T(8,128)(2,1)S(1)}, u32[]{:S(2)}, u32[]{:S(2)}) collective-permute-start(bf16[256,384]{1,0:T(8,128)(2,1)S(1)} %collective-permute-done.6.refs_4_), channel_id=1, source_target_pairs={{0,2},{1,3},{2,0},{3,1},{4,6},{5,7},{6,4},{7,5},{8,10},{9,11},{10,... | collective-permute-start | bytes 589832 | tf_op jit(solution)/shard_map/ppermute | solution.py:33
  58.5 7.5 %collective-permute-start.7 = (bf16[256,384]{1,0:T(8,128)(2,1)S(1)}, bf16[256,384]{1,0:T(8,128)(2,1)S(1)}, u32[]{:S(2)}, u32[]{:S(2)}) collective-permute-start(bf16[256,384]{1,0:T(8,128)(2,1)S(1)} %collective-permute-done.6.refs_4_), channel_id=1, source_target_pairs={{0,4},{1,5},{2,6},{3,7},{4,0},{5,1},{6,2},{7,3},{8,12},{9,13},{10,... | collective-permute-start | bytes 589832 | tf_op jit(solution)/shard_map/ppermute | solution.py:33
  64.7 10.8 %collective-permute-start.22 = (bf16[384,384]{1,0:T(8,128)(2,1)S(1)}, bf16[384,384]{1,0:T(8,128)(2,1)S(1)}, u32[]{:S(2)}, u32[]{:S(2)}) collective-permute-start(bf16[384,384]{1,0:T(8,128)(2,1)S(1)} %broadcast_select_fusion.1.refs_19_), channel_id=1, source_target_pairs={{8,0},{9,1},{10,2},{11,3},{12,4},{13,5},{14,6},{15,7},{16,24},{17,... | collective-permute-start | bytes 884744 | tf_op jit(solution)/shard_map/ppermute | solution.py:33
  66.0 13.2 %collective-permute-start.25 = (bf16[384,384]{1,0:T(8,128)(2,1)S(1)}, bf16[384,384]{1,0:T(8,128)(2,1)S(1)}, u32[]{:S(2)}, u32[]{:S(2)}) collective-permute-start(bf16[384,384]{1,0:T(8,128)(2,1)S(1)} %collective-permute-done.19.refs_18_), channel_id=1, source_target_pairs={{0,1},{1,0},{2,3},{3,2},{4,5},{5,4},{6,7},{7,6},{8,9},{9,8},{10,11... | collective-permute-start | bytes 884744 | tf_op jit(solution)/shard_map/ppermute | solution.py:33
  67.2 6.7 %collective-permute-start.4 = (bf16[272,384]{1,0:T(8,128)(2,1)S(1)}, bf16[272,384]{1,0:T(8,128)(2,1)S(1)}, u32[]{:S(2)}, u32[]{:S(2)}) collective-permute-start(bf16[272,384]{1,0:T(8,128)(2,1)S(1)} %collective-permute-done.2.refs_1_.refs_4_), channel_id=1, source_target_pairs={{0,2},{1,3},{2,0},{3,1},{4,6},{5,7},{6,4},{7,5},{8,10},{9,11},{10,... | collective-permute-start | bytes 626696 | tf_op jit(solution)/shard_map/ppermute | solution.py:33
  67.2 7.5 %collective-permute-start.16 = (bf16[256,384]{1,0:T(8,128)(2,1)}, bf16[256,384]{1,0:T(8,128)(2,1)S(1)}, u32[]{:S(2)}, u32[]{:S(2)}) collective-permute-start(bf16[256,384]{1,0:T(8,128)(2,1)} %collective-permute-done.15.refs_14_), channel_id=1, source_target_pairs={{0,4},{1,5},{2,6},{3,7},{4,0},{5,1},{6,2},{7,3},{8,12},{9,13},{10,... | collective-permute-start | bytes 589832 | tf_op jit(solution)/shard_map/ppermute | solution.py:33
  68.2 9.6 %collective-permute-start.9 = (bf16[256,384]{1,0:T(8,128)(2,1)S(1)}, bf16[256,384]{1,0:T(8,128)(2,1)S(1)}, u32[]{:S(2)}, u32[]{:S(2)}) collective-permute-start(bf16[256,384]{1,0:T(8,128)(2,1)S(1)} %collective-permute-done.8.refs_6_), channel_id=1, source_target_pairs={{0,4},{1,5},{2,6},{3,7},{4,0},{5,1},{6,2},{7,3},{8,12},{9,13},{10,... | collective-permute-start | bytes 589832 | tf_op jit(solution)/shard_map/ppermute | solution.py:33
  74.8 6.1 %collective-permute-start.26 = (bf16[384,384]{1,0:T(8,128)(2,1)S(1)}, bf16[384,384]{1,0:T(8,128)(2,1)S(1)}, u32[]{:S(2)}, u32[]{:S(2)}) collective-permute-start(bf16[384,384]{1,0:T(8,128)(2,1)S(1)} %broadcast_select_fusion.1.refs_19_), channel_id=1, source_target_pairs={{0,1},{1,0},{2,3},{3,2},{4,5},{5,4},{6,7},{7,6},{8,9},{9,8},{10,11... | collective-permute-start | bytes 884744 | tf_op jit(solution)/shard_map/ppermute | solution.py:33
  75.5 6.8 %collective-permute-start.27 = (bf16[384,384]{1,0:T(8,128)(2,1)S(1)}, bf16[384,384]{1,0:T(8,128)(2,1)S(1)}, u32[]{:S(2)}, u32[]{:S(2)}) collective-permute-start(bf16[384,384]{1,0:T(8,128)(2,1)S(1)} %collective-permute-done.22.refs_20_), channel_id=1, source_target_pairs={{0,1},{1,0},{2,3},{3,2},{4,5},{5,4},{6,7},{7,6},{8,9},{9,8},{10,11... | collective-permute-start | bytes 884744 | tf_op jit(solution)/shard_map/ppermute | solution.py:33
  77.9 17.7 %collective-permute-start.35 = (bf16[384,384]{1,0:T(8,128)(2,1)S(1)}, bf16[384,384]{1,0:T(8,128)(2,1)S(1)}, u32[]{:S(2)}, u32[]{:S(2)}) collective-permute-start(bf16[384,384]{1,0:T(8,128)(2,1)S(1)} %collective-permute-done.34.refs_8_), channel_id=1, source_target_pairs={{8,0},{9,1},{10,2},{11,3},{12,4},{13,5},{14,6},{15,7},{16,8},{17,9... | collective-permute-start | bytes 884744 | tf_op jit(solution)/shard_map/ppermute | solution.py:33
  79.2 16.4 %collective-permute-start.36 = (bf16[384,384]{1,0:T(8,128)(2,1)S(1)}, bf16[384,384]{1,0:T(8,128)(2,1)S(1)}, u32[]{:S(2)}, u32[]{:S(2)}) collective-permute-start(bf16[384,384]{1,0:T(8,128)(2,1)S(1)} %collective-permute-done.33.refs_7_), channel_id=1, source_target_pairs={{8,16},{9,17},{10,18},{11,19},{12,20},{13,21},{14,22},{15,23},{16,... | collective-permute-start | bytes 884744 | tf_op jit(solution)/shard_map/ppermute | solution.py:33
  79.9 23.6 %collective-permute-start.29 = (bf16[256,384]{1,0:T(8,128)(2,1)}, bf16[256,384]{1,0:T(8,128)(2,1)}, u32[]{:S(2)}, u32[]{:S(2)}) collective-permute-start(bf16[256,384]{1,0:T(8,128)(2,1)} %collective-permute-done.28.refs_2_), channel_id=1, source_target_pairs={{0,4},{1,5},{2,6},{3,7},{4,0},{5,1},{6,2},{7,3},{8,12},{9,13},{10,... | collective-permute-start | bytes 589832 | tf_op jit(solution)/shard_map/ppermute | solution.py:33
  80.8 29.3 %collective-permute-start.38 = (bf16[384,384]{1,0:T(8,128)(2,1)S(1)}, bf16[384,384]{1,0:T(8,128)(2,1)}, u32[]{:S(2)}, u32[]{:S(2)}) collective-permute-start(bf16[384,384]{1,0:T(8,128)(2,1)S(1)} %collective-permute-done.32.refs_6_), channel_id=1, source_target_pairs={{0,1},{1,0},{2,3},{3,2},{4,5},{5,4},{6,7},{7,6},{8,9},{9,8},{10,11... | collective-permute-start | bytes 884744 | tf_op jit(solution)/shard_map/ppermute | solution.py:33
  95.6 16.9 %collective-permute-start.43 = (bf16[512,768]{1,0:T(8,128)(2,1)}, bf16[512,768]{1,0:T(8,128)(2,1)S(1)}, u32[]{:S(2)}, u32[]{:S(2)}) collective-permute-start(bf16[512,768]{1,0:T(8,128)(2,1)} %get-tuple-element.20), channel_id=1, source_target_pairs={{0,1},{1,0},{2,3},{3,2},{4,5},{5,4},{6,7},{7,6},{8,9},{9,8},{10,11... | collective-permute-start | bytes 2359304 | tf_op jit(solution)/shard_map/ppermute | solution.py:33
  95.6 15.0 %collective-permute-start.37 = (bf16[384,384]{1,0:T(8,128)(2,1)S(1)}, bf16[384,384]{1,0:T(8,128)(2,1)S(1)}, u32[]{:S(2)}, u32[]{:S(2)}) collective-permute-start(bf16[384,384]{1,0:T(8,128)(2,1)S(1)} %broadcast_select_fusion.refs_9_), channel_id=1, source_target_pairs={{8,0},{9,1},{10,2},{11,3},{12,4},{13,5},{14,6},{15,7},{16,24},{17,... | collective-permute-start | bytes 884744 | tf_op jit(solution)/shard_map/ppermute | solution.py:33
  103.4 6.6 %collective-permute-start.31 = (bf16[256,384]{1,0:T(8,128)(2,1)}, bf16[256,384]{1,0:T(8,128)(2,1)S(1)}, u32[]{:S(2)}, u32[]{:S(2)}) collective-permute-start(bf16[256,384]{1,0:T(8,128)(2,1)} %collective-permute-done.29.refs_3_), channel_id=1, source_target_pairs={{0,2},{1,3},{2,0},{3,1},{4,6},{5,7},{6,4},{7,5},{8,10},{9,11},{10,... | collective-permute-start | bytes 589832 | tf_op jit(solution)/shard_map/ppermute | solution.py:33
  133.2 23.8 %collective-permute-start.44 = (bf16[2,2,256,384]{3,2,1,0:T(8,128)(2,1)}, bf16[2,2,256,384]{3,2,1,0:T(8,128)(2,1)}, u32[]{:S(2)}, u32[]{:S(2)}) collective-permute-start(bf16[2,2,256,384]{3,2,1,0:T(8,128)(2,1)} %get-tuple-element.25), channel_id=1, source_target_pairs={{0,2},{1,3},{2,0},{3,1},{4,6},{5,7},{6,4},{7,5},{8,10},{9,11},{10,... | collective-permute-start | bytes 2359304 | tf_op jit(solution)/shard_map/ppermute | solution.py:33
  134.4 26.2 %collective-permute-start.51 = (bf16[512,768]{1,0:T(8,128)(2,1)}, bf16[512,768]{1,0:T(8,128)(2,1)S(1)}, u32[]{:S(2)}, u32[]{:S(2)}) collective-permute-start(bf16[512,768]{1,0:T(8,128)(2,1)} %get-tuple-element.29), channel_id=1, source_target_pairs={{0,1},{1,0},{2,3},{3,2},{4,5},{5,4},{6,7},{7,6},{8,9},{9,8},{10,11... | collective-permute-start | bytes 2359304 | tf_op jit(solution)/shard_map/ppermute | solution.py:33
  135.0 17.4 %collective-permute-start.48 = (f32[2,128]{1,0:T(2,128)S(1)}, f32[2,128]{1,0:T(2,128)S(1)}, u32[]{:S(2)}, u32[]{:S(2)}) collective-permute-start(f32[2,128]{1,0:T(2,128)S(1)} %bitcast.35), channel_id=1, source_target_pairs={{0,2},{1,3},{2,0},{3,1},{4,6},{5,7},{6,4},{7,5},{8,10},{9,11},{10,... | collective-permute-start | bytes 3080 | tf_op jit(solution)/shard_map/ppermute | solution.py:33
  135.5 25.4 %collective-permute-start.47 = (f32[2,128]{1,0:T(2,128)S(1)}, f32[2,128]{1,0:T(2,128)S(1)}, u32[]{:S(2)}, u32[]{:S(2)}) collective-permute-start(f32[2,128]{1,0:T(2,128)S(1)} %bitcast.36), channel_id=1, source_target_pairs={{0,1},{1,0},{2,3},{3,2},{4,5},{5,4},{6,7},{7,6},{8,9},{9,8},{10,11... | collective-permute-start | bytes 3080 | tf_op jit(solution)/shard_map/ppermute | solution.py:33
  152.5 9.0 %collective-permute-start.50 = (f32[2,128]{1,0:T(2,128)S(1)}, f32[2,128]{1,0:T(2,128)S(1)}, u32[]{:S(2)}, u32[]{:S(2)}) collective-permute-start(f32[2,128]{1,0:T(2,128)S(1)} %bitcast_add_fusion), channel_id=1, source_target_pairs={{0,1},{1,5},{2,3},{3,7},{4,0},{5,4},{6,2},{7,6},{8,9},{9,13},{10,1... | collective-permute-start | bytes 3080 | tf_op jit(solution)/shard_map/ppermute | solution.py:33
  152.8 14.3 %collective-permute-start.49 = (f32[2,128]{1,0:T(2,128)S(1)}, f32[2,128]{1,0:T(2,128)S(1)}, u32[]{:S(2)}, u32[]{:S(2)}) collective-permute-start(f32[2,128]{1,0:T(2,128)S(1)} %bitcast_add_fusion), channel_id=1, source_target_pairs={{0,0},{1,4},{2,2},{3,6},{4,1},{5,5},{6,3},{7,7},{8,8},{9,12},{10,1... | collective-permute-start | bytes 3080 | tf_op jit(solution)/shard_map/ppermute | solution.py:33
  158.7 28.4 %collective-permute-start.45 = (bf16[2,256,384]{2,1,0:T(8,128)(2,1)S(1)}, bf16[2,256,384]{2,1,0:T(8,128)(2,1)S(1)}, u32[]{:S(2)}, u32[]{:S(2)}) collective-permute-start(bf16[2,256,384]{2,1,0:T(8,128)(2,1)S(1)} %get-tuple-element.38), channel_id=1, source_target_pairs={{0,0},{1,4},{2,2},{3,6},{4,1},{5,5},{6,3},{7,7},{8,8},{9,12},{10,1... | collective-permute-start | bytes 1179656 | tf_op jit(solution)/shard_map/ppermute | solution.py:33
  160.6 26.4 %collective-permute-start.46 = (bf16[2,256,384]{2,1,0:T(8,128)(2,1)S(1)}, bf16[2,256,384]{2,1,0:T(8,128)(2,1)S(1)}, u32[]{:S(2)}, u32[]{:S(2)}) collective-permute-start(bf16[2,256,384]{2,1,0:T(8,128)(2,1)S(1)} %get-tuple-element.39), channel_id=1, source_target_pairs={{0,1},{1,5},{2,3},{3,7},{4,0},{5,4},{6,2},{7,6},{8,9},{9,13},{10,1... | collective-permute-start | bytes 1179656 | tf_op jit(solution)/shard_map/ppermute | solution.py:33
  160.9 15.1 %collective-permute-start.53 = (bf16[256,768]{1,0:T(8,128)(2,1)S(1)}, bf16[256,768]{1,0:T(8,128)(2,1)S(1)}, u32[]{:S(2)}, u32[]{:S(2)}) collective-permute-start(bf16[256,768]{1,0:T(8,128)(2,1)S(1)} %get-tuple-element.35), channel_id=1, source_target_pairs={{0,24},{1,25},{2,26},{3,27},{4,28},{5,29},{6,30},{7,31},{8,0},{9,1... | collective-permute-start | bytes 1179656 | tf_op jit(solution)/shard_map/ppermute | solution.py:33
  161.4 23.4 %collective-permute-start.52 = (bf16[256,768]{1,0:T(8,128)(2,1)S(1)}, bf16[256,768]{1,0:T(8,128)(2,1)S(1)}, u32[]{:S(2)}, u32[]{:S(2)}) collective-permute-start(bf16[256,768]{1,0:T(8,128)(2,1)S(1)} %get-tuple-element.36), channel_id=1, source_target_pairs={{0,8},{1,9},{2,10},{3,11},{4,12},{5,13},{6,14},{7,15},{8,16},{9,17... | collective-permute-start | bytes 1179656 | tf_op jit(solution)/shard_map/ppermute | solution.py:33
  185.8 9.3 %collective-permute-start.54 = (bf16[2,256,384]{2,1,0:T(8,128)(2,1)S(1)}, bf16[2,256,384]{2,1,0:T(8,128)(2,1)S(1)}, u32[]{:S(2)}, u32[]{:S(2)}) collective-permute-start(bf16[2,256,384]{2,1,0:T(8,128)(2,1)S(1)} %get-tuple-element.32), channel_id=1, source_target_pairs={{0,2},{1,3},{2,0},{3,1},{4,6},{5,7},{6,4},{7,5},{8,10},{9,11},{10,... | collective-permute-start | bytes 1179656 | tf_op jit(solution)/shard_map/ppermute | solution.py:33
  195.2 9.8 %collective-permute-start.55 = (bf16[256,384]{1,0:T(8,128)(2,1)S(1)}, bf16[256,384]{1,0:T(8,128)(2,1)S(1)}, u32[]{:S(2)}, u32[]{:S(2)}) collective-permute-start(bf16[256,384]{1,0:T(8,128)(2,1)S(1)} %get-tuple-element.40), channel_id=1, source_target_pairs={{0,0},{1,4},{2,2},{3,6},{4,1},{5,5},{6,3},{7,7},{8,8},{9,12},{10,1... | collective-permute-start | bytes 589832 | tf_op jit(solution)/shard_map/ppermute | solution.py:33
  (41 other events, 345.6 us)

commit v2 on v1

v2 whole, which is shorter than its diff:
```python
import jax
import jax.numpy as jnp
from jax import lax
from jax.experimental import pallas as pl
from jax.experimental.pallas import tpu as pltpu
from jax.sharding import PartitionSpec as P

HD = 128
STRETCH = 64
NBR = 2
RET = 128
OWN_DEV = 2
OWN_ROWS = OWN_DEV * RET
EXTRA = 16
LOW = jnp.bfloat16
F32 = jnp.float32
epsilon = 1e-05
ANY = pl.BlockSpec(memory_space=pl.ANY)
VMEM = pl.BlockSpec(memory_space=pltpu.VMEM)
SMEM = pl.BlockSpec(memory_space=pltpu.SMEM)
ACROSS = (((1,), (1,)), ((), ()))
DOWN = (((0,), (0,)), ((), ()))


def move(value, step):
    seq_count, mp_count = lax.axis_size("seq"), lax.axis_size("mp")
    z_count = seq_count // 2
    pairs = []
    for d in range(seq_count):
        for m in range(mp_count):
            target = step(d // 2, d % 2, m // 2, m % 2)
            if target is not None:
                z, y, x, c = target
                pairs.append((d * mp_count + m, ((z % z_count) * 2 + y) * mp_count + 2 * x + c))
    return lax.ppermute(value, ("seq", "mp"), pairs)


def spread(k):
    return lambda z, y, x, c: (z, c ^ (k % 2), x ^ (k // 2), y)


def gather_back(k):
    return lambda z, y, x, c: (z, c, x ^ (k // 2), y ^ (k % 2))


def flip_core(z, y, x, c):
    return (z, y, x, 1 - c)


def ring_up(z, y, x, c):
    return (z + 1, y, x, c)


def ring_down(z, y, x, c):
    return (z - 1, y, x, c)


def place():
    d, m = lax.axis_index("seq"), lax.axis_index("mp")
    return d // 2, d % 2, m // 2, m % 2


def tie(*values):
    return lax.optimization_barrier(values)


def any_weights(own, c, g):
    seq_count = lax.axis_size("seq")
    z_count = seq_count // 2
    rows, width = own.shape[0] // 4, own.shape[1]
    groups = [[2 * i + j for i in range(z_count)] for j in range(2)]
    mine = lax.all_gather(own, "seq", axis=0, axis_index_groups=groups)
    theirs = move(mine, flip_core)
    both = jnp.stack([jnp.where(c == 0, mine, theirs), jnp.where(c == 0, theirs, mine)], axis=1)
    both = jnp.moveaxis(both.reshape(seq_count, 4, rows, width), 1, 0)
    both = both.reshape(4, 4, seq_count * rows // 4, width)
    both = jnp.take(both, g ^ jnp.arange(4), axis=1).reshape(4, seq_count * rows, width)
    return [jnp.concatenate([both[0], both[1]], axis=1)], [jnp.concatenate([both[2], both[3]], axis=1)]


def run_copies(pairs, sems):
    copies = [pltpu.make_async_copy(a, b, sems.at[i]) for i, (a, b) in enumerate(pairs)]
    for copy in copies:
        copy.start()
    for copy in copies:
        copy.wait()


def weight_copies(pieces, whole, first):
    if len(pieces) == 1:
        return [(pieces[0], whole)]
    z, y, x, c = place()
    g = 2 * x + y
    rows, width = pieces[0].shape[0] // 4, pieces[0].shape[1]
    pairs = []
    for side in range(2):
        side_c = c if side == 0 else 1 - c
        for step, ref in zip((0, 3, 1, 2), pieces[4 * side : 4 * side + 4]):
            start = pl.multiple_of((((z + step) % 4 ^ g) * 2 + side_c) * rows, 64)
            for j in range(2):
                pairs.append(
                    (
                        ref.at[pl.ds((first + j) * rows, rows)],
                        whole.at[pl.ds(start, rows), pl.ds(j * width, width)],
                    )
                )
    return pairs


def norm_kernel(token_count, *refs):
    token_refs, normed, inv_out, rows_in, sems = refs[:4], *refs[4:]
    width = token_refs[0].shape[1]
    run_copies(
        [(ref.at[pl.ds(0, token_count + EXTRA)], rows_in.at[k]) for k, ref in enumerate(token_refs)],
        sems,
    )
    total = None
    for k in range(4):
        rows = rows_in[k, 0:token_count, :].astype(F32)
        part = jnp.sum(rows * rows, axis=1, keepdims=True)
        total = part if total is None else total + part
    inv_rms = lax.rsqrt(total / (4 * width) + epsilon)
    inv_out[...] = inv_rms
    for k in range(4):
        rows = rows_in[k, 0:token_count, :].astype(F32)
        gain = rows_in[k, token_count : token_count + 1, :].astype(F32)
        normed[:, k * width : (k + 1) * width] = (rows * inv_rms * gain).astype(LOW)


def table_kernel(token_count, *refs):
    token_refs, outer_refs = refs[:4], refs[4:8]
    pieces, (whole, tables, shared, encs, sems) = refs[8:-5], refs[-5:]
    width = token_refs[0].shape[1]
    pairs = weight_copies(pieces, whole, 0)
    for k in range(4):
        block = pl.ds(k * width, width)
        for i, (ref, start) in enumerate(
            ((outer_refs[k], 0), (token_refs[k], 2 * token_count + EXTRA), (outer_refs[k], OWN_ROWS))
        ):
            pairs.append((ref.at[pl.ds(start, OWN_ROWS)], encs.at[pl.ds(i * OWN_ROWS, OWN_ROWS), block]))
    run_copies(pairs, sems)
    tables[...] = jnp.dot(encs[...], whole[...], preferred_element_type=F32).astype(LOW)
    shared[0:OWN_ROWS, :] = tables[OWN_ROWS : 2 * OWN_ROWS, :]
    z, y, x, c = place()
    start = pl.multiple_of(jnp.where(c == 1, 0, 2 * OWN_ROWS), OWN_ROWS)
    shared[OWN_ROWS : 2 * OWN_ROWS, :] = tables[pl.ds(start, OWN_ROWS), :]


def query_kernel(token_count, *refs):
    normed, token_refs = refs[0], refs[1:5]
    pieces, (whole, queries, d_attended, rows_in, grads, sems) = refs[5:-6], refs[-6:]
    width = token_refs[0].shape[1]
    pairs = weight_copies(pieces, whole, 2) + [(normed, rows_in)]
    for k, ref in enumerate(token_refs):
        pairs.append(
            (ref.at[pl.ds(token_count + EXTRA, token_count)], grads.at[:, pl.ds(k * width, width)])
        )
    run_copies(pairs, sems)
    queries[...] = jnp.dot(rows_in[...], whole[:, 0:width], preferred_element_type=F32).astype(LOW)
    d_attended[...] = jnp.dot(grads[...], whole[:, width:], preferred_element_type=F32).astype(LOW)


def attention_kernel(seq_count, *refs):
    chosen, tables, shared, queries, d_attended = refs[:5]
    attended, d_queries, d_own, d_outer, d_shared, window, d_window, sems = refs[5:]
    token_count, width = queries.shape
    run_copies(
        [
            (tables, window.at[pl.ds(0, 3 * OWN_ROWS)]),
            (shared, window.at[pl.ds(3 * OWN_ROWS, 2 * OWN_ROWS)]),
        ],
        sems,
    )
    d_window[...] = jnp.zeros_like(d_window)
    scale = HD ** (-0.5)
    z, y, x, c = place()
    t = 2 * z + c
    for s in range(token_count // STRETCH):
        starts = []
        for j in range(NBR):
            name = chosen[s * NBR + j]
            away = (name // OWN_DEV - t + 2 + seq_count) % seq_count
            odd = 3 + jnp.where(away == 1, 1 - c, c)
            index = jnp.where(away % 2 == 0, away // 2, odd)
            starts.append(pl.multiple_of(index * OWN_ROWS + (name % OWN_DEV) * RET, RET))
        tokens = slice(s * STRETCH, (s + 1) * STRETCH)
        for h in range(width // HD):
            left = slice(h * HD, (h + 1) * HD)
            right = slice(width + h * HD, width + (h + 1) * HD)
            keys = jnp.concatenate([window[pl.ds(a, RET), left] for a in starts], axis=0)
            values = jnp.concatenate([window[pl.ds(a, RET), right] for a in starts], axis=0)
            query = queries[tokens, left]
            d_att = d_attended[tokens, left]
            scores = lax.dot_general(query, keys, ACROSS, preferred_element_type=F32) * scale
            exponent = jnp.exp(scores - jnp.max(scores, axis=1, keepdims=True))
            weights = exponent / jnp.sum(exponent, axis=1, keepdims=True)
            weights_low = weights.astype(LOW)
            attended[tokens, left] = jnp.dot(
                weights_low, values, preferred_element_type=F32
            ).astype(LOW)
            d_weights = lax.dot_general(d_att, values, ACROSS, preferred_element_type=F32)
            inner = jnp.sum(d_weights * weights, axis=1, keepdims=True)
            d_scores = (weights * (d_weights - inner) * scale).astype(LOW)
            d_queries[tokens, left] = jnp.dot(d_scores, keys, preferred_element_type=F32).astype(LOW)
            d_keys = lax.dot_general(d_scores, query, DOWN, preferred_element_type=F32)
            d_values = lax.dot_general(weights_low, d_att, DOWN, preferred_element_type=F32)
            for j, a in enumerate(starts):
                d_window[pl.ds(a, RET), left] += d_keys[j * RET : (j + 1) * RET, :]
                d_window[pl.ds(a, RET), right] += d_values[j * RET : (j + 1) * RET, :]
    d_own[...] = d_window[OWN_ROWS : 2 * OWN_ROWS, :]
    d_outer[0:OWN_ROWS, :] = d_window[0:OWN_ROWS, :].astype(LOW)
    d_outer[OWN_ROWS : 2 * OWN_ROWS, :] = d_window[2 * OWN_ROWS : 3 * OWN_ROWS, :].astype(LOW)
    d_shared[...] = d_window[3 * OWN_ROWS : 5 * OWN_ROWS, :].astype(LOW)


def as_row(column):
    return jnp.transpose(jnp.broadcast_to(column, (column.shape[0], 128)))[0:1, :]


def product_kernel(*refs):
    attended, d_queries, inv_rms, whole_in = refs[:4]
    token_refs, outs, (whole, rows_in, sems) = refs[4:8], refs[8:12], refs[12:]
    token_count, width = attended.shape
    pairs = [(whole_in, whole)]
    for k, ref in enumerate(token_refs):
        pairs.append((ref.at[pl.ds(0, token_count + EXTRA)], rows_in.at[k]))
    run_copies(pairs, sems)
    total = None
    for k, out in enumerate(outs):
        block = slice(k * width, (k + 1) * width)
        out[0:token_count, :] = lax.dot_general(
            attended[...], whole[block, width:], ACROSS, preferred_element_type=F32
        ).astype(LOW)
        back = lax.dot_general(
            d_queries[...], whole[block, 0:width], ACROSS, preferred_element_type=F32
        ).astype(LOW)
        out[token_count : 2 * token_count, :] = back
        rows = rows_in[k, 0:token_count, :].astype(F32)
        gain = rows_in[k, token_count : token_count + 1, :].astype(F32)
        part = jnp.sum(rows * gain * back.astype(F32), axis=1, keepdims=True)
        total = part if total is None else total + part
    lines = []
    for column in (total, inv_rms[...]):
        line = as_row(column)
        high = line.astype(LOW).astype(F32)
        lines += [high, line - high]
    lines.append(jnp.zeros((EXTRA - 4, token_count), F32))
    extra = jnp.concatenate(lines, axis=0)
    extra = jnp.concatenate([extra, jnp.zeros((EXTRA, width - token_count), F32)], axis=1).astype(LOW)
    for out in outs:
        out[2 * token_count : 2 * token_count + EXTRA, :] = extra


def finish_kernel(hidden, gain, *refs):
    terms, (branch_out, grad_rows) = refs[:4], refs[4:]
    token_count, width = hidden.shape
    branch, normed_grad, extra = None, None, None
    for k, term in enumerate(terms):
        out = term[0:token_count, :].astype(F32)
        back = term[token_count : 2 * token_count, :].astype(F32)
        lines = term[2 * token_count : 2 * token_count + EXTRA, :].astype(F32)
        branch = out if k == 0 else branch + out
        normed_grad = back if k == 0 else normed_grad + back
        extra = lines if k == 0 else extra + lines
        if k == 0:
            inv_row = lines[2:3, 0:token_count] + lines[3:4, 0:token_count]
    branch_out[...] = branch.astype(LOW)
    stat_row = extra[0:1, 0:token_count] + extra[1:2, 0:token_count]

    def as_column(row):
        return jnp.transpose(jnp.broadcast_to(row, (128, token_count)))[:, 0:1]

    statistic = as_column(stat_row) / (4 * width)
    inv_rms = as_column(inv_row)
    rows = hidden[...].astype(F32)
    grad_rows[...] = (
        inv_rms * gain[...].astype(F32) * normed_grad - rows * inv_rms * inv_rms * inv_rms * statistic
    ).astype(LOW)


def encoding_kernel(own, from_core, up, down, whole, *outs):
    width = whole.shape[1] // 2
    own_low = own[...] + from_core[0:OWN_ROWS, :].astype(F32)
    own_low = (own_low + up[...].astype(F32) + down[...].astype(F32)).astype(LOW)
    for k, out in enumerate(outs):
        out[...] = lax.dot_general(
            own_low, whole[k * width : (k + 1) * width, :], ACROSS, preferred_element_type=F32
        ).astype(LOW)


def call(kernel, operands, specs, outs, scratch=(), copies=0):
    scratch = list(scratch)
    if copies:
        scratch.append(pltpu.SemaphoreType.DMA((copies,)))
    return pl.pallas_call(
        kernel,
        out_shape=[jax.ShapeDtypeStruct(shape, dtype) for shape, dtype in outs],
        in_specs=specs,
        out_specs=[VMEM] * len(outs),
        scratch_shapes=scratch,
        compiler_params=pltpu.CompilerParams(vmem_limit_bytes=40 * 1024 * 1024),
    )(*operands)


def shards(hidden_rows, norm_gain, encodings, w_query, w_key, w_value, w_out, neighbours, grad_out):
    seq_count = lax.axis_size("seq")
    z, y, x, c = place()
    g = 2 * x + y
    token_count, width = hidden_rows.shape
    full_width = 4 * width
    ids = neighbours.size
    wide = 2 * width

    own_enc = encodings.reshape(OWN_ROWS, width)
    weights = move(jnp.concatenate([w_key, w_value, w_query, w_out.T], axis=0), spread(0))
    enc_below, enc_above = move(own_enc, ring_up), move(own_enc, ring_down)
    extra = jnp.pad(norm_gain[None, :], ((0, EXTRA - 1), (0, 0)))
    extra = extra + jnp.pad(neighbours.reshape(1, ids).astype(LOW), ((1, EXTRA - 2), (0, width - ids)))
    packed = jnp.concatenate([hidden_rows, extra, grad_out, own_enc], axis=0)
    weights, enc_below, enc_above, packed = tie(weights, enc_below, enc_above, packed)
    tokens = [move(packed, spread(k)) for k in range(4)]
    outer = jnp.concatenate([enc_below, enc_above], axis=0)
    if seq_count == 8:
        below, above = move(weights, ring_up), move(weights, ring_down)
        outer, below, above, *tokens = tie(outer, below, above, *tokens)
        two_below = move(below, lambda z, y, x, c: (z + 1, y, x, c) if z in (1, 2) else None)
        two_above = move(above, lambda z, y, x, c: (z - 1, y, x, c) if z in (1, 2) else None)
        pieces = [weights, below, above, jnp.where(z <= 1, two_above, two_below)]
        pieces = pieces + [move(piece, flip_core) for piece in pieces]
        kv_pieces = qo_pieces = pieces
    else:
        kv_pieces, qo_pieces = any_weights(weights, c, g)
    outer = [move(outer, spread(k)) for k in range(4)]
    piece_count = len(kv_pieces)

    chosen = tokens[0][token_count + 1, :ids].astype(jnp.int32)
    normed, inv_rms = call(
        lambda *refs: norm_kernel(token_count, *refs),
        tokens,
        [ANY] * 4,
        [((token_count, full_width), LOW), ((token_count, 1), F32)],
        [pltpu.VMEM((4, token_count + EXTRA, width), LOW)],
        4,
    )
    whole_kv, tables, shared = call(
        lambda *refs: table_kernel(token_count, *refs),
        tokens + outer + kv_pieces,
        [ANY] * (8 + piece_count),
        [((full_width, wide), LOW), ((3 * OWN_ROWS, wide), LOW), ((2 * OWN_ROWS, wide), LOW)],
        [pltpu.VMEM((3 * OWN_ROWS, full_width), LOW)],
        12 + 2 * piece_count,
    )
    shared = move(shared, flip_core)
    whole_qo, queries, d_attended = call(
        lambda *refs: query_kernel(token_count, *refs),
        [normed] + tokens + qo_pieces,
        [ANY] * (5 + piece_count),
        [((full_width, wide), LOW), ((token_count, width), LOW), ((token_count, width), LOW)],
        [pltpu.VMEM((token_count, full_width), LOW), pltpu.VMEM((token_count, full_width), LOW)],
        5 + 2 * piece_count,
    )
    attended, d_queries, d_own, d_outer, d_shared = call(
        lambda *refs: attention_kernel(seq_count, *refs),
        [chosen, tables, shared, queries, d_attended],
        [SMEM, ANY, ANY, VMEM, VMEM],
        [
            ((token_count, width), LOW),
            ((token_count, width), LOW),
            ((OWN_ROWS, wide), F32),
            ((2 * OWN_ROWS, wide), LOW),
            ((2 * OWN_ROWS, wide), LOW),
        ],
        [pltpu.VMEM((5 * OWN_ROWS, wide), LOW), pltpu.VMEM((5 * OWN_ROWS, wide), F32)],
        2,
    )
    from_core = move(d_shared, flip_core)
    shared_grad = from_core[OWN_ROWS:].astype(F32)
    to_below = (d_outer[:OWN_ROWS] + jnp.where(c == 1, shared_grad, 0.0)).astype(LOW)
    to_above = (d_outer[OWN_ROWS:] + jnp.where(c == 0, shared_grad, 0.0)).astype(LOW)
    terms = call(
        product_kernel,
        [attended, d_queries, inv_rms, whole_qo] + tokens,
        [VMEM, VMEM, VMEM] + [ANY] * 5,
        [((2 * token_count + EXTRA, width), LOW)] * 4,
        [
            pltpu.VMEM((full_width, wide), LOW),
            pltpu.VMEM((4, token_count + EXTRA, width), LOW),
        ],
        5,
    )
    to_below, to_above, *terms = tie(to_below, to_above, *terms)
    up, down = move(to_above, ring_up), move(to_below, ring_down)
    terms = [move(term, gather_back(k)) for k, term in enumerate(terms)]
    branch_out, grad_rows = call(
        finish_kernel,
        [hidden_rows, norm_gain[None, :]] + terms,
        [VMEM] * 6,
        [((token_count, width), LOW), ((token_count, width), LOW)],
    )
    enc_terms = call(
        encoding_kernel,
        [d_own, from_core, up, down, whole_kv],
        [VMEM] * 5,
        [((OWN_ROWS, width), LOW)] * 4,
    )
    enc_terms = [move(term, gather_back(k)).astype(F32) for k, term in enumerate(enc_terms)]
    grad_encodings = (enc_terms[0] + enc_terms[1] + enc_terms[2] + enc_terms[3]).astype(LOW)
    return (branch_out, grad_rows, grad_encodings.reshape(encodings.shape))


def solution(mesh):
    placed = (
        P("seq", "mp"),
        P("mp"),
        P("seq", None, "mp"),
        P("seq", "mp"),
        P("seq", "mp"),
        P("seq", "mp"),
        P("mp", "seq"),
        P("seq", None),
        P("seq", "mp"),
    )
    return jax.shard_map(
        shards,
        mesh=mesh,
        in_specs=placed,
        out_specs=(P("seq", "mp"), P("seq", "mp"), P("seq", None, "mp")),
        check_vma=False,
    )
```

time: 210 us -> 160 us (0.76)
  the two profiles are of different devices: /device:TPU:1 before, /device:TPU:19 now
where the time goes in v2:
time: 160 us; the launch traced here: 159 us
  waiting for transfers between devices  83.1 us (52%)
  starting transfers between devices  39.8 us (25%)
  Pallas kernels  20.5 us (13%)
  local copies, waits for them, and re-layouts  9 us (6%)
  other arithmetic  5.87 us (4%)
    ppermute x31, waiting for transfers between devices, move(): return lax.ppermute(value, ('seq', 'mp'), pairs)  83.1 us
    ppermute x31, starting transfers between devices, move(): return lax.ppermute(value, ('seq', 'mp'), pairs)  39.8 us
    pallas_call x7, Pallas kernels, call(): pl.pallas_call(kernel, out_shape=[jax.ShapeDtypeStruct(shape, dtype) for...  20.5 us
    unnamed x34, local copies, waits for them, and re-layouts  8.12 us
  transfers between devices with their start and end apart: 31, of which 14 were waited for; matrix products, arithmetic and copies ran while one was open for 3% of the time, Pallas kernels for 6%

profile of v2, /device:TPU:19, one launch (start us, length us, event | category | flops | bytes accessed | tf_op | source)
XLA Modules:
  0.0 159.2 jit_solution(14827775019329720812)
XLA Ops:
  0.7 1.2 pad_maximum_fusion.1
  1.9 3.7 %collective-permute-start = (bf16[768,384]{1,0:T(8,128)(2,1)S(1)}, bf16[768,384]{1,0:T(8,128)(2,1)S(1)}, u32[]{:S(2)}, u32[]{:S(2)}) collective-permute-start(bf16[768,384]{1,0:T(8,128)(2,1)S(1)} %pad_maximum_fusion.1), channel_id=1, source_target_pairs={{0,0},{1,4},{2,2},{3,6},{4,1},{5,5},{6,3},{7,7},{8,8},{9,12},{10,1... | collective-permute-start | bytes 1769480 | tf_op jit(solution)/shard_map/ppermute | solution.py:35
  5.6 1.3 collective-permute-start.1
  8.8 6.0 %collective-permute-done.1 = bf16[256,384]{1,0:T(8,128)(2,1)S(1)} collective-permute-done((bf16[256,384]{1,0:T(8,128)(2,1)}, bf16[256,384]{1,0:T(8,128)(2,1)S(1)}, u32[]{:S(2)}, u32[]{:S(2)}) %collective-permute-start.1) | collective-permute-done | bytes 196640 | tf_op jit(solution)/shard_map/ppermute | solution.py:35
  14.9 1.3 collective-permute-start.3
  16.2 2.9 %collective-permute-start.5 = (bf16[784,384]{1,0:T(8,128)(2,1)S(1)}, bf16[784,384]{1,0:T(8,128)(2,1)S(1)}, u32[]{:S(2)}, u32[]{:S(2)}) collective-permute-start(bf16[784,384]{1,0:T(8,128)(2,1)S(1)} %pad_maximum_fusion), channel_id=1, source_target_pairs={{0,0},{1,4},{2,2},{3,6},{4,1},{5,5},{6,3},{7,7},{8,8},{9,12},{10,1... | collective-permute-start | bytes 1806344 | tf_op jit(solution)/shard_map/ppermute | solution.py:35
  19.2 0.8 collective-permute-start.7
  19.9 2.0 %collective-permute-start.8 = (bf16[784,384]{1,0:T(8,128)(2,1)S(1)}, bf16[784,384]{1,0:T(8,128)(2,1)S(1)}, u32[]{:S(2)}, u32[]{:S(2)}) collective-permute-start(bf16[784,384]{1,0:T(8,128)(2,1)S(1)} %pad_maximum_fusion), channel_id=1, source_target_pairs={{0,6},{1,2},{2,4},{3,0},{4,7},{5,3},{6,5},{7,1},{8,14},{9,10},{10,... | collective-permute-start | bytes 1806344 | tf_op jit(solution)/shard_map/ppermute | solution.py:35
  21.9 8.3 %collective-permute-done.3.refs_9_.refs_6_ = bf16[768,384]{1,0:T(8,128)(2,1)} collective-permute-done((bf16[768,384]{1,0:T(8,128)(2,1)S(1)}, bf16[768,384]{1,0:T(8,128)(2,1)}, u32[]{:S(2)}, u32[]{:S(2)}) %collective-permute-start.3) | collective-permute-done | bytes 589856 | tf_op jit(solution)/shard_map/ppermute | solution.py:35
  30.6 1.7 %pad_maximum_fusion.2 = bf16[512,384]{1,0:T(8,128)(2,1)} fusion(bf16[256,384]{1,0:T(8,128)(2,1)} %copy-done.16, bf16[256,384]{1,0:T(8,128)(2,1)S(1)} %collective-permute-done.1), kind=kLoop, calls=%fused_computation.9 | loop fusion | flops 786432 | bytes 786432 | tf_op jit(solution)/shard_map/concatenate | solution.py:322
  32.4 12.2 %collective-permute-done.4.refs_10_.refs_7_ = bf16[768,384]{1,0:T(8,128)(2,1)} collective-permute-done((bf16[768,384]{1,0:T(8,128)(2,1)S(1)}, bf16[768,384]{1,0:T(8,128)(2,1)}, u32[]{:S(2)}, u32[]{:S(2)}) %collective-permute-start.4) | collective-permute-done | bytes 589856 | tf_op jit(solution)/shard_map/ppermute | solution.py:35
  45.1 0.7 collective-permute-done.6.refs_1_.refs_2_.refs_5_
  45.8 2.5 %collective-permute-done.8.refs_3_.refs_4_.refs_7_ = bf16[784,384]{1,0:T(8,128)(2,1)S(1)} collective-permute-done((bf16[784,384]{1,0:T(8,128)(2,1)S(1)}, bf16[784,384]{1,0:T(8,128)(2,1)S(1)}, u32[]{:S(2)}, u32[]{:S(2)}) %collective-permute-start.8) | collective-permute-done | bytes 602144 | tf_op jit(solution)/shard_map/ppermute | solution.py:35
  48.3 2.8 %collective-permute-start.13 = (bf16[768,384]{1,0:T(8,128)(2,1)}, bf16[768,384]{1,0:T(8,128)(2,1)}, u32[]{:S(2)}, u32[]{:S(2)}) collective-permute-start(bf16[768,384]{1,0:T(8,128)(2,1)} %collective-permute-done.4.refs_10_.refs_7_), channel_id=1, source_target_pairs={{8,0},{9,1},{10,2},{11,3},{12,4},{13,5},{14,6},{15,7},{16,8},{17,9... | collective-permute-start | bytes 1769480 | tf_op jit(solution)/shard_map/ppermute | solution.py:35
  51.1 1.9 %collective-permute-start.14 = (bf16[768,384]{1,0:T(8,128)(2,1)}, bf16[768,384]{1,0:T(8,128)(2,1)}, u32[]{:S(2)}, u32[]{:S(2)}) collective-permute-start(bf16[768,384]{1,0:T(8,128)(2,1)} %collective-permute-done.3.refs_9_.refs_6_), channel_id=1, source_target_pairs={{8,16},{9,17},{10,18},{11,19},{12,20},{13,21},{14,22},{15,23},{16,... | collective-permute-start | bytes 1769480 | tf_op jit(solution)/shard_map/ppermute | solution.py:35
  53.1 4.1 %collective-permute-start.9 = (bf16[512,384]{1,0:T(8,128)(2,1)}, bf16[512,384]{1,0:T(8,128)(2,1)S(1)}, u32[]{:S(2)}, u32[]{:S(2)}) collective-permute-start(bf16[512,384]{1,0:T(8,128)(2,1)} %pad_maximum_fusion.2), channel_id=1, source_target_pairs={{0,0},{1,4},{2,2},{3,6},{4,1},{5,5},{6,3},{7,7},{8,8},{9,12},{10,1... | collective-permute-start | bytes 1179656 | tf_op jit(solution)/shard_map/ppermute | solution.py:35
  57.3 6.3 %collective-permute-done.13 = bf16[768,384]{1,0:T(8,128)(2,1)} collective-permute-done((bf16[768,384]{1,0:T(8,128)(2,1)}, bf16[768,384]{1,0:T(8,128)(2,1)}, u32[]{:S(2)}, u32[]{:S(2)}) %collective-permute-start.13) | collective-permute-done | bytes 589856 | tf_op jit(solution)/shard_map/ppermute | solution.py:35
  64.1 4.2 %collective-permute-done.14 = bf16[768,384]{1,0:T(8,128)(2,1)} collective-permute-done((bf16[768,384]{1,0:T(8,128)(2,1)}, bf16[768,384]{1,0:T(8,128)(2,1)}, u32[]{:S(2)}, u32[]{:S(2)}) %collective-permute-start.14) | collective-permute-done | bytes 589856 | tf_op jit(solution)/shard_map/ppermute | solution.py:35
  68.3 0.7 collective-permute-start.17
  69.1 1.1 broadcast_select_fusion.refs_11_.refs_8_
  70.3 1.2 collective-permute-start.11
  71.5 0.9 collective-permute-start.12
  72.4 10.2 %collective-permute-done.11.refs_6_ = bf16[512,384]{1,0:T(8,128)(2,1)S(1)} collective-permute-done((bf16[512,384]{1,0:T(8,128)(2,1)S(1)}, bf16[512,384]{1,0:T(8,128)(2,1)S(1)}, u32[]{:S(2)}, u32[]{:S(2)}) %collective-permute-start.11) | collective-permute-done | bytes 393248 | tf_op jit(solution)/shard_map/ppermute | solution.py:35
  82.7 6.7 %collective-permute-done.12.refs_7_ = bf16[512,384]{1,0:T(8,128)(2,1)S(1)} collective-permute-done((bf16[512,384]{1,0:T(8,128)(2,1)S(1)}, bf16[512,384]{1,0:T(8,128)(2,1)S(1)}, u32[]{:S(2)}, u32[]{:S(2)}) %collective-permute-start.12) | collective-permute-done | bytes 393248 | tf_op jit(solution)/shard_map/ppermute | solution.py:35
  89.4 3.7 %shard_map.112 = (bf16[1536,768]{1,0:T(8,128)(2,1)S(1)}, bf16[768,768]{1,0:T(8,128)(2,1)S(1)}, bf16[512,768]{1,0:T(8,128)(2,1)S(1)}) custom-call(bf16[784,384]{1,0:T(8,128)(2,1)S(1)} %collective-permute-done.5.refs_0_.refs_1_.refs_4_, bf16[784,384]{1,0:T(8,128)(2,1)S(1)} %collective-permute-done.6.refs_1_.refs_2_.refs_5_, ...), custom_call_target="tpu_custom_call" | custom-call | tf_op jit(solution)/shard_map/pallas_call | solution.py:295
  93.0 2.0 %collective-permute-start.19 = (bf16[512,768]{1,0:T(8,128)(2,1)S(1)}, bf16[512,768]{1,0:T(8,128)(2,1)S(1)}, u32[]{:S(2)}, u32[]{:S(2)}) collective-permute-start(bf16[512,768]{1,0:T(8,128)(2,1)S(1)} %get-tuple-element.55), channel_id=1, source_target_pairs={{0,1},{1,0},{2,3},{3,2},{4,5},{5,4},{6,7},{7,6},{8,9},{9,8},{10,11... | collective-permute-start | bytes 2359304 | tf_op jit(solution)/shard_map/ppermute | solution.py:35
  95.0 1.5 shard_map.113
  96.5 2.5 %shard_map.114 = (bf16[1536,768]{1,0:T(8,128)(2,1)S(1)}, bf16[256,384]{1,0:T(8,128)(2,1)S(1)}, bf16[256,384]{1,0:T(8,128)(2,1)S(1)}) custom-call(bf16[256,1536]{1,0:T(8,128)(2,1)S(1)} %get-tuple-element.56.refs_0_, bf16[784,384]{1,0:T(8,128)(2,1)S(1)} %collective-permute-done.5.refs_0_.refs_1_.refs_4_, ...), custom_call_target="tpu_custom_call" | custom-call | tf_op jit(solution)/shard_map/pallas_call | solution.py:295
  99.0 1.4 copy-done.2
  100.5 8.0 %shard_map.115 = (bf16[256,384]{1,0:T(8,128)(2,1)S(1)}, bf16[256,384]{1,0:T(8,128)(2,1)S(1)}, f32[256,768]{1,0:T(8,128)S(1)}, bf16[512,768]{1,0:T(8,128)(2,1)S(1)}, bf16[512,768]{1,0:T(8,128)(2,1)}) custom-call(s32[8]{0:T(128)S(1)} %bitcast_convert_fusion.refs_0_, bf16[768,768]{1,0:T(8,128)(2,1)S(1)} %get-tuple-element.54.refs_1_, ...), custom_call_target="tpu_custom_call" | custom-call | tf_op jit(solution)/shard_map/pallas_call | solution.py:295
  108.5 0.9 copy-done.4
  109.4 0.9 copy-done.6
  111.6 1.7 %copy-done.3 = bf16[1536,768]{1,0:T(8,128)(2,1)S(1)} copy-done((bf16[1536,768]{1,0:T(8,128)(2,1)S(1)}, bf16[1536,768]{1,0:T(8,128)(2,1)}, u32[]{:S(2)}) %copy-start.3) | copy-done | bytes 2359320
  113.3 0.9 copy-done.10
  114.2 0.9 copy-done.12
  115.2 2.7 %shard_map.116 = (bf16[528,384]{1,0:T(8,128)(2,1)S(1)}, bf16[528,384]{1,0:T(8,128)(2,1)S(1)}, bf16[528,384]{1,0:T(8,128)(2,1)S(1)}, bf16[528,384]{1,0:T(8,128)(2,1)S(1)}) custom-call(bf16[256,384]{1,0:T(8,128)(2,1)S(1)} %copy-done.10, bf16[256,384]{1,0:T(8,128)(2,1)S(1)} %copy-done.12, f32[256,1]{1,0:T(8,128)S(1)} %get-tuple-element.63.refs_2_, ...), custom_call_target="tpu_custom_call" | custom-call | tf_op jit(solution)/shard_map/pallas_call | solution.py:295
  118.2 3.7 %collective-permute-start.21 = (bf16[528,384]{1,0:T(8,128)(2,1)S(1)}, bf16[528,384]{1,0:T(8,128)(2,1)S(1)}, u32[]{:S(2)}, u32[]{:S(2)}) collective-permute-start(bf16[528,384]{1,0:T(8,128)(2,1)S(1)} %get-tuple-element.69), channel_id=1, source_target_pairs={{0,0},{1,4},{2,2},{3,6},{4,1},{5,5},{6,3},{7,7},{8,8},{9,12},{10,1... | collective-permute-start | bytes 1216520 | tf_op jit(solution)/shard_map/ppermute | solution.py:35
  122.0 1.5 collective-permute-start.26
  123.5 13.3 %collective-permute-done.25.up = bf16[256,768]{1,0:T(8,128)(2,1)S(1)} collective-permute-done((bf16[256,768]{1,0:T(8,128)(2,1)S(1)}, bf16[256,768]{1,0:T(8,128)(2,1)S(1)}, u32[]{:S(2)}, u32[]{:S(2)}) %collective-permute-start.25) | collective-permute-done | bytes 393248 | tf_op jit(solution)/shard_map/ppermute | solution.py:35
  136.8 1.2 collective-permute-start.24
  138.0 1.0 shard_map.118
  139.0 2.5 %collective-permute-start.30 = (bf16[256,384]{1,0:T(8,128)(2,1)S(1)}, bf16[256,384]{1,0:T(8,128)(2,1)S(1)}, u32[]{:S(2)}, u32[]{:S(2)}) collective-permute-start(bf16[256,384]{1,0:T(8,128)(2,1)S(1)} %get-tuple-element.82), channel_id=1, source_target_pairs={{0,3},{1,7},{2,1},{3,5},{4,2},{5,6},{6,0},{7,4},{8,11},{9,15},{10,... | collective-permute-start | bytes 589832 | tf_op jit(solution)/shard_map/ppermute | solution.py:35
  142.3 2.8 %collective-permute-start.27 = (bf16[256,384]{1,0:T(8,128)(2,1)S(1)}, bf16[256,384]{1,0:T(8,128)(2,1)S(1)}, u32[]{:S(2)}, u32[]{:S(2)}) collective-permute-start(bf16[256,384]{1,0:T(8,128)(2,1)S(1)} %get-tuple-element.79), channel_id=1, source_target_pairs={{0,0},{1,4},{2,2},{3,6},{4,1},{5,5},{6,3},{7,7},{8,8},{9,12},{10,1... | collective-permute-start | bytes 589832 | tf_op jit(solution)/shard_map/ppermute | solution.py:35
  145.1 3.3 %collective-permute-done.24.refs_3_ = bf16[528,384]{1,0:T(8,128)(2,1)S(1)} collective-permute-done((bf16[528,384]{1,0:T(8,128)(2,1)S(1)}, bf16[528,384]{1,0:T(8,128)(2,1)S(1)}, u32[]{:S(2)}, u32[]{:S(2)}) %collective-permute-start.24) | collective-permute-done | bytes 405536 | tf_op jit(solution)/shard_map/ppermute | solution.py:35
  148.5 1.2 shard_map.117
  149.6 3.0 %collective-permute-done.30 = bf16[256,384]{1,0:T(8,128)(2,1)S(1)} collective-permute-done((bf16[256,384]{1,0:T(8,128)(2,1)S(1)}, bf16[256,384]{1,0:T(8,128)(2,1)S(1)}, u32[]{:S(2)}, u32[]{:S(2)}) %collective-permute-start.30) | collective-permute-done | bytes 196640 | tf_op jit(solution)/shard_map/ppermute | solution.py:35
  152.7 5.8 %collective-permute-done.29 = bf16[256,384]{1,0:T(8,128)(2,1)S(1)} collective-permute-done((bf16[256,384]{1,0:T(8,128)(2,1)S(1)}, bf16[256,384]{1,0:T(8,128)(2,1)S(1)}, u32[]{:S(2)}, u32[]{:S(2)}) %collective-permute-start.29) | collective-permute-done | bytes 196640 | tf_op jit(solution)/shard_map/ppermute | solution.py:35
  158.5 0.8 add_convert_fusion
  (67 shorter events, 6.2 us)
Async XLA Ops:
  0.6 8.1 %copy-start.15 = (bf16[2,128,384]{2,1,0:T(8,128)(2,1)S(1)}, bf16[2,128,384]{2,1,0:T(8,128)(2,1)}, u32[]{:S(2)}) copy-start(bf16[2,128,384]{2,1,0:T(8,128)(2,1)} %param.11) | copy-start | bytes 589828
  0.6 8.1 %copy-start.8 = (bf16[256,384]{1,0:T(8,128)(2,1)S(1)}, bf16[256,384]{1,0:T(8,128)(2,1)}, u32[]{:S(2)}) copy-start(bf16[256,384]{1,0:T(8,128)(2,1)} %hidden.1) | copy-start | bytes 589828
  0.7 8.1 %copy-start.14 = (bf16[256,384]{1,0:T(8,128)(2,1)S(1)}, bf16[256,384]{1,0:T(8,128)(2,1)}, u32[]{:S(2)}) copy-start(bf16[256,384]{1,0:T(8,128)(2,1)} %param.17) | copy-start | bytes 589828
  1.9 13.0 %collective-permute-start = (bf16[768,384]{1,0:T(8,128)(2,1)S(1)}, bf16[768,384]{1,0:T(8,128)(2,1)S(1)}, u32[]{:S(2)}, u32[]{:S(2)}) collective-permute-start(bf16[768,384]{1,0:T(8,128)(2,1)S(1)} %pad_maximum_fusion.1), channel_id=1, source_target_pairs={{0,0},{1,4},{2,2},{3,6},{4,1},{5,5},{6,3},{7,7},{8,8},{9,12},{10,1... | collective-permute-start | bytes 1769480 | tf_op jit(solution)/shard_map/ppermute | solution.py:35
  5.6 9.2 %collective-permute-start.1 = (bf16[256,384]{1,0:T(8,128)(2,1)}, bf16[256,384]{1,0:T(8,128)(2,1)S(1)}, u32[]{:S(2)}, u32[]{:S(2)}) collective-permute-start(bf16[256,384]{1,0:T(8,128)(2,1)} %bitcast.6), channel_id=1, source_target_pairs={{0,8},{1,9},{2,10},{3,11},{4,12},{5,13},{6,14},{7,15},{8,16},{9,17... | collective-permute-start | bytes 589832 | tf_op jit(solution)/shard_map/ppermute | solution.py:35
  7.0 7.9 %collective-permute-start.2 = (bf16[256,384]{1,0:T(8,128)(2,1)}, bf16[256,384]{1,0:T(8,128)(2,1)S(1)}, u32[]{:S(2)}, u32[]{:S(2)}) collective-permute-start(bf16[256,384]{1,0:T(8,128)(2,1)} %bitcast.7), channel_id=1, source_target_pairs={{0,24},{1,25},{2,26},{3,27},{4,28},{5,29},{6,30},{7,31},{8,0},{9,1... | collective-permute-start | bytes 589832 | tf_op jit(solution)/shard_map/ppermute | solution.py:35
  14.9 1.4 copy-start.16
  14.9 15.3 %collective-permute-start.3 = (bf16[768,384]{1,0:T(8,128)(2,1)S(1)}, bf16[768,384]{1,0:T(8,128)(2,1)}, u32[]{:S(2)}, u32[]{:S(2)}) collective-permute-start(bf16[768,384]{1,0:T(8,128)(2,1)S(1)} %collective-permute-done.refs_8_.refs_5_), channel_id=1, source_target_pairs={{0,8},{1,9},{2,10},{3,11},{4,12},{5,13},{6,14},{7,15},{8,16},{9,17... | collective-permute-start | bytes 1769480 | tf_op jit(solution)/shard_map/ppermute | solution.py:35
  16.2 28.9 %collective-permute-start.5 = (bf16[784,384]{1,0:T(8,128)(2,1)S(1)}, bf16[784,384]{1,0:T(8,128)(2,1)S(1)}, u32[]{:S(2)}, u32[]{:S(2)}) collective-permute-start(bf16[784,384]{1,0:T(8,128)(2,1)S(1)} %pad_maximum_fusion), channel_id=1, source_target_pairs={{0,0},{1,4},{2,2},{3,6},{4,1},{5,5},{6,3},{7,7},{8,8},{9,12},{10,1... | collective-permute-start | bytes 1806344 | tf_op jit(solution)/shard_map/ppermute | solution.py:35
  19.1 26.7 %collective-permute-start.6 = (bf16[784,384]{1,0:T(8,128)(2,1)S(1)}, bf16[784,384]{1,0:T(8,128)(2,1)S(1)}, u32[]{:S(2)}, u32[]{:S(2)}) collective-permute-start(bf16[784,384]{1,0:T(8,128)(2,1)S(1)} %pad_maximum_fusion), channel_id=1, source_target_pairs={{0,4},{1,0},{2,6},{3,2},{4,5},{5,1},{6,7},{7,3},{8,12},{9,8},{10,1... | collective-permute-start | bytes 1806344 | tf_op jit(solution)/shard_map/ppermute | solution.py:35
  19.2 26.6 %collective-permute-start.7 = (bf16[784,384]{1,0:T(8,128)(2,1)S(1)}, bf16[784,384]{1,0:T(8,128)(2,1)S(1)}, u32[]{:S(2)}, u32[]{:S(2)}) collective-permute-start(bf16[784,384]{1,0:T(8,128)(2,1)S(1)} %pad_maximum_fusion), channel_id=1, source_target_pairs={{0,2},{1,6},{2,0},{3,4},{4,3},{5,7},{6,1},{7,5},{8,10},{9,14},{10,... | collective-permute-start | bytes 1806344 | tf_op jit(solution)/shard_map/ppermute | solution.py:35
  19.9 28.3 %collective-permute-start.8 = (bf16[784,384]{1,0:T(8,128)(2,1)S(1)}, bf16[784,384]{1,0:T(8,128)(2,1)S(1)}, u32[]{:S(2)}, u32[]{:S(2)}) collective-permute-start(bf16[784,384]{1,0:T(8,128)(2,1)S(1)} %pad_maximum_fusion), channel_id=1, source_target_pairs={{0,6},{1,2},{2,4},{3,0},{4,7},{5,3},{6,5},{7,1},{8,14},{9,10},{10,... | collective-permute-start | bytes 1806344 | tf_op jit(solution)/shard_map/ppermute | solution.py:35
  30.2 14.4 %collective-permute-start.4 = (bf16[768,384]{1,0:T(8,128)(2,1)S(1)}, bf16[768,384]{1,0:T(8,128)(2,1)}, u32[]{:S(2)}, u32[]{:S(2)}) collective-permute-start(bf16[768,384]{1,0:T(8,128)(2,1)S(1)} %collective-permute-done.refs_8_.refs_5_), channel_id=1, source_target_pairs={{0,24},{1,25},{2,26},{3,27},{4,28},{5,29},{6,30},{7,31},{8,0},{9,1... | collective-permute-start | bytes 1769480 | tf_op jit(solution)/shard_map/ppermute | solution.py:35
  48.3 15.3 %collective-permute-start.13 = (bf16[768,384]{1,0:T(8,128)(2,1)}, bf16[768,384]{1,0:T(8,128)(2,1)}, u32[]{:S(2)}, u32[]{:S(2)}) collective-permute-start(bf16[768,384]{1,0:T(8,128)(2,1)} %collective-permute-done.4.refs_10_.refs_7_), channel_id=1, source_target_pairs={{8,0},{9,1},{10,2},{11,3},{12,4},{13,5},{14,6},{15,7},{16,8},{17,9... | collective-permute-start | bytes 1769480 | tf_op jit(solution)/shard_map/ppermute | solution.py:35
  51.1 17.2 %collective-permute-start.14 = (bf16[768,384]{1,0:T(8,128)(2,1)}, bf16[768,384]{1,0:T(8,128)(2,1)}, u32[]{:S(2)}, u32[]{:S(2)}) collective-permute-start(bf16[768,384]{1,0:T(8,128)(2,1)} %collective-permute-done.3.refs_9_.refs_6_), channel_id=1, source_target_pairs={{8,16},{9,17},{10,18},{11,19},{12,20},{13,21},{14,22},{15,23},{16,... | collective-permute-start | bytes 1769480 | tf_op jit(solution)/shard_map/ppermute | solution.py:35
  53.0 17.2 %collective-permute-start.15 = (bf16[768,384]{1,0:T(8,128)(2,1)S(1)}, bf16[768,384]{1,0:T(8,128)(2,1)}, u32[]{:S(2)}, u32[]{:S(2)}) collective-permute-start(bf16[768,384]{1,0:T(8,128)(2,1)S(1)} %collective-permute-done.refs_8_.refs_5_), channel_id=1, source_target_pairs={{0,1},{1,0},{2,3},{3,2},{4,5},{5,4},{6,7},{7,6},{8,9},{9,8},{10,11... | collective-permute-start | bytes 1769480 | tf_op jit(solution)/shard_map/ppermute | solution.py:35
  53.1 17.2 %copy-start.13 = (bf16[512,384]{1,0:T(8,128)(2,1)S(1)}, bf16[512,384]{1,0:T(8,128)(2,1)}, u32[]{:S(2)}) copy-start(bf16[512,384]{1,0:T(8,128)(2,1)} %pad_maximum_fusion.2) | copy-start | bytes 1179652
  53.1 17.2 %collective-permute-start.9 = (bf16[512,384]{1,0:T(8,128)(2,1)}, bf16[512,384]{1,0:T(8,128)(2,1)S(1)}, u32[]{:S(2)}, u32[]{:S(2)}) collective-permute-start(bf16[512,384]{1,0:T(8,128)(2,1)} %pad_maximum_fusion.2), channel_id=1, source_target_pairs={{0,0},{1,4},{2,2},{3,6},{4,1},{5,5},{6,3},{7,7},{8,8},{9,12},{10,1... | collective-permute-start | bytes 1179656 | tf_op jit(solution)/shard_map/ppermute | solution.py:35
  57.2 14.3 %collective-permute-start.10 = (bf16[512,384]{1,0:T(8,128)(2,1)}, bf16[512,384]{1,0:T(8,128)(2,1)S(1)}, u32[]{:S(2)}, u32[]{:S(2)}) collective-permute-start(bf16[512,384]{1,0:T(8,128)(2,1)} %pad_maximum_fusion.2), channel_id=1, source_target_pairs={{0,4},{1,0},{2,6},{3,2},{4,5},{5,1},{6,7},{7,3},{8,12},{9,8},{10,1... | collective-permute-start | bytes 1179656 | tf_op jit(solution)/shard_map/ppermute | solution.py:35
  63.6 25.8 %collective-permute-start.16 = (bf16[768,384]{1,0:T(8,128)(2,1)}, bf16[768,384]{1,0:T(8,128)(2,1)S(1)}, u32[]{:S(2)}, u32[]{:S(2)}) collective-permute-start(bf16[768,384]{1,0:T(8,128)(2,1)} %collective-permute-done.3.refs_9_.refs_6_), channel_id=1, source_target_pairs={{0,1},{1,0},{2,3},{3,2},{4,5},{5,4},{6,7},{7,6},{8,9},{9,8},{10,11... | collective-permute-start | bytes 1769480 | tf_op jit(solution)/shard_map/ppermute | solution.py:35
  68.3 21.0 %collective-permute-start.17 = (bf16[768,384]{1,0:T(8,128)(2,1)}, bf16[768,384]{1,0:T(8,128)(2,1)S(1)}, u32[]{:S(2)}, u32[]{:S(2)}) collective-permute-start(bf16[768,384]{1,0:T(8,128)(2,1)} %collective-permute-done.4.refs_10_.refs_7_), channel_id=1, source_target_pairs={{0,1},{1,0},{2,3},{3,2},{4,5},{5,4},{6,7},{7,6},{8,9},{9,8},{10,11... | collective-permute-start | bytes 1769480 | tf_op jit(solution)/shard_map/ppermute | solution.py:35
  70.2 19.1 %collective-permute-start.18 = (bf16[768,384]{1,0:T(8,128)(2,1)S(1)}, bf16[768,384]{1,0:T(8,128)(2,1)S(1)}, u32[]{:S(2)}, u32[]{:S(2)}) collective-permute-start(bf16[768,384]{1,0:T(8,128)(2,1)S(1)} %broadcast_select_fusion.refs_11_.refs_8_), channel_id=1, source_target_pairs={{0,1},{1,0},{2,3},{3,2},{4,5},{5,4},{6,7},{7,6},{8,9},{9,8},{10,11... | collective-permute-start | bytes 1769480 | tf_op jit(solution)/shard_map/ppermute | solution.py:35
  70.3 12.4 %collective-permute-start.11 = (bf16[512,384]{1,0:T(8,128)(2,1)S(1)}, bf16[512,384]{1,0:T(8,128)(2,1)S(1)}, u32[]{:S(2)}, u32[]{:S(2)}) collective-permute-start(bf16[512,384]{1,0:T(8,128)(2,1)S(1)} %copy-done.13), channel_id=1, source_target_pairs={{0,2},{1,6},{2,0},{3,4},{4,3},{5,7},{6,1},{7,5},{8,10},{9,14},{10,... | collective-permute-start | bytes 1179656 | tf_op jit(solution)/shard_map/ppermute | solution.py:35
  71.5 17.8 %collective-permute-start.12 = (bf16[512,384]{1,0:T(8,128)(2,1)S(1)}, bf16[512,384]{1,0:T(8,128)(2,1)S(1)}, u32[]{:S(2)}, u32[]{:S(2)}) collective-permute-start(bf16[512,384]{1,0:T(8,128)(2,1)S(1)} %copy-done.13), channel_id=1, source_target_pairs={{0,6},{1,2},{2,4},{3,0},{4,7},{5,3},{6,5},{7,1},{8,14},{9,10},{10,... | collective-permute-start | bytes 1179656 | tf_op jit(solution)/shard_map/ppermute | solution.py:35
  93.0 3.5 %copy-start = (bf16[1536,768]{1,0:T(8,128)(2,1)}, bf16[1536,768]{1,0:T(8,128)(2,1)S(1)}, u32[]{:S(2)}) copy-start(bf16[1536,768]{1,0:T(8,128)(2,1)S(1)} %get-tuple-element.78.whole) | copy-start | bytes 7077892
  93.0 7.5 %collective-permute-start.19 = (bf16[512,768]{1,0:T(8,128)(2,1)S(1)}, bf16[512,768]{1,0:T(8,128)(2,1)S(1)}, u32[]{:S(2)}, u32[]{:S(2)}) collective-permute-start(bf16[512,768]{1,0:T(8,128)(2,1)S(1)} %get-tuple-element.55), channel_id=1, source_target_pairs={{0,1},{1,0},{2,3},{3,2},{4,5},{5,4},{6,7},{7,6},{8,9},{9,8},{10,11... | collective-permute-start | bytes 2359304 | tf_op jit(solution)/shard_map/ppermute | solution.py:35
  99.0 1.5 copy-start.2
  108.5 0.9 copy-start.4
  109.4 0.9 copy-start.6
  110.2 0.7 copy-start.9
  110.9 0.7 copy-start.11
  111.6 6.3 %collective-permute-start.20 = (bf16[512,768]{1,0:T(8,128)(2,1)}, bf16[512,768]{1,0:T(8,128)(2,1)S(1)}, u32[]{:S(2)}, u32[]{:S(2)}) collective-permute-start(bf16[512,768]{1,0:T(8,128)(2,1)} %get-tuple-element.60), channel_id=1, source_target_pairs={{0,1},{1,0},{2,3},{3,2},{4,5},{5,4},{6,7},{7,6},{8,9},{9,8},{10,11... | collective-permute-start | bytes 2359304 | tf_op jit(solution)/shard_map/ppermute | solution.py:35
  111.6 1.7 %copy-start.3 = (bf16[1536,768]{1,0:T(8,128)(2,1)S(1)}, bf16[1536,768]{1,0:T(8,128)(2,1)}, u32[]{:S(2)}) copy-start(bf16[1536,768]{1,0:T(8,128)(2,1)} %copy-done.2) | copy-start | bytes 7077892
  113.3 0.9 copy-start.10
  114.2 0.9 copy-start.12
  115.2 2.7 %copy-start.7 = (bf16[512,768]{1,0:T(8,128)(2,1)S(1)}, bf16[512,768]{1,0:T(8,128)(2,1)}, u32[]{:S(2)}) copy-start(bf16[512,768]{1,0:T(8,128)(2,1)} %copy-done.6) | copy-start | bytes 2359300
  115.2 22.8 %copy-start.1 = (bf16[1536,768]{1,0:T(8,128)(2,1)S(1)}, bf16[1536,768]{1,0:T(8,128)(2,1)}, u32[]{:S(2)}) copy-start(bf16[1536,768]{1,0:T(8,128)(2,1)} %copy-done) | copy-start | bytes 7077892
  117.9 20.1 %copy-start.5 = (f32[256,768]{1,0:T(8,128)S(1)}, f32[256,768]{1,0:T(8,128)}, u32[]{:S(2)}) copy-start(f32[256,768]{1,0:T(8,128)} %copy-done.4) | copy-start | bytes 2359300
  118.1 18.7 %collective-permute-start.25 = (bf16[256,768]{1,0:T(8,128)(2,1)S(1)}, bf16[256,768]{1,0:T(8,128)(2,1)S(1)}, u32[]{:S(2)}, u32[]{:S(2)}) collective-permute-start(bf16[256,768]{1,0:T(8,128)(2,1)S(1)} %get-tuple-element.76), channel_id=1, source_target_pairs={{0,8},{1,9},{2,10},{3,11},{4,12},{5,13},{6,14},{7,15},{8,16},{9,17... | collective-permute-start | bytes 1179656 | tf_op jit(solution)/shard_map/ppermute | solution.py:35
  118.2 23.3 %collective-permute-start.21 = (bf16[528,384]{1,0:T(8,128)(2,1)S(1)}, bf16[528,384]{1,0:T(8,128)(2,1)S(1)}, u32[]{:S(2)}, u32[]{:S(2)}) collective-permute-start(bf16[528,384]{1,0:T(8,128)(2,1)S(1)} %get-tuple-element.69), channel_id=1, source_target_pairs={{0,0},{1,4},{2,2},{3,6},{4,1},{5,5},{6,3},{7,7},{8,8},{9,12},{10,1... | collective-permute-start | bytes 1216520 | tf_op jit(solution)/shard_map/ppermute | solution.py:35
  121.9 19.9 %collective-permute-start.22 = (bf16[528,384]{1,0:T(8,128)(2,1)S(1)}, bf16[528,384]{1,0:T(8,128)(2,1)S(1)}, u32[]{:S(2)}, u32[]{:S(2)}) collective-permute-start(bf16[528,384]{1,0:T(8,128)(2,1)S(1)} %get-tuple-element.70), channel_id=1, source_target_pairs={{0,1},{1,5},{2,3},{3,7},{4,0},{5,4},{6,2},{7,6},{8,9},{9,13},{10,1... | collective-permute-start | bytes 1216520 | tf_op jit(solution)/shard_map/ppermute | solution.py:35
  121.9 20.4 %collective-permute-start.23 = (bf16[528,384]{1,0:T(8,128)(2,1)S(1)}, bf16[528,384]{1,0:T(8,128)(2,1)S(1)}, u32[]{:S(2)}, u32[]{:S(2)}) collective-permute-start(bf16[528,384]{1,0:T(8,128)(2,1)S(1)} %get-tuple-element.71), channel_id=1, source_target_pairs={{0,2},{1,6},{2,0},{3,4},{4,3},{5,7},{6,1},{7,5},{8,10},{9,14},{10,... | collective-permute-start | bytes 1216520 | tf_op jit(solution)/shard_map/ppermute | solution.py:35
  122.0 16.0 %collective-permute-start.26 = (bf16[256,768]{1,0:T(8,128)(2,1)S(1)}, bf16[256,768]{1,0:T(8,128)(2,1)S(1)}, u32[]{:S(2)}, u32[]{:S(2)}) collective-permute-start(bf16[256,768]{1,0:T(8,128)(2,1)S(1)} %get-tuple-element.77), channel_id=1, source_target_pairs={{0,24},{1,25},{2,26},{3,27},{4,28},{5,29},{6,30},{7,31},{8,0},{9,1... | collective-permute-start | bytes 1179656 | tf_op jit(solution)/shard_map/ppermute | solution.py:35
  136.8 11.6 %collective-permute-start.24 = (bf16[528,384]{1,0:T(8,128)(2,1)S(1)}, bf16[528,384]{1,0:T(8,128)(2,1)S(1)}, u32[]{:S(2)}, u32[]{:S(2)}) collective-permute-start(bf16[528,384]{1,0:T(8,128)(2,1)S(1)} %get-tuple-element.72), channel_id=1, source_target_pairs={{0,3},{1,7},{2,1},{3,5},{4,2},{5,6},{6,0},{7,4},{8,11},{9,15},{10,... | collective-permute-start | bytes 1216520 | tf_op jit(solution)/shard_map/ppermute | solution.py:35
  139.0 13.7 %collective-permute-start.30 = (bf16[256,384]{1,0:T(8,128)(2,1)S(1)}, bf16[256,384]{1,0:T(8,128)(2,1)S(1)}, u32[]{:S(2)}, u32[]{:S(2)}) collective-permute-start(bf16[256,384]{1,0:T(8,128)(2,1)S(1)} %get-tuple-element.82), channel_id=1, source_target_pairs={{0,3},{1,7},{2,1},{3,5},{4,2},{5,6},{6,0},{7,4},{8,11},{9,15},{10,... | collective-permute-start | bytes 589832 | tf_op jit(solution)/shard_map/ppermute | solution.py:35
  141.5 17.0 %collective-permute-start.29 = (bf16[256,384]{1,0:T(8,128)(2,1)S(1)}, bf16[256,384]{1,0:T(8,128)(2,1)S(1)}, u32[]{:S(2)}, u32[]{:S(2)}) collective-permute-start(bf16[256,384]{1,0:T(8,128)(2,1)S(1)} %get-tuple-element.81), channel_id=1, source_target_pairs={{0,2},{1,6},{2,0},{3,4},{4,3},{5,7},{6,1},{7,5},{8,10},{9,14},{10,... | collective-permute-start | bytes 589832 | tf_op jit(solution)/shard_map/ppermute | solution.py:35
  141.8 16.6 %collective-permute-start.28 = (bf16[256,384]{1,0:T(8,128)(2,1)S(1)}, bf16[256,384]{1,0:T(8,128)(2,1)S(1)}, u32[]{:S(2)}, u32[]{:S(2)}) collective-permute-start(bf16[256,384]{1,0:T(8,128)(2,1)S(1)} %get-tuple-element.80), channel_id=1, source_target_pairs={{0,1},{1,5},{2,3},{3,7},{4,0},{5,4},{6,2},{7,6},{8,9},{9,13},{10,1... | collective-permute-start | bytes 589832 | tf_op jit(solution)/shard_map/ppermute | solution.py:35
  142.3 16.1 %collective-permute-start.27 = (bf16[256,384]{1,0:T(8,128)(2,1)S(1)}, bf16[256,384]{1,0:T(8,128)(2,1)S(1)}, u32[]{:S(2)}, u32[]{:S(2)}) collective-permute-start(bf16[256,384]{1,0:T(8,128)(2,1)S(1)} %get-tuple-element.79), channel_id=1, source_target_pairs={{0,0},{1,4},{2,2},{3,6},{4,1},{5,5},{6,3},{7,7},{8,8},{9,12},{10,1... | collective-permute-start | bytes 589832 | tf_op jit(solution)/shard_map/ppermute | solution.py:35

commit v3 on v2

--- a/solution.py
+++ b/solution.py
@@ -298,7 +298,7 @@
         in_specs=specs,
         out_specs=[VMEM] * len(outs),
         scratch_shapes=scratch,
-        compiler_params=pltpu.CompilerParams(vmem_limit_bytes=40 * 1024 * 1024),
+        compiler_params=pltpu.CompilerParams(vmem_limit_bytes=16 * 1024 * 1024),
     )(*operands)
 
 
@@ -318,19 +318,29 @@
     extra = extra + jnp.pad(neighbours.reshape(1, ids).astype(LOW), ((1, EXTRA - 2), (0, width - ids)))
     packed = jnp.concatenate([hidden_rows, extra, grad_out, own_enc], axis=0)
     weights, enc_below, enc_above, packed = tie(weights, enc_below, enc_above, packed)
-    tokens = [move(packed, spread(k)) for k in range(4)]
     outer = jnp.concatenate([enc_below, enc_above], axis=0)
+    tokens, outers = [None] * 4, [None] * 4
     if seq_count == 8:
         below, above = move(weights, ring_up), move(weights, ring_down)
+        own_other = move(weights, flip_core)
+        tokens[2], tokens[3] = move(packed, spread(2)), move(packed, spread(3))
+        packed, own_other = tie(packed, own_other)
+        tokens[0] = move(packed, spread(0))
+        packed, tokens[0] = tie(packed, tokens[0])
+        tokens[1] = move(packed, spread(1))
         outer, below, above, *tokens = tie(outer, below, above, *tokens)
-        two_below = move(below, lambda z, y, x, c: (z + 1, y, x, c) if z in (1, 2) else None)
-        two_above = move(above, lambda z, y, x, c: (z - 1, y, x, c) if z in (1, 2) else None)
-        pieces = [weights, below, above, jnp.where(z <= 1, two_above, two_below)]
-        pieces = pieces + [move(piece, flip_core) for piece in pieces]
-        kv_pieces = qo_pieces = pieces
+        two = move(jnp.where(z % 2 == 0, below, above), lambda z, y, x, c: (z ^ 1, y, x, c))
+        below_other, above_other = move(below, flip_core), move(above, flip_core)
+        outers[2], outers[3] = move(outer, spread(2)), move(outer, spread(3))
+        outer, below_other, above_other = tie(outer, below_other, above_other)
+        outers[0], outers[1] = move(outer, spread(0)), move(outer, spread(1))
+        two_other = move(two, flip_core)
+        kv_pieces = [weights, below, above, two, own_other, below_other, above_other, two_other]
+        qo_pieces = kv_pieces
     else:
         kv_pieces, qo_pieces = any_weights(weights, c, g)
-    outer = [move(outer, spread(k)) for k in range(4)]
+        tokens = [move(packed, spread(k)) for k in range(4)]
+        outers = [move(outer, spread(k)) for k in range(4)]
     piece_count = len(kv_pieces)
 
     chosen = tokens[0][token_count + 1, :ids].astype(jnp.int32)
@@ -344,7 +354,7 @@
     )
     whole_kv, tables, shared = call(
         lambda *refs: table_kernel(token_count, *refs),
-        tokens + outer + kv_pieces,
+        tokens + outers + kv_pieces,
         [ANY] * (8 + piece_count),
         [((full_width, wide), LOW), ((3 * OWN_ROWS, wide), LOW), ((2 * OWN_ROWS, wide), LOW)],
         [pltpu.VMEM((3 * OWN_ROWS, full_width), LOW)],
@@ -390,6 +400,7 @@
     )
     to_below, to_above, *terms = tie(to_below, to_above, *terms)
     up, down = move(to_above, ring_up), move(to_below, ring_down)
+    terms[1], up = tie(terms[1], up)
     terms = [move(term, gather_back(k)) for k, term in enumerate(terms)]
     branch_out, grad_rows = call(
         finish_kernel,

time: 160 us -> 189 us (1.18)
  the two profiles are of different devices: /device:TPU:19 before, /device:TPU:1 now
where the time goes in v3:
time: 189 us; the launch traced here: 187 us
  waiting for transfers between devices  111 us (59%)
  starting transfers between devices  39.3 us (21%)
  Pallas kernels  20 us (11%)
  local copies, waits for them, and re-layouts  10.3 us (5%)
  other arithmetic  5.02 us (3%)
    ppermute x30, waiting for transfers between devices, move(): return lax.ppermute(value, ('seq', 'mp'), pairs)  111 us
    ppermute x30, starting transfers between devices, move(): return lax.ppermute(value, ('seq', 'mp'), pairs)  39.3 us
    pallas_call x7, Pallas kernels, call(): pl.pallas_call(kernel, out_shape=[jax.ShapeDtypeStruct(shape, dtype) for...  20 us
    unnamed x40, local copies, waits for them, and re-layouts  9.39 us
  transfers between devices with their start and end apart: 30, of which 17 were waited for; matrix products, arithmetic and copies ran while one was open for 2% of the time, Pallas kernels for 3%

profile of v3, /device:TPU:1, one launch (start us, length us, event | category | flops | bytes accessed | tf_op | source)
XLA Modules:
  0.0 186.9 jit_solution(14339266385101959761)
XLA Ops:
  0.7 1.2 pad_maximum_fusion.1
  1.9 4.5 %collective-permute-start = (bf16[768,384]{1,0:T(8,128)(2,1)S(1)}, bf16[768,384]{1,0:T(8,128)(2,1)S(1)}, u32[]{:S(2)}, u32[]{:S(2)}) collective-permute-start(bf16[768,384]{1,0:T(8,128)(2,1)S(1)} %pad_maximum_fusion.1), channel_id=1, source_target_pairs={{0,0},{1,4},{2,2},{3,6},{4,1},{5,5},{6,3},{7,7},{8,8},{9,12},{10,1... | collective-permute-start | bytes 1769480 | tf_op jit(solution)/shard_map/ppermute | solution.py:35
  6.5 1.3 collective-permute-start.1
  7.8 2.1 %collective-permute-start.2 = (bf16[256,384]{1,0:T(8,128)(2,1)}, bf16[256,384]{1,0:T(8,128)(2,1)S(1)}, u32[]{:S(2)}, u32[]{:S(2)}) collective-permute-start(bf16[256,384]{1,0:T(8,128)(2,1)} %bitcast.7), channel_id=1, source_target_pairs={{0,24},{1,25},{2,26},{3,27},{4,28},{5,29},{6,30},{7,31},{8,0},{9,1... | collective-permute-start | bytes 589832 | tf_op jit(solution)/shard_map/ppermute | solution.py:35
  11.5 0.9 pad_maximum_fusion
  12.4 2.9 %collective-permute-done.1 = bf16[256,384]{1,0:T(8,128)(2,1)S(1)} collective-permute-done((bf16[256,384]{1,0:T(8,128)(2,1)}, bf16[256,384]{1,0:T(8,128)(2,1)S(1)}, u32[]{:S(2)}, u32[]{:S(2)}) %collective-permute-start.1) | collective-permute-done | bytes 196640 | tf_op jit(solution)/shard_map/ppermute | solution.py:35
  15.3 2.1 %collective-permute-done.2 = bf16[256,384]{1,0:T(8,128)(2,1)S(1)} collective-permute-done((bf16[256,384]{1,0:T(8,128)(2,1)}, bf16[256,384]{1,0:T(8,128)(2,1)S(1)}, u32[]{:S(2)}, u32[]{:S(2)}) %collective-permute-start.2) | collective-permute-done | bytes 196640 | tf_op jit(solution)/shard_map/ppermute | solution.py:35
  18.2 1.2 collective-permute-done.5.refs_12_.refs_9_
  20.3 2.2 %collective-permute-start.6 = (bf16[784,384]{1,0:T(8,128)(2,1)}, bf16[784,384]{1,0:T(8,128)(2,1)S(1)}, u32[]{:S(2)}, u32[]{:S(2)}) collective-permute-start(bf16[784,384]{1,0:T(8,128)(2,1)} %pad_maximum_fusion), channel_id=1, source_target_pairs={{0,0},{1,4},{2,2},{3,6},{4,1},{5,5},{6,3},{7,7},{8,8},{9,12},{10,1... | collective-permute-start | bytes 1806344 | tf_op jit(solution)/shard_map/ppermute | solution.py:35
  22.5 2.3 %collective-permute-start.8 = (bf16[784,384]{1,0:T(8,128)(2,1)}, bf16[784,384]{1,0:T(8,128)(2,1)S(1)}, u32[]{:S(2)}, u32[]{:S(2)}) collective-permute-start(bf16[784,384]{1,0:T(8,128)(2,1)} %pad_maximum_fusion), channel_id=1, source_target_pairs={{0,2},{1,6},{2,0},{3,4},{4,3},{5,7},{6,1},{7,5},{8,10},{9,14},{10,... | collective-permute-start | bytes 1806344 | tf_op jit(solution)/shard_map/ppermute | solution.py:35
  24.8 17.0 %collective-permute-done.6.refs_0_.refs_1_.refs_4_ = bf16[784,384]{1,0:T(8,128)(2,1)S(1)} collective-permute-done((bf16[784,384]{1,0:T(8,128)(2,1)}, bf16[784,384]{1,0:T(8,128)(2,1)S(1)}, u32[]{:S(2)}, u32[]{:S(2)}) %collective-permute-start.6) | collective-permute-done | bytes 602144 | tf_op jit(solution)/shard_map/ppermute | solution.py:35
  41.8 3.3 %collective-permute-start.4 = (bf16[768,384]{1,0:T(8,128)(2,1)}, bf16[768,384]{1,0:T(8,128)(2,1)}, u32[]{:S(2)}, u32[]{:S(2)}) collective-permute-start(bf16[768,384]{1,0:T(8,128)(2,1)} %copy-done.4), channel_id=1, source_target_pairs={{0,24},{1,25},{2,26},{3,27},{4,28},{5,29},{6,30},{7,31},{8,0},{9,1... | collective-permute-start | bytes 1769480 | tf_op jit(solution)/shard_map/ppermute | solution.py:35
  45.1 1.1 pad_maximum_fusion.2
  46.2 12.8 %collective-permute-done.3.refs_9_.refs_6_ = bf16[768,384]{1,0:T(8,128)(2,1)S(1)} collective-permute-done((bf16[768,384]{1,0:T(8,128)(2,1)}, bf16[768,384]{1,0:T(8,128)(2,1)S(1)}, u32[]{:S(2)}, u32[]{:S(2)}) %collective-permute-start.3) | collective-permute-done | bytes 589856 | tf_op jit(solution)/shard_map/ppermute | solution.py:35
  59.0 10.9 %collective-permute-done.4.refs_10_.refs_7_ = bf16[768,384]{1,0:T(8,128)(2,1)} collective-permute-done((bf16[768,384]{1,0:T(8,128)(2,1)}, bf16[768,384]{1,0:T(8,128)(2,1)}, u32[]{:S(2)}, u32[]{:S(2)}) %collective-permute-start.4) | collective-permute-done | bytes 589856 | tf_op jit(solution)/shard_map/ppermute | solution.py:35
  70.0 1.3 collective-permute-start.16
  71.3 1.3 collective-permute-start.10
  72.6 11.7 %collective-permute-done.16.refs_11_.refs_8_ = bf16[768,384]{1,0:T(8,128)(2,1)S(1)} collective-permute-done((bf16[768,384]{1,0:T(8,128)(2,1)S(1)}, bf16[768,384]{1,0:T(8,128)(2,1)S(1)}, u32[]{:S(2)}, u32[]{:S(2)}) %collective-permute-start.16) | collective-permute-done | bytes 589856 | tf_op jit(solution)/shard_map/ppermute | solution.py:35
  84.3 1.6 collective-permute-start.17
  85.8 1.5 collective-permute-start.14
  87.5 3.0 %collective-permute-start.12 = (bf16[512,384]{1,0:T(8,128)(2,1)S(1)}, bf16[512,384]{1,0:T(8,128)(2,1)S(1)}, u32[]{:S(2)}, u32[]{:S(2)}) collective-permute-start(bf16[512,384]{1,0:T(8,128)(2,1)S(1)} %pad_maximum_fusion.2), channel_id=1, source_target_pairs={{0,0},{1,4},{2,2},{3,6},{4,1},{5,5},{6,3},{7,7},{8,8},{9,12},{10,1... | collective-permute-start | bytes 1179656 | tf_op jit(solution)/shard_map/ppermute | solution.py:35
  90.5 7.8 %collective-permute-done.14.refs_6_ = bf16[512,384]{1,0:T(8,128)(2,1)S(1)} collective-permute-done((bf16[512,384]{1,0:T(8,128)(2,1)S(1)}, bf16[512,384]{1,0:T(8,128)(2,1)S(1)}, u32[]{:S(2)}, u32[]{:S(2)}) %collective-permute-start.14) | collective-permute-done | bytes 393248 | tf_op jit(solution)/shard_map/ppermute | solution.py:35
  98.3 6.2 %collective-permute-done.15.refs_7_ = bf16[512,384]{1,0:T(8,128)(2,1)S(1)} collective-permute-done((bf16[512,384]{1,0:T(8,128)(2,1)S(1)}, bf16[512,384]{1,0:T(8,128)(2,1)S(1)}, u32[]{:S(2)}, u32[]{:S(2)}) %collective-permute-start.15) | collective-permute-done | bytes 393248 | tf_op jit(solution)/shard_map/ppermute | solution.py:35
  104.5 3.1 %collective-permute-done.12.refs_4_ = bf16[512,384]{1,0:T(8,128)(2,1)S(1)} collective-permute-done((bf16[512,384]{1,0:T(8,128)(2,1)S(1)}, bf16[512,384]{1,0:T(8,128)(2,1)S(1)}, u32[]{:S(2)}, u32[]{:S(2)}) %collective-permute-start.12) | collective-permute-done | bytes 393248 | tf_op jit(solution)/shard_map/ppermute | solution.py:35
  107.9 3.4 %shard_map.112 = (bf16[1536,768]{1,0:T(8,128)(2,1)S(1)}, bf16[768,768]{1,0:T(8,128)(2,1)S(1)}, bf16[512,768]{1,0:T(8,128)(2,1)S(1)}) custom-call(bf16[784,384]{1,0:T(8,128)(2,1)S(1)} %collective-permute-done.6.refs_0_.refs_1_.refs_4_, bf16[784,384]{1,0:T(8,128)(2,1)S(1)} %collective-permute-done.7.refs_1_.refs_2_.refs_5_, ...), custom_call_target="tpu_custom_call" | custom-call | tf_op jit(solution)/shard_map/pallas_call | solution.py:295
  111.5 1.5 shard_map.113
  113.0 2.3 %shard_map.114 = (bf16[1536,768]{1,0:T(8,128)(2,1)S(1)}, bf16[256,384]{1,0:T(8,128)(2,1)S(1)}, bf16[256,384]{1,0:T(8,128)(2,1)S(1)}) custom-call(bf16[256,1536]{1,0:T(8,128)(2,1)S(1)} %get-tuple-element.72.refs_0_, bf16[784,384]{1,0:T(8,128)(2,1)S(1)} %collective-permute-done.6.refs_0_.refs_1_.refs_4_, ...), custom_call_target="tpu_custom_call" | custom-call | tf_op jit(solution)/shard_map/pallas_call | solution.py:295
  115.3 1.5 copy-done.2
  116.8 8.0 %shard_map.115 = (bf16[256,384]{1,0:T(8,128)(2,1)S(1)}, bf16[256,384]{1,0:T(8,128)(2,1)S(1)}, f32[256,768]{1,0:T(8,128)S(1)}, bf16[512,768]{1,0:T(8,128)(2,1)S(1)}, bf16[512,768]{1,0:T(8,128)(2,1)}) custom-call(s32[8]{0:T(128)S(1)} %bitcast_convert_fusion.refs_0_, bf16[768,768]{1,0:T(8,128)(2,1)S(1)} %get-tuple-element.70.refs_1_, ...), custom_call_target="tpu_custom_call" | custom-call | tf_op jit(solution)/shard_map/pallas_call | solution.py:295
  125.6 0.9 copy-done.10
  128.3 1.7 copy-done.3
  130.0 0.9 copy-done.14
  130.9 0.9 copy-done.16
  131.9 2.7 %shard_map.116 = (bf16[528,384]{1,0:T(8,128)(2,1)S(1)}, bf16[528,384]{1,0:T(8,128)(2,1)S(1)}, bf16[528,384]{1,0:T(8,128)(2,1)S(1)}, bf16[528,384]{1,0:T(8,128)(2,1)S(1)}) custom-call(bf16[256,384]{1,0:T(8,128)(2,1)S(1)} %copy-done.14, bf16[256,384]{1,0:T(8,128)(2,1)S(1)} %copy-done.16, f32[256,1]{1,0:T(8,128)S(1)} %get-tuple-element.79.refs_2_, ...), custom_call_target="tpu_custom_call" | custom-call | tf_op jit(solution)/shard_map/pallas_call | solution.py:295
  134.8 1.3 collective-permute-start.21
  136.1 2.0 %collective-permute-start.25 = (bf16[256,768]{1,0:T(8,128)(2,1)S(1)}, bf16[256,768]{1,0:T(8,128)(2,1)S(1)}, u32[]{:S(2)}, u32[]{:S(2)}) collective-permute-start(bf16[256,768]{1,0:T(8,128)(2,1)S(1)} %get-tuple-element.95), channel_id=1, source_target_pairs={{0,24},{1,25},{2,26},{3,27},{4,28},{5,29},{6,30},{7,31},{8,0},{9,1... | collective-permute-start | bytes 1179656 | tf_op jit(solution)/shard_map/ppermute | solution.py:35
  138.1 9.3 %collective-permute-done.21.up = bf16[256,768]{1,0:T(8,128)(2,1)S(1)} collective-permute-done((bf16[256,768]{1,0:T(8,128)(2,1)S(1)}, bf16[256,768]{1,0:T(8,128)(2,1)S(1)}, u32[]{:S(2)}, u32[]{:S(2)}) %collective-permute-start.21) | collective-permute-done | bytes 393248 | tf_op jit(solution)/shard_map/ppermute | solution.py:35
  147.4 7.6 %collective-permute-done.25.down = bf16[256,768]{1,0:T(8,128)(2,1)S(1)} collective-permute-done((bf16[256,768]{1,0:T(8,128)(2,1)S(1)}, bf16[256,768]{1,0:T(8,128)(2,1)S(1)}, u32[]{:S(2)}, u32[]{:S(2)}) %collective-permute-start.25) | collective-permute-done | bytes 393248 | tf_op jit(solution)/shard_map/ppermute | solution.py:35
  155.0 1.0 shard_map.118
  156.0 1.2 collective-permute-start.29
  157.3 2.4 %collective-permute-start.28 = (bf16[256,384]{1,0:T(8,128)(2,1)S(1)}, bf16[256,384]{1,0:T(8,128)(2,1)S(1)}, u32[]{:S(2)}, u32[]{:S(2)}) collective-permute-start(bf16[256,384]{1,0:T(8,128)(2,1)S(1)} %get-tuple-element.99), channel_id=1, source_target_pairs={{0,2},{1,6},{2,0},{3,4},{4,3},{5,7},{6,1},{7,5},{8,10},{9,14},{10,... | collective-permute-start | bytes 589832 | tf_op jit(solution)/shard_map/ppermute | solution.py:35
  159.7 2.6 %collective-permute-start.26 = (bf16[256,384]{1,0:T(8,128)(2,1)S(1)}, bf16[256,384]{1,0:T(8,128)(2,1)S(1)}, u32[]{:S(2)}, u32[]{:S(2)}) collective-permute-start(bf16[256,384]{1,0:T(8,128)(2,1)S(1)} %get-tuple-element.97), channel_id=1, source_target_pairs={{0,0},{1,4},{2,2},{3,6},{4,1},{5,5},{6,3},{7,7},{8,8},{9,12},{10,1... | collective-permute-start | bytes 589832 | tf_op jit(solution)/shard_map/ppermute | solution.py:35
  162.2 3.0 %collective-permute-start.20 = (bf16[528,384]{1,0:T(8,128)(2,1)S(1)}, bf16[528,384]{1,0:T(8,128)(2,1)S(1)}, u32[]{:S(2)}, u32[]{:S(2)}) collective-permute-start(bf16[528,384]{1,0:T(8,128)(2,1)S(1)} %get-tuple-element.85), channel_id=1, source_target_pairs={{0,0},{1,4},{2,2},{3,6},{4,1},{5,5},{6,3},{7,7},{8,8},{9,12},{10,1... | collective-permute-start | bytes 1216520 | tf_op jit(solution)/shard_map/ppermute | solution.py:35
  165.2 1.2 collective-permute-start.23
  166.5 2.9 %collective-permute-done.28 = bf16[256,384]{1,0:T(8,128)(2,1)S(1)} collective-permute-done((bf16[256,384]{1,0:T(8,128)(2,1)S(1)}, bf16[256,384]{1,0:T(8,128)(2,1)S(1)}, u32[]{:S(2)}, u32[]{:S(2)}) %collective-permute-start.28) | collective-permute-done | bytes 196640 | tf_op jit(solution)/shard_map/ppermute | solution.py:35
  171.1 7.9 %collective-permute-done.20.refs_0_ = bf16[528,384]{1,0:T(8,128)(2,1)S(1)} collective-permute-done((bf16[528,384]{1,0:T(8,128)(2,1)S(1)}, bf16[528,384]{1,0:T(8,128)(2,1)S(1)}, u32[]{:S(2)}, u32[]{:S(2)}) %collective-permute-start.20) | collective-permute-done | bytes 405536 | tf_op jit(solution)/shard_map/ppermute | solution.py:35
  179.0 6.8 %collective-permute-done.24.refs_3_ = bf16[528,384]{1,0:T(8,128)(2,1)S(1)} collective-permute-done((bf16[528,384]{1,0:T(8,128)(2,1)S(1)}, bf16[528,384]{1,0:T(8,128)(2,1)S(1)}, u32[]{:S(2)}, u32[]{:S(2)}) %collective-permute-start.24) | collective-permute-done | bytes 405536 | tf_op jit(solution)/shard_map/ppermute | solution.py:35
  185.8 1.2 shard_map.117
  (71 shorter events, 8.6 us)
Async XLA Ops:
  0.6 10.8 %copy-start.18 = (bf16[2,128,384]{2,1,0:T(8,128)(2,1)S(1)}, bf16[2,128,384]{2,1,0:T(8,128)(2,1)}, u32[]{:S(2)}) copy-start(bf16[2,128,384]{2,1,0:T(8,128)(2,1)} %param.11) | copy-start | bytes 589828
  0.6 10.8 %copy-start.12 = (bf16[256,384]{1,0:T(8,128)(2,1)S(1)}, bf16[256,384]{1,0:T(8,128)(2,1)}, u32[]{:S(2)}) copy-start(bf16[256,384]{1,0:T(8,128)(2,1)} %hidden.1) | copy-start | bytes 589828
  0.7 10.8 %copy-start.17 = (bf16[256,384]{1,0:T(8,128)(2,1)S(1)}, bf16[256,384]{1,0:T(8,128)(2,1)}, u32[]{:S(2)}) copy-start(bf16[256,384]{1,0:T(8,128)(2,1)} %param.17) | copy-start | bytes 589828
  1.9 15.4 %collective-permute-start = (bf16[768,384]{1,0:T(8,128)(2,1)S(1)}, bf16[768,384]{1,0:T(8,128)(2,1)S(1)}, u32[]{:S(2)}, u32[]{:S(2)}) collective-permute-start(bf16[768,384]{1,0:T(8,128)(2,1)S(1)} %pad_maximum_fusion.1), channel_id=1, source_target_pairs={{0,0},{1,4},{2,2},{3,6},{4,1},{5,5},{6,3},{7,7},{8,8},{9,12},{10,1... | collective-permute-start | bytes 1769480 | tf_op jit(solution)/shard_map/ppermute | solution.py:35
  6.5 8.8 %collective-permute-start.1 = (bf16[256,384]{1,0:T(8,128)(2,1)}, bf16[256,384]{1,0:T(8,128)(2,1)S(1)}, u32[]{:S(2)}, u32[]{:S(2)}) collective-permute-start(bf16[256,384]{1,0:T(8,128)(2,1)} %bitcast.6), channel_id=1, source_target_pairs={{0,8},{1,9},{2,10},{3,11},{4,12},{5,13},{6,14},{7,15},{8,16},{9,17... | collective-permute-start | bytes 589832 | tf_op jit(solution)/shard_map/ppermute | solution.py:35
  7.8 9.5 %collective-permute-start.2 = (bf16[256,384]{1,0:T(8,128)(2,1)}, bf16[256,384]{1,0:T(8,128)(2,1)S(1)}, u32[]{:S(2)}, u32[]{:S(2)}) collective-permute-start(bf16[256,384]{1,0:T(8,128)(2,1)} %bitcast.7), channel_id=1, source_target_pairs={{0,24},{1,25},{2,26},{3,27},{4,28},{5,29},{6,30},{7,31},{8,0},{9,1... | collective-permute-start | bytes 589832 | tf_op jit(solution)/shard_map/ppermute | solution.py:35
  17.4 24.5 %copy-start.19 = (bf16[256,384]{1,0:T(8,128)(2,1)}, bf16[256,384]{1,0:T(8,128)(2,1)S(1)}, u32[]{:S(2)}) copy-start(bf16[256,384]{1,0:T(8,128)(2,1)S(1)} %collective-permute-done.2) | copy-start | bytes 589828
  17.4 0.9 copy-start.4
  17.4 2.1 %collective-permute-start.5 = (bf16[768,384]{1,0:T(8,128)(2,1)S(1)}, bf16[768,384]{1,0:T(8,128)(2,1)S(1)}, u32[]{:S(2)}, u32[]{:S(2)}) collective-permute-start(bf16[768,384]{1,0:T(8,128)(2,1)S(1)} %collective-permute-done.refs_8_.refs_5_), channel_id=1, source_target_pairs={{0,1},{1,0},{2,3},{3,2},{4,5},{5,4},{6,7},{7,6},{8,9},{9,8},{10,11... | collective-permute-start | bytes 1769480 | tf_op jit(solution)/shard_map/ppermute | solution.py:35
  19.4 0.8 copy-start.6
  20.3 21.6 %collective-permute-start.6 = (bf16[784,384]{1,0:T(8,128)(2,1)}, bf16[784,384]{1,0:T(8,128)(2,1)S(1)}, u32[]{:S(2)}, u32[]{:S(2)}) collective-permute-start(bf16[784,384]{1,0:T(8,128)(2,1)} %pad_maximum_fusion), channel_id=1, source_target_pairs={{0,0},{1,4},{2,2},{3,6},{4,1},{5,5},{6,3},{7,7},{8,8},{9,12},{10,1... | collective-permute-start | bytes 1806344 | tf_op jit(solution)/shard_map/ppermute | solution.py:35
  22.5 47.4 %collective-permute-start.8 = (bf16[784,384]{1,0:T(8,128)(2,1)}, bf16[784,384]{1,0:T(8,128)(2,1)S(1)}, u32[]{:S(2)}, u32[]{:S(2)}) collective-permute-start(bf16[784,384]{1,0:T(8,128)(2,1)} %pad_maximum_fusion), channel_id=1, source_target_pairs={{0,2},{1,6},{2,0},{3,4},{4,3},{5,7},{6,1},{7,5},{8,10},{9,14},{10,... | collective-permute-start | bytes 1806344 | tf_op jit(solution)/shard_map/ppermute | solution.py:35
  24.8 45.1 %collective-permute-start.9 = (bf16[784,384]{1,0:T(8,128)(2,1)}, bf16[784,384]{1,0:T(8,128)(2,1)S(1)}, u32[]{:S(2)}, u32[]{:S(2)}) collective-permute-start(bf16[784,384]{1,0:T(8,128)(2,1)} %pad_maximum_fusion), channel_id=1, source_target_pairs={{0,6},{1,2},{2,4},{3,0},{4,7},{5,3},{6,5},{7,1},{8,14},{9,10},{10,... | collective-permute-start | bytes 1806344 | tf_op jit(solution)/shard_map/ppermute | solution.py:35
  41.8 28.1 %collective-permute-start.7 = (bf16[784,384]{1,0:T(8,128)(2,1)}, bf16[784,384]{1,0:T(8,128)(2,1)S(1)}, u32[]{:S(2)}, u32[]{:S(2)}) collective-permute-start(bf16[784,384]{1,0:T(8,128)(2,1)} %pad_maximum_fusion), channel_id=1, source_target_pairs={{0,4},{1,0},{2,6},{3,2},{4,5},{5,1},{6,7},{7,3},{8,12},{9,8},{10,1... | collective-permute-start | bytes 1806344 | tf_op jit(solution)/shard_map/ppermute | solution.py:35
  41.8 17.1 %collective-permute-start.3 = (bf16[768,384]{1,0:T(8,128)(2,1)}, bf16[768,384]{1,0:T(8,128)(2,1)S(1)}, u32[]{:S(2)}, u32[]{:S(2)}) collective-permute-start(bf16[768,384]{1,0:T(8,128)(2,1)} %copy-done.4), channel_id=1, source_target_pairs={{0,8},{1,9},{2,10},{3,11},{4,12},{5,13},{6,14},{7,15},{8,16},{9,17... | collective-permute-start | bytes 1769480 | tf_op jit(solution)/shard_map/ppermute | solution.py:35
  41.8 28.1 %collective-permute-start.4 = (bf16[768,384]{1,0:T(8,128)(2,1)}, bf16[768,384]{1,0:T(8,128)(2,1)}, u32[]{:S(2)}, u32[]{:S(2)}) collective-permute-start(bf16[768,384]{1,0:T(8,128)(2,1)} %copy-done.4), channel_id=1, source_target_pairs={{0,24},{1,25},{2,26},{3,27},{4,28},{5,29},{6,30},{7,31},{8,0},{9,1... | collective-permute-start | bytes 1769480 | tf_op jit(solution)/shard_map/ppermute | solution.py:35
  45.1 62.8 %copy-start.5 = (bf16[768,384]{1,0:T(8,128)(2,1)S(1)}, bf16[768,384]{1,0:T(8,128)(2,1)}, u32[]{:S(2)}) copy-start(bf16[768,384]{1,0:T(8,128)(2,1)} %copy-done.4) | copy-start | bytes 1769476
  45.1 62.8 %copy-start.7 = (bf16[768,384]{1,0:T(8,128)(2,1)S(1)}, bf16[768,384]{1,0:T(8,128)(2,1)}, u32[]{:S(2)}) copy-start(bf16[768,384]{1,0:T(8,128)(2,1)} %copy-done.6) | copy-start | bytes 1769476
  70.0 14.2 %collective-permute-start.16 = (bf16[768,384]{1,0:T(8,128)(2,1)S(1)}, bf16[768,384]{1,0:T(8,128)(2,1)S(1)}, u32[]{:S(2)}, u32[]{:S(2)}) collective-permute-start(bf16[768,384]{1,0:T(8,128)(2,1)S(1)} %broadcast_select_fusion), channel_id=1, source_target_pairs={{0,8},{1,9},{2,10},{3,11},{4,12},{5,13},{6,14},{7,15},{8,0},{9,1},... | collective-permute-start | bytes 1769480 | tf_op jit(solution)/shard_map/ppermute | solution.py:35
  71.3 16.1 %collective-permute-start.10 = (bf16[768,384]{1,0:T(8,128)(2,1)S(1)}, bf16[768,384]{1,0:T(8,128)(2,1)S(1)}, u32[]{:S(2)}, u32[]{:S(2)}) collective-permute-start(bf16[768,384]{1,0:T(8,128)(2,1)S(1)} %collective-permute-done.3.refs_9_.refs_6_), channel_id=1, source_target_pairs={{0,1},{1,0},{2,3},{3,2},{4,5},{5,4},{6,7},{7,6},{8,9},{9,8},{10,11... | collective-permute-start | bytes 1769480 | tf_op jit(solution)/shard_map/ppermute | solution.py:35
  72.6 14.9 %collective-permute-start.11 = (bf16[768,384]{1,0:T(8,128)(2,1)}, bf16[768,384]{1,0:T(8,128)(2,1)S(1)}, u32[]{:S(2)}, u32[]{:S(2)}) collective-permute-start(bf16[768,384]{1,0:T(8,128)(2,1)} %collective-permute-done.4.refs_10_.refs_7_), channel_id=1, source_target_pairs={{0,1},{1,0},{2,3},{3,2},{4,5},{5,4},{6,7},{7,6},{8,9},{9,8},{10,11... | collective-permute-start | bytes 1769480 | tf_op jit(solution)/shard_map/ppermute | solution.py:35
  84.3 23.7 %collective-permute-start.17 = (bf16[768,384]{1,0:T(8,128)(2,1)S(1)}, bf16[768,384]{1,0:T(8,128)(2,1)S(1)}, u32[]{:S(2)}, u32[]{:S(2)}) collective-permute-start(bf16[768,384]{1,0:T(8,128)(2,1)S(1)} %collective-permute-done.16.refs_11_.refs_8_), channel_id=1, source_target_pairs={{0,1},{1,0},{2,3},{3,2},{4,5},{5,4},{6,7},{7,6},{8,9},{9,8},{10,11... | collective-permute-start | bytes 1769480 | tf_op jit(solution)/shard_map/ppermute | solution.py:35
  85.8 12.5 %collective-permute-start.14 = (bf16[512,384]{1,0:T(8,128)(2,1)S(1)}, bf16[512,384]{1,0:T(8,128)(2,1)S(1)}, u32[]{:S(2)}, u32[]{:S(2)}) collective-permute-start(bf16[512,384]{1,0:T(8,128)(2,1)S(1)} %pad_maximum_fusion.2), channel_id=1, source_target_pairs={{0,2},{1,6},{2,0},{3,4},{4,3},{5,7},{6,1},{7,5},{8,10},{9,14},{10,... | collective-permute-start | bytes 1179656 | tf_op jit(solution)/shard_map/ppermute | solution.py:35
  87.3 17.2 %collective-permute-start.15 = (bf16[512,384]{1,0:T(8,128)(2,1)S(1)}, bf16[512,384]{1,0:T(8,128)(2,1)S(1)}, u32[]{:S(2)}, u32[]{:S(2)}) collective-permute-start(bf16[512,384]{1,0:T(8,128)(2,1)S(1)} %pad_maximum_fusion.2), channel_id=1, source_target_pairs={{0,6},{1,2},{2,4},{3,0},{4,7},{5,3},{6,5},{7,1},{8,14},{9,10},{10,... | collective-permute-start | bytes 1179656 | tf_op jit(solution)/shard_map/ppermute | solution.py:35
  87.5 20.2 %collective-permute-start.12 = (bf16[512,384]{1,0:T(8,128)(2,1)S(1)}, bf16[512,384]{1,0:T(8,128)(2,1)S(1)}, u32[]{:S(2)}, u32[]{:S(2)}) collective-permute-start(bf16[512,384]{1,0:T(8,128)(2,1)S(1)} %pad_maximum_fusion.2), channel_id=1, source_target_pairs={{0,0},{1,4},{2,2},{3,6},{4,1},{5,5},{6,3},{7,7},{8,8},{9,12},{10,1... | collective-permute-start | bytes 1179656 | tf_op jit(solution)/shard_map/ppermute | solution.py:35
  90.5 17.5 %collective-permute-start.13 = (bf16[512,384]{1,0:T(8,128)(2,1)S(1)}, bf16[512,384]{1,0:T(8,128)(2,1)S(1)}, u32[]{:S(2)}, u32[]{:S(2)}) collective-permute-start(bf16[512,384]{1,0:T(8,128)(2,1)S(1)} %pad_maximum_fusion.2), channel_id=1, source_target_pairs={{0,4},{1,0},{2,6},{3,2},{4,5},{5,1},{6,7},{7,3},{8,12},{9,8},{10,1... | collective-permute-start | bytes 1179656 | tf_op jit(solution)/shard_map/ppermute | solution.py:35
  111.4 1.6 copy-start
  111.4 5.4 %collective-permute-start.18 = (bf16[512,768]{1,0:T(8,128)(2,1)S(1)}, bf16[512,768]{1,0:T(8,128)(2,1)S(1)}, u32[]{:S(2)}, u32[]{:S(2)}) collective-permute-start(bf16[512,768]{1,0:T(8,128)(2,1)S(1)} %get-tuple-element.71), channel_id=1, source_target_pairs={{0,1},{1,0},{2,3},{3,2},{4,5},{5,4},{6,7},{7,6},{8,9},{9,8},{10,11... | collective-permute-start | bytes 2359304 | tf_op jit(solution)/shard_map/ppermute | solution.py:35
  115.3 1.5 copy-start.2
  124.8 0.9 copy-start.8
  125.6 0.9 copy-start.10
  127.9 6.7 %collective-permute-start.19 = (bf16[512,768]{1,0:T(8,128)(2,1)}, bf16[512,768]{1,0:T(8,128)(2,1)S(1)}, u32[]{:S(2)}, u32[]{:S(2)}) collective-permute-start(bf16[512,768]{1,0:T(8,128)(2,1)} %get-tuple-element.76), channel_id=1, source_target_pairs={{0,1},{1,0},{2,3},{3,2},{4,5},{5,4},{6,7},{7,6},{8,9},{9,8},{10,11... | collective-permute-start | bytes 2359304 | tf_op jit(solution)/shard_map/ppermute | solution.py:35
  128.3 1.7 copy-start.3
  130.0 0.9 copy-start.14
  130.9 0.9 copy-start.16
  131.9 2.7 %copy-start.11 = (bf16[512,768]{1,0:T(8,128)(2,1)S(1)}, bf16[512,768]{1,0:T(8,128)(2,1)}, u32[]{:S(2)}) copy-start(bf16[512,768]{1,0:T(8,128)(2,1)} %copy-done.10) | copy-start | bytes 2359300
  131.9 23.2 %copy-start.1 = (bf16[1536,768]{1,0:T(8,128)(2,1)S(1)}, bf16[1536,768]{1,0:T(8,128)(2,1)}, u32[]{:S(2)}) copy-start(bf16[1536,768]{1,0:T(8,128)(2,1)} %copy-done) | copy-start | bytes 7077892
  134.6 20.5 %copy-start.9 = (f32[256,768]{1,0:T(8,128)S(1)}, f32[256,768]{1,0:T(8,128)}, u32[]{:S(2)}) copy-start(f32[256,768]{1,0:T(8,128)} %copy-done.8) | copy-start | bytes 2359300
  134.8 12.6 %collective-permute-start.21 = (bf16[256,768]{1,0:T(8,128)(2,1)S(1)}, bf16[256,768]{1,0:T(8,128)(2,1)S(1)}, u32[]{:S(2)}, u32[]{:S(2)}) collective-permute-start(bf16[256,768]{1,0:T(8,128)(2,1)S(1)} %get-tuple-element.87), channel_id=1, source_target_pairs={{0,8},{1,9},{2,10},{3,11},{4,12},{5,13},{6,14},{7,15},{8,16},{9,17... | collective-permute-start | bytes 1179656 | tf_op jit(solution)/shard_map/ppermute | solution.py:35
  136.1 18.9 %collective-permute-start.25 = (bf16[256,768]{1,0:T(8,128)(2,1)S(1)}, bf16[256,768]{1,0:T(8,128)(2,1)S(1)}, u32[]{:S(2)}, u32[]{:S(2)}) collective-permute-start(bf16[256,768]{1,0:T(8,128)(2,1)S(1)} %get-tuple-element.95), channel_id=1, source_target_pairs={{0,24},{1,25},{2,26},{3,27},{4,28},{5,29},{6,30},{7,31},{8,0},{9,1... | collective-permute-start | bytes 1179656 | tf_op jit(solution)/shard_map/ppermute | solution.py:35
  156.0 9.2 %collective-permute-start.29 = (bf16[256,384]{1,0:T(8,128)(2,1)S(1)}, bf16[256,384]{1,0:T(8,128)(2,1)S(1)}, u32[]{:S(2)}, u32[]{:S(2)}) collective-permute-start(bf16[256,384]{1,0:T(8,128)(2,1)S(1)} %get-tuple-element.100), channel_id=1, source_target_pairs={{0,3},{1,7},{2,1},{3,5},{4,2},{5,6},{6,0},{7,4},{8,11},{9,15},{10,... | collective-permute-start | bytes 589832 | tf_op jit(solution)/shard_map/ppermute | solution.py:35
  157.3 12.1 %collective-permute-start.28 = (bf16[256,384]{1,0:T(8,128)(2,1)S(1)}, bf16[256,384]{1,0:T(8,128)(2,1)S(1)}, u32[]{:S(2)}, u32[]{:S(2)}) collective-permute-start(bf16[256,384]{1,0:T(8,128)(2,1)S(1)} %get-tuple-element.99), channel_id=1, source_target_pairs={{0,2},{1,6},{2,0},{3,4},{4,3},{5,7},{6,1},{7,5},{8,10},{9,14},{10,... | collective-permute-start | bytes 589832 | tf_op jit(solution)/shard_map/ppermute | solution.py:35
  159.7 9.7 %collective-permute-start.27 = (bf16[256,384]{1,0:T(8,128)(2,1)S(1)}, bf16[256,384]{1,0:T(8,128)(2,1)S(1)}, u32[]{:S(2)}, u32[]{:S(2)}) collective-permute-start(bf16[256,384]{1,0:T(8,128)(2,1)S(1)} %get-tuple-element.98), channel_id=1, source_target_pairs={{0,1},{1,5},{2,3},{3,7},{4,0},{5,4},{6,2},{7,6},{8,9},{9,13},{10,1... | collective-permute-start | bytes 589832 | tf_op jit(solution)/shard_map/ppermute | solution.py:35
  159.7 10.6 %collective-permute-start.26 = (bf16[256,384]{1,0:T(8,128)(2,1)S(1)}, bf16[256,384]{1,0:T(8,128)(2,1)S(1)}, u32[]{:S(2)}, u32[]{:S(2)}) collective-permute-start(bf16[256,384]{1,0:T(8,128)(2,1)S(1)} %get-tuple-element.97), channel_id=1, source_target_pairs={{0,0},{1,4},{2,2},{3,6},{4,1},{5,5},{6,3},{7,7},{8,8},{9,12},{10,1... | collective-permute-start | bytes 589832 | tf_op jit(solution)/shard_map/ppermute | solution.py:35
  162.2 16.7 %collective-permute-start.20 = (bf16[528,384]{1,0:T(8,128)(2,1)S(1)}, bf16[528,384]{1,0:T(8,128)(2,1)S(1)}, u32[]{:S(2)}, u32[]{:S(2)}) collective-permute-start(bf16[528,384]{1,0:T(8,128)(2,1)S(1)} %get-tuple-element.85), channel_id=1, source_target_pairs={{0,0},{1,4},{2,2},{3,6},{4,1},{5,5},{6,3},{7,7},{8,8},{9,12},{10,1... | collective-permute-start | bytes 1216520 | tf_op jit(solution)/shard_map/ppermute | solution.py:35
  165.2 13.7 %collective-permute-start.23 = (bf16[528,384]{1,0:T(8,128)(2,1)S(1)}, bf16[528,384]{1,0:T(8,128)(2,1)S(1)}, u32[]{:S(2)}, u32[]{:S(2)}) collective-permute-start(bf16[528,384]{1,0:T(8,128)(2,1)S(1)} %get-tuple-element.89), channel_id=1, source_target_pairs={{0,2},{1,6},{2,0},{3,4},{4,3},{5,7},{6,1},{7,5},{8,10},{9,14},{10,... | collective-permute-start | bytes 1216520 | tf_op jit(solution)/shard_map/ppermute | solution.py:35
  169.4 16.4 %collective-permute-start.24 = (bf16[528,384]{1,0:T(8,128)(2,1)S(1)}, bf16[528,384]{1,0:T(8,128)(2,1)S(1)}, u32[]{:S(2)}, u32[]{:S(2)}) collective-permute-start(bf16[528,384]{1,0:T(8,128)(2,1)S(1)} %get-tuple-element.90), channel_id=1, source_target_pairs={{0,3},{1,7},{2,1},{3,5},{4,2},{5,6},{6,0},{7,4},{8,11},{9,15},{10,... | collective-permute-start | bytes 1216520 | tf_op jit(solution)/shard_map/ppermute | solution.py:35
  169.4 16.4 %collective-permute-start.22 = (bf16[528,384]{1,0:T(8,128)(2,1)S(1)}, bf16[528,384]{1,0:T(8,128)(2,1)S(1)}, u32[]{:S(2)}, u32[]{:S(2)}) collective-permute-start(bf16[528,384]{1,0:T(8,128)(2,1)S(1)} %get-tuple-element.88), channel_id=1, source_target_pairs={{0,1},{1,5},{2,3},{3,7},{4,0},{5,4},{6,2},{7,6},{8,9},{9,13},{10,1... | collective-permute-start | bytes 1216520 | tf_op jit(solution)/shard_map/ppermute | solution.py:35
  (2 other events, 1.4 us)

commit v4 on v2

--- a/solution.py
+++ b/solution.py
@@ -129,7 +129,7 @@
 
 def table_kernel(token_count, *refs):
     token_refs, outer_refs = refs[:4], refs[4:8]
-    pieces, (whole, tables, shared, encs, sems) = refs[8:-5], refs[-5:]
+    pieces, (tables, shared, whole, encs, sems) = refs[8:-5], refs[-5:]
     width = token_refs[0].shape[1]
     pairs = weight_copies(pieces, whole, 0)
     for k in range(4):
@@ -148,7 +148,7 @@
 
 def query_kernel(token_count, *refs):
     normed, token_refs = refs[0], refs[1:5]
-    pieces, (whole, queries, d_attended, rows_in, grads, sems) = refs[5:-6], refs[-6:]
+    pieces, (queries, d_attended, whole, rows_in, grads, sems) = refs[5:-6], refs[-6:]
     width = token_refs[0].shape[1]
     pairs = weight_copies(pieces, whole, 2) + [(normed, rows_in)]
     for k, ref in enumerate(token_refs):
@@ -218,10 +218,10 @@
 
 
 def product_kernel(*refs):
-    attended, d_queries, inv_rms, whole_in = refs[:4]
-    token_refs, outs, (whole, rows_in, sems) = refs[4:8], refs[8:12], refs[12:]
+    attended, d_queries, inv_rms = refs[:3]
+    token_refs, pieces, outs, (whole, rows_in, sems) = refs[3:7], refs[7:-7], refs[-7:-3], refs[-3:]
     token_count, width = attended.shape
-    pairs = [(whole_in, whole)]
+    pairs = weight_copies(pieces, whole, 2)
     for k, ref in enumerate(token_refs):
         pairs.append((ref.at[pl.ds(0, token_count + EXTRA)], rows_in.at[k]))
     run_copies(pairs, sems)
@@ -278,8 +278,10 @@
     ).astype(LOW)
 
 
-def encoding_kernel(own, from_core, up, down, whole, *outs):
+def encoding_kernel(own, from_core, up, down, *refs):
+    pieces, outs, (whole, sems) = refs[:-6], refs[-6:-2], refs[-2:]
     width = whole.shape[1] // 2
+    run_copies(weight_copies(pieces, whole, 0), sems)
     own_low = own[...] + from_core[0:OWN_ROWS, :].astype(F32)
     own_low = (own_low + up[...].astype(F32) + down[...].astype(F32)).astype(LOW)
     for k, out in enumerate(outs):
@@ -298,7 +300,7 @@
         in_specs=specs,
         out_specs=[VMEM] * len(outs),
         scratch_shapes=scratch,
-        compiler_params=pltpu.CompilerParams(vmem_limit_bytes=40 * 1024 * 1024),
+        compiler_params=pltpu.CompilerParams(vmem_limit_bytes=16 * 1024 * 1024),
     )(*operands)
 
 
@@ -323,14 +325,14 @@
     if seq_count == 8:
         below, above = move(weights, ring_up), move(weights, ring_down)
         outer, below, above, *tokens = tie(outer, below, above, *tokens)
-        two_below = move(below, lambda z, y, x, c: (z + 1, y, x, c) if z in (1, 2) else None)
-        two_above = move(above, lambda z, y, x, c: (z - 1, y, x, c) if z in (1, 2) else None)
-        pieces = [weights, below, above, jnp.where(z <= 1, two_above, two_below)]
-        pieces = pieces + [move(piece, flip_core) for piece in pieces]
-        kv_pieces = qo_pieces = pieces
+        two = move(jnp.where(z % 2 == 0, below, above), lambda z, y, x, c: (z ^ 1, y, x, c))
+        outers = [move(outer, spread(k)) for k in range(4)]
+        two, *outers = tie(two, *outers)
+        pieces = [weights, below, above, two]
+        kv_pieces = qo_pieces = pieces + [move(piece, flip_core) for piece in pieces]
     else:
         kv_pieces, qo_pieces = any_weights(weights, c, g)
-    outer = [move(outer, spread(k)) for k in range(4)]
+        outers = [move(outer, spread(k)) for k in range(4)]
     piece_count = len(kv_pieces)
 
     chosen = tokens[0][token_count + 1, :ids].astype(jnp.int32)
@@ -342,21 +344,21 @@
         [pltpu.VMEM((4, token_count + EXTRA, width), LOW)],
         4,
     )
-    whole_kv, tables, shared = call(
+    tables, shared = call(
         lambda *refs: table_kernel(token_count, *refs),
-        tokens + outer + kv_pieces,
+        tokens + outers + kv_pieces,
         [ANY] * (8 + piece_count),
-        [((full_width, wide), LOW), ((3 * OWN_ROWS, wide), LOW), ((2 * OWN_ROWS, wide), LOW)],
-        [pltpu.VMEM((3 * OWN_ROWS, full_width), LOW)],
+        [((3 * OWN_ROWS, wide), LOW), ((2 * OWN_ROWS, wide), LOW)],
+        [pltpu.VMEM((full_width, wide), LOW), pltpu.VMEM((3 * OWN_ROWS, full_width), LOW)],
         12 + 2 * piece_count,
     )
     shared = move(shared, flip_core)
-    whole_qo, queries, d_attended = call(
+    queries, d_attended = call(
         lambda *refs: query_kernel(token_count, *refs),
         [normed] + tokens + qo_pieces,
         [ANY] * (5 + piece_count),
-        [((full_width, wide), LOW), ((token_count, width), LOW), ((token_count, width), LOW)],
-        [pltpu.VMEM((token_count, full_width), LOW), pltpu.VMEM((token_count, full_width), LOW)],
+        [((token_count, width), LOW), ((token_count, width), LOW)],
+        [pltpu.VMEM((full_width, wide), LOW)] + [pltpu.VMEM((token_count, full_width), LOW)] * 2,
         5 + 2 * piece_count,
     )
     attended, d_queries, d_own, d_outer, d_shared = call(
@@ -379,14 +381,14 @@
     to_above = (d_outer[OWN_ROWS:] + jnp.where(c == 0, shared_grad, 0.0)).astype(LOW)
     terms = call(
         product_kernel,
-        [attended, d_queries, inv_rms, whole_qo] + tokens,
-        [VMEM, VMEM, VMEM] + [ANY] * 5,
+        [attended, d_queries, inv_rms] + tokens + qo_pieces,
+        [VMEM, VMEM, VMEM] + [ANY] * (4 + piece_count),
         [((2 * token_count + EXTRA, width), LOW)] * 4,
         [
             pltpu.VMEM((full_width, wide), LOW),
             pltpu.VMEM((4, token_count + EXTRA, width), LOW),
         ],
-        5,
+        4 + 2 * piece_count,
     )
     to_below, to_above, *terms = tie(to_below, to_above, *terms)
     up, down = move(to_above, ring_up), move(to_below, ring_down)
@@ -399,9 +401,11 @@
     )
     enc_terms = call(
         encoding_kernel,
-        [d_own, from_core, up, down, whole_kv],
-        [VMEM] * 5,
+        [d_own, from_core, up, down] + kv_pieces,
+        [VMEM] * 4 + [ANY] * piece_count,
         [((OWN_ROWS, width), LOW)] * 4,
+        [pltpu.VMEM((full_width, wide), LOW)],
+        2 * piece_count,
     )
     enc_terms = [move(term, gather_back(k)).astype(F32) for k, term in enumerate(enc_terms)]
     grad_encodings = (enc_terms[0] + enc_terms[1] + enc_terms[2] + enc_terms[3]).astype(LOW)

time: 160 us -> 150 us (0.938)
  the two profiles are of different devices: /device:TPU:19 before, /device:TPU:1 now
where the time goes in v4:
time: 150 us; the launch traced here: 149 us
  waiting for transfers between devices  72 us (48%)
  starting transfers between devices  35.5 us (24%)
  Pallas kernels  24 us (16%)
  local copies, waits for them, and re-layouts  10.7 us (7%)
  other arithmetic  5.44 us (4%)
    ppermute x30, waiting for transfers between devices, move(): return lax.ppermute(value, ('seq', 'mp'), pairs)  72 us
    ppermute x30, starting transfers between devices, move(): return lax.ppermute(value, ('seq', 'mp'), pairs)  35.5 us
    pallas_call x7, Pallas kernels, call(): pl.pallas_call(kernel, out_shape=[jax.ShapeDtypeStruct(shape, dtype) for...  24 us
    unnamed x62, local copies, waits for them, and re-layouts  10.5 us
  transfers between devices with their start and end apart: 30, of which 15 were waited for; matrix products, arithmetic and copies ran while one was open for 1% of the time, Pallas kernels for 8%

profile of v4, /device:TPU:1, one launch (start us, length us, event | category | flops | bytes accessed | tf_op | source)
XLA Modules:
  0.0 148.7 jit_solution(5505998891579251309)
XLA Ops:
  0.7 1.3 pad_maximum_fusion.1
  2.0 4.5 %collective-permute-start = (bf16[768,384]{1,0:T(8,128)(2,1)S(1)}, bf16[768,384]{1,0:T(8,128)(2,1)S(1)}, u32[]{:S(2)}, u32[]{:S(2)}) collective-permute-start(bf16[768,384]{1,0:T(8,128)(2,1)S(1)} %pad_maximum_fusion.1), channel_id=1, source_target_pairs={{0,0},{1,4},{2,2},{3,6},{4,1},{5,5},{6,3},{7,7},{8,8},{9,12},{10,1... | collective-permute-start | bytes 1769480 | tf_op jit(solution)/shard_map/ppermute | solution.py:35
  6.5 1.3 collective-permute-start.1
  7.9 2.1 %collective-permute-start.2 = (bf16[256,384]{1,0:T(8,128)(2,1)S(1)}, bf16[256,384]{1,0:T(8,128)(2,1)S(1)}, u32[]{:S(2)}, u32[]{:S(2)}) collective-permute-start(bf16[256,384]{1,0:T(8,128)(2,1)S(1)} %bitcast.7), channel_id=1, source_target_pairs={{0,24},{1,25},{2,26},{3,27},{4,28},{5,29},{6,30},{7,31},{8,0},{9,1... | collective-permute-start | bytes 589832 | tf_op jit(solution)/shard_map/ppermute | solution.py:35
  11.1 4.0 %collective-permute-done.1 = bf16[256,384]{1,0:T(8,128)(2,1)S(1)} collective-permute-done((bf16[256,384]{1,0:T(8,128)(2,1)S(1)}, bf16[256,384]{1,0:T(8,128)(2,1)S(1)}, u32[]{:S(2)}, u32[]{:S(2)}) %collective-permute-start.1) | collective-permute-done | bytes 196640 | tf_op jit(solution)/shard_map/ppermute | solution.py:35
  15.1 2.1 %collective-permute-done.2 = bf16[256,384]{1,0:T(8,128)(2,1)S(1)} collective-permute-done((bf16[256,384]{1,0:T(8,128)(2,1)S(1)}, bf16[256,384]{1,0:T(8,128)(2,1)S(1)}, u32[]{:S(2)}, u32[]{:S(2)}) %collective-permute-start.2) | collective-permute-done | bytes 196640 | tf_op jit(solution)/shard_map/ppermute | solution.py:35
  18.2 3.1 %collective-permute-start.5 = (bf16[784,384]{1,0:T(8,128)(2,1)}, bf16[784,384]{1,0:T(8,128)(2,1)S(1)}, u32[]{:S(2)}, u32[]{:S(2)}) collective-permute-start(bf16[784,384]{1,0:T(8,128)(2,1)} %pad_maximum_fusion), channel_id=1, source_target_pairs={{0,0},{1,4},{2,2},{3,6},{4,1},{5,5},{6,3},{7,7},{8,8},{9,12},{10,1... | collective-permute-start | bytes 1806344 | tf_op jit(solution)/shard_map/ppermute | solution.py:35
  21.3 1.9 %collective-permute-start.7 = (bf16[784,384]{1,0:T(8,128)(2,1)}, bf16[784,384]{1,0:T(8,128)(2,1)S(1)}, u32[]{:S(2)}, u32[]{:S(2)}) collective-permute-start(bf16[784,384]{1,0:T(8,128)(2,1)} %pad_maximum_fusion), channel_id=1, source_target_pairs={{0,2},{1,6},{2,0},{3,4},{4,3},{5,7},{6,1},{7,5},{8,10},{9,14},{10,... | collective-permute-start | bytes 1806344 | tf_op jit(solution)/shard_map/ppermute | solution.py:35
  23.9 10.4 %collective-permute-done.3.refs_9_.refs_6_.refs_8_.refs_1_ = bf16[768,384]{1,0:T(8,128)(2,1)S(1)} collective-permute-done((bf16[768,384]{1,0:T(8,128)(2,1)S(1)}, bf16[768,384]{1,0:T(8,128)(2,1)S(1)}, u32[]{:S(2)}, u32[]{:S(2)}) %collective-permute-start.3) | collective-permute-done | bytes 589856 | tf_op jit(solution)/shard_map/ppermute | solution.py:35
  34.2 1.0 pad_maximum_fusion.2
  35.3 12.9 %collective-permute-done.4.refs_10_.refs_7_.refs_9_.refs_2_ = bf16[768,384]{1,0:T(8,128)(2,1)S(1)} collective-permute-done((bf16[768,384]{1,0:T(8,128)(2,1)}, bf16[768,384]{1,0:T(8,128)(2,1)S(1)}, u32[]{:S(2)}, u32[]{:S(2)}) %collective-permute-start.4) | collective-permute-done | bytes 589856 | tf_op jit(solution)/shard_map/ppermute | solution.py:35
  48.1 2.6 %collective-permute-done.8.refs_3_.refs_4_.refs_6_ = bf16[784,384]{1,0:T(8,128)(2,1)} collective-permute-done((bf16[784,384]{1,0:T(8,128)(2,1)}, bf16[784,384]{1,0:T(8,128)(2,1)}, u32[]{:S(2)}, u32[]{:S(2)}) %collective-permute-start.8) | collective-permute-done | bytes 602144 | tf_op jit(solution)/shard_map/ppermute | solution.py:35
  51.3 3.7 %collective-permute-start.10 = (bf16[512,384]{1,0:T(8,128)(2,1)S(1)}, bf16[512,384]{1,0:T(8,128)(2,1)S(1)}, u32[]{:S(2)}, u32[]{:S(2)}) collective-permute-start(bf16[512,384]{1,0:T(8,128)(2,1)S(1)} %pad_maximum_fusion.2), channel_id=1, source_target_pairs={{0,0},{1,4},{2,2},{3,6},{4,1},{5,5},{6,3},{7,7},{8,8},{9,12},{10,1... | collective-permute-start | bytes 1179656 | tf_op jit(solution)/shard_map/ppermute | solution.py:35
  55.0 1.0 collective-permute-start.12
  56.0 1.0 collective-permute-start.13
  57.0 11.8 %collective-permute-done.10.refs_4_ = bf16[512,384]{1,0:T(8,128)(2,1)S(1)} collective-permute-done((bf16[512,384]{1,0:T(8,128)(2,1)S(1)}, bf16[512,384]{1,0:T(8,128)(2,1)S(1)}, u32[]{:S(2)}, u32[]{:S(2)}) %collective-permute-start.10) | collective-permute-done | bytes 393248 | tf_op jit(solution)/shard_map/ppermute | solution.py:35
  68.8 2.5 %collective-permute-done.11.refs_5_ = bf16[512,384]{1,0:T(8,128)(2,1)S(1)} collective-permute-done((bf16[512,384]{1,0:T(8,128)(2,1)S(1)}, bf16[512,384]{1,0:T(8,128)(2,1)S(1)}, u32[]{:S(2)}, u32[]{:S(2)}) %collective-permute-start.11) | collective-permute-done | bytes 393248 | tf_op jit(solution)/shard_map/ppermute | solution.py:35
  71.7 3.4 %collective-permute-done.13.refs_7_ = bf16[512,384]{1,0:T(8,128)(2,1)S(1)} collective-permute-done((bf16[512,384]{1,0:T(8,128)(2,1)S(1)}, bf16[512,384]{1,0:T(8,128)(2,1)S(1)}, u32[]{:S(2)}, u32[]{:S(2)}) %collective-permute-start.13) | collective-permute-done | bytes 393248 | tf_op jit(solution)/shard_map/ppermute | solution.py:35
  75.2 1.9 %collective-permute-done.17.refs_15_.refs_12_.refs_14_.refs_7_ = bf16[768,384]{1,0:T(8,128)(2,1)S(1)} collective-permute-done((bf16[768,384]{1,0:T(8,128)(2,1)S(1)}, bf16[768,384]{1,0:T(8,128)(2,1)S(1)}, u32[]{:S(2)}, u32[]{:S(2)}) %collective-permute-start.17) | collective-permute-done | bytes 589856 | tf_op jit(solution)/shard_map/ppermute | solution.py:35
  77.2 3.7 %shard_map.112 = (bf16[768,768]{1,0:T(8,128)(2,1)S(1)}, bf16[512,768]{1,0:T(8,128)(2,1)S(1)}) custom-call(bf16[784,384]{1,0:T(8,128)(2,1)S(1)} %collective-permute-done.5.refs_0_.refs_1_.refs_3_, bf16[784,384]{1,0:T(8,128)(2,1)S(1)} %collective-permute-done.6.refs_1_.refs_2_.refs_4_, bf16[784,384]{1,0:T(8,128)(2,1)S(1)} %collective-permute-done.7.refs_2_.refs_3_.refs_5_, ...), custom_call_target="tpu_custom_call" | custom-call | tf_op jit(solution)/shard_map/pallas_call | solution.py:297
  81.1 2.1 %shard_map.113 = (bf16[256,1536]{1,0:T(8,128)(2,1)S(1)}, f32[256,1]{1,0:T(8,128)S(1)}) custom-call(bf16[784,384]{1,0:T(8,128)(2,1)S(1)} %collective-permute-done.5.refs_0_.refs_1_.refs_3_, bf16[784,384]{1,0:T(8,128)(2,1)S(1)} %collective-permute-done.6.refs_1_.refs_2_.refs_4_, bf16[784,384]{1,0:T(8,128)(2,1)S(1)} %collective-permute-done.7.refs_2_.refs_3_.refs_5_, ...), custom_call_target="tpu_custom_call" | custom-call | tf_op jit(solution)/shard_map/pallas_call | solution.py:297
  83.3 2.5 %shard_map.114 = (bf16[256,384]{1,0:T(8,128)(2,1)S(1)}, bf16[256,384]{1,0:T(8,128)(2,1)S(1)}) custom-call(bf16[256,1536]{1,0:T(8,128)(2,1)S(1)} %get-tuple-element.64.refs_0_, bf16[784,384]{1,0:T(8,128)(2,1)S(1)} %collective-permute-done.5.refs_0_.refs_1_.refs_3_, bf16[784,384]{1,0:T(8,128)(2,1)S(1)} %collective-permute-done.6.refs_1_.refs_2_.refs_4_, ...), custom_call_target="tpu_custom_call" | custom-call | tf_op jit(solution)/shard_map/pallas_call | solution.py:297
  85.9 8.0 %shard_map.115 = (bf16[256,384]{1,0:T(8,128)(2,1)S(1)}, bf16[256,384]{1,0:T(8,128)(2,1)S(1)}, f32[256,768]{1,0:T(8,128)S(1)}, bf16[512,768]{1,0:T(8,128)(2,1)S(1)}, bf16[512,768]{1,0:T(8,128)(2,1)}) custom-call(s32[8]{0:T(128)S(1)} %bitcast_convert_fusion.refs_0_, bf16[768,768]{1,0:T(8,128)(2,1)S(1)} %get-tuple-element.62.refs_1_, ...), custom_call_target="tpu_custom_call" | custom-call | tf_op jit(solution)/shard_map/pallas_call | solution.py:297
  94.7 0.9 copy-done.21
  96.7 1.1 copy-done.2
  97.7 1.1 copy-done.5
  98.8 1.1 copy-done.8
  99.9 1.1 copy-done.11
  100.9 1.1 copy-done.14
  102.0 1.1 copy-done.17
  103.1 0.9 copy-done.25
  104.0 3.8 %shard_map.116 = (bf16[528,384]{1,0:T(8,128)(2,1)S(1)}, bf16[528,384]{1,0:T(8,128)(2,1)S(1)}, bf16[528,384]{1,0:T(8,128)(2,1)S(1)}, bf16[528,384]{1,0:T(8,128)(2,1)S(1)}) custom-call(bf16[256,384]{1,0:T(8,128)(2,1)S(1)} %get-tuple-element.69.refs_0_, bf16[256,384]{1,0:T(8,128)(2,1)S(1)} %copy-done.25, f32[256,1]{1,0:T(8,128)S(1)} %get-tuple-element.71.refs_2_, ...), custom_call_target="tpu_custom_call" | custom-call | tf_op jit(solution)/shard_map/pallas_call | solution.py:297
  107.9 1.3 fusion.3
  109.2 0.9 collective-permute-start.24
  110.2 3.2 %collective-permute-start.20 = (bf16[528,384]{1,0:T(8,128)(2,1)S(1)}, bf16[528,384]{1,0:T(8,128)(2,1)S(1)}, u32[]{:S(2)}, u32[]{:S(2)}) collective-permute-start(bf16[528,384]{1,0:T(8,128)(2,1)S(1)} %get-tuple-element.76), channel_id=1, source_target_pairs={{0,0},{1,4},{2,2},{3,6},{4,1},{5,5},{6,3},{7,7},{8,8},{9,12},{10,1... | collective-permute-start | bytes 1216520 | tf_op jit(solution)/shard_map/ppermute | solution.py:35
  113.3 1.7 %collective-permute-start.22 = (bf16[528,384]{1,0:T(8,128)(2,1)S(1)}, bf16[528,384]{1,0:T(8,128)(2,1)S(1)}, u32[]{:S(2)}, u32[]{:S(2)}) collective-permute-start(bf16[528,384]{1,0:T(8,128)(2,1)S(1)} %get-tuple-element.78), channel_id=1, source_target_pairs={{0,2},{1,6},{2,0},{3,4},{4,3},{5,7},{6,1},{7,5},{8,10},{9,14},{10,... | collective-permute-start | bytes 1216520 | tf_op jit(solution)/shard_map/ppermute | solution.py:35
  115.1 2.1 %collective-permute-start.25 = (bf16[256,768]{1,0:T(8,128)(2,1)S(1)}, bf16[256,768]{1,0:T(8,128)(2,1)S(1)}, u32[]{:S(2)}, u32[]{:S(2)}) collective-permute-start(bf16[256,768]{1,0:T(8,128)(2,1)S(1)} %get-tuple-element.84), channel_id=1, source_target_pairs={{0,24},{1,25},{2,26},{3,27},{4,28},{5,29},{6,30},{7,31},{8,0},{9,1... | collective-permute-start | bytes 1179656 | tf_op jit(solution)/shard_map/ppermute | solution.py:35
  117.2 4.5 %collective-permute-done.24.up = bf16[256,768]{1,0:T(8,128)(2,1)S(1)} collective-permute-done((bf16[256,768]{1,0:T(8,128)(2,1)S(1)}, bf16[256,768]{1,0:T(8,128)(2,1)S(1)}, u32[]{:S(2)}, u32[]{:S(2)}) %collective-permute-start.24) | collective-permute-done | bytes 393248 | tf_op jit(solution)/shard_map/ppermute | solution.py:35
  121.7 1.3 collective-permute-start.23
  123.0 7.6 %collective-permute-done.25.down = bf16[256,768]{1,0:T(8,128)(2,1)S(1)} collective-permute-done((bf16[256,768]{1,0:T(8,128)(2,1)S(1)}, bf16[256,768]{1,0:T(8,128)(2,1)S(1)}, u32[]{:S(2)}, u32[]{:S(2)}) %collective-permute-start.25) | collective-permute-done | bytes 393248 | tf_op jit(solution)/shard_map/ppermute | solution.py:35
  130.6 2.6 %shard_map.118 = (bf16[256,384]{1,0:T(8,128)(2,1)S(1)}, bf16[256,384]{1,0:T(8,128)(2,1)S(1)}, bf16[256,384]{1,0:T(8,128)(2,1)S(1)}, bf16[256,384]{1,0:T(8,128)(2,1)S(1)}) custom-call(f32[256,768]{1,0:T(8,128)S(1)} %copy-done.20, bf16[512,768]{1,0:T(8,128)(2,1)} %collective-permute-done.19.from_core, bf16[256,768]{1,0:T(8,128)(2,1)S(1)} %collective-permute-done.24.up, ...), custom_call_target="tpu_custom_call" | custom-call | tf_op jit(solution)/shard_map/pallas_call | solution.py:297
  133.3 2.8 %collective-permute-start.26 = (bf16[256,384]{1,0:T(8,128)(2,1)S(1)}, bf16[256,384]{1,0:T(8,128)(2,1)S(1)}, u32[]{:S(2)}, u32[]{:S(2)}) collective-permute-start(bf16[256,384]{1,0:T(8,128)(2,1)S(1)} %get-tuple-element.85), channel_id=1, source_target_pairs={{0,0},{1,4},{2,2},{3,6},{4,1},{5,5},{6,3},{7,7},{8,8},{9,12},{10,1... | collective-permute-start | bytes 589832 | tf_op jit(solution)/shard_map/ppermute | solution.py:35
  136.1 1.8 %collective-permute-start.28 = (bf16[256,384]{1,0:T(8,128)(2,1)S(1)}, bf16[256,384]{1,0:T(8,128)(2,1)S(1)}, u32[]{:S(2)}, u32[]{:S(2)}) collective-permute-start(bf16[256,384]{1,0:T(8,128)(2,1)S(1)} %get-tuple-element.87), channel_id=1, source_target_pairs={{0,2},{1,6},{2,0},{3,4},{4,3},{5,7},{6,1},{7,5},{8,10},{9,14},{10,... | collective-permute-start | bytes 589832 | tf_op jit(solution)/shard_map/ppermute | solution.py:35
  138.3 1.2 shard_map.117
  139.4 1.3 collective-permute-done.26
  140.7 2.5 %collective-permute-done.27 = bf16[256,384]{1,0:T(8,128)(2,1)S(1)} collective-permute-done((bf16[256,384]{1,0:T(8,128)(2,1)S(1)}, bf16[256,384]{1,0:T(8,128)(2,1)S(1)}, u32[]{:S(2)}, u32[]{:S(2)}) %collective-permute-start.27) | collective-permute-done | bytes 196640 | tf_op jit(solution)/shard_map/ppermute | solution.py:35
  143.3 1.0 collective-permute-done.28
  144.3 3.6 %collective-permute-done.29 = bf16[256,384]{1,0:T(8,128)(2,1)S(1)} collective-permute-done((bf16[256,384]{1,0:T(8,128)(2,1)S(1)}, bf16[256,384]{1,0:T(8,128)(2,1)S(1)}, u32[]{:S(2)}, u32[]{:S(2)}) %collective-permute-start.29) | collective-permute-done | bytes 196640 | tf_op jit(solution)/shard_map/ppermute | solution.py:35
  (93 shorter events, 7.3 us)
Async XLA Ops:
  0.6 9.3 %copy-start.29 = (bf16[384]{0:T(512)(128)(2,1)S(1)}, bf16[384]{0:T(512)(128)(2,1)}, u32[]{:S(2)}) copy-start(bf16[384]{0:T(512)(128)(2,1)} %param.10) | copy-start | bytes 2308
  0.7 9.3 %copy-start.30 = (s32[4,2]{0,1:T(2,128)S(1)}, s32[4,2]{0,1:T(2,128)}, u32[]{:S(2)}) copy-start(s32[4,2]{0,1:T(2,128)} %param.16) | copy-start | bytes 100
  0.7 9.5 %copy-start.26 = (bf16[256,384]{1,0:T(8,128)(2,1)S(1)}, bf16[256,384]{1,0:T(8,128)(2,1)}, u32[]{:S(2)}) copy-start(bf16[256,384]{1,0:T(8,128)(2,1)} %param.17) | copy-start | bytes 589828
  0.7 9.5 %copy-start.23 = (bf16[256,384]{1,0:T(8,128)(2,1)S(1)}, bf16[256,384]{1,0:T(8,128)(2,1)}, u32[]{:S(2)}) copy-start(bf16[256,384]{1,0:T(8,128)(2,1)} %hidden.1) | copy-start | bytes 589828
  2.0 15.9 %collective-permute-start = (bf16[768,384]{1,0:T(8,128)(2,1)S(1)}, bf16[768,384]{1,0:T(8,128)(2,1)S(1)}, u32[]{:S(2)}, u32[]{:S(2)}) collective-permute-start(bf16[768,384]{1,0:T(8,128)(2,1)S(1)} %pad_maximum_fusion.1), channel_id=1, source_target_pairs={{0,0},{1,4},{2,2},{3,6},{4,1},{5,5},{6,3},{7,7},{8,8},{9,12},{10,1... | collective-permute-start | bytes 1769480 | tf_op jit(solution)/shard_map/ppermute | solution.py:35
  6.5 8.6 %collective-permute-start.1 = (bf16[256,384]{1,0:T(8,128)(2,1)S(1)}, bf16[256,384]{1,0:T(8,128)(2,1)S(1)}, u32[]{:S(2)}, u32[]{:S(2)}) collective-permute-start(bf16[256,384]{1,0:T(8,128)(2,1)S(1)} %bitcast.6), channel_id=1, source_target_pairs={{0,8},{1,9},{2,10},{3,11},{4,12},{5,13},{6,14},{7,15},{8,16},{9,17... | collective-permute-start | bytes 589832 | tf_op jit(solution)/shard_map/ppermute | solution.py:35
  7.9 9.3 %collective-permute-start.2 = (bf16[256,384]{1,0:T(8,128)(2,1)S(1)}, bf16[256,384]{1,0:T(8,128)(2,1)S(1)}, u32[]{:S(2)}, u32[]{:S(2)}) collective-permute-start(bf16[256,384]{1,0:T(8,128)(2,1)S(1)} %bitcast.7), channel_id=1, source_target_pairs={{0,24},{1,25},{2,26},{3,27},{4,28},{5,29},{6,30},{7,31},{8,0},{9,1... | collective-permute-start | bytes 589832 | tf_op jit(solution)/shard_map/ppermute | solution.py:35
  17.9 6.0 %copy-start = (bf16[768,384]{1,0:T(8,128)(2,1)}, bf16[768,384]{1,0:T(8,128)(2,1)S(1)}, u32[]{:S(2)}) copy-start(bf16[768,384]{1,0:T(8,128)(2,1)S(1)} %collective-permute-done.refs_8_.refs_5_.refs_7_.refs_0_) | copy-start | bytes 1769476
  17.9 16.3 %collective-permute-start.3 = (bf16[768,384]{1,0:T(8,128)(2,1)S(1)}, bf16[768,384]{1,0:T(8,128)(2,1)S(1)}, u32[]{:S(2)}, u32[]{:S(2)}) collective-permute-start(bf16[768,384]{1,0:T(8,128)(2,1)S(1)} %collective-permute-done.refs_8_.refs_5_.refs_7_.refs_0_), channel_id=1, source_target_pairs={{0,8},{1,9},{2,10},{3,11},{4,12},{5,13},{6,14},{7,15},{8,16},{9,17... | collective-permute-start | bytes 1769480 | tf_op jit(solution)/shard_map/ppermute | solution.py:35
  18.2 30.0 %collective-permute-start.5 = (bf16[784,384]{1,0:T(8,128)(2,1)}, bf16[784,384]{1,0:T(8,128)(2,1)S(1)}, u32[]{:S(2)}, u32[]{:S(2)}) collective-permute-start(bf16[784,384]{1,0:T(8,128)(2,1)} %pad_maximum_fusion), channel_id=1, source_target_pairs={{0,0},{1,4},{2,2},{3,6},{4,1},{5,5},{6,3},{7,7},{8,8},{9,12},{10,1... | collective-permute-start | bytes 1806344 | tf_op jit(solution)/shard_map/ppermute | solution.py:35
  21.2 26.9 %collective-permute-start.6 = (bf16[784,384]{1,0:T(8,128)(2,1)}, bf16[784,384]{1,0:T(8,128)(2,1)S(1)}, u32[]{:S(2)}, u32[]{:S(2)}) collective-permute-start(bf16[784,384]{1,0:T(8,128)(2,1)} %pad_maximum_fusion), channel_id=1, source_target_pairs={{0,4},{1,0},{2,6},{3,2},{4,5},{5,1},{6,7},{7,3},{8,12},{9,8},{10,1... | collective-permute-start | bytes 1806344 | tf_op jit(solution)/shard_map/ppermute | solution.py:35
  21.3 26.9 %collective-permute-start.7 = (bf16[784,384]{1,0:T(8,128)(2,1)}, bf16[784,384]{1,0:T(8,128)(2,1)S(1)}, u32[]{:S(2)}, u32[]{:S(2)}) collective-permute-start(bf16[784,384]{1,0:T(8,128)(2,1)} %pad_maximum_fusion), channel_id=1, source_target_pairs={{0,2},{1,6},{2,0},{3,4},{4,3},{5,7},{6,1},{7,5},{8,10},{9,14},{10,... | collective-permute-start | bytes 1806344 | tf_op jit(solution)/shard_map/ppermute | solution.py:35
  23.2 27.5 %collective-permute-start.8 = (bf16[784,384]{1,0:T(8,128)(2,1)}, bf16[784,384]{1,0:T(8,128)(2,1)}, u32[]{:S(2)}, u32[]{:S(2)}) collective-permute-start(bf16[784,384]{1,0:T(8,128)(2,1)} %pad_maximum_fusion), channel_id=1, source_target_pairs={{0,6},{1,2},{2,4},{3,0},{4,7},{5,3},{6,5},{7,1},{8,14},{9,10},{10,... | collective-permute-start | bytes 1806344 | tf_op jit(solution)/shard_map/ppermute | solution.py:35
  34.2 13.9 %collective-permute-start.4 = (bf16[768,384]{1,0:T(8,128)(2,1)}, bf16[768,384]{1,0:T(8,128)(2,1)S(1)}, u32[]{:S(2)}, u32[]{:S(2)}) collective-permute-start(bf16[768,384]{1,0:T(8,128)(2,1)} %copy-done), channel_id=1, source_target_pairs={{0,24},{1,25},{2,26},{3,27},{4,28},{5,29},{6,30},{7,31},{8,0},{9,1... | collective-permute-start | bytes 1769480 | tf_op jit(solution)/shard_map/ppermute | solution.py:35
  34.2 34.5 %copy-start.1 = (bf16[768,384]{1,0:T(8,128)(2,1)S(1)}, bf16[768,384]{1,0:T(8,128)(2,1)}, u32[]{:S(2)}) copy-start(bf16[768,384]{1,0:T(8,128)(2,1)} %copy-done) | copy-start | bytes 1769476
  50.8 24.4 %collective-permute-start.9 = (bf16[768,384]{1,0:T(8,128)(2,1)S(1)}, bf16[768,384]{1,0:T(8,128)(2,1)S(1)}, u32[]{:S(2)}, u32[]{:S(2)}) collective-permute-start(bf16[768,384]{1,0:T(8,128)(2,1)S(1)} %broadcast_select_fusion), channel_id=1, source_target_pairs={{0,8},{1,9},{2,10},{3,11},{4,12},{5,13},{6,14},{7,15},{8,0},{9,1},... | collective-permute-start | bytes 1769480 | tf_op jit(solution)/shard_map/ppermute | solution.py:35
  51.3 17.5 %collective-permute-start.10 = (bf16[512,384]{1,0:T(8,128)(2,1)S(1)}, bf16[512,384]{1,0:T(8,128)(2,1)S(1)}, u32[]{:S(2)}, u32[]{:S(2)}) collective-permute-start(bf16[512,384]{1,0:T(8,128)(2,1)S(1)} %pad_maximum_fusion.2), channel_id=1, source_target_pairs={{0,0},{1,4},{2,2},{3,6},{4,1},{5,5},{6,3},{7,7},{8,8},{9,12},{10,1... | collective-permute-start | bytes 1179656 | tf_op jit(solution)/shard_map/ppermute | solution.py:35
  55.0 16.3 %collective-permute-start.11 = (bf16[512,384]{1,0:T(8,128)(2,1)S(1)}, bf16[512,384]{1,0:T(8,128)(2,1)S(1)}, u32[]{:S(2)}, u32[]{:S(2)}) collective-permute-start(bf16[512,384]{1,0:T(8,128)(2,1)S(1)} %pad_maximum_fusion.2), channel_id=1, source_target_pairs={{0,4},{1,0},{2,6},{3,2},{4,5},{5,1},{6,7},{7,3},{8,12},{9,8},{10,1... | collective-permute-start | bytes 1179656 | tf_op jit(solution)/shard_map/ppermute | solution.py:35
  55.0 16.3 %collective-permute-start.12 = (bf16[512,384]{1,0:T(8,128)(2,1)S(1)}, bf16[512,384]{1,0:T(8,128)(2,1)S(1)}, u32[]{:S(2)}, u32[]{:S(2)}) collective-permute-start(bf16[512,384]{1,0:T(8,128)(2,1)S(1)} %pad_maximum_fusion.2), channel_id=1, source_target_pairs={{0,2},{1,6},{2,0},{3,4},{4,3},{5,7},{6,1},{7,5},{8,10},{9,14},{10,... | collective-permute-start | bytes 1179656 | tf_op jit(solution)/shard_map/ppermute | solution.py:35
  56.0 19.2 %collective-permute-start.13 = (bf16[512,384]{1,0:T(8,128)(2,1)S(1)}, bf16[512,384]{1,0:T(8,128)(2,1)S(1)}, u32[]{:S(2)}, u32[]{:S(2)}) collective-permute-start(bf16[512,384]{1,0:T(8,128)(2,1)S(1)} %pad_maximum_fusion.2), channel_id=1, source_target_pairs={{0,6},{1,2},{2,4},{3,0},{4,7},{5,3},{6,5},{7,1},{8,14},{9,10},{10,... | collective-permute-start | bytes 1179656 | tf_op jit(solution)/shard_map/ppermute | solution.py:35
  68.8 6.4 %collective-permute-start.14 = (bf16[768,384]{1,0:T(8,128)(2,1)S(1)}, bf16[768,384]{1,0:T(8,128)(2,1)S(1)}, u32[]{:S(2)}, u32[]{:S(2)}) collective-permute-start(bf16[768,384]{1,0:T(8,128)(2,1)S(1)} %copy-done.1), channel_id=1, source_target_pairs={{0,1},{1,0},{2,3},{3,2},{4,5},{5,4},{6,7},{7,6},{8,9},{9,8},{10,11... | collective-permute-start | bytes 1769480 | tf_op jit(solution)/shard_map/ppermute | solution.py:35
  71.2 3.9 %collective-permute-start.15 = (bf16[768,384]{1,0:T(8,128)(2,1)S(1)}, bf16[768,384]{1,0:T(8,128)(2,1)S(1)}, u32[]{:S(2)}, u32[]{:S(2)}) collective-permute-start(bf16[768,384]{1,0:T(8,128)(2,1)S(1)} %collective-permute-done.3.refs_9_.refs_6_.refs_8_.refs_1_), channel_id=1, source_target_pairs={{0,1},{1,0},{2,3},{3,2},{4,5},{5,4},{6,7},{7,6},{8,9},{9,8},{10,11... | collective-permute-start | bytes 1769480 | tf_op jit(solution)/shard_map/ppermute | solution.py:35
  71.2 4.0 %collective-permute-start.16 = (bf16[768,384]{1,0:T(8,128)(2,1)S(1)}, bf16[768,384]{1,0:T(8,128)(2,1)S(1)}, u32[]{:S(2)}, u32[]{:S(2)}) collective-permute-start(bf16[768,384]{1,0:T(8,128)(2,1)S(1)} %collective-permute-done.4.refs_10_.refs_7_.refs_9_.refs_2_), channel_id=1, source_target_pairs={{0,1},{1,0},{2,3},{3,2},{4,5},{5,4},{6,7},{7,6},{8,9},{9,8},{10,11... | collective-permute-start | bytes 1769480 | tf_op jit(solution)/shard_map/ppermute | solution.py:35
  75.1 8.1 %copy-start.4 = (bf16[768,384]{1,0:T(8,128)(2,1)}, bf16[768,384]{1,0:T(8,128)(2,1)S(1)}, u32[]{:S(2)}) copy-start(bf16[768,384]{1,0:T(8,128)(2,1)S(1)} %collective-permute-done.9.refs_11_.refs_8_.refs_10_.refs_3_) | copy-start | bytes 1769476
  75.1 2.0 %collective-permute-start.17 = (bf16[768,384]{1,0:T(8,128)(2,1)S(1)}, bf16[768,384]{1,0:T(8,128)(2,1)S(1)}, u32[]{:S(2)}, u32[]{:S(2)}) collective-permute-start(bf16[768,384]{1,0:T(8,128)(2,1)S(1)} %collective-permute-done.9.refs_11_.refs_8_.refs_10_.refs_3_), channel_id=1, source_target_pairs={{0,1},{1,0},{2,3},{3,2},{4,5},{5,4},{6,7},{7,6},{8,9},{9,8},{10,11... | collective-permute-start | bytes 1769480 | tf_op jit(solution)/shard_map/ppermute | solution.py:35
  75.2 8.1 %copy-start.7 = (bf16[768,384]{1,0:T(8,128)(2,1)}, bf16[768,384]{1,0:T(8,128)(2,1)S(1)}, u32[]{:S(2)}) copy-start(bf16[768,384]{1,0:T(8,128)(2,1)S(1)} %collective-permute-done.14.refs_12_.refs_9_.refs_11_.refs_4_) | copy-start | bytes 1769476
  75.2 8.1 %copy-start.10 = (bf16[768,384]{1,0:T(8,128)(2,1)}, bf16[768,384]{1,0:T(8,128)(2,1)S(1)}, u32[]{:S(2)}) copy-start(bf16[768,384]{1,0:T(8,128)(2,1)S(1)} %collective-permute-done.15.refs_13_.refs_10_.refs_12_.refs_5_) | copy-start | bytes 1769476
  75.2 8.1 %copy-start.13 = (bf16[768,384]{1,0:T(8,128)(2,1)}, bf16[768,384]{1,0:T(8,128)(2,1)S(1)}, u32[]{:S(2)}) copy-start(bf16[768,384]{1,0:T(8,128)(2,1)S(1)} %collective-permute-done.16.refs_14_.refs_11_.refs_13_.refs_6_) | copy-start | bytes 1769476
  77.1 6.2 %copy-start.16 = (bf16[768,384]{1,0:T(8,128)(2,1)}, bf16[768,384]{1,0:T(8,128)(2,1)S(1)}, u32[]{:S(2)}) copy-start(bf16[768,384]{1,0:T(8,128)(2,1)S(1)} %collective-permute-done.17.refs_15_.refs_12_.refs_14_.refs_7_) | copy-start | bytes 1769476
  80.9 5.0 %collective-permute-start.18 = (bf16[512,768]{1,0:T(8,128)(2,1)S(1)}, bf16[512,768]{1,0:T(8,128)(2,1)S(1)}, u32[]{:S(2)}, u32[]{:S(2)}) collective-permute-start(bf16[512,768]{1,0:T(8,128)(2,1)S(1)} %get-tuple-element.63), channel_id=1, source_target_pairs={{0,1},{1,0},{2,3},{3,2},{4,5},{5,4},{6,7},{7,6},{8,9},{9,8},{10,11... | collective-permute-start | bytes 2359304 | tf_op jit(solution)/shard_map/ppermute | solution.py:35
  96.3 11.5 %collective-permute-start.19 = (bf16[512,768]{1,0:T(8,128)(2,1)}, bf16[512,768]{1,0:T(8,128)(2,1)}, u32[]{:S(2)}, u32[]{:S(2)}) collective-permute-start(bf16[512,768]{1,0:T(8,128)(2,1)} %get-tuple-element.68), channel_id=1, source_target_pairs={{0,1},{1,0},{2,3},{3,2},{4,5},{5,4},{6,7},{7,6},{8,9},{9,8},{10,11... | collective-permute-start | bytes 2359304 | tf_op jit(solution)/shard_map/ppermute | solution.py:35
  104.0 26.6 %copy-start.12 = (bf16[768,384]{1,0:T(8,128)(2,1)S(1)}, bf16[768,384]{1,0:T(8,128)(2,1)}, u32[]{:S(2)}) copy-start(bf16[768,384]{1,0:T(8,128)(2,1)} %copy-done.10) | copy-start | bytes 1769476
  104.0 26.6 %copy-start.15 = (bf16[768,384]{1,0:T(8,128)(2,1)S(1)}, bf16[768,384]{1,0:T(8,128)(2,1)}, u32[]{:S(2)}) copy-start(bf16[768,384]{1,0:T(8,128)(2,1)} %copy-done.13) | copy-start | bytes 1769476
  104.0 26.6 %copy-start.18 = (bf16[768,384]{1,0:T(8,128)(2,1)S(1)}, bf16[768,384]{1,0:T(8,128)(2,1)}, u32[]{:S(2)}) copy-start(bf16[768,384]{1,0:T(8,128)(2,1)} %copy-done.16) | copy-start | bytes 1769476
  104.0 26.6 %copy-start.20 = (f32[256,768]{1,0:T(8,128)S(1)}, f32[256,768]{1,0:T(8,128)}, u32[]{:S(2)}) copy-start(f32[256,768]{1,0:T(8,128)} %copy-done.19) | copy-start | bytes 2359300
  107.8 22.8 %copy-start.3 = (bf16[768,384]{1,0:T(8,128)(2,1)S(1)}, bf16[768,384]{1,0:T(8,128)(2,1)}, u32[]{:S(2)}) copy-start(bf16[768,384]{1,0:T(8,128)(2,1)} %copy-done) | copy-start | bytes 1769476
  107.8 22.8 %copy-start.6 = (bf16[768,384]{1,0:T(8,128)(2,1)S(1)}, bf16[768,384]{1,0:T(8,128)(2,1)}, u32[]{:S(2)}) copy-start(bf16[768,384]{1,0:T(8,128)(2,1)} %copy-done.4) | copy-start | bytes 1769476
  107.8 22.8 %copy-start.9 = (bf16[768,384]{1,0:T(8,128)(2,1)S(1)}, bf16[768,384]{1,0:T(8,128)(2,1)}, u32[]{:S(2)}) copy-start(bf16[768,384]{1,0:T(8,128)(2,1)} %copy-done.7) | copy-start | bytes 1769476
  109.2 12.5 %collective-permute-start.24 = (bf16[256,768]{1,0:T(8,128)(2,1)S(1)}, bf16[256,768]{1,0:T(8,128)(2,1)S(1)}, u32[]{:S(2)}, u32[]{:S(2)}) collective-permute-start(bf16[256,768]{1,0:T(8,128)(2,1)S(1)} %get-tuple-element.83), channel_id=1, source_target_pairs={{0,8},{1,9},{2,10},{3,11},{4,12},{5,13},{6,14},{7,15},{8,16},{9,17... | collective-permute-start | bytes 1179656 | tf_op jit(solution)/shard_map/ppermute | solution.py:35
  110.2 25.9 %collective-permute-start.20 = (bf16[528,384]{1,0:T(8,128)(2,1)S(1)}, bf16[528,384]{1,0:T(8,128)(2,1)S(1)}, u32[]{:S(2)}, u32[]{:S(2)}) collective-permute-start(bf16[528,384]{1,0:T(8,128)(2,1)S(1)} %get-tuple-element.76), channel_id=1, source_target_pairs={{0,0},{1,4},{2,2},{3,6},{4,1},{5,5},{6,3},{7,7},{8,8},{9,12},{10,1... | collective-permute-start | bytes 1216520 | tf_op jit(solution)/shard_map/ppermute | solution.py:35
  113.3 22.8 %collective-permute-start.21 = (bf16[528,384]{1,0:T(8,128)(2,1)S(1)}, bf16[528,384]{1,0:T(8,128)(2,1)S(1)}, u32[]{:S(2)}, u32[]{:S(2)}) collective-permute-start(bf16[528,384]{1,0:T(8,128)(2,1)S(1)} %get-tuple-element.77), channel_id=1, source_target_pairs={{0,1},{1,5},{2,3},{3,7},{4,0},{5,4},{6,2},{7,6},{8,9},{9,13},{10,1... | collective-permute-start | bytes 1216520 | tf_op jit(solution)/shard_map/ppermute | solution.py:35
  113.3 24.6 %collective-permute-start.22 = (bf16[528,384]{1,0:T(8,128)(2,1)S(1)}, bf16[528,384]{1,0:T(8,128)(2,1)S(1)}, u32[]{:S(2)}, u32[]{:S(2)}) collective-permute-start(bf16[528,384]{1,0:T(8,128)(2,1)S(1)} %get-tuple-element.78), channel_id=1, source_target_pairs={{0,2},{1,6},{2,0},{3,4},{4,3},{5,7},{6,1},{7,5},{8,10},{9,14},{10,... | collective-permute-start | bytes 1216520 | tf_op jit(solution)/shard_map/ppermute | solution.py:35
  115.1 15.5 %collective-permute-start.25 = (bf16[256,768]{1,0:T(8,128)(2,1)S(1)}, bf16[256,768]{1,0:T(8,128)(2,1)S(1)}, u32[]{:S(2)}, u32[]{:S(2)}) collective-permute-start(bf16[256,768]{1,0:T(8,128)(2,1)S(1)} %get-tuple-element.84), channel_id=1, source_target_pairs={{0,24},{1,25},{2,26},{3,27},{4,28},{5,29},{6,30},{7,31},{8,0},{9,1... | collective-permute-start | bytes 1179656 | tf_op jit(solution)/shard_map/ppermute | solution.py:35
  121.7 16.6 %collective-permute-start.23 = (bf16[528,384]{1,0:T(8,128)(2,1)S(1)}, bf16[528,384]{1,0:T(8,128)(2,1)S(1)}, u32[]{:S(2)}, u32[]{:S(2)}) collective-permute-start(bf16[528,384]{1,0:T(8,128)(2,1)S(1)} %get-tuple-element.79), channel_id=1, source_target_pairs={{0,3},{1,7},{2,1},{3,5},{4,2},{5,6},{6,0},{7,4},{8,11},{9,15},{10,... | collective-permute-start | bytes 1216520 | tf_op jit(solution)/shard_map/ppermute | solution.py:35
  133.3 7.5 %collective-permute-start.26 = (bf16[256,384]{1,0:T(8,128)(2,1)S(1)}, bf16[256,384]{1,0:T(8,128)(2,1)S(1)}, u32[]{:S(2)}, u32[]{:S(2)}) collective-permute-start(bf16[256,384]{1,0:T(8,128)(2,1)S(1)} %get-tuple-element.85), channel_id=1, source_target_pairs={{0,0},{1,4},{2,2},{3,6},{4,1},{5,5},{6,3},{7,7},{8,8},{9,12},{10,1... | collective-permute-start | bytes 589832 | tf_op jit(solution)/shard_map/ppermute | solution.py:35
  136.1 7.2 %collective-permute-start.27 = (bf16[256,384]{1,0:T(8,128)(2,1)S(1)}, bf16[256,384]{1,0:T(8,128)(2,1)S(1)}, u32[]{:S(2)}, u32[]{:S(2)}) collective-permute-start(bf16[256,384]{1,0:T(8,128)(2,1)S(1)} %get-tuple-element.86), channel_id=1, source_target_pairs={{0,1},{1,5},{2,3},{3,7},{4,0},{5,4},{6,2},{7,6},{8,9},{9,13},{10,1... | collective-permute-start | bytes 589832 | tf_op jit(solution)/shard_map/ppermute | solution.py:35
  136.1 8.1 %collective-permute-start.28 = (bf16[256,384]{1,0:T(8,128)(2,1)S(1)}, bf16[256,384]{1,0:T(8,128)(2,1)S(1)}, u32[]{:S(2)}, u32[]{:S(2)}) collective-permute-start(bf16[256,384]{1,0:T(8,128)(2,1)S(1)} %get-tuple-element.87), channel_id=1, source_target_pairs={{0,2},{1,6},{2,0},{3,4},{4,3},{5,7},{6,1},{7,5},{8,10},{9,14},{10,... | collective-permute-start | bytes 589832 | tf_op jit(solution)/shard_map/ppermute | solution.py:35
  138.0 9.9 %collective-permute-start.29 = (bf16[256,384]{1,0:T(8,128)(2,1)S(1)}, bf16[256,384]{1,0:T(8,128)(2,1)S(1)}, u32[]{:S(2)}, u32[]{:S(2)}) collective-permute-start(bf16[256,384]{1,0:T(8,128)(2,1)S(1)} %get-tuple-element.88), channel_id=1, source_target_pairs={{0,3},{1,7},{2,1},{3,5},{4,2},{5,6},{6,0},{7,4},{8,11},{9,15},{10,... | collective-permute-start | bytes 589832 | tf_op jit(solution)/shard_map/ppermute | solution.py:35
  (13 other events, 20.2 us)

commit v5 on v4

--- a/solution.py
+++ b/solution.py
@@ -381,7 +381,7 @@
     to_above = (d_outer[OWN_ROWS:] + jnp.where(c == 0, shared_grad, 0.0)).astype(LOW)
     terms = call(
         product_kernel,
-        [attended, d_queries, inv_rms] + tokens + qo_pieces,
+        [attended, d_queries, inv_rms] + [pltpu.with_memory_space_constraint(o, pltpu.HBM) for o in tokens + qo_pieces],
         [VMEM, VMEM, VMEM] + [ANY] * (4 + piece_count),
         [((2 * token_count + EXTRA, width), LOW)] * 4,
         [
@@ -401,7 +401,7 @@
     )
     enc_terms = call(
         encoding_kernel,
-        [d_own, from_core, up, down] + kv_pieces,
+        [d_own, from_core, up, down] + [pltpu.with_memory_space_constraint(o, pltpu.HBM) for o in kv_pieces],
         [VMEM] * 4 + [ANY] * piece_count,
         [((OWN_ROWS, width), LOW)] * 4,
         [pltpu.VMEM((full_width, wide), LOW)],

time: 150 us -> 138 us (0.920)
  local copies, waits for them, and re-layouts: 10.7 us -> 0.27 us
    unnamed x62 -> x34, local copies, waits for them, and re-layouts: 10.5 us -> 0.07 us
  transfers between devices with their start and end apart: 30 -> 30, of which waited for: 15 -> 15; matrix products, arithmetic and copies ran while one was open for 1% -> 2% of each run, Pallas kernels for 8% -> 9%
where the time goes in v5:
time: 138 us; the launch traced here: 137 us
  waiting for transfers between devices  71.9 us (52%)
  starting transfers between devices  35.5 us (26%)
  Pallas kernels  23.9 us (17%)
  other arithmetic  4.5 us (3%)
    ppermute x30, waiting for transfers between devices, move(): return lax.ppermute(value, ('seq', 'mp'), pairs)  71.9 us
    ppermute x30, starting transfers between devices, move(): return lax.ppermute(value, ('seq', 'mp'), pairs)  35.5 us
    pallas_call x7, Pallas kernels, call(): pl.pallas_call(kernel, out_shape=[jax.ShapeDtypeStruct(shape, dtype) for...  23.9 us
  transfers between devices with their start and end apart: 30, of which 15 were waited for; matrix products, arithmetic and copies ran while one was open for 2% of the time, Pallas kernels for 9%

profile of v5, /device:TPU:1, one launch (start us, length us, event | category | flops | bytes accessed | tf_op | source)
XLA Modules:
  0.0 137.1 jit_solution(4338854628342181669)
XLA Ops:
  0.7 1.3 pad_maximum_fusion.1
  2.0 4.5 %collective-permute-start = (bf16[768,384]{1,0:T(8,128)(2,1)S(1)}, bf16[768,384]{1,0:T(8,128)(2,1)S(1)}, u32[]{:S(2)}, u32[]{:S(2)}) collective-permute-start(bf16[768,384]{1,0:T(8,128)(2,1)S(1)} %pad_maximum_fusion.1), channel_id=1, source_target_pairs={{0,0},{1,4},{2,2},{3,6},{4,1},{5,5},{6,3},{7,7},{8,8},{9,12},{10,1... | collective-permute-start | bytes 1769480 | tf_op jit(solution)/shard_map/ppermute | solution.py:35
  6.5 1.3 collective-permute-start.1
  7.9 2.1 %collective-permute-start.2 = (bf16[256,384]{1,0:T(8,128)(2,1)S(1)}, bf16[256,384]{1,0:T(8,128)(2,1)}, u32[]{:S(2)}, u32[]{:S(2)}) collective-permute-start(bf16[256,384]{1,0:T(8,128)(2,1)S(1)} %bitcast.7), channel_id=1, source_target_pairs={{0,24},{1,25},{2,26},{3,27},{4,28},{5,29},{6,30},{7,31},{8,0},{9,1... | collective-permute-start | bytes 589832 | tf_op jit(solution)/shard_map/ppermute | solution.py:35
  10.2 0.9 pad_maximum_fusion
  11.1 4.0 %collective-permute-done.1 = bf16[256,384]{1,0:T(8,128)(2,1)S(1)} collective-permute-done((bf16[256,384]{1,0:T(8,128)(2,1)S(1)}, bf16[256,384]{1,0:T(8,128)(2,1)S(1)}, u32[]{:S(2)}, u32[]{:S(2)}) %collective-permute-start.1) | collective-permute-done | bytes 196640 | tf_op jit(solution)/shard_map/ppermute | solution.py:35
  15.1 2.2 %collective-permute-done.2 = bf16[256,384]{1,0:T(8,128)(2,1)} collective-permute-done((bf16[256,384]{1,0:T(8,128)(2,1)S(1)}, bf16[256,384]{1,0:T(8,128)(2,1)}, u32[]{:S(2)}, u32[]{:S(2)}) %collective-permute-start.2) | collective-permute-done | bytes 196640 | tf_op jit(solution)/shard_map/ppermute | solution.py:35
  17.3 0.3 collective-permute-start.3
  17.6 3.1 %collective-permute-start.5 = (bf16[784,384]{1,0:T(8,128)(2,1)}, bf16[784,384]{1,0:T(8,128)(2,1)S(1)}, u32[]{:S(2)}, u32[]{:S(2)}) collective-permute-start(bf16[784,384]{1,0:T(8,128)(2,1)} %pad_maximum_fusion), channel_id=1, source_target_pairs={{0,0},{1,4},{2,2},{3,6},{4,1},{5,5},{6,3},{7,7},{8,8},{9,12},{10,1... | collective-permute-start | bytes 1806344 | tf_op jit(solution)/shard_map/ppermute | solution.py:35
  20.7 1.9 %collective-permute-start.7 = (bf16[784,384]{1,0:T(8,128)(2,1)}, bf16[784,384]{1,0:T(8,128)(2,1)S(1)}, u32[]{:S(2)}, u32[]{:S(2)}) collective-permute-start(bf16[784,384]{1,0:T(8,128)(2,1)} %pad_maximum_fusion), channel_id=1, source_target_pairs={{0,2},{1,6},{2,0},{3,4},{4,3},{5,7},{6,1},{7,5},{8,10},{9,14},{10,... | collective-permute-start | bytes 1806344 | tf_op jit(solution)/shard_map/ppermute | solution.py:35
  22.6 0.7 collective-permute-start.8
  23.3 10.4 %collective-permute-done.3.refs_9_.refs_6_.refs_8_.refs_1_ = bf16[768,384]{1,0:T(8,128)(2,1)S(1)} collective-permute-done((bf16[768,384]{1,0:T(8,128)(2,1)S(1)}, bf16[768,384]{1,0:T(8,128)(2,1)S(1)}, u32[]{:S(2)}, u32[]{:S(2)}) %collective-permute-start.3) | collective-permute-done | bytes 589856 | tf_op jit(solution)/shard_map/ppermute | solution.py:35
  33.7 1.2 pad_maximum_fusion.2
  34.9 12.7 %collective-permute-done.4.refs_10_.refs_7_.refs_9_.refs_2_ = bf16[768,384]{1,0:T(8,128)(2,1)S(1)} collective-permute-done((bf16[768,384]{1,0:T(8,128)(2,1)}, bf16[768,384]{1,0:T(8,128)(2,1)S(1)}, u32[]{:S(2)}, u32[]{:S(2)}) %collective-permute-start.4) | collective-permute-done | bytes 589856 | tf_op jit(solution)/shard_map/ppermute | solution.py:35
  47.6 2.5 %collective-permute-done.8.refs_3_.refs_4_.refs_6_ = bf16[784,384]{1,0:T(8,128)(2,1)} collective-permute-done((bf16[784,384]{1,0:T(8,128)(2,1)}, bf16[784,384]{1,0:T(8,128)(2,1)}, u32[]{:S(2)}, u32[]{:S(2)}) %collective-permute-start.8) | collective-permute-done | bytes 602144 | tf_op jit(solution)/shard_map/ppermute | solution.py:35
  50.2 0.5 collective-permute-start.9
  50.7 3.7 %collective-permute-start.10 = (bf16[512,384]{1,0:T(8,128)(2,1)S(1)}, bf16[512,384]{1,0:T(8,128)(2,1)S(1)}, u32[]{:S(2)}, u32[]{:S(2)}) collective-permute-start(bf16[512,384]{1,0:T(8,128)(2,1)S(1)} %pad_maximum_fusion.2), channel_id=1, source_target_pairs={{0,0},{1,4},{2,2},{3,6},{4,1},{5,5},{6,3},{7,7},{8,8},{9,12},{10,1... | collective-permute-start | bytes 1179656 | tf_op jit(solution)/shard_map/ppermute | solution.py:35
  54.4 1.0 collective-permute-start.12
  55.4 1.0 collective-permute-start.13
  56.4 11.8 %collective-permute-done.10.refs_4_ = bf16[512,384]{1,0:T(8,128)(2,1)S(1)} collective-permute-done((bf16[512,384]{1,0:T(8,128)(2,1)S(1)}, bf16[512,384]{1,0:T(8,128)(2,1)S(1)}, u32[]{:S(2)}, u32[]{:S(2)}) %collective-permute-start.10) | collective-permute-done | bytes 393248 | tf_op jit(solution)/shard_map/ppermute | solution.py:35
  68.2 2.5 %collective-permute-done.11.refs_5_ = bf16[512,384]{1,0:T(8,128)(2,1)S(1)} collective-permute-done((bf16[512,384]{1,0:T(8,128)(2,1)S(1)}, bf16[512,384]{1,0:T(8,128)(2,1)S(1)}, u32[]{:S(2)}, u32[]{:S(2)}) %collective-permute-start.11) | collective-permute-done | bytes 393248 | tf_op jit(solution)/shard_map/ppermute | solution.py:35
  70.6 0.5 collective-permute-start.16
  71.1 3.4 %collective-permute-done.13.refs_7_ = bf16[512,384]{1,0:T(8,128)(2,1)S(1)} collective-permute-done((bf16[512,384]{1,0:T(8,128)(2,1)S(1)}, bf16[512,384]{1,0:T(8,128)(2,1)S(1)}, u32[]{:S(2)}, u32[]{:S(2)}) %collective-permute-start.13) | collective-permute-done | bytes 393248 | tf_op jit(solution)/shard_map/ppermute | solution.py:35
  74.6 1.9 %collective-permute-done.17.refs_15_.refs_12_.refs_14_.refs_7_ = bf16[768,384]{1,0:T(8,128)(2,1)S(1)} collective-permute-done((bf16[768,384]{1,0:T(8,128)(2,1)S(1)}, bf16[768,384]{1,0:T(8,128)(2,1)S(1)}, u32[]{:S(2)}, u32[]{:S(2)}) %collective-permute-start.17) | collective-permute-done | bytes 589856 | tf_op jit(solution)/shard_map/ppermute | solution.py:35
  76.6 3.7 %shard_map.112 = (bf16[768,768]{1,0:T(8,128)(2,1)S(1)}, bf16[512,768]{1,0:T(8,128)(2,1)S(1)}) custom-call(bf16[784,384]{1,0:T(8,128)(2,1)S(1)} %collective-permute-done.5.refs_0_.refs_1_.refs_3_, bf16[784,384]{1,0:T(8,128)(2,1)S(1)} %collective-permute-done.6.refs_1_.refs_2_.refs_4_, bf16[784,384]{1,0:T(8,128)(2,1)S(1)} %collective-permute-done.7.refs_2_.refs_3_.refs_5_, ...), custom_call_target="tpu_custom_call" | custom-call | tf_op jit(solution)/shard_map/pallas_call | solution.py:297
  80.3 0.2 collective-permute-start.18
  80.5 2.1 %shard_map.113 = (bf16[256,1536]{1,0:T(8,128)(2,1)S(1)}, f32[256,1]{1,0:T(8,128)S(1)}) custom-call(bf16[784,384]{1,0:T(8,128)(2,1)S(1)} %collective-permute-done.5.refs_0_.refs_1_.refs_3_, bf16[784,384]{1,0:T(8,128)(2,1)S(1)} %collective-permute-done.6.refs_1_.refs_2_.refs_4_, bf16[784,384]{1,0:T(8,128)(2,1)S(1)} %collective-permute-done.7.refs_2_.refs_3_.refs_5_, ...), custom_call_target="tpu_custom_call" | custom-call | tf_op jit(solution)/shard_map/pallas_call | solution.py:297
  82.8 2.5 %shard_map.114 = (bf16[256,384]{1,0:T(8,128)(2,1)S(1)}, bf16[256,384]{1,0:T(8,128)(2,1)S(1)}) custom-call(bf16[256,1536]{1,0:T(8,128)(2,1)S(1)} %get-tuple-element.64.refs_0_, bf16[784,384]{1,0:T(8,128)(2,1)S(1)} %collective-permute-done.5.refs_0_.refs_1_.refs_3_, bf16[784,384]{1,0:T(8,128)(2,1)S(1)} %collective-permute-done.6.refs_1_.refs_2_.refs_4_, ...), custom_call_target="tpu_custom_call" | custom-call | tf_op jit(solution)/shard_map/pallas_call | solution.py:297
  85.3 8.0 %shard_map.115 = (bf16[256,384]{1,0:T(8,128)(2,1)S(1)}, bf16[256,384]{1,0:T(8,128)(2,1)S(1)}, f32[256,768]{1,0:T(8,128)S(1)}, bf16[512,768]{1,0:T(8,128)(2,1)S(1)}, bf16[512,768]{1,0:T(8,128)(2,1)}) custom-call(s32[8]{0:T(128)S(1)} %bitcast_convert_fusion.refs_0_, bf16[768,768]{1,0:T(8,128)(2,1)S(1)} %get-tuple-element.62.refs_1_, ...), custom_call_target="tpu_custom_call" | custom-call | tf_op jit(solution)/shard_map/pallas_call | solution.py:297
  93.3 0.4 collective-permute-start.19
  93.7 3.5 %shard_map.116 = (bf16[528,384]{1,0:T(8,128)(2,1)S(1)}, bf16[528,384]{1,0:T(8,128)(2,1)S(1)}, bf16[528,384]{1,0:T(8,128)(2,1)S(1)}, bf16[528,384]{1,0:T(8,128)(2,1)S(1)}) custom-call(bf16[256,384]{1,0:T(8,128)(2,1)S(1)} %get-tuple-element.69.refs_0_, bf16[256,384]{1,0:T(8,128)(2,1)S(1)} %get-tuple-element.70.refs_1_, ...), custom_call_target="tpu_custom_call" | custom-call | tf_op jit(solution)/shard_map/pallas_call | solution.py:297
  97.5 1.0 collective-permute-start.24
  98.5 3.2 %collective-permute-start.20 = (bf16[528,384]{1,0:T(8,128)(2,1)S(1)}, bf16[528,384]{1,0:T(8,128)(2,1)S(1)}, u32[]{:S(2)}, u32[]{:S(2)}) collective-permute-start(bf16[528,384]{1,0:T(8,128)(2,1)S(1)} %get-tuple-element.76), channel_id=1, source_target_pairs={{0,0},{1,4},{2,2},{3,6},{4,1},{5,5},{6,3},{7,7},{8,8},{9,12},{10,1... | collective-permute-start | bytes 1216520 | tf_op jit(solution)/shard_map/ppermute | solution.py:35
  101.6 1.7 %collective-permute-start.22 = (bf16[528,384]{1,0:T(8,128)(2,1)S(1)}, bf16[528,384]{1,0:T(8,128)(2,1)S(1)}, u32[]{:S(2)}, u32[]{:S(2)}) collective-permute-start(bf16[528,384]{1,0:T(8,128)(2,1)S(1)} %get-tuple-element.78), channel_id=1, source_target_pairs={{0,2},{1,6},{2,0},{3,4},{4,3},{5,7},{6,1},{7,5},{8,10},{9,14},{10,... | collective-permute-start | bytes 1216520 | tf_op jit(solution)/shard_map/ppermute | solution.py:35
  103.4 2.1 %collective-permute-start.25 = (bf16[256,768]{1,0:T(8,128)(2,1)S(1)}, bf16[256,768]{1,0:T(8,128)(2,1)S(1)}, u32[]{:S(2)}, u32[]{:S(2)}) collective-permute-start(bf16[256,768]{1,0:T(8,128)(2,1)S(1)} %get-tuple-element.84), channel_id=1, source_target_pairs={{0,24},{1,25},{2,26},{3,27},{4,28},{5,29},{6,30},{7,31},{8,0},{9,1... | collective-permute-start | bytes 1179656 | tf_op jit(solution)/shard_map/ppermute | solution.py:35
  105.5 4.5 %collective-permute-done.24.up = bf16[256,768]{1,0:T(8,128)(2,1)S(1)} collective-permute-done((bf16[256,768]{1,0:T(8,128)(2,1)S(1)}, bf16[256,768]{1,0:T(8,128)(2,1)S(1)}, u32[]{:S(2)}, u32[]{:S(2)}) %collective-permute-start.24) | collective-permute-done | bytes 393248 | tf_op jit(solution)/shard_map/ppermute | solution.py:35
  109.9 1.3 collective-permute-start.23
  111.3 7.6 %collective-permute-done.25.down = bf16[256,768]{1,0:T(8,128)(2,1)S(1)} collective-permute-done((bf16[256,768]{1,0:T(8,128)(2,1)S(1)}, bf16[256,768]{1,0:T(8,128)(2,1)S(1)}, u32[]{:S(2)}, u32[]{:S(2)}) %collective-permute-start.25) | collective-permute-done | bytes 393248 | tf_op jit(solution)/shard_map/ppermute | solution.py:35
  118.8 2.8 %shard_map.118 = (bf16[256,384]{1,0:T(8,128)(2,1)S(1)}, bf16[256,384]{1,0:T(8,128)(2,1)S(1)}, bf16[256,384]{1,0:T(8,128)(2,1)S(1)}, bf16[256,384]{1,0:T(8,128)(2,1)S(1)}) custom-call(f32[256,768]{1,0:T(8,128)S(1)} %get-tuple-element.82.own, bf16[512,768]{1,0:T(8,128)(2,1)S(1)} %collective-permute-done.19.from_core, ...), custom_call_target="tpu_custom_call" | custom-call | tf_op jit(solution)/shard_map/pallas_call | solution.py:297
  121.7 2.8 %collective-permute-start.26 = (bf16[256,384]{1,0:T(8,128)(2,1)S(1)}, bf16[256,384]{1,0:T(8,128)(2,1)S(1)}, u32[]{:S(2)}, u32[]{:S(2)}) collective-permute-start(bf16[256,384]{1,0:T(8,128)(2,1)S(1)} %get-tuple-element.85), channel_id=1, source_target_pairs={{0,0},{1,4},{2,2},{3,6},{4,1},{5,5},{6,3},{7,7},{8,8},{9,12},{10,1... | collective-permute-start | bytes 589832 | tf_op jit(solution)/shard_map/ppermute | solution.py:35
  124.5 1.9 %collective-permute-start.28 = (bf16[256,384]{1,0:T(8,128)(2,1)S(1)}, bf16[256,384]{1,0:T(8,128)(2,1)S(1)}, u32[]{:S(2)}, u32[]{:S(2)}) collective-permute-start(bf16[256,384]{1,0:T(8,128)(2,1)S(1)} %get-tuple-element.87), channel_id=1, source_target_pairs={{0,2},{1,6},{2,0},{3,4},{4,3},{5,7},{6,1},{7,5},{8,10},{9,14},{10,... | collective-permute-start | bytes 589832 | tf_op jit(solution)/shard_map/ppermute | solution.py:35
  126.4 0.3 collective-permute-start.29
  126.7 1.2 shard_map.117
  127.8 1.3 collective-permute-done.26
  129.2 2.5 %collective-permute-done.27 = bf16[256,384]{1,0:T(8,128)(2,1)S(1)} collective-permute-done((bf16[256,384]{1,0:T(8,128)(2,1)S(1)}, bf16[256,384]{1,0:T(8,128)(2,1)S(1)}, u32[]{:S(2)}, u32[]{:S(2)}) %collective-permute-start.27) | collective-permute-done | bytes 196640 | tf_op jit(solution)/shard_map/ppermute | solution.py:35
  131.7 1.0 collective-permute-done.28
  132.7 3.6 %collective-permute-done.29 = bf16[256,384]{1,0:T(8,128)(2,1)S(1)} collective-permute-done((bf16[256,384]{1,0:T(8,128)(2,1)S(1)}, bf16[256,384]{1,0:T(8,128)(2,1)S(1)}, u32[]{:S(2)}, u32[]{:S(2)}) %collective-permute-start.29) | collective-permute-done | bytes 196640 | tf_op jit(solution)/shard_map/ppermute | solution.py:35
  136.3 0.8 add_convert_fusion
  (65 shorter events, 0.7 us)
Async XLA Ops:
  0.6 5.9 %copy-start.14 = (bf16[2,128,384]{2,1,0:T(8,128)(2,1)S(1)}, bf16[2,128,384]{2,1,0:T(8,128)(2,1)}, u32[]{:S(2)}) copy-start(bf16[2,128,384]{2,1,0:T(8,128)(2,1)} %param.11) | copy-start | bytes 589828
  0.6 9.3 %copy-start.15 = (bf16[384]{0:T(512)(128)(2,1)S(1)}, bf16[384]{0:T(512)(128)(2,1)}, u32[]{:S(2)}) copy-start(bf16[384]{0:T(512)(128)(2,1)} %param.10) | copy-start | bytes 2308
  0.7 9.3 %copy-start.16 = (s32[4,2]{0,1:T(2,128)S(1)}, s32[4,2]{0,1:T(2,128)}, u32[]{:S(2)}) copy-start(s32[4,2]{0,1:T(2,128)} %param.16) | copy-start | bytes 100
  0.7 9.5 %copy-start.13 = (bf16[256,384]{1,0:T(8,128)(2,1)S(1)}, bf16[256,384]{1,0:T(8,128)(2,1)}, u32[]{:S(2)}) copy-start(bf16[256,384]{1,0:T(8,128)(2,1)} %param.17) | copy-start | bytes 589828
  0.7 9.5 %copy-start.12 = (bf16[256,384]{1,0:T(8,128)(2,1)S(1)}, bf16[256,384]{1,0:T(8,128)(2,1)}, u32[]{:S(2)}) copy-start(bf16[256,384]{1,0:T(8,128)(2,1)} %hidden.1) | copy-start | bytes 589828
  2.0 15.4 %collective-permute-start = (bf16[768,384]{1,0:T(8,128)(2,1)S(1)}, bf16[768,384]{1,0:T(8,128)(2,1)S(1)}, u32[]{:S(2)}, u32[]{:S(2)}) collective-permute-start(bf16[768,384]{1,0:T(8,128)(2,1)S(1)} %pad_maximum_fusion.1), channel_id=1, source_target_pairs={{0,0},{1,4},{2,2},{3,6},{4,1},{5,5},{6,3},{7,7},{8,8},{9,12},{10,1... | collective-permute-start | bytes 1769480 | tf_op jit(solution)/shard_map/ppermute | solution.py:35
  6.5 8.6 %collective-permute-start.1 = (bf16[256,384]{1,0:T(8,128)(2,1)S(1)}, bf16[256,384]{1,0:T(8,128)(2,1)S(1)}, u32[]{:S(2)}, u32[]{:S(2)}) collective-permute-start(bf16[256,384]{1,0:T(8,128)(2,1)S(1)} %bitcast.6), channel_id=1, source_target_pairs={{0,8},{1,9},{2,10},{3,11},{4,12},{5,13},{6,14},{7,15},{8,16},{9,17... | collective-permute-start | bytes 589832 | tf_op jit(solution)/shard_map/ppermute | solution.py:35
  7.9 9.4 %collective-permute-start.2 = (bf16[256,384]{1,0:T(8,128)(2,1)S(1)}, bf16[256,384]{1,0:T(8,128)(2,1)}, u32[]{:S(2)}, u32[]{:S(2)}) collective-permute-start(bf16[256,384]{1,0:T(8,128)(2,1)S(1)} %bitcast.7), channel_id=1, source_target_pairs={{0,24},{1,25},{2,26},{3,27},{4,28},{5,29},{6,30},{7,31},{8,0},{9,1... | collective-permute-start | bytes 589832 | tf_op jit(solution)/shard_map/ppermute | solution.py:35
  17.3 6.0 %copy-start.5 = (bf16[768,384]{1,0:T(8,128)(2,1)}, bf16[768,384]{1,0:T(8,128)(2,1)S(1)}, u32[]{:S(2)}) copy-start(bf16[768,384]{1,0:T(8,128)(2,1)S(1)} %collective-permute-done.refs_8_.refs_5_.refs_7_.refs_0_) | copy-start | bytes 1769476
  17.3 16.3 %collective-permute-start.3 = (bf16[768,384]{1,0:T(8,128)(2,1)S(1)}, bf16[768,384]{1,0:T(8,128)(2,1)S(1)}, u32[]{:S(2)}, u32[]{:S(2)}) collective-permute-start(bf16[768,384]{1,0:T(8,128)(2,1)S(1)} %collective-permute-done.refs_8_.refs_5_.refs_7_.refs_0_), channel_id=1, source_target_pairs={{0,8},{1,9},{2,10},{3,11},{4,12},{5,13},{6,14},{7,15},{8,16},{9,17... | collective-permute-start | bytes 1769480 | tf_op jit(solution)/shard_map/ppermute | solution.py:35
  17.6 30.0 %collective-permute-start.5 = (bf16[784,384]{1,0:T(8,128)(2,1)}, bf16[784,384]{1,0:T(8,128)(2,1)S(1)}, u32[]{:S(2)}, u32[]{:S(2)}) collective-permute-start(bf16[784,384]{1,0:T(8,128)(2,1)} %pad_maximum_fusion), channel_id=1, source_target_pairs={{0,0},{1,4},{2,2},{3,6},{4,1},{5,5},{6,3},{7,7},{8,8},{9,12},{10,1... | collective-permute-start | bytes 1806344 | tf_op jit(solution)/shard_map/ppermute | solution.py:35
  20.7 26.9 %collective-permute-start.6 = (bf16[784,384]{1,0:T(8,128)(2,1)}, bf16[784,384]{1,0:T(8,128)(2,1)S(1)}, u32[]{:S(2)}, u32[]{:S(2)}) collective-permute-start(bf16[784,384]{1,0:T(8,128)(2,1)} %pad_maximum_fusion), channel_id=1, source_target_pairs={{0,4},{1,0},{2,6},{3,2},{4,5},{5,1},{6,7},{7,3},{8,12},{9,8},{10,1... | collective-permute-start | bytes 1806344 | tf_op jit(solution)/shard_map/ppermute | solution.py:35
  20.7 26.9 %collective-permute-start.7 = (bf16[784,384]{1,0:T(8,128)(2,1)}, bf16[784,384]{1,0:T(8,128)(2,1)S(1)}, u32[]{:S(2)}, u32[]{:S(2)}) collective-permute-start(bf16[784,384]{1,0:T(8,128)(2,1)} %pad_maximum_fusion), channel_id=1, source_target_pairs={{0,2},{1,6},{2,0},{3,4},{4,3},{5,7},{6,1},{7,5},{8,10},{9,14},{10,... | collective-permute-start | bytes 1806344 | tf_op jit(solution)/shard_map/ppermute | solution.py:35
  22.6 27.5 %collective-permute-start.8 = (bf16[784,384]{1,0:T(8,128)(2,1)}, bf16[784,384]{1,0:T(8,128)(2,1)}, u32[]{:S(2)}, u32[]{:S(2)}) collective-permute-start(bf16[784,384]{1,0:T(8,128)(2,1)} %pad_maximum_fusion), channel_id=1, source_target_pairs={{0,6},{1,2},{2,4},{3,0},{4,7},{5,3},{6,5},{7,1},{8,14},{9,10},{10,... | collective-permute-start | bytes 1806344 | tf_op jit(solution)/shard_map/ppermute | solution.py:35
  33.6 49.0 %copy-start = (bf16[768,384]{1,0:T(8,128)(2,1)}, bf16[768,384]{1,0:T(8,128)(2,1)S(1)}, u32[]{:S(2)}) copy-start(bf16[768,384]{1,0:T(8,128)(2,1)S(1)} %collective-permute-done.3.refs_9_.refs_6_.refs_8_.refs_1_) | copy-start | bytes 1769476
  33.6 13.9 %collective-permute-start.4 = (bf16[768,384]{1,0:T(8,128)(2,1)}, bf16[768,384]{1,0:T(8,128)(2,1)S(1)}, u32[]{:S(2)}, u32[]{:S(2)}) collective-permute-start(bf16[768,384]{1,0:T(8,128)(2,1)} %copy-done.5), channel_id=1, source_target_pairs={{0,24},{1,25},{2,26},{3,27},{4,28},{5,29},{6,30},{7,31},{8,0},{9,1... | collective-permute-start | bytes 1769480 | tf_op jit(solution)/shard_map/ppermute | solution.py:35
  33.7 34.5 %copy-start.6 = (bf16[768,384]{1,0:T(8,128)(2,1)S(1)}, bf16[768,384]{1,0:T(8,128)(2,1)}, u32[]{:S(2)}) copy-start(bf16[768,384]{1,0:T(8,128)(2,1)} %copy-done.5) | copy-start | bytes 1769476
  47.6 35.1 %copy-start.1 = (bf16[768,384]{1,0:T(8,128)(2,1)}, bf16[768,384]{1,0:T(8,128)(2,1)S(1)}, u32[]{:S(2)}) copy-start(bf16[768,384]{1,0:T(8,128)(2,1)S(1)} %collective-permute-done.4.refs_10_.refs_7_.refs_9_.refs_2_) | copy-start | bytes 1769476
  47.6 35.1 %copy-start.2 = (bf16[784,384]{1,0:T(8,128)(2,1)}, bf16[784,384]{1,0:T(8,128)(2,1)S(1)}, u32[]{:S(2)}) copy-start(bf16[784,384]{1,0:T(8,128)(2,1)S(1)} %collective-permute-done.5.refs_0_.refs_1_.refs_3_) | copy-start | bytes 1806340
  47.6 35.1 %copy-start.3 = (bf16[784,384]{1,0:T(8,128)(2,1)}, bf16[784,384]{1,0:T(8,128)(2,1)S(1)}, u32[]{:S(2)}) copy-start(bf16[784,384]{1,0:T(8,128)(2,1)S(1)} %collective-permute-done.6.refs_1_.refs_2_.refs_4_) | copy-start | bytes 1806340
  47.6 35.1 %copy-start.4 = (bf16[784,384]{1,0:T(8,128)(2,1)}, bf16[784,384]{1,0:T(8,128)(2,1)S(1)}, u32[]{:S(2)}) copy-start(bf16[784,384]{1,0:T(8,128)(2,1)S(1)} %collective-permute-done.7.refs_2_.refs_3_.refs_5_) | copy-start | bytes 1806340
  50.2 24.3 %collective-permute-start.9 = (bf16[768,384]{1,0:T(8,128)(2,1)S(1)}, bf16[768,384]{1,0:T(8,128)(2,1)S(1)}, u32[]{:S(2)}, u32[]{:S(2)}) collective-permute-start(bf16[768,384]{1,0:T(8,128)(2,1)S(1)} %broadcast_select_fusion), channel_id=1, source_target_pairs={{0,8},{1,9},{2,10},{3,11},{4,12},{5,13},{6,14},{7,15},{8,0},{9,1},... | collective-permute-start | bytes 1769480 | tf_op jit(solution)/shard_map/ppermute | solution.py:35
  50.7 17.5 %collective-permute-start.10 = (bf16[512,384]{1,0:T(8,128)(2,1)S(1)}, bf16[512,384]{1,0:T(8,128)(2,1)S(1)}, u32[]{:S(2)}, u32[]{:S(2)}) collective-permute-start(bf16[512,384]{1,0:T(8,128)(2,1)S(1)} %pad_maximum_fusion.2), channel_id=1, source_target_pairs={{0,0},{1,4},{2,2},{3,6},{4,1},{5,5},{6,3},{7,7},{8,8},{9,12},{10,1... | collective-permute-start | bytes 1179656 | tf_op jit(solution)/shard_map/ppermute | solution.py:35
  54.4 16.3 %collective-permute-start.11 = (bf16[512,384]{1,0:T(8,128)(2,1)S(1)}, bf16[512,384]{1,0:T(8,128)(2,1)S(1)}, u32[]{:S(2)}, u32[]{:S(2)}) collective-permute-start(bf16[512,384]{1,0:T(8,128)(2,1)S(1)} %pad_maximum_fusion.2), channel_id=1, source_target_pairs={{0,4},{1,0},{2,6},{3,2},{4,5},{5,1},{6,7},{7,3},{8,12},{9,8},{10,1... | collective-permute-start | bytes 1179656 | tf_op jit(solution)/shard_map/ppermute | solution.py:35
  54.4 16.3 %collective-permute-start.12 = (bf16[512,384]{1,0:T(8,128)(2,1)S(1)}, bf16[512,384]{1,0:T(8,128)(2,1)S(1)}, u32[]{:S(2)}, u32[]{:S(2)}) collective-permute-start(bf16[512,384]{1,0:T(8,128)(2,1)S(1)} %pad_maximum_fusion.2), channel_id=1, source_target_pairs={{0,2},{1,6},{2,0},{3,4},{4,3},{5,7},{6,1},{7,5},{8,10},{9,14},{10,... | collective-permute-start | bytes 1179656 | tf_op jit(solution)/shard_map/ppermute | solution.py:35
  55.4 19.2 %collective-permute-start.13 = (bf16[512,384]{1,0:T(8,128)(2,1)S(1)}, bf16[512,384]{1,0:T(8,128)(2,1)S(1)}, u32[]{:S(2)}, u32[]{:S(2)}) collective-permute-start(bf16[512,384]{1,0:T(8,128)(2,1)S(1)} %pad_maximum_fusion.2), channel_id=1, source_target_pairs={{0,6},{1,2},{2,4},{3,0},{4,7},{5,3},{6,5},{7,1},{8,14},{9,10},{10,... | collective-permute-start | bytes 1179656 | tf_op jit(solution)/shard_map/ppermute | solution.py:35
  68.2 6.4 %collective-permute-start.14 = (bf16[768,384]{1,0:T(8,128)(2,1)S(1)}, bf16[768,384]{1,0:T(8,128)(2,1)S(1)}, u32[]{:S(2)}, u32[]{:S(2)}) collective-permute-start(bf16[768,384]{1,0:T(8,128)(2,1)S(1)} %copy-done.6), channel_id=1, source_target_pairs={{0,1},{1,0},{2,3},{3,2},{4,5},{5,4},{6,7},{7,6},{8,9},{9,8},{10,11... | collective-permute-start | bytes 1769480 | tf_op jit(solution)/shard_map/ppermute | solution.py:35
  70.6 3.9 %collective-permute-start.15 = (bf16[768,384]{1,0:T(8,128)(2,1)S(1)}, bf16[768,384]{1,0:T(8,128)(2,1)S(1)}, u32[]{:S(2)}, u32[]{:S(2)}) collective-permute-start(bf16[768,384]{1,0:T(8,128)(2,1)S(1)} %collective-permute-done.3.refs_9_.refs_6_.refs_8_.refs_1_), channel_id=1, source_target_pairs={{0,1},{1,0},{2,3},{3,2},{4,5},{5,4},{6,7},{7,6},{8,9},{9,8},{10,11... | collective-permute-start | bytes 1769480 | tf_op jit(solution)/shard_map/ppermute | solution.py:35
  70.6 4.0 %collective-permute-start.16 = (bf16[768,384]{1,0:T(8,128)(2,1)S(1)}, bf16[768,384]{1,0:T(8,128)(2,1)S(1)}, u32[]{:S(2)}, u32[]{:S(2)}) collective-permute-start(bf16[768,384]{1,0:T(8,128)(2,1)S(1)} %collective-permute-done.4.refs_10_.refs_7_.refs_9_.refs_2_), channel_id=1, source_target_pairs={{0,1},{1,0},{2,3},{3,2},{4,5},{5,4},{6,7},{7,6},{8,9},{9,8},{10,11... | collective-permute-start | bytes 1769480 | tf_op jit(solution)/shard_map/ppermute | solution.py:35
  74.5 8.2 %copy-start.7 = (bf16[768,384]{1,0:T(8,128)(2,1)}, bf16[768,384]{1,0:T(8,128)(2,1)S(1)}, u32[]{:S(2)}) copy-start(bf16[768,384]{1,0:T(8,128)(2,1)S(1)} %collective-permute-done.9.refs_11_.refs_8_.refs_10_.refs_3_) | copy-start | bytes 1769476
  74.5 2.0 %collective-permute-start.17 = (bf16[768,384]{1,0:T(8,128)(2,1)S(1)}, bf16[768,384]{1,0:T(8,128)(2,1)S(1)}, u32[]{:S(2)}, u32[]{:S(2)}) collective-permute-start(bf16[768,384]{1,0:T(8,128)(2,1)S(1)} %collective-permute-done.9.refs_11_.refs_8_.refs_10_.refs_3_), channel_id=1, source_target_pairs={{0,1},{1,0},{2,3},{3,2},{4,5},{5,4},{6,7},{7,6},{8,9},{9,8},{10,11... | collective-permute-start | bytes 1769480 | tf_op jit(solution)/shard_map/ppermute | solution.py:35
  74.6 8.2 %copy-start.8 = (bf16[768,384]{1,0:T(8,128)(2,1)}, bf16[768,384]{1,0:T(8,128)(2,1)S(1)}, u32[]{:S(2)}) copy-start(bf16[768,384]{1,0:T(8,128)(2,1)S(1)} %collective-permute-done.14.refs_12_.refs_9_.refs_11_.refs_4_) | copy-start | bytes 1769476
  74.6 8.2 %copy-start.9 = (bf16[768,384]{1,0:T(8,128)(2,1)}, bf16[768,384]{1,0:T(8,128)(2,1)S(1)}, u32[]{:S(2)}) copy-start(bf16[768,384]{1,0:T(8,128)(2,1)S(1)} %collective-permute-done.15.refs_13_.refs_10_.refs_12_.refs_5_) | copy-start | bytes 1769476
  74.6 8.2 %copy-start.10 = (bf16[768,384]{1,0:T(8,128)(2,1)}, bf16[768,384]{1,0:T(8,128)(2,1)S(1)}, u32[]{:S(2)}) copy-start(bf16[768,384]{1,0:T(8,128)(2,1)S(1)} %collective-permute-done.16.refs_14_.refs_11_.refs_13_.refs_6_) | copy-start | bytes 1769476
  76.6 6.2 %copy-start.11 = (bf16[768,384]{1,0:T(8,128)(2,1)}, bf16[768,384]{1,0:T(8,128)(2,1)S(1)}, u32[]{:S(2)}) copy-start(bf16[768,384]{1,0:T(8,128)(2,1)S(1)} %collective-permute-done.17.refs_15_.refs_12_.refs_14_.refs_7_) | copy-start | bytes 1769476
  80.3 5.0 %collective-permute-start.18 = (bf16[512,768]{1,0:T(8,128)(2,1)S(1)}, bf16[512,768]{1,0:T(8,128)(2,1)S(1)}, u32[]{:S(2)}, u32[]{:S(2)}) collective-permute-start(bf16[512,768]{1,0:T(8,128)(2,1)S(1)} %get-tuple-element.63), channel_id=1, source_target_pairs={{0,1},{1,0},{2,3},{3,2},{4,5},{5,4},{6,7},{7,6},{8,9},{9,8},{10,11... | collective-permute-start | bytes 2359304 | tf_op jit(solution)/shard_map/ppermute | solution.py:35
  93.3 3.9 %collective-permute-start.19 = (bf16[512,768]{1,0:T(8,128)(2,1)}, bf16[512,768]{1,0:T(8,128)(2,1)S(1)}, u32[]{:S(2)}, u32[]{:S(2)}) collective-permute-start(bf16[512,768]{1,0:T(8,128)(2,1)} %get-tuple-element.68), channel_id=1, source_target_pairs={{0,1},{1,0},{2,3},{3,2},{4,5},{5,4},{6,7},{7,6},{8,9},{9,8},{10,11... | collective-permute-start | bytes 2359304 | tf_op jit(solution)/shard_map/ppermute | solution.py:35
  97.5 12.5 %collective-permute-start.24 = (bf16[256,768]{1,0:T(8,128)(2,1)S(1)}, bf16[256,768]{1,0:T(8,128)(2,1)S(1)}, u32[]{:S(2)}, u32[]{:S(2)}) collective-permute-start(bf16[256,768]{1,0:T(8,128)(2,1)S(1)} %get-tuple-element.83), channel_id=1, source_target_pairs={{0,8},{1,9},{2,10},{3,11},{4,12},{5,13},{6,14},{7,15},{8,16},{9,17... | collective-permute-start | bytes 1179656 | tf_op jit(solution)/shard_map/ppermute | solution.py:35
  98.5 26.0 %collective-permute-start.20 = (bf16[528,384]{1,0:T(8,128)(2,1)S(1)}, bf16[528,384]{1,0:T(8,128)(2,1)S(1)}, u32[]{:S(2)}, u32[]{:S(2)}) collective-permute-start(bf16[528,384]{1,0:T(8,128)(2,1)S(1)} %get-tuple-element.76), channel_id=1, source_target_pairs={{0,0},{1,4},{2,2},{3,6},{4,1},{5,5},{6,3},{7,7},{8,8},{9,12},{10,1... | collective-permute-start | bytes 1216520 | tf_op jit(solution)/shard_map/ppermute | solution.py:35
  101.6 22.9 %collective-permute-start.21 = (bf16[528,384]{1,0:T(8,128)(2,1)S(1)}, bf16[528,384]{1,0:T(8,128)(2,1)S(1)}, u32[]{:S(2)}, u32[]{:S(2)}) collective-permute-start(bf16[528,384]{1,0:T(8,128)(2,1)S(1)} %get-tuple-element.77), channel_id=1, source_target_pairs={{0,1},{1,5},{2,3},{3,7},{4,0},{5,4},{6,2},{7,6},{8,9},{9,13},{10,1... | collective-permute-start | bytes 1216520 | tf_op jit(solution)/shard_map/ppermute | solution.py:35
  101.6 24.8 %collective-permute-start.22 = (bf16[528,384]{1,0:T(8,128)(2,1)S(1)}, bf16[528,384]{1,0:T(8,128)(2,1)S(1)}, u32[]{:S(2)}, u32[]{:S(2)}) collective-permute-start(bf16[528,384]{1,0:T(8,128)(2,1)S(1)} %get-tuple-element.78), channel_id=1, source_target_pairs={{0,2},{1,6},{2,0},{3,4},{4,3},{5,7},{6,1},{7,5},{8,10},{9,14},{10,... | collective-permute-start | bytes 1216520 | tf_op jit(solution)/shard_map/ppermute | solution.py:35
  103.4 15.5 %collective-permute-start.25 = (bf16[256,768]{1,0:T(8,128)(2,1)S(1)}, bf16[256,768]{1,0:T(8,128)(2,1)S(1)}, u32[]{:S(2)}, u32[]{:S(2)}) collective-permute-start(bf16[256,768]{1,0:T(8,128)(2,1)S(1)} %get-tuple-element.84), channel_id=1, source_target_pairs={{0,24},{1,25},{2,26},{3,27},{4,28},{5,29},{6,30},{7,31},{8,0},{9,1... | collective-permute-start | bytes 1179656 | tf_op jit(solution)/shard_map/ppermute | solution.py:35
  109.9 16.8 %collective-permute-start.23 = (bf16[528,384]{1,0:T(8,128)(2,1)S(1)}, bf16[528,384]{1,0:T(8,128)(2,1)S(1)}, u32[]{:S(2)}, u32[]{:S(2)}) collective-permute-start(bf16[528,384]{1,0:T(8,128)(2,1)S(1)} %get-tuple-element.79), channel_id=1, source_target_pairs={{0,3},{1,7},{2,1},{3,5},{4,2},{5,6},{6,0},{7,4},{8,11},{9,15},{10,... | collective-permute-start | bytes 1216520 | tf_op jit(solution)/shard_map/ppermute | solution.py:35
  121.7 7.5 %collective-permute-start.26 = (bf16[256,384]{1,0:T(8,128)(2,1)S(1)}, bf16[256,384]{1,0:T(8,128)(2,1)S(1)}, u32[]{:S(2)}, u32[]{:S(2)}) collective-permute-start(bf16[256,384]{1,0:T(8,128)(2,1)S(1)} %get-tuple-element.85), channel_id=1, source_target_pairs={{0,0},{1,4},{2,2},{3,6},{4,1},{5,5},{6,3},{7,7},{8,8},{9,12},{10,1... | collective-permute-start | bytes 589832 | tf_op jit(solution)/shard_map/ppermute | solution.py:35
  124.5 7.2 %collective-permute-start.27 = (bf16[256,384]{1,0:T(8,128)(2,1)S(1)}, bf16[256,384]{1,0:T(8,128)(2,1)S(1)}, u32[]{:S(2)}, u32[]{:S(2)}) collective-permute-start(bf16[256,384]{1,0:T(8,128)(2,1)S(1)} %get-tuple-element.86), channel_id=1, source_target_pairs={{0,1},{1,5},{2,3},{3,7},{4,0},{5,4},{6,2},{7,6},{8,9},{9,13},{10,1... | collective-permute-start | bytes 589832 | tf_op jit(solution)/shard_map/ppermute | solution.py:35
  124.5 8.1 %collective-permute-start.28 = (bf16[256,384]{1,0:T(8,128)(2,1)S(1)}, bf16[256,384]{1,0:T(8,128)(2,1)S(1)}, u32[]{:S(2)}, u32[]{:S(2)}) collective-permute-start(bf16[256,384]{1,0:T(8,128)(2,1)S(1)} %get-tuple-element.87), channel_id=1, source_target_pairs={{0,2},{1,6},{2,0},{3,4},{4,3},{5,7},{6,1},{7,5},{8,10},{9,14},{10,... | collective-permute-start | bytes 589832 | tf_op jit(solution)/shard_map/ppermute | solution.py:35
  126.4 9.9 %collective-permute-start.29 = (bf16[256,384]{1,0:T(8,128)(2,1)S(1)}, bf16[256,384]{1,0:T(8,128)(2,1)S(1)}, u32[]{:S(2)}, u32[]{:S(2)}) collective-permute-start(bf16[256,384]{1,0:T(8,128)(2,1)S(1)} %get-tuple-element.88), channel_id=1, source_target_pairs={{0,3},{1,7},{2,1},{3,5},{4,2},{5,6},{6,0},{7,4},{8,11},{9,15},{10,... | collective-permute-start | bytes 589832 | tf_op jit(solution)/shard_map/ppermute | solution.py:35

commit v6 on v5

--- a/solution.py
+++ b/solution.py
@@ -58,6 +58,10 @@
 def place():
     d, m = lax.axis_index("seq"), lax.axis_index("mp")
     return d // 2, d % 2, m // 2, m % 2
+
+
+def in_hbm(value):
+    return pltpu.with_memory_space_constraint(value, pltpu.HBM)
 
 
 def tie(*values):
@@ -107,11 +111,23 @@
     return pairs
 
 
+def block(refs, k, start, rows):
+    if len(refs) == 4:
+        return refs[k].at[pl.ds(start, rows)]
+    ref = refs[k // 2]
+    return ref.at[pl.ds((k % 2) * (ref.shape[0] // 2) + start, rows)]
+
+
+def whole_kernel(*refs):
+    pieces, (whole, sems) = refs[:-2], refs[-2:]
+    run_copies(weight_copies(pieces, whole, 0), sems)
+
+
 def norm_kernel(token_count, *refs):
-    token_refs, normed, inv_out, rows_in, sems = refs[:4], *refs[4:]
-    width = token_refs[0].shape[1]
+    tokens, (normed, inv_out, rows_in, sems) = refs[:4], refs[4:]
+    width = tokens[0].shape[1]
     run_copies(
-        [(ref.at[pl.ds(0, token_count + EXTRA)], rows_in.at[k]) for k, ref in enumerate(token_refs)],
+        [(block(tokens, k, 0, token_count + EXTRA), rows_in.at[k]) for k in range(4)],
         sems,
     )
     total = None
@@ -128,16 +144,15 @@
 
 
 def table_kernel(token_count, *refs):
-    token_refs, outer_refs = refs[:4], refs[4:8]
-    pieces, (tables, shared, whole, encs, sems) = refs[8:-5], refs[-5:]
-    width = token_refs[0].shape[1]
+    tokens, outers = refs[:4], refs[4:6]
+    pieces, (tables, shared, whole, encs, sems) = refs[6:-5], refs[-5:]
+    width = tokens[0].shape[1]
     pairs = weight_copies(pieces, whole, 0)
-    for k in range(4):
-        block = pl.ds(k * width, width)
-        for i, (ref, start) in enumerate(
-            ((outer_refs[k], 0), (token_refs[k], 2 * token_count + EXTRA), (outer_refs[k], OWN_ROWS))
-        ):
-            pairs.append((ref.at[pl.ds(start, OWN_ROWS)], encs.at[pl.ds(i * OWN_ROWS, OWN_ROWS), block]))
+    sources = ((outers, 0), (tokens, 2 * token_count + EXTRA), (outers, OWN_ROWS))
+    for i, (pair, start) in enumerate(sources):
+        for k in range(4):
+            target = encs.at[pl.ds(i * OWN_ROWS, OWN_ROWS), pl.ds(k * width, width)]
+            pairs.append((block(pair, k, start, OWN_ROWS), target))
     run_copies(pairs, sems)
     tables[...] = jnp.dot(encs[...], whole[...], preferred_element_type=F32).astype(LOW)
     shared[0:OWN_ROWS, :] = tables[OWN_ROWS : 2 * OWN_ROWS, :]
@@ -147,14 +162,13 @@
 
 
 def query_kernel(token_count, *refs):
-    normed, token_refs = refs[0], refs[1:5]
+    normed, tokens = refs[0], refs[1:5]
     pieces, (queries, d_attended, whole, rows_in, grads, sems) = refs[5:-6], refs[-6:]
-    width = token_refs[0].shape[1]
+    width = tokens[0].shape[1]
     pairs = weight_copies(pieces, whole, 2) + [(normed, rows_in)]
-    for k, ref in enumerate(token_refs):
-        pairs.append(
-            (ref.at[pl.ds(token_count + EXTRA, token_count)], grads.at[:, pl.ds(k * width, width)])
-        )
+    for k in range(4):
+        source = block(tokens, k, token_count + EXTRA, token_count)
+        pairs.append((source, grads.at[:, pl.ds(k * width, width)]))
     run_copies(pairs, sems)
     queries[...] = jnp.dot(rows_in[...], whole[:, 0:width], preferred_element_type=F32).astype(LOW)
     d_attended[...] = jnp.dot(grads[...], whole[:, width:], preferred_element_type=F32).astype(LOW)
@@ -218,23 +232,24 @@
 
 
 def product_kernel(*refs):
-    attended, d_queries, inv_rms = refs[:3]
-    token_refs, pieces, outs, (whole, rows_in, sems) = refs[3:7], refs[7:-7], refs[-7:-3], refs[-3:]
+    attended, d_queries, inv_rms, tokens = refs[0], refs[1], refs[2], refs[3:7]
+    pieces, outs, (whole, rows_in, sems) = refs[7:-7], refs[-7:-3], refs[-3:]
     token_count, width = attended.shape
+    term_rows = 2 * token_count + EXTRA
     pairs = weight_copies(pieces, whole, 2)
-    for k, ref in enumerate(token_refs):
-        pairs.append((ref.at[pl.ds(0, token_count + EXTRA)], rows_in.at[k]))
+    for k in range(4):
+        pairs.append((block(tokens, k, 0, token_count + EXTRA), rows_in.at[k]))
     run_copies(pairs, sems)
     total = None
-    for k, out in enumerate(outs):
-        block = slice(k * width, (k + 1) * width)
-        out[0:token_count, :] = lax.dot_general(
-            attended[...], whole[block, width:], ACROSS, preferred_element_type=F32
+    for k in range(4):
+        columns = slice(k * width, (k + 1) * width)
+        outs[k][0:token_count, :] = lax.dot_general(
+            attended[...], whole[columns, width:], ACROSS, preferred_element_type=F32
         ).astype(LOW)
         back = lax.dot_general(
-            d_queries[...], whole[block, 0:width], ACROSS, preferred_element_type=F32
+            d_queries[...], whole[columns, 0:width], ACROSS, preferred_element_type=F32
         ).astype(LOW)
-        out[token_count : 2 * token_count, :] = back
+        outs[k][token_count : 2 * token_count, :] = back
         rows = rows_in[k, 0:token_count, :].astype(F32)
         gain = rows_in[k, token_count : token_count + 1, :].astype(F32)
         part = jnp.sum(rows * gain * back.astype(F32), axis=1, keepdims=True)
@@ -248,7 +263,7 @@
     extra = jnp.concatenate(lines, axis=0)
     extra = jnp.concatenate([extra, jnp.zeros((EXTRA, width - token_count), F32)], axis=1).astype(LOW)
     for out in outs:
-        out[2 * token_count : 2 * token_count + EXTRA, :] = extra
+        out[term_rows - EXTRA : term_rows, :] = extra
 
 
 def finish_kernel(hidden, gain, *refs):
@@ -274,14 +289,12 @@
     inv_rms = as_column(inv_row)
     rows = hidden[...].astype(F32)
     grad_rows[...] = (
-        inv_rms * gain[...].astype(F32) * normed_grad - rows * inv_rms * inv_rms * inv_rms * statistic
+        inv_rms * gain[...].astype(F32)[None, :] * normed_grad - rows * inv_rms * inv_rms * inv_rms * statistic
     ).astype(LOW)
 
 
-def encoding_kernel(own, from_core, up, down, *refs):
-    pieces, outs, (whole, sems) = refs[:-6], refs[-6:-2], refs[-2:]
+def encoding_kernel(own, from_core, up, down, whole, *outs):
     width = whole.shape[1] // 2
-    run_copies(weight_copies(pieces, whole, 0), sems)
     own_low = own[...] + from_core[0:OWN_ROWS, :].astype(F32)
     own_low = (own_low + up[...].astype(F32) + down[...].astype(F32)).astype(LOW)
     for k, out in enumerate(outs):
@@ -290,7 +303,7 @@
         ).astype(LOW)
 
 
-def call(kernel, operands, specs, outs, scratch=(), copies=0):
+def call(kernel, operands, specs, outs, scratch=(), copies=0, out_specs=None):
     scratch = list(scratch)
     if copies:
         scratch.append(pltpu.SemaphoreType.DMA((copies,)))
@@ -298,7 +311,7 @@
         kernel,
         out_shape=[jax.ShapeDtypeStruct(shape, dtype) for shape, dtype in outs],
         in_specs=specs,
-        out_specs=[VMEM] * len(outs),
+        out_specs=out_specs or [VMEM] * len(outs),
         scratch_shapes=scratch,
         compiler_params=pltpu.CompilerParams(vmem_limit_bytes=16 * 1024 * 1024),
     )(*operands)
@@ -316,26 +329,18 @@
     own_enc = encodings.reshape(OWN_ROWS, width)
     weights = move(jnp.concatenate([w_key, w_value, w_query, w_out.T], axis=0), spread(0))
     enc_below, enc_above = move(own_enc, ring_up), move(own_enc, ring_down)
-    extra = jnp.pad(norm_gain[None, :], ((0, EXTRA - 1), (0, 0)))
-    extra = extra + jnp.pad(neighbours.reshape(1, ids).astype(LOW), ((1, EXTRA - 2), (0, width - ids)))
+    id_row = jnp.pad(neighbours.reshape(1, ids).astype(LOW), ((1, EXTRA - 2), (0, width - ids)))
+    extra = jnp.pad(norm_gain[None, :], ((0, EXTRA - 1), (0, 0))) + id_row
     packed = jnp.concatenate([hidden_rows, extra, grad_out, own_enc], axis=0)
     weights, enc_below, enc_above, packed = tie(weights, enc_below, enc_above, packed)
     tokens = [move(packed, spread(k)) for k in range(4)]
-    outer = jnp.concatenate([enc_below, enc_above], axis=0)
+    outer = jnp.concatenate(
+        [enc_below, enc_above, move(enc_below, flip_core), move(enc_above, flip_core)], axis=0
+    )
     if seq_count == 8:
         below, above = move(weights, ring_up), move(weights, ring_down)
-        outer, below, above, *tokens = tie(outer, below, above, *tokens)
-        two = move(jnp.where(z % 2 == 0, below, above), lambda z, y, x, c: (z ^ 1, y, x, c))
-        outers = [move(outer, spread(k)) for k in range(4)]
-        two, *outers = tie(two, *outers)
-        pieces = [weights, below, above, two]
-        kv_pieces = qo_pieces = pieces + [move(piece, flip_core) for piece in pieces]
-    else:
-        kv_pieces, qo_pieces = any_weights(weights, c, g)
-        outers = [move(outer, spread(k)) for k in range(4)]
-    piece_count = len(kv_pieces)
-
-    chosen = tokens[0][token_count + 1, :ids].astype(jnp.int32)
+        below, above, *tokens = tie(below, above, *tokens)
+    outers = [move(outer, spread(0)), move(outer, spread(2))]
     normed, inv_rms = call(
         lambda *refs: norm_kernel(token_count, *refs),
         tokens,
@@ -344,10 +349,21 @@
         [pltpu.VMEM((4, token_count + EXTRA, width), LOW)],
         4,
     )
+    if seq_count == 8:
+        two = move(jnp.where(z % 2 == 0, below, above), lambda z, y, x, c: (z ^ 1, y, x, c))
+        pieces = [weights, below, above, two]
+        others = [move(piece, flip_core) for piece in pieces[:3]]
+        two, normed, *outers = tie(two, normed, *outers)
+        kv_pieces = qo_pieces = pieces[:3] + [two] + others + [move(two, flip_core)]
+    else:
+        kv_pieces, qo_pieces = any_weights(weights, c, g)
+    piece_count = len(kv_pieces)
+
+    chosen = tokens[0][token_count + 1, :ids].astype(jnp.int32)
     tables, shared = call(
         lambda *refs: table_kernel(token_count, *refs),
         tokens + outers + kv_pieces,
-        [ANY] * (8 + piece_count),
+        [ANY] * (6 + piece_count),
         [((3 * OWN_ROWS, wide), LOW), ((2 * OWN_ROWS, wide), LOW)],
         [pltpu.VMEM((full_width, wide), LOW), pltpu.VMEM((3 * OWN_ROWS, full_width), LOW)],
         12 + 2 * piece_count,
@@ -381,7 +397,7 @@
     to_above = (d_outer[OWN_ROWS:] + jnp.where(c == 0, shared_grad, 0.0)).astype(LOW)
     terms = call(
         product_kernel,
-        [attended, d_queries, inv_rms] + [pltpu.with_memory_space_constraint(o, pltpu.HBM) for o in tokens + qo_pieces],
+        [attended, d_queries, inv_rms] + [in_hbm(o) for o in tokens + qo_pieces],
         [VMEM, VMEM, VMEM] + [ANY] * (4 + piece_count),
         [((2 * token_count + EXTRA, width), LOW)] * 4,
         [
@@ -395,19 +411,25 @@
     terms = [move(term, gather_back(k)) for k, term in enumerate(terms)]
     branch_out, grad_rows = call(
         finish_kernel,
-        [hidden_rows, norm_gain[None, :]] + terms,
+        [hidden_rows, norm_gain] + terms,
         [VMEM] * 6,
         [((token_count, width), LOW), ((token_count, width), LOW)],
     )
+    (whole,) = call(
+        whole_kernel,
+        [in_hbm(piece) for piece in kv_pieces],
+        [ANY] * piece_count,
+        [((full_width, wide), LOW)],
+        copies=2 * piece_count,
+    )
     enc_terms = call(
         encoding_kernel,
-        [d_own, from_core, up, down] + [pltpu.with_memory_space_constraint(o, pltpu.HBM) for o in kv_pieces],
-        [VMEM] * 4 + [ANY] * piece_count,
+        [d_own, from_core, up, down, whole],
+        [VMEM] * 5,
         [((OWN_ROWS, width), LOW)] * 4,
-        [pltpu.VMEM((full_width, wide), LOW)],
-        2 * piece_count,
-    )
-    enc_terms = [move(term, gather_back(k)).astype(F32) for k, term in enumerate(enc_terms)]
+    )
+    enc_terms = [move(term, gather_back(k)) for k, term in enumerate(enc_terms)]
+    enc_terms = [term.astype(F32) for term in enc_terms]
     grad_encodings = (enc_terms[0] + enc_terms[1] + enc_terms[2] + enc_terms[3]).astype(LOW)
     return (branch_out, grad_rows, grad_encodings.reshape(encodings.shape))
 

time: 138 us -> 128 us (0.928)
  waiting for transfers between devices: 71.9 us -> 57.7 us
  local copies, waits for them, and re-layouts: 0.27 us -> 3.24 us
  starting transfers between devices: 35.5 us -> 37.8 us
    ppermute x30, waiting for transfers between devices: 71.9 us -> 57.7 us  [move(): return lax.ppermute(value, ('seq', 'mp'), pairs)]
    unnamed x34 -> x39, local copies, waits for them, and re-layouts: 0.07 us -> 2.32 us
    ppermute x30, starting transfers between devices: 35.5 us -> 37.8 us  [move(): return lax.ppermute(value, ('seq', 'mp'), pairs)]
    pallas_call x7 -> x8, Pallas kernels: 23.9 us -> 23.8 us  [call(): pl.pallas_call(kernel, out_shape=[jax.ShapeDtypeStruct(shape, dtype) for...]
  transfers between devices with their start and end apart: 30 -> 30, of which waited for: 15 -> 12; matrix products, arithmetic and copies ran while one was open for 2% -> 4% of each run, Pallas kernels for 9% -> 10%
where the time goes in v6:
time: 128 us
  waiting for transfers between devices  57.7 us (45%)
  starting transfers between devices  37.8 us (30%)
  Pallas kernels  23.8 us (19%)
  other arithmetic  3.94 us (3%)
  local copies, waits for them, and re-layouts  3.24 us (3%)
    ppermute x30, waiting for transfers between devices, move(): return lax.ppermute(value, ('seq', 'mp'), pairs)  57.7 us
    ppermute x30, starting transfers between devices, move(): return lax.ppermute(value, ('seq', 'mp'), pairs)  37.8 us
    pallas_call x8, Pallas kernels, call(): pl.pallas_call(kernel, out_shape=[jax.ShapeDtypeStruct(shape, dtype) for...  23.8 us
  transfers between devices with their start and end apart: 30, of which 12 were waited for; matrix products, arithmetic and copies ran while one was open for 4% of the time, Pallas kernels for 10%

profile of v6, /device:TPU:1, one launch (start us, length us, event | category | flops | bytes accessed | tf_op | source)
XLA Modules:
  0.0 127.6 jit_solution(7886100498647186901)
XLA Ops:
  0.7 1.2 pad_maximum_fusion.1
  1.9 4.5 %collective-permute-start = (bf16[768,384]{1,0:T(8,128)(2,1)S(1)}, bf16[768,384]{1,0:T(8,128)(2,1)S(1)}, u32[]{:S(2)}, u32[]{:S(2)}) collective-permute-start(bf16[768,384]{1,0:T(8,128)(2,1)S(1)} %pad_maximum_fusion.1), channel_id=1, source_target_pairs={{0,0},{1,4},{2,2},{3,6},{4,1},{5,5},{6,3},{7,7},{8,8},{9,12},{10,1... | collective-permute-start | bytes 1769480 | tf_op jit(solution)/shard_map/ppermute | solution.py:35
  6.5 1.3 %collective-permute-start.1 = (bf16[256,384]{1,0:T(8,128)(2,1)}, bf16[256,384]{1,0:T(8,128)(2,1)S(1)}, u32[]{:S(2)}, u32[]{:S(2)}) collective-permute-start(bf16[256,384]{1,0:T(8,128)(2,1)} %bitcast.6), channel_id=1, source_target_pairs={{0,8},{1,9},{2,10},{3,11},{4,12},{5,13},{6,14},{7,15},{8,16},{9,17... | collective-permute-start | bytes 589832 | tf_op jit(solution)/shard_map/ppermute | solution.py:35
  7.8 2.1 %collective-permute-start.2 = (bf16[256,384]{1,0:T(8,128)(2,1)}, bf16[256,384]{1,0:T(8,128)(2,1)}, u32[]{:S(2)}, u32[]{:S(2)}) collective-permute-start(bf16[256,384]{1,0:T(8,128)(2,1)} %bitcast.7), channel_id=1, source_target_pairs={{0,24},{1,25},{2,26},{3,27},{4,28},{5,29},{6,30},{7,31},{8,0},{9,1... | collective-permute-start | bytes 589832 | tf_op jit(solution)/shard_map/ppermute | solution.py:35
  9.9 0.7 convert_element_type.53
  10.8 0.7 broadcast_in_dim.8
  11.5 0.9 pad_maximum_fusion
  12.4 2.8 %collective-permute-done.1 = bf16[256,384]{1,0:T(8,128)(2,1)S(1)} collective-permute-done((bf16[256,384]{1,0:T(8,128)(2,1)}, bf16[256,384]{1,0:T(8,128)(2,1)S(1)}, u32[]{:S(2)}, u32[]{:S(2)}) %collective-permute-start.1) | collective-permute-done | bytes 196640 | tf_op jit(solution)/shard_map/ppermute | solution.py:35
  15.3 2.2 %collective-permute-done.2 = bf16[256,384]{1,0:T(8,128)(2,1)} collective-permute-done((bf16[256,384]{1,0:T(8,128)(2,1)}, bf16[256,384]{1,0:T(8,128)(2,1)}, u32[]{:S(2)}, u32[]{:S(2)}) %collective-permute-start.2) | collective-permute-done | bytes 196640 | tf_op jit(solution)/shard_map/ppermute | solution.py:35
  17.5 0.3 collective-permute-start.3
  17.7 0.7 collective-permute-start.10
  18.4 2.9 %collective-permute-start.5 = (bf16[784,384]{1,0:T(8,128)(2,1)}, bf16[784,384]{1,0:T(8,128)(2,1)S(1)}, u32[]{:S(2)}, u32[]{:S(2)}) collective-permute-start(bf16[784,384]{1,0:T(8,128)(2,1)} %pad_maximum_fusion), channel_id=1, source_target_pairs={{0,0},{1,4},{2,2},{3,6},{4,1},{5,5},{6,3},{7,7},{8,8},{9,12},{10,1... | collective-permute-start | bytes 1806344 | tf_op jit(solution)/shard_map/ppermute | solution.py:35
  21.4 2.1 %collective-permute-start.7 = (bf16[784,384]{1,0:T(8,128)(2,1)}, bf16[784,384]{1,0:T(8,128)(2,1)S(1)}, u32[]{:S(2)}, u32[]{:S(2)}) collective-permute-start(bf16[784,384]{1,0:T(8,128)(2,1)} %pad_maximum_fusion), channel_id=1, source_target_pairs={{0,2},{1,6},{2,0},{3,4},{4,3},{5,7},{6,1},{7,5},{8,10},{9,14},{10,... | collective-permute-start | bytes 1806344 | tf_op jit(solution)/shard_map/ppermute | solution.py:35
  23.4 0.7 collective-permute-start.8
  24.1 9.7 %collective-permute-done.3.refs_7_.refs_6_.refs_8_.refs_1_ = bf16[768,384]{1,0:T(8,128)(2,1)S(1)} collective-permute-done((bf16[768,384]{1,0:T(8,128)(2,1)S(1)}, bf16[768,384]{1,0:T(8,128)(2,1)S(1)}, u32[]{:S(2)}, u32[]{:S(2)}) %collective-permute-start.3) | collective-permute-done | bytes 589856 | tf_op jit(solution)/shard_map/ppermute | solution.py:35
  33.9 1.2 constant_dynamic-update-slice_fusion.2
  35.1 1.0 constant_dynamic-update-slice_fusion.1
  36.2 11.5 %collective-permute-done.4.refs_8_.refs_7_.refs_9_.refs_2_ = bf16[768,384]{1,0:T(8,128)(2,1)S(1)} collective-permute-done((bf16[768,384]{1,0:T(8,128)(2,1)}, bf16[768,384]{1,0:T(8,128)(2,1)S(1)}, u32[]{:S(2)}, u32[]{:S(2)}) %collective-permute-start.4) | collective-permute-done | bytes 589856 | tf_op jit(solution)/shard_map/ppermute | solution.py:35
  47.7 2.2 %collective-permute-start.12 = (bf16[1024,384]{1,0:T(8,128)(2,1)S(1)}, bf16[1024,384]{1,0:T(8,128)(2,1)S(1)}, u32[]{:S(2)}, u32[]{:S(2)}) collective-permute-start(bf16[1024,384]{1,0:T(8,128)(2,1)S(1)} %constant_dynamic-update-slice_fusion), channel_id=1, source_target_pairs={{0,0},{1,4},{2,2},{3,6},{4,1},{5,5},{6,3},{7,7},{8,8},{9,12},{10,1... | collective-permute-start | bytes 2359304 | tf_op jit(solution)/shard_map/ppermute | solution.py:35
  49.9 2.6 %collective-permute-start.13 = (bf16[1024,384]{1,0:T(8,128)(2,1)S(1)}, bf16[1024,384]{1,0:T(8,128)(2,1)S(1)}, u32[]{:S(2)}, u32[]{:S(2)}) collective-permute-start(bf16[1024,384]{1,0:T(8,128)(2,1)S(1)} %constant_dynamic-update-slice_fusion), channel_id=1, source_target_pairs={{0,2},{1,6},{2,0},{3,4},{4,3},{5,7},{6,1},{7,5},{8,10},{9,14},{10,... | collective-permute-start | bytes 2359304 | tf_op jit(solution)/shard_map/ppermute | solution.py:35
  52.8 0.5 collective-permute-start.15
  53.3 2.1 %shard_map.112 = (bf16[256,1536]{1,0:T(8,128)(2,1)S(1)}, f32[256,1]{1,0:T(8,128)S(1)}) custom-call(bf16[784,384]{1,0:T(8,128)(2,1)S(1)} %collective-permute-done.5.refs_0_.refs_1_.refs_3_, bf16[784,384]{1,0:T(8,128)(2,1)S(1)} %collective-permute-done.6.refs_1_.refs_2_.refs_4_, bf16[784,384]{1,0:T(8,128)(2,1)S(1)} %collective-permute-done.7.refs_2_.refs_3_.refs_5_, ...), custom_call_target="tpu_custom_call" | custom-call | tf_op jit(solution)/shard_map/pallas_call | solution.py:310
  55.5 14.2 %collective-permute-done.12.refs_4_ = bf16[1024,384]{1,0:T(8,128)(2,1)S(1)} collective-permute-done((bf16[1024,384]{1,0:T(8,128)(2,1)S(1)}, bf16[1024,384]{1,0:T(8,128)(2,1)S(1)}, u32[]{:S(2)}, u32[]{:S(2)}) %collective-permute-start.12) | collective-permute-done | bytes 786464 | tf_op jit(solution)/shard_map/ppermute | solution.py:35
  69.7 1.1 collective-permute-start.17
  70.8 0.9 collective-permute-done.16.refs_12_.refs_11_.refs_13_.refs_6_
  71.7 0.8 collective-permute-done.17.refs_13_.refs_12_.refs_14_.refs_7_
  72.6 3.7 %shard_map.113 = (bf16[768,768]{1,0:T(8,128)(2,1)S(1)}, bf16[512,768]{1,0:T(8,128)(2,1)S(1)}) custom-call(bf16[784,384]{1,0:T(8,128)(2,1)S(1)} %collective-permute-done.5.refs_0_.refs_1_.refs_3_, bf16[784,384]{1,0:T(8,128)(2,1)S(1)} %collective-permute-done.6.refs_1_.refs_2_.refs_4_, bf16[784,384]{1,0:T(8,128)(2,1)S(1)} %collective-permute-done.7.refs_2_.refs_3_.refs_5_, ...), custom_call_target="tpu_custom_call" | custom-call | tf_op jit(solution)/shard_map/pallas_call | solution.py:310
  76.2 0.3 collective-permute-start.18
  76.7 2.5 %shard_map.114 = (bf16[256,384]{1,0:T(8,128)(2,1)S(1)}, bf16[256,384]{1,0:T(8,128)(2,1)S(1)}) custom-call(bf16[256,1536]{1,0:T(8,128)(2,1)S(1)} %get-tuple-element.60.refs_0_, bf16[784,384]{1,0:T(8,128)(2,1)S(1)} %collective-permute-done.5.refs_0_.refs_1_.refs_3_, bf16[784,384]{1,0:T(8,128)(2,1)S(1)} %collective-permute-done.6.refs_1_.refs_2_.refs_4_, ...), custom_call_target="tpu_custom_call" | custom-call | tf_op jit(solution)/shard_map/pallas_call | solution.py:310
  79.2 8.0 %shard_map.115 = (bf16[256,384]{1,0:T(8,128)(2,1)S(1)}, bf16[256,384]{1,0:T(8,128)(2,1)S(1)}, f32[256,768]{1,0:T(8,128)S(1)}, bf16[512,768]{1,0:T(8,128)(2,1)S(1)}, bf16[512,768]{1,0:T(8,128)(2,1)}) custom-call(s32[8]{0:T(128)S(1)} %bitcast_convert_fusion.refs_0_, bf16[768,768]{1,0:T(8,128)(2,1)S(1)} %get-tuple-element.58.refs_1_, ...), custom_call_target="tpu_custom_call" | custom-call | tf_op jit(solution)/shard_map/pallas_call | solution.py:310
  87.2 0.3 collective-permute-start.19
  87.5 3.5 %shard_map.116 = (bf16[528,384]{1,0:T(8,128)(2,1)S(1)}, bf16[528,384]{1,0:T(8,128)(2,1)S(1)}, bf16[528,384]{1,0:T(8,128)(2,1)S(1)}, bf16[528,384]{1,0:T(8,128)(2,1)S(1)}) custom-call(bf16[256,384]{1,0:T(8,128)(2,1)S(1)} %get-tuple-element.65.refs_0_, bf16[256,384]{1,0:T(8,128)(2,1)S(1)} %get-tuple-element.66.refs_1_, ...), custom_call_target="tpu_custom_call" | custom-call | tf_op jit(solution)/shard_map/pallas_call | solution.py:310
  91.4 3.4 %collective-permute-start.20 = (bf16[528,384]{1,0:T(8,128)(2,1)S(1)}, bf16[528,384]{1,0:T(8,128)(2,1)S(1)}, u32[]{:S(2)}, u32[]{:S(2)}) collective-permute-start(bf16[528,384]{1,0:T(8,128)(2,1)S(1)} %get-tuple-element.72), channel_id=1, source_target_pairs={{0,0},{1,4},{2,2},{3,6},{4,1},{5,5},{6,3},{7,7},{8,8},{9,12},{10,1... | collective-permute-start | bytes 1216520 | tf_op jit(solution)/shard_map/ppermute | solution.py:35
  94.8 1.4 %collective-permute-start.22 = (bf16[528,384]{1,0:T(8,128)(2,1)S(1)}, bf16[528,384]{1,0:T(8,128)(2,1)S(1)}, u32[]{:S(2)}, u32[]{:S(2)}) collective-permute-start(bf16[528,384]{1,0:T(8,128)(2,1)S(1)} %get-tuple-element.74), channel_id=1, source_target_pairs={{0,2},{1,6},{2,0},{3,4},{4,3},{5,7},{6,1},{7,5},{8,10},{9,14},{10,... | collective-permute-start | bytes 1216520 | tf_op jit(solution)/shard_map/ppermute | solution.py:35
  96.2 3.2 %collective-permute-start.25 = (bf16[256,768]{1,0:T(8,128)(2,1)S(1)}, bf16[256,768]{1,0:T(8,128)(2,1)S(1)}, u32[]{:S(2)}, u32[]{:S(2)}) collective-permute-start(bf16[256,768]{1,0:T(8,128)(2,1)S(1)} %get-tuple-element.80), channel_id=1, source_target_pairs={{0,24},{1,25},{2,26},{3,27},{4,28},{5,29},{6,30},{7,31},{8,0},{9,1... | collective-permute-start | bytes 1179656 | tf_op jit(solution)/shard_map/ppermute | solution.py:35
  99.5 4.2 %collective-permute-done.24.up = bf16[256,768]{1,0:T(8,128)(2,1)S(1)} collective-permute-done((bf16[256,768]{1,0:T(8,128)(2,1)S(1)}, bf16[256,768]{1,0:T(8,128)(2,1)S(1)}, u32[]{:S(2)}, u32[]{:S(2)}) %collective-permute-start.24) | collective-permute-done | bytes 393248 | tf_op jit(solution)/shard_map/ppermute | solution.py:35
  103.6 2.0 %collective-permute-start.23 = (bf16[528,384]{1,0:T(8,128)(2,1)S(1)}, bf16[528,384]{1,0:T(8,128)(2,1)S(1)}, u32[]{:S(2)}, u32[]{:S(2)}) collective-permute-start(bf16[528,384]{1,0:T(8,128)(2,1)S(1)} %get-tuple-element.75), channel_id=1, source_target_pairs={{0,3},{1,7},{2,1},{3,5},{4,2},{5,6},{6,0},{7,4},{8,11},{9,15},{10,... | collective-permute-start | bytes 1216520 | tf_op jit(solution)/shard_map/ppermute | solution.py:35
  105.6 1.8 %shard_map.118.whole = bf16[1536,768]{1,0:T(8,128)(2,1)S(1)} custom-call(bf16[768,384]{1,0:T(8,128)(2,1)} %copy-done.5, bf16[768,384]{1,0:T(8,128)(2,1)} %copy-done, bf16[768,384]{1,0:T(8,128)(2,1)} %copy-done.1, bf16[768,384]{1,0:T(8,128)(2,1)} %copy-done.7, bf16[768,384]{1,0:T(8,128)(2,1)} %copy-done.8, bf16[768,384]{1,0:T(8,128)(2,1)} %copy-done.9, ...), custom_call_target="tpu_custom_call" | custom-call | tf_op jit(solution)/shard_map/pallas_call | solution.py:310
  107.5 5.1 %collective-permute-done.25.down = bf16[256,768]{1,0:T(8,128)(2,1)S(1)} collective-permute-done((bf16[256,768]{1,0:T(8,128)(2,1)S(1)}, bf16[256,768]{1,0:T(8,128)(2,1)S(1)}, u32[]{:S(2)}, u32[]{:S(2)}) %collective-permute-start.25) | collective-permute-done | bytes 393248 | tf_op jit(solution)/shard_map/ppermute | solution.py:35
  112.6 1.0 shard_map.119
  113.6 2.2 %collective-permute-start.29 = (bf16[256,384]{1,0:T(8,128)(2,1)S(1)}, bf16[256,384]{1,0:T(8,128)(2,1)S(1)}, u32[]{:S(2)}, u32[]{:S(2)}) collective-permute-start(bf16[256,384]{1,0:T(8,128)(2,1)S(1)} %get-tuple-element.84), channel_id=1, source_target_pairs={{0,3},{1,7},{2,1},{3,5},{4,2},{5,6},{6,0},{7,4},{8,11},{9,15},{10,... | collective-permute-start | bytes 589832 | tf_op jit(solution)/shard_map/ppermute | solution.py:35
  115.8 0.9 collective-permute-start.28
  116.7 2.7 %collective-permute-start.26 = (bf16[256,384]{1,0:T(8,128)(2,1)S(1)}, bf16[256,384]{1,0:T(8,128)(2,1)S(1)}, u32[]{:S(2)}, u32[]{:S(2)}) collective-permute-start(bf16[256,384]{1,0:T(8,128)(2,1)S(1)} %get-tuple-element.81), channel_id=1, source_target_pairs={{0,0},{1,4},{2,2},{3,6},{4,1},{5,5},{6,3},{7,7},{8,8},{9,12},{10,1... | collective-permute-start | bytes 589832 | tf_op jit(solution)/shard_map/ppermute | solution.py:35
  119.5 1.2 shard_map.117
  120.7 0.3 collective-permute-done.29
  120.9 5.1 %collective-permute-done.28 = bf16[256,384]{1,0:T(8,128)(2,1)S(1)} collective-permute-done((bf16[256,384]{1,0:T(8,128)(2,1)S(1)}, bf16[256,384]{1,0:T(8,128)(2,1)S(1)}, u32[]{:S(2)}, u32[]{:S(2)}) %collective-permute-start.28) | collective-permute-done | bytes 196640 | tf_op jit(solution)/shard_map/ppermute | solution.py:35
  126.0 0.8 collective-permute-done.26
  126.8 0.8 add_convert_fusion
  (71 shorter events, 1.0 us)
Async XLA Ops:
  0.6 10.8 %copy-start.15 = (bf16[2,128,384]{2,1,0:T(8,128)(2,1)S(1)}, bf16[2,128,384]{2,1,0:T(8,128)(2,1)}, u32[]{:S(2)}) copy-start(bf16[2,128,384]{2,1,0:T(8,128)(2,1)} %param.11) | copy-start | bytes 589828
  0.6 10.8 %copy-start.12 = (bf16[256,384]{1,0:T(8,128)(2,1)S(1)}, bf16[256,384]{1,0:T(8,128)(2,1)}, u32[]{:S(2)}) copy-start(bf16[256,384]{1,0:T(8,128)(2,1)} %hidden.1) | copy-start | bytes 589828
  0.7 10.8 %copy-start.14 = (bf16[256,384]{1,0:T(8,128)(2,1)S(1)}, bf16[256,384]{1,0:T(8,128)(2,1)}, u32[]{:S(2)}) copy-start(bf16[256,384]{1,0:T(8,128)(2,1)} %param.17) | copy-start | bytes 589828
  1.9 15.6 %collective-permute-start = (bf16[768,384]{1,0:T(8,128)(2,1)S(1)}, bf16[768,384]{1,0:T(8,128)(2,1)S(1)}, u32[]{:S(2)}, u32[]{:S(2)}) collective-permute-start(bf16[768,384]{1,0:T(8,128)(2,1)S(1)} %pad_maximum_fusion.1), channel_id=1, source_target_pairs={{0,0},{1,4},{2,2},{3,6},{4,1},{5,5},{6,3},{7,7},{8,8},{9,12},{10,1... | collective-permute-start | bytes 1769480 | tf_op jit(solution)/shard_map/ppermute | solution.py:35
  6.5 8.8 %collective-permute-start.1 = (bf16[256,384]{1,0:T(8,128)(2,1)}, bf16[256,384]{1,0:T(8,128)(2,1)S(1)}, u32[]{:S(2)}, u32[]{:S(2)}) collective-permute-start(bf16[256,384]{1,0:T(8,128)(2,1)} %bitcast.6), channel_id=1, source_target_pairs={{0,8},{1,9},{2,10},{3,11},{4,12},{5,13},{6,14},{7,15},{8,16},{9,17... | collective-permute-start | bytes 589832 | tf_op jit(solution)/shard_map/ppermute | solution.py:35
  7.8 9.7 %collective-permute-start.2 = (bf16[256,384]{1,0:T(8,128)(2,1)}, bf16[256,384]{1,0:T(8,128)(2,1)}, u32[]{:S(2)}, u32[]{:S(2)}) collective-permute-start(bf16[256,384]{1,0:T(8,128)(2,1)} %bitcast.7), channel_id=1, source_target_pairs={{0,24},{1,25},{2,26},{3,27},{4,28},{5,29},{6,30},{7,31},{8,0},{9,1... | collective-permute-start | bytes 589832 | tf_op jit(solution)/shard_map/ppermute | solution.py:35
  17.5 6.7 %copy-start.5 = (bf16[768,384]{1,0:T(8,128)(2,1)}, bf16[768,384]{1,0:T(8,128)(2,1)S(1)}, u32[]{:S(2)}) copy-start(bf16[768,384]{1,0:T(8,128)(2,1)S(1)} %collective-permute-done.refs_6_.refs_5_.refs_7_.refs_0_) | copy-start | bytes 1769476
  17.5 16.3 %collective-permute-start.3 = (bf16[768,384]{1,0:T(8,128)(2,1)S(1)}, bf16[768,384]{1,0:T(8,128)(2,1)S(1)}, u32[]{:S(2)}, u32[]{:S(2)}) collective-permute-start(bf16[768,384]{1,0:T(8,128)(2,1)S(1)} %collective-permute-done.refs_6_.refs_5_.refs_7_.refs_0_), channel_id=1, source_target_pairs={{0,8},{1,9},{2,10},{3,11},{4,12},{5,13},{6,14},{7,15},{8,16},{9,17... | collective-permute-start | bytes 1769480 | tf_op jit(solution)/shard_map/ppermute | solution.py:35
  17.7 3.6 %collective-permute-start.10 = (bf16[256,384]{1,0:T(8,128)(2,1)S(1)}, bf16[256,384]{1,0:T(8,128)(2,1)}, u32[]{:S(2)}, u32[]{:S(2)}) collective-permute-start(bf16[256,384]{1,0:T(8,128)(2,1)S(1)} %collective-permute-done.1), channel_id=1, source_target_pairs={{0,1},{1,0},{2,3},{3,2},{4,5},{5,4},{6,7},{7,6},{8,9},{9,8},{10,11... | collective-permute-start | bytes 589832 | tf_op jit(solution)/shard_map/ppermute | solution.py:35
  18.4 5.0 %collective-permute-start.11 = (bf16[256,384]{1,0:T(8,128)(2,1)}, bf16[256,384]{1,0:T(8,128)(2,1)S(1)}, u32[]{:S(2)}, u32[]{:S(2)}) collective-permute-start(bf16[256,384]{1,0:T(8,128)(2,1)} %collective-permute-done.2), channel_id=1, source_target_pairs={{0,1},{1,0},{2,3},{3,2},{4,5},{5,4},{6,7},{7,6},{8,9},{9,8},{10,11... | collective-permute-start | bytes 589832 | tf_op jit(solution)/shard_map/ppermute | solution.py:35
  18.4 31.5 %collective-permute-start.5 = (bf16[784,384]{1,0:T(8,128)(2,1)}, bf16[784,384]{1,0:T(8,128)(2,1)S(1)}, u32[]{:S(2)}, u32[]{:S(2)}) collective-permute-start(bf16[784,384]{1,0:T(8,128)(2,1)} %pad_maximum_fusion), channel_id=1, source_target_pairs={{0,0},{1,4},{2,2},{3,6},{4,1},{5,5},{6,3},{7,7},{8,8},{9,12},{10,1... | collective-permute-start | bytes 1806344 | tf_op jit(solution)/shard_map/ppermute | solution.py:35
  21.3 31.2 %collective-permute-start.6 = (bf16[784,384]{1,0:T(8,128)(2,1)}, bf16[784,384]{1,0:T(8,128)(2,1)S(1)}, u32[]{:S(2)}, u32[]{:S(2)}) collective-permute-start(bf16[784,384]{1,0:T(8,128)(2,1)} %pad_maximum_fusion), channel_id=1, source_target_pairs={{0,4},{1,0},{2,6},{3,2},{4,5},{5,1},{6,7},{7,3},{8,12},{9,8},{10,1... | collective-permute-start | bytes 1806344 | tf_op jit(solution)/shard_map/ppermute | solution.py:35
  21.4 31.2 %collective-permute-start.7 = (bf16[784,384]{1,0:T(8,128)(2,1)}, bf16[784,384]{1,0:T(8,128)(2,1)S(1)}, u32[]{:S(2)}, u32[]{:S(2)}) collective-permute-start(bf16[784,384]{1,0:T(8,128)(2,1)} %pad_maximum_fusion), channel_id=1, source_target_pairs={{0,2},{1,6},{2,0},{3,4},{4,3},{5,7},{6,1},{7,5},{8,10},{9,14},{10,... | collective-permute-start | bytes 1806344 | tf_op jit(solution)/shard_map/ppermute | solution.py:35
  23.4 10.3 %copy-start.16 = (bf16[256,384]{1,0:T(8,128)(2,1)}, bf16[256,384]{1,0:T(8,128)(2,1)S(1)}, u32[]{:S(2)}) copy-start(bf16[256,384]{1,0:T(8,128)(2,1)S(1)} %collective-permute-done.11) | copy-start | bytes 589828
  23.4 29.1 %collective-permute-start.8 = (bf16[784,384]{1,0:T(8,128)(2,1)}, bf16[784,384]{1,0:T(8,128)(2,1)}, u32[]{:S(2)}, u32[]{:S(2)}) collective-permute-start(bf16[784,384]{1,0:T(8,128)(2,1)} %pad_maximum_fusion), channel_id=1, source_target_pairs={{0,6},{1,2},{2,4},{3,0},{4,7},{5,3},{6,5},{7,1},{8,14},{9,10},{10,... | collective-permute-start | bytes 1806344 | tf_op jit(solution)/shard_map/ppermute | solution.py:35
  33.8 42.8 %copy-start = (bf16[768,384]{1,0:T(8,128)(2,1)}, bf16[768,384]{1,0:T(8,128)(2,1)S(1)}, u32[]{:S(2)}) copy-start(bf16[768,384]{1,0:T(8,128)(2,1)S(1)} %collective-permute-done.3.refs_7_.refs_6_.refs_8_.refs_1_) | copy-start | bytes 1769476
  33.8 13.9 %collective-permute-start.4 = (bf16[768,384]{1,0:T(8,128)(2,1)}, bf16[768,384]{1,0:T(8,128)(2,1)S(1)}, u32[]{:S(2)}, u32[]{:S(2)}) collective-permute-start(bf16[768,384]{1,0:T(8,128)(2,1)} %copy-done.5), channel_id=1, source_target_pairs={{0,24},{1,25},{2,26},{3,27},{4,28},{5,29},{6,30},{7,31},{8,0},{9,1... | collective-permute-start | bytes 1769480 | tf_op jit(solution)/shard_map/ppermute | solution.py:35
  33.8 2.3 %copy-start.17 = (bf16[256,384]{1,0:T(8,128)(2,1)S(1)}, bf16[256,384]{1,0:T(8,128)(2,1)}, u32[]{:S(2)}) copy-start(bf16[256,384]{1,0:T(8,128)(2,1)} %copy-done.16) | copy-start | bytes 589828
  35.1 17.7 %copy-start.6 = (bf16[768,384]{1,0:T(8,128)(2,1)S(1)}, bf16[768,384]{1,0:T(8,128)(2,1)}, u32[]{:S(2)}) copy-start(bf16[768,384]{1,0:T(8,128)(2,1)} %copy-done.5) | copy-start | bytes 1769476
  47.7 28.9 %copy-start.1 = (bf16[768,384]{1,0:T(8,128)(2,1)}, bf16[768,384]{1,0:T(8,128)(2,1)S(1)}, u32[]{:S(2)}) copy-start(bf16[768,384]{1,0:T(8,128)(2,1)S(1)} %collective-permute-done.4.refs_8_.refs_7_.refs_9_.refs_2_) | copy-start | bytes 1769476
  47.7 22.0 %collective-permute-start.12 = (bf16[1024,384]{1,0:T(8,128)(2,1)S(1)}, bf16[1024,384]{1,0:T(8,128)(2,1)S(1)}, u32[]{:S(2)}, u32[]{:S(2)}) collective-permute-start(bf16[1024,384]{1,0:T(8,128)(2,1)S(1)} %constant_dynamic-update-slice_fusion), channel_id=1, source_target_pairs={{0,0},{1,4},{2,2},{3,6},{4,1},{5,5},{6,3},{7,7},{8,8},{9,12},{10,1... | collective-permute-start | bytes 2359304 | tf_op jit(solution)/shard_map/ppermute | solution.py:35
  49.9 26.7 %copy-start.2 = (bf16[784,384]{1,0:T(8,128)(2,1)}, bf16[784,384]{1,0:T(8,128)(2,1)S(1)}, u32[]{:S(2)}) copy-start(bf16[784,384]{1,0:T(8,128)(2,1)S(1)} %collective-permute-done.5.refs_0_.refs_1_.refs_3_) | copy-start | bytes 1806340
  49.9 19.8 %collective-permute-start.13 = (bf16[1024,384]{1,0:T(8,128)(2,1)S(1)}, bf16[1024,384]{1,0:T(8,128)(2,1)S(1)}, u32[]{:S(2)}, u32[]{:S(2)}) collective-permute-start(bf16[1024,384]{1,0:T(8,128)(2,1)S(1)} %constant_dynamic-update-slice_fusion), channel_id=1, source_target_pairs={{0,2},{1,6},{2,0},{3,4},{4,3},{5,7},{6,1},{7,5},{8,10},{9,14},{10,... | collective-permute-start | bytes 2359304 | tf_op jit(solution)/shard_map/ppermute | solution.py:35
  52.5 24.1 %copy-start.3 = (bf16[784,384]{1,0:T(8,128)(2,1)}, bf16[784,384]{1,0:T(8,128)(2,1)S(1)}, u32[]{:S(2)}) copy-start(bf16[784,384]{1,0:T(8,128)(2,1)S(1)} %collective-permute-done.6.refs_1_.refs_2_.refs_4_) | copy-start | bytes 1806340
  52.6 24.1 %copy-start.4 = (bf16[784,384]{1,0:T(8,128)(2,1)}, bf16[784,384]{1,0:T(8,128)(2,1)S(1)}, u32[]{:S(2)}) copy-start(bf16[784,384]{1,0:T(8,128)(2,1)S(1)} %collective-permute-done.7.refs_2_.refs_3_.refs_5_) | copy-start | bytes 1806340
  52.7 17.0 %collective-permute-start.9 = (bf16[768,384]{1,0:T(8,128)(2,1)S(1)}, bf16[768,384]{1,0:T(8,128)(2,1)S(1)}, u32[]{:S(2)}, u32[]{:S(2)}) collective-permute-start(bf16[768,384]{1,0:T(8,128)(2,1)S(1)} %broadcast_select_fusion), channel_id=1, source_target_pairs={{0,8},{1,9},{2,10},{3,11},{4,12},{5,13},{6,14},{7,15},{8,0},{9,1},... | collective-permute-start | bytes 1769480 | tf_op jit(solution)/shard_map/ppermute | solution.py:35
  52.8 18.0 %collective-permute-start.14 = (bf16[768,384]{1,0:T(8,128)(2,1)S(1)}, bf16[768,384]{1,0:T(8,128)(2,1)S(1)}, u32[]{:S(2)}, u32[]{:S(2)}) collective-permute-start(bf16[768,384]{1,0:T(8,128)(2,1)S(1)} %copy-done.6), channel_id=1, source_target_pairs={{0,1},{1,0},{2,3},{3,2},{4,5},{5,4},{6,7},{7,6},{8,9},{9,8},{10,11... | collective-permute-start | bytes 1769480 | tf_op jit(solution)/shard_map/ppermute | solution.py:35
  52.8 18.0 %collective-permute-start.15 = (bf16[768,384]{1,0:T(8,128)(2,1)S(1)}, bf16[768,384]{1,0:T(8,128)(2,1)S(1)}, u32[]{:S(2)}, u32[]{:S(2)}) collective-permute-start(bf16[768,384]{1,0:T(8,128)(2,1)S(1)} %collective-permute-done.3.refs_7_.refs_6_.refs_8_.refs_1_), channel_id=1, source_target_pairs={{0,1},{1,0},{2,3},{3,2},{4,5},{5,4},{6,7},{7,6},{8,9},{9,8},{10,11... | collective-permute-start | bytes 1769480 | tf_op jit(solution)/shard_map/ppermute | solution.py:35
  69.7 2.0 %collective-permute-start.16 = (bf16[768,384]{1,0:T(8,128)(2,1)S(1)}, bf16[768,384]{1,0:T(8,128)(2,1)S(1)}, u32[]{:S(2)}, u32[]{:S(2)}) collective-permute-start(bf16[768,384]{1,0:T(8,128)(2,1)S(1)} %collective-permute-done.4.refs_8_.refs_7_.refs_9_.refs_2_), channel_id=1, source_target_pairs={{0,1},{1,0},{2,3},{3,2},{4,5},{5,4},{6,7},{7,6},{8,9},{9,8},{10,11... | collective-permute-start | bytes 1769480 | tf_op jit(solution)/shard_map/ppermute | solution.py:35
  69.7 6.9 %copy-start.7 = (bf16[768,384]{1,0:T(8,128)(2,1)}, bf16[768,384]{1,0:T(8,128)(2,1)S(1)}, u32[]{:S(2)}) copy-start(bf16[768,384]{1,0:T(8,128)(2,1)S(1)} %collective-permute-done.9.refs_9_.refs_8_.refs_10_.refs_3_) | copy-start | bytes 1769476
  69.7 2.8 %collective-permute-start.17 = (bf16[768,384]{1,0:T(8,128)(2,1)S(1)}, bf16[768,384]{1,0:T(8,128)(2,1)S(1)}, u32[]{:S(2)}, u32[]{:S(2)}) collective-permute-start(bf16[768,384]{1,0:T(8,128)(2,1)S(1)} %collective-permute-done.9.refs_9_.refs_8_.refs_10_.refs_3_), channel_id=1, source_target_pairs={{0,1},{1,0},{2,3},{3,2},{4,5},{5,4},{6,7},{7,6},{8,9},{9,8},{10,11... | collective-permute-start | bytes 1769480 | tf_op jit(solution)/shard_map/ppermute | solution.py:35
  70.8 5.8 %copy-start.8 = (bf16[768,384]{1,0:T(8,128)(2,1)}, bf16[768,384]{1,0:T(8,128)(2,1)S(1)}, u32[]{:S(2)}) copy-start(bf16[768,384]{1,0:T(8,128)(2,1)S(1)} %collective-permute-done.14.refs_10_.refs_9_.refs_11_.refs_4_) | copy-start | bytes 1769476
  70.8 5.8 %copy-start.9 = (bf16[768,384]{1,0:T(8,128)(2,1)}, bf16[768,384]{1,0:T(8,128)(2,1)S(1)}, u32[]{:S(2)}) copy-start(bf16[768,384]{1,0:T(8,128)(2,1)S(1)} %collective-permute-done.15.refs_11_.refs_10_.refs_12_.refs_5_) | copy-start | bytes 1769476
  71.7 4.9 %copy-start.10 = (bf16[768,384]{1,0:T(8,128)(2,1)}, bf16[768,384]{1,0:T(8,128)(2,1)S(1)}, u32[]{:S(2)}) copy-start(bf16[768,384]{1,0:T(8,128)(2,1)S(1)} %collective-permute-done.16.refs_12_.refs_11_.refs_13_.refs_6_) | copy-start | bytes 1769476
  72.6 4.1 %copy-start.11 = (bf16[768,384]{1,0:T(8,128)(2,1)}, bf16[768,384]{1,0:T(8,128)(2,1)S(1)}, u32[]{:S(2)}) copy-start(bf16[768,384]{1,0:T(8,128)(2,1)S(1)} %collective-permute-done.17.refs_13_.refs_12_.refs_14_.refs_7_) | copy-start | bytes 1769476
  76.2 3.0 %collective-permute-start.18 = (bf16[512,768]{1,0:T(8,128)(2,1)S(1)}, bf16[512,768]{1,0:T(8,128)(2,1)S(1)}, u32[]{:S(2)}, u32[]{:S(2)}) collective-permute-start(bf16[512,768]{1,0:T(8,128)(2,1)S(1)} %get-tuple-element.59), channel_id=1, source_target_pairs={{0,1},{1,0},{2,3},{3,2},{4,5},{5,4},{6,7},{7,6},{8,9},{9,8},{10,11... | collective-permute-start | bytes 2359304 | tf_op jit(solution)/shard_map/ppermute | solution.py:35
  87.2 3.8 %collective-permute-start.19 = (bf16[512,768]{1,0:T(8,128)(2,1)}, bf16[512,768]{1,0:T(8,128)(2,1)S(1)}, u32[]{:S(2)}, u32[]{:S(2)}) collective-permute-start(bf16[512,768]{1,0:T(8,128)(2,1)} %get-tuple-element.64), channel_id=1, source_target_pairs={{0,1},{1,0},{2,3},{3,2},{4,5},{5,4},{6,7},{7,6},{8,9},{9,8},{10,11... | collective-permute-start | bytes 2359304 | tf_op jit(solution)/shard_map/ppermute | solution.py:35
  91.3 12.3 %collective-permute-start.24 = (bf16[256,768]{1,0:T(8,128)(2,1)S(1)}, bf16[256,768]{1,0:T(8,128)(2,1)S(1)}, u32[]{:S(2)}, u32[]{:S(2)}) collective-permute-start(bf16[256,768]{1,0:T(8,128)(2,1)S(1)} %get-tuple-element.79), channel_id=1, source_target_pairs={{0,8},{1,9},{2,10},{3,11},{4,12},{5,13},{6,14},{7,15},{8,16},{9,17... | collective-permute-start | bytes 1179656 | tf_op jit(solution)/shard_map/ppermute | solution.py:35
  91.4 24.5 %collective-permute-start.20 = (bf16[528,384]{1,0:T(8,128)(2,1)S(1)}, bf16[528,384]{1,0:T(8,128)(2,1)S(1)}, u32[]{:S(2)}, u32[]{:S(2)}) collective-permute-start(bf16[528,384]{1,0:T(8,128)(2,1)S(1)} %get-tuple-element.72), channel_id=1, source_target_pairs={{0,0},{1,4},{2,2},{3,6},{4,1},{5,5},{6,3},{7,7},{8,8},{9,12},{10,1... | collective-permute-start | bytes 1216520 | tf_op jit(solution)/shard_map/ppermute | solution.py:35
  94.8 21.9 %collective-permute-start.21 = (bf16[528,384]{1,0:T(8,128)(2,1)S(1)}, bf16[528,384]{1,0:T(8,128)(2,1)S(1)}, u32[]{:S(2)}, u32[]{:S(2)}) collective-permute-start(bf16[528,384]{1,0:T(8,128)(2,1)S(1)} %get-tuple-element.73), channel_id=1, source_target_pairs={{0,1},{1,5},{2,3},{3,7},{4,0},{5,4},{6,2},{7,6},{8,9},{9,13},{10,1... | collective-permute-start | bytes 1216520 | tf_op jit(solution)/shard_map/ppermute | solution.py:35
  94.8 21.9 %collective-permute-start.22 = (bf16[528,384]{1,0:T(8,128)(2,1)S(1)}, bf16[528,384]{1,0:T(8,128)(2,1)S(1)}, u32[]{:S(2)}, u32[]{:S(2)}) collective-permute-start(bf16[528,384]{1,0:T(8,128)(2,1)S(1)} %get-tuple-element.74), channel_id=1, source_target_pairs={{0,2},{1,6},{2,0},{3,4},{4,3},{5,7},{6,1},{7,5},{8,10},{9,14},{10,... | collective-permute-start | bytes 1216520 | tf_op jit(solution)/shard_map/ppermute | solution.py:35
  96.2 16.4 %collective-permute-start.25 = (bf16[256,768]{1,0:T(8,128)(2,1)S(1)}, bf16[256,768]{1,0:T(8,128)(2,1)S(1)}, u32[]{:S(2)}, u32[]{:S(2)}) collective-permute-start(bf16[256,768]{1,0:T(8,128)(2,1)S(1)} %get-tuple-element.80), channel_id=1, source_target_pairs={{0,24},{1,25},{2,26},{3,27},{4,28},{5,29},{6,30},{7,31},{8,0},{9,1... | collective-permute-start | bytes 1179656 | tf_op jit(solution)/shard_map/ppermute | solution.py:35
  103.6 15.9 %collective-permute-start.23 = (bf16[528,384]{1,0:T(8,128)(2,1)S(1)}, bf16[528,384]{1,0:T(8,128)(2,1)S(1)}, u32[]{:S(2)}, u32[]{:S(2)}) collective-permute-start(bf16[528,384]{1,0:T(8,128)(2,1)S(1)} %get-tuple-element.75), channel_id=1, source_target_pairs={{0,3},{1,7},{2,1},{3,5},{4,2},{5,6},{6,0},{7,4},{8,11},{9,15},{10,... | collective-permute-start | bytes 1216520 | tf_op jit(solution)/shard_map/ppermute | solution.py:35
  112.6 6.9 %copy-start.13 = (bf16[384]{0:T(512)(128)(2,1)S(1)}, bf16[384]{0:T(512)(128)(2,1)}, u32[]{:S(2)}) copy-start(bf16[384]{0:T(512)(128)(2,1)} %gain.1) | copy-start | bytes 2308
  113.6 7.3 %collective-permute-start.29 = (bf16[256,384]{1,0:T(8,128)(2,1)S(1)}, bf16[256,384]{1,0:T(8,128)(2,1)S(1)}, u32[]{:S(2)}, u32[]{:S(2)}) collective-permute-start(bf16[256,384]{1,0:T(8,128)(2,1)S(1)} %get-tuple-element.84), channel_id=1, source_target_pairs={{0,3},{1,7},{2,1},{3,5},{4,2},{5,6},{6,0},{7,4},{8,11},{9,15},{10,... | collective-permute-start | bytes 589832 | tf_op jit(solution)/shard_map/ppermute | solution.py:35
  115.8 10.2 %collective-permute-start.28 = (bf16[256,384]{1,0:T(8,128)(2,1)S(1)}, bf16[256,384]{1,0:T(8,128)(2,1)S(1)}, u32[]{:S(2)}, u32[]{:S(2)}) collective-permute-start(bf16[256,384]{1,0:T(8,128)(2,1)S(1)} %get-tuple-element.83), channel_id=1, source_target_pairs={{0,2},{1,6},{2,0},{3,4},{4,3},{5,7},{6,1},{7,5},{8,10},{9,14},{10,... | collective-permute-start | bytes 589832 | tf_op jit(solution)/shard_map/ppermute | solution.py:35
  116.7 9.3 %collective-permute-start.27 = (bf16[256,384]{1,0:T(8,128)(2,1)S(1)}, bf16[256,384]{1,0:T(8,128)(2,1)S(1)}, u32[]{:S(2)}, u32[]{:S(2)}) collective-permute-start(bf16[256,384]{1,0:T(8,128)(2,1)S(1)} %get-tuple-element.82), channel_id=1, source_target_pairs={{0,1},{1,5},{2,3},{3,7},{4,0},{5,4},{6,2},{7,6},{8,9},{9,13},{10,1... | collective-permute-start | bytes 589832 | tf_op jit(solution)/shard_map/ppermute | solution.py:35
  116.7 10.0 %collective-permute-start.26 = (bf16[256,384]{1,0:T(8,128)(2,1)S(1)}, bf16[256,384]{1,0:T(8,128)(2,1)S(1)}, u32[]{:S(2)}, u32[]{:S(2)}) collective-permute-start(bf16[256,384]{1,0:T(8,128)(2,1)S(1)} %get-tuple-element.81), channel_id=1, source_target_pairs={{0,0},{1,4},{2,2},{3,6},{4,1},{5,5},{6,3},{7,7},{8,8},{9,12},{10,1... | collective-permute-start | bytes 589832 | tf_op jit(solution)/shard_map/ppermute | solution.py:35

commit v7 on v6

--- a/solution.py
+++ b/solution.py
@@ -176,19 +176,20 @@
 
 def attention_kernel(seq_count, *refs):
     chosen, tables, shared, queries, d_attended = refs[:5]
-    attended, d_queries, d_own, d_outer, d_shared, window, d_window, sems = refs[5:]
+    attended, d_queries, d_own, d_outer, d_shared, window, d_window, logits, slopes, weights, d_scores, sems = refs[5:]
     token_count, width = queries.shape
-    run_copies(
-        [
-            (tables, window.at[pl.ds(0, 3 * OWN_ROWS)]),
-            (shared, window.at[pl.ds(3 * OWN_ROWS, 2 * OWN_ROWS)]),
-        ],
-        sems,
-    )
+    sources = [
+        (tables, window.at[pl.ds(0, 3 * OWN_ROWS)]),
+        (shared, window.at[pl.ds(3 * OWN_ROWS, 2 * OWN_ROWS)]),
+    ]
+    copies = [pltpu.make_async_copy(a, b, sems.at[i]) for i, (a, b) in enumerate(sources)]
+    for copy in copies:
+        copy.start()
     d_window[...] = jnp.zeros_like(d_window)
     scale = HD ** (-0.5)
     z, y, x, c = place()
     t = 2 * z + c
+    items = []
     for s in range(token_count // STRETCH):
         starts = []
         for j in range(NBR):
@@ -197,30 +198,47 @@
             odd = 3 + jnp.where(away == 1, 1 - c, c)
             index = jnp.where(away % 2 == 0, away // 2, odd)
             starts.append(pl.multiple_of(index * OWN_ROWS + (name % OWN_DEV) * RET, RET))
-        tokens = slice(s * STRETCH, (s + 1) * STRETCH)
         for h in range(width // HD):
-            left = slice(h * HD, (h + 1) * HD)
-            right = slice(width + h * HD, width + (h + 1) * HD)
-            keys = jnp.concatenate([window[pl.ds(a, RET), left] for a in starts], axis=0)
-            values = jnp.concatenate([window[pl.ds(a, RET), right] for a in starts], axis=0)
-            query = queries[tokens, left]
-            d_att = d_attended[tokens, left]
-            scores = lax.dot_general(query, keys, ACROSS, preferred_element_type=F32) * scale
-            exponent = jnp.exp(scores - jnp.max(scores, axis=1, keepdims=True))
-            weights = exponent / jnp.sum(exponent, axis=1, keepdims=True)
-            weights_low = weights.astype(LOW)
-            attended[tokens, left] = jnp.dot(
-                weights_low, values, preferred_element_type=F32
-            ).astype(LOW)
-            d_weights = lax.dot_general(d_att, values, ACROSS, preferred_element_type=F32)
-            inner = jnp.sum(d_weights * weights, axis=1, keepdims=True)
-            d_scores = (weights * (d_weights - inner) * scale).astype(LOW)
-            d_queries[tokens, left] = jnp.dot(d_scores, keys, preferred_element_type=F32).astype(LOW)
-            d_keys = lax.dot_general(d_scores, query, DOWN, preferred_element_type=F32)
-            d_values = lax.dot_general(weights_low, d_att, DOWN, preferred_element_type=F32)
-            for j, a in enumerate(starts):
-                d_window[pl.ds(a, RET), left] += d_keys[j * RET : (j + 1) * RET, :]
-                d_window[pl.ds(a, RET), right] += d_values[j * RET : (j + 1) * RET, :]
+            rows = slice(len(items) * STRETCH, (len(items) + 1) * STRETCH)
+            tokens = slice(s * STRETCH, (s + 1) * STRETCH)
+            items.append((rows, tokens, slice(h * HD, (h + 1) * HD), slice(width + h * HD, width + (h + 1) * HD), starts))
+
+    def picked(starts, columns):
+        return jnp.concatenate([window[pl.ds(a, RET), columns] for a in starts], axis=0)
+
+    for copy in copies:
+        copy.wait()
+    for rows, tokens, left, right, starts in items:
+        logits[rows, :] = lax.dot_general(
+            queries[tokens, left], picked(starts, left), ACROSS, preferred_element_type=F32
+        )
+        slopes[rows, :] = lax.dot_general(
+            d_attended[tokens, left], picked(starts, right), ACROSS, preferred_element_type=F32
+        )
+    scores = logits[...] * scale
+    exponent = jnp.exp(scores - jnp.max(scores, axis=1, keepdims=True))
+    soft = exponent / jnp.sum(exponent, axis=1, keepdims=True)
+    d_weights = slopes[...]
+    inner = jnp.sum(d_weights * soft, axis=1, keepdims=True)
+    weights[...] = soft.astype(LOW)
+    d_scores[...] = (soft * (d_weights - inner) * scale).astype(LOW)
+    for rows, tokens, left, right, starts in items:
+        attended[tokens, left] = jnp.dot(
+            weights[rows, :], picked(starts, right), preferred_element_type=F32
+        ).astype(LOW)
+        d_queries[tokens, left] = jnp.dot(
+            d_scores[rows, :], picked(starts, left), preferred_element_type=F32
+        ).astype(LOW)
+    for rows, tokens, left, right, starts in items:
+        d_keys = lax.dot_general(
+            d_scores[rows, :], queries[tokens, left], DOWN, preferred_element_type=F32
+        )
+        d_values = lax.dot_general(
+            weights[rows, :], d_attended[tokens, left], DOWN, preferred_element_type=F32
+        )
+        for j, a in enumerate(starts):
+            d_window[pl.ds(a, RET), left] += d_keys[j * RET : (j + 1) * RET, :]
+            d_window[pl.ds(a, RET), right] += d_values[j * RET : (j + 1) * RET, :]
     d_own[...] = d_window[OWN_ROWS : 2 * OWN_ROWS, :]
     d_outer[0:OWN_ROWS, :] = d_window[0:OWN_ROWS, :].astype(LOW)
     d_outer[OWN_ROWS : 2 * OWN_ROWS, :] = d_window[2 * OWN_ROWS : 3 * OWN_ROWS, :].astype(LOW)
@@ -388,7 +406,8 @@
             ((2 * OWN_ROWS, wide), LOW),
             ((2 * OWN_ROWS, wide), LOW),
         ],
-        [pltpu.VMEM((5 * OWN_ROWS, wide), LOW), pltpu.VMEM((5 * OWN_ROWS, wide), F32)],
+        [pltpu.VMEM((5 * OWN_ROWS, wide), LOW), pltpu.VMEM((5 * OWN_ROWS, wide), F32)]
+        + [pltpu.VMEM((token_count * width // HD, NBR * RET), dtype) for dtype in (F32, F32, LOW, LOW)],
         2,
     )
     from_core = move(d_shared, flip_core)

time: 128 us -> 124 us (0.969)
  Pallas kernels: 23.8 us -> 19.6 us
    pallas_call x8, Pallas kernels: 23.8 us -> 19.6 us  [call(): pl.pallas_call(kernel, out_shape=[jax.ShapeDtypeStruct(shape, dtype) for...]
where the time goes in v7:
time: 124 us; the launch traced here: 123 us
  waiting for transfers between devices  57.7 us (47%)
  starting transfers between devices  37.8 us (30%)
  Pallas kernels  19.6 us (16%)
  other arithmetic  3.94 us (3%)
  local copies, waits for them, and re-layouts  3.24 us (3%)
    ppermute x30, waiting for transfers between devices, move(): return lax.ppermute(value, ('seq', 'mp'), pairs)  57.7 us
    ppermute x30, starting transfers between devices, move(): return lax.ppermute(value, ('seq', 'mp'), pairs)  37.8 us
    pallas_call x8, Pallas kernels, call(): pl.pallas_call(kernel, out_shape=[jax.ShapeDtypeStruct(shape, dtype) for...  19.6 us
  transfers between devices with their start and end apart: 30, of which 12 were waited for; matrix products, arithmetic and copies ran while one was open for 4% of the time, Pallas kernels for 10%

profile of v7, /device:TPU:1, one launch (start us, length us, event | category | flops | bytes accessed | tf_op | source)
XLA Modules:
  0.0 123.4 jit_solution(2744708277922831496)
XLA Ops:
  0.7 1.2 %pad_maximum_fusion.1 = bf16[768,384]{1,0:T(8,128)(2,1)S(1)} fusion(bf16[192,384]{1,0:T(8,128)(2,1)} %bitcast.10, bf16[192,384]{1,0:T(8,128)(2,1)} %param.12, bf16[192,384]{1,0:T(8,128)(2,1)} %param.14, bf16[192,384]{1,0:T(8,128)(2,1)} %param.13), kind=kLoop, calls=%fused_computation.7 | loop fusion | flops 2359296 | bytes 1179648 | tf_op jit(solution)/shard_map/concatenate | solution.py:348
  1.9 4.5 %collective-permute-start = (bf16[768,384]{1,0:T(8,128)(2,1)S(1)}, bf16[768,384]{1,0:T(8,128)(2,1)S(1)}, u32[]{:S(2)}, u32[]{:S(2)}) collective-permute-start(bf16[768,384]{1,0:T(8,128)(2,1)S(1)} %pad_maximum_fusion.1), channel_id=1, source_target_pairs={{0,0},{1,4},{2,2},{3,6},{4,1},{5,5},{6,3},{7,7},{8,8},{9,12},{10,1... | collective-permute-start | bytes 1769480 | tf_op jit(solution)/shard_map/ppermute | solution.py:35
  6.5 1.3 %collective-permute-start.1 = (bf16[256,384]{1,0:T(8,128)(2,1)}, bf16[256,384]{1,0:T(8,128)(2,1)S(1)}, u32[]{:S(2)}, u32[]{:S(2)}) collective-permute-start(bf16[256,384]{1,0:T(8,128)(2,1)} %bitcast.6), channel_id=1, source_target_pairs={{0,8},{1,9},{2,10},{3,11},{4,12},{5,13},{6,14},{7,15},{8,16},{9,17... | collective-permute-start | bytes 589832 | tf_op jit(solution)/shard_map/ppermute | solution.py:35
  7.8 2.1 %collective-permute-start.2 = (bf16[256,384]{1,0:T(8,128)(2,1)}, bf16[256,384]{1,0:T(8,128)(2,1)}, u32[]{:S(2)}, u32[]{:S(2)}) collective-permute-start(bf16[256,384]{1,0:T(8,128)(2,1)} %bitcast.7), channel_id=1, source_target_pairs={{0,24},{1,25},{2,26},{3,27},{4,28},{5,29},{6,30},{7,31},{8,0},{9,1... | collective-permute-start | bytes 589832 | tf_op jit(solution)/shard_map/ppermute | solution.py:35
  9.9 0.7 convert_element_type.53
  10.8 0.7 broadcast_in_dim.8
  11.5 0.9 pad_maximum_fusion
  12.4 2.8 %collective-permute-done.1 = bf16[256,384]{1,0:T(8,128)(2,1)S(1)} collective-permute-done((bf16[256,384]{1,0:T(8,128)(2,1)}, bf16[256,384]{1,0:T(8,128)(2,1)S(1)}, u32[]{:S(2)}, u32[]{:S(2)}) %collective-permute-start.1) | collective-permute-done | bytes 196640 | tf_op jit(solution)/shard_map/ppermute | solution.py:35
  15.3 2.2 %collective-permute-done.2 = bf16[256,384]{1,0:T(8,128)(2,1)} collective-permute-done((bf16[256,384]{1,0:T(8,128)(2,1)}, bf16[256,384]{1,0:T(8,128)(2,1)}, u32[]{:S(2)}, u32[]{:S(2)}) %collective-permute-start.2) | collective-permute-done | bytes 196640 | tf_op jit(solution)/shard_map/ppermute | solution.py:35
  17.5 0.3 collective-permute-start.3
  17.7 0.7 collective-permute-start.10
  18.4 2.9 %collective-permute-start.5 = (bf16[784,384]{1,0:T(8,128)(2,1)}, bf16[784,384]{1,0:T(8,128)(2,1)S(1)}, u32[]{:S(2)}, u32[]{:S(2)}) collective-permute-start(bf16[784,384]{1,0:T(8,128)(2,1)} %pad_maximum_fusion), channel_id=1, source_target_pairs={{0,0},{1,4},{2,2},{3,6},{4,1},{5,5},{6,3},{7,7},{8,8},{9,12},{10,1... | collective-permute-start | bytes 1806344 | tf_op jit(solution)/shard_map/ppermute | solution.py:35
  21.4 2.1 %collective-permute-start.7 = (bf16[784,384]{1,0:T(8,128)(2,1)}, bf16[784,384]{1,0:T(8,128)(2,1)S(1)}, u32[]{:S(2)}, u32[]{:S(2)}) collective-permute-start(bf16[784,384]{1,0:T(8,128)(2,1)} %pad_maximum_fusion), channel_id=1, source_target_pairs={{0,2},{1,6},{2,0},{3,4},{4,3},{5,7},{6,1},{7,5},{8,10},{9,14},{10,... | collective-permute-start | bytes 1806344 | tf_op jit(solution)/shard_map/ppermute | solution.py:35
  23.4 0.7 collective-permute-start.8
  24.1 9.7 %collective-permute-done.3.refs_7_.refs_6_.refs_8_.refs_1_ = bf16[768,384]{1,0:T(8,128)(2,1)S(1)} collective-permute-done((bf16[768,384]{1,0:T(8,128)(2,1)S(1)}, bf16[768,384]{1,0:T(8,128)(2,1)S(1)}, u32[]{:S(2)}, u32[]{:S(2)}) %collective-permute-start.3) | collective-permute-done | bytes 589856 | tf_op jit(solution)/shard_map/ppermute | solution.py:35
  33.9 1.2 constant_dynamic-update-slice_fusion.2
  35.1 1.0 constant_dynamic-update-slice_fusion.1
  36.2 11.5 %collective-permute-done.4.refs_8_.refs_7_.refs_9_.refs_2_ = bf16[768,384]{1,0:T(8,128)(2,1)S(1)} collective-permute-done((bf16[768,384]{1,0:T(8,128)(2,1)}, bf16[768,384]{1,0:T(8,128)(2,1)S(1)}, u32[]{:S(2)}, u32[]{:S(2)}) %collective-permute-start.4) | collective-permute-done | bytes 589856 | tf_op jit(solution)/shard_map/ppermute | solution.py:35
  47.7 2.2 %collective-permute-start.12 = (bf16[1024,384]{1,0:T(8,128)(2,1)S(1)}, bf16[1024,384]{1,0:T(8,128)(2,1)S(1)}, u32[]{:S(2)}, u32[]{:S(2)}) collective-permute-start(bf16[1024,384]{1,0:T(8,128)(2,1)S(1)} %constant_dynamic-update-slice_fusion), channel_id=1, source_target_pairs={{0,0},{1,4},{2,2},{3,6},{4,1},{5,5},{6,3},{7,7},{8,8},{9,12},{10,1... | collective-permute-start | bytes 2359304 | tf_op jit(solution)/shard_map/ppermute | solution.py:35
  49.9 2.6 %collective-permute-start.13 = (bf16[1024,384]{1,0:T(8,128)(2,1)S(1)}, bf16[1024,384]{1,0:T(8,128)(2,1)S(1)}, u32[]{:S(2)}, u32[]{:S(2)}) collective-permute-start(bf16[1024,384]{1,0:T(8,128)(2,1)S(1)} %constant_dynamic-update-slice_fusion), channel_id=1, source_target_pairs={{0,2},{1,6},{2,0},{3,4},{4,3},{5,7},{6,1},{7,5},{8,10},{9,14},{10,... | collective-permute-start | bytes 2359304 | tf_op jit(solution)/shard_map/ppermute | solution.py:35
  52.8 0.5 collective-permute-start.15
  53.3 2.1 %shard_map.112 = (bf16[256,1536]{1,0:T(8,128)(2,1)S(1)}, f32[256,1]{1,0:T(8,128)S(1)}) custom-call(bf16[784,384]{1,0:T(8,128)(2,1)S(1)} %collective-permute-done.5.refs_0_.refs_1_.refs_3_, bf16[784,384]{1,0:T(8,128)(2,1)S(1)} %collective-permute-done.6.refs_1_.refs_2_.refs_4_, bf16[784,384]{1,0:T(8,128)(2,1)S(1)} %collective-permute-done.7.refs_2_.refs_3_.refs_5_, ...), custom_call_target="tpu_custom_call" | custom-call | tf_op jit(solution)/shard_map/pallas_call | solution.py:328
  55.5 14.2 %collective-permute-done.12.refs_4_ = bf16[1024,384]{1,0:T(8,128)(2,1)S(1)} collective-permute-done((bf16[1024,384]{1,0:T(8,128)(2,1)S(1)}, bf16[1024,384]{1,0:T(8,128)(2,1)S(1)}, u32[]{:S(2)}, u32[]{:S(2)}) %collective-permute-start.12) | collective-permute-done | bytes 786464 | tf_op jit(solution)/shard_map/ppermute | solution.py:35
  69.7 1.1 collective-permute-start.17
  70.8 0.9 collective-permute-done.16.refs_12_.refs_11_.refs_13_.refs_6_
  71.7 0.8 collective-permute-done.17.refs_13_.refs_12_.refs_14_.refs_7_
  72.6 3.7 %shard_map.113 = (bf16[768,768]{1,0:T(8,128)(2,1)S(1)}, bf16[512,768]{1,0:T(8,128)(2,1)S(1)}) custom-call(bf16[784,384]{1,0:T(8,128)(2,1)S(1)} %collective-permute-done.5.refs_0_.refs_1_.refs_3_, bf16[784,384]{1,0:T(8,128)(2,1)S(1)} %collective-permute-done.6.refs_1_.refs_2_.refs_4_, bf16[784,384]{1,0:T(8,128)(2,1)S(1)} %collective-permute-done.7.refs_2_.refs_3_.refs_5_, ...), custom_call_target="tpu_custom_call" | custom-call | tf_op jit(solution)/shard_map/pallas_call | solution.py:328
  76.2 0.3 collective-permute-start.18
  76.7 2.5 %shard_map.114 = (bf16[256,384]{1,0:T(8,128)(2,1)S(1)}, bf16[256,384]{1,0:T(8,128)(2,1)S(1)}) custom-call(bf16[256,1536]{1,0:T(8,128)(2,1)S(1)} %get-tuple-element.60.refs_0_, bf16[784,384]{1,0:T(8,128)(2,1)S(1)} %collective-permute-done.5.refs_0_.refs_1_.refs_3_, bf16[784,384]{1,0:T(8,128)(2,1)S(1)} %collective-permute-done.6.refs_1_.refs_2_.refs_4_, ...), custom_call_target="tpu_custom_call" | custom-call | tf_op jit(solution)/shard_map/pallas_call | solution.py:328
  79.2 3.8 %shard_map.115 = (bf16[256,384]{1,0:T(8,128)(2,1)S(1)}, bf16[256,384]{1,0:T(8,128)(2,1)S(1)}, f32[256,768]{1,0:T(8,128)S(1)}, bf16[512,768]{1,0:T(8,128)(2,1)S(1)}, bf16[512,768]{1,0:T(8,128)(2,1)}) custom-call(s32[8]{0:T(128)S(1)} %bitcast_convert_fusion.refs_0_, bf16[768,768]{1,0:T(8,128)(2,1)S(1)} %get-tuple-element.58.refs_1_, ...), custom_call_target="tpu_custom_call" | custom-call | tf_op jit(solution)/shard_map/pallas_call | solution.py:328
  83.0 0.3 collective-permute-start.19
  83.3 3.5 %shard_map.116 = (bf16[528,384]{1,0:T(8,128)(2,1)S(1)}, bf16[528,384]{1,0:T(8,128)(2,1)S(1)}, bf16[528,384]{1,0:T(8,128)(2,1)S(1)}, bf16[528,384]{1,0:T(8,128)(2,1)S(1)}) custom-call(bf16[256,384]{1,0:T(8,128)(2,1)S(1)} %get-tuple-element.65.refs_0_, bf16[256,384]{1,0:T(8,128)(2,1)S(1)} %get-tuple-element.66.refs_1_, ...), custom_call_target="tpu_custom_call" | custom-call | tf_op jit(solution)/shard_map/pallas_call | solution.py:328
  87.2 3.4 %collective-permute-start.20 = (bf16[528,384]{1,0:T(8,128)(2,1)S(1)}, bf16[528,384]{1,0:T(8,128)(2,1)S(1)}, u32[]{:S(2)}, u32[]{:S(2)}) collective-permute-start(bf16[528,384]{1,0:T(8,128)(2,1)S(1)} %get-tuple-element.72), channel_id=1, source_target_pairs={{0,0},{1,4},{2,2},{3,6},{4,1},{5,5},{6,3},{7,7},{8,8},{9,12},{10,1... | collective-permute-start | bytes 1216520 | tf_op jit(solution)/shard_map/ppermute | solution.py:35
  90.6 1.4 %collective-permute-start.22 = (bf16[528,384]{1,0:T(8,128)(2,1)S(1)}, bf16[528,384]{1,0:T(8,128)(2,1)S(1)}, u32[]{:S(2)}, u32[]{:S(2)}) collective-permute-start(bf16[528,384]{1,0:T(8,128)(2,1)S(1)} %get-tuple-element.74), channel_id=1, source_target_pairs={{0,2},{1,6},{2,0},{3,4},{4,3},{5,7},{6,1},{7,5},{8,10},{9,14},{10,... | collective-permute-start | bytes 1216520 | tf_op jit(solution)/shard_map/ppermute | solution.py:35
  92.0 3.2 %collective-permute-start.25 = (bf16[256,768]{1,0:T(8,128)(2,1)S(1)}, bf16[256,768]{1,0:T(8,128)(2,1)S(1)}, u32[]{:S(2)}, u32[]{:S(2)}) collective-permute-start(bf16[256,768]{1,0:T(8,128)(2,1)S(1)} %get-tuple-element.80), channel_id=1, source_target_pairs={{0,24},{1,25},{2,26},{3,27},{4,28},{5,29},{6,30},{7,31},{8,0},{9,1... | collective-permute-start | bytes 1179656 | tf_op jit(solution)/shard_map/ppermute | solution.py:35
  95.3 4.2 %collective-permute-done.24.up = bf16[256,768]{1,0:T(8,128)(2,1)S(1)} collective-permute-done((bf16[256,768]{1,0:T(8,128)(2,1)S(1)}, bf16[256,768]{1,0:T(8,128)(2,1)S(1)}, u32[]{:S(2)}, u32[]{:S(2)}) %collective-permute-start.24) | collective-permute-done | bytes 393248 | tf_op jit(solution)/shard_map/ppermute | solution.py:35
  99.4 2.0 %collective-permute-start.23 = (bf16[528,384]{1,0:T(8,128)(2,1)S(1)}, bf16[528,384]{1,0:T(8,128)(2,1)S(1)}, u32[]{:S(2)}, u32[]{:S(2)}) collective-permute-start(bf16[528,384]{1,0:T(8,128)(2,1)S(1)} %get-tuple-element.75), channel_id=1, source_target_pairs={{0,3},{1,7},{2,1},{3,5},{4,2},{5,6},{6,0},{7,4},{8,11},{9,15},{10,... | collective-permute-start | bytes 1216520 | tf_op jit(solution)/shard_map/ppermute | solution.py:35
  101.5 1.8 %shard_map.118.whole = bf16[1536,768]{1,0:T(8,128)(2,1)S(1)} custom-call(bf16[768,384]{1,0:T(8,128)(2,1)} %copy-done.5, bf16[768,384]{1,0:T(8,128)(2,1)} %copy-done, bf16[768,384]{1,0:T(8,128)(2,1)} %copy-done.1, bf16[768,384]{1,0:T(8,128)(2,1)} %copy-done.7, bf16[768,384]{1,0:T(8,128)(2,1)} %copy-done.8, bf16[768,384]{1,0:T(8,128)(2,1)} %copy-done.9, ...), custom_call_target="tpu_custom_call" | custom-call | tf_op jit(solution)/shard_map/pallas_call | solution.py:328
  103.3 5.1 %collective-permute-done.25.down = bf16[256,768]{1,0:T(8,128)(2,1)S(1)} collective-permute-done((bf16[256,768]{1,0:T(8,128)(2,1)S(1)}, bf16[256,768]{1,0:T(8,128)(2,1)S(1)}, u32[]{:S(2)}, u32[]{:S(2)}) %collective-permute-start.25) | collective-permute-done | bytes 393248 | tf_op jit(solution)/shard_map/ppermute | solution.py:35
  108.4 1.0 shard_map.119
  109.4 2.2 %collective-permute-start.29 = (bf16[256,384]{1,0:T(8,128)(2,1)S(1)}, bf16[256,384]{1,0:T(8,128)(2,1)S(1)}, u32[]{:S(2)}, u32[]{:S(2)}) collective-permute-start(bf16[256,384]{1,0:T(8,128)(2,1)S(1)} %get-tuple-element.84), channel_id=1, source_target_pairs={{0,3},{1,7},{2,1},{3,5},{4,2},{5,6},{6,0},{7,4},{8,11},{9,15},{10,... | collective-permute-start | bytes 589832 | tf_op jit(solution)/shard_map/ppermute | solution.py:35
  111.6 0.9 collective-permute-start.28
  112.5 2.7 %collective-permute-start.26 = (bf16[256,384]{1,0:T(8,128)(2,1)S(1)}, bf16[256,384]{1,0:T(8,128)(2,1)S(1)}, u32[]{:S(2)}, u32[]{:S(2)}) collective-permute-start(bf16[256,384]{1,0:T(8,128)(2,1)S(1)} %get-tuple-element.81), channel_id=1, source_target_pairs={{0,0},{1,4},{2,2},{3,6},{4,1},{5,5},{6,3},{7,7},{8,8},{9,12},{10,1... | collective-permute-start | bytes 589832 | tf_op jit(solution)/shard_map/ppermute | solution.py:35
  115.3 1.2 shard_map.117
  116.5 0.3 collective-permute-done.29
  116.7 5.1 %collective-permute-done.28 = bf16[256,384]{1,0:T(8,128)(2,1)S(1)} collective-permute-done((bf16[256,384]{1,0:T(8,128)(2,1)S(1)}, bf16[256,384]{1,0:T(8,128)(2,1)S(1)}, u32[]{:S(2)}, u32[]{:S(2)}) %collective-permute-start.28) | collective-permute-done | bytes 196640 | tf_op jit(solution)/shard_map/ppermute | solution.py:35
  121.8 0.8 collective-permute-done.26
  122.6 0.8 add_convert_fusion
  (71 shorter events, 1.0 us)
Async XLA Ops:
  0.6 10.8 %copy-start.15 = (bf16[2,128,384]{2,1,0:T(8,128)(2,1)S(1)}, bf16[2,128,384]{2,1,0:T(8,128)(2,1)}, u32[]{:S(2)}) copy-start(bf16[2,128,384]{2,1,0:T(8,128)(2,1)} %param.11) | copy-start | bytes 589828
  0.6 10.8 %copy-start.12 = (bf16[256,384]{1,0:T(8,128)(2,1)S(1)}, bf16[256,384]{1,0:T(8,128)(2,1)}, u32[]{:S(2)}) copy-start(bf16[256,384]{1,0:T(8,128)(2,1)} %hidden.1) | copy-start | bytes 589828
  0.7 10.8 %copy-start.14 = (bf16[256,384]{1,0:T(8,128)(2,1)S(1)}, bf16[256,384]{1,0:T(8,128)(2,1)}, u32[]{:S(2)}) copy-start(bf16[256,384]{1,0:T(8,128)(2,1)} %param.17) | copy-start | bytes 589828
  1.9 15.6 %collective-permute-start = (bf16[768,384]{1,0:T(8,128)(2,1)S(1)}, bf16[768,384]{1,0:T(8,128)(2,1)S(1)}, u32[]{:S(2)}, u32[]{:S(2)}) collective-permute-start(bf16[768,384]{1,0:T(8,128)(2,1)S(1)} %pad_maximum_fusion.1), channel_id=1, source_target_pairs={{0,0},{1,4},{2,2},{3,6},{4,1},{5,5},{6,3},{7,7},{8,8},{9,12},{10,1... | collective-permute-start | bytes 1769480 | tf_op jit(solution)/shard_map/ppermute | solution.py:35
  6.5 8.8 %collective-permute-start.1 = (bf16[256,384]{1,0:T(8,128)(2,1)}, bf16[256,384]{1,0:T(8,128)(2,1)S(1)}, u32[]{:S(2)}, u32[]{:S(2)}) collective-permute-start(bf16[256,384]{1,0:T(8,128)(2,1)} %bitcast.6), channel_id=1, source_target_pairs={{0,8},{1,9},{2,10},{3,11},{4,12},{5,13},{6,14},{7,15},{8,16},{9,17... | collective-permute-start | bytes 589832 | tf_op jit(solution)/shard_map/ppermute | solution.py:35
  7.8 9.7 %collective-permute-start.2 = (bf16[256,384]{1,0:T(8,128)(2,1)}, bf16[256,384]{1,0:T(8,128)(2,1)}, u32[]{:S(2)}, u32[]{:S(2)}) collective-permute-start(bf16[256,384]{1,0:T(8,128)(2,1)} %bitcast.7), channel_id=1, source_target_pairs={{0,24},{1,25},{2,26},{3,27},{4,28},{5,29},{6,30},{7,31},{8,0},{9,1... | collective-permute-start | bytes 589832 | tf_op jit(solution)/shard_map/ppermute | solution.py:35
  17.5 6.7 %copy-start.5 = (bf16[768,384]{1,0:T(8,128)(2,1)}, bf16[768,384]{1,0:T(8,128)(2,1)S(1)}, u32[]{:S(2)}) copy-start(bf16[768,384]{1,0:T(8,128)(2,1)S(1)} %collective-permute-done.refs_6_.refs_5_.refs_7_.refs_0_) | copy-start | bytes 1769476
  17.5 16.3 %collective-permute-start.3 = (bf16[768,384]{1,0:T(8,128)(2,1)S(1)}, bf16[768,384]{1,0:T(8,128)(2,1)S(1)}, u32[]{:S(2)}, u32[]{:S(2)}) collective-permute-start(bf16[768,384]{1,0:T(8,128)(2,1)S(1)} %collective-permute-done.refs_6_.refs_5_.refs_7_.refs_0_), channel_id=1, source_target_pairs={{0,8},{1,9},{2,10},{3,11},{4,12},{5,13},{6,14},{7,15},{8,16},{9,17... | collective-permute-start | bytes 1769480 | tf_op jit(solution)/shard_map/ppermute | solution.py:35
  17.7 3.6 %collective-permute-start.10 = (bf16[256,384]{1,0:T(8,128)(2,1)S(1)}, bf16[256,384]{1,0:T(8,128)(2,1)}, u32[]{:S(2)}, u32[]{:S(2)}) collective-permute-start(bf16[256,384]{1,0:T(8,128)(2,1)S(1)} %collective-permute-done.1), channel_id=1, source_target_pairs={{0,1},{1,0},{2,3},{3,2},{4,5},{5,4},{6,7},{7,6},{8,9},{9,8},{10,11... | collective-permute-start | bytes 589832 | tf_op jit(solution)/shard_map/ppermute | solution.py:35
  18.4 5.0 %collective-permute-start.11 = (bf16[256,384]{1,0:T(8,128)(2,1)}, bf16[256,384]{1,0:T(8,128)(2,1)S(1)}, u32[]{:S(2)}, u32[]{:S(2)}) collective-permute-start(bf16[256,384]{1,0:T(8,128)(2,1)} %collective-permute-done.2), channel_id=1, source_target_pairs={{0,1},{1,0},{2,3},{3,2},{4,5},{5,4},{6,7},{7,6},{8,9},{9,8},{10,11... | collective-permute-start | bytes 589832 | tf_op jit(solution)/shard_map/ppermute | solution.py:35
  18.4 31.5 %collective-permute-start.5 = (bf16[784,384]{1,0:T(8,128)(2,1)}, bf16[784,384]{1,0:T(8,128)(2,1)S(1)}, u32[]{:S(2)}, u32[]{:S(2)}) collective-permute-start(bf16[784,384]{1,0:T(8,128)(2,1)} %pad_maximum_fusion), channel_id=1, source_target_pairs={{0,0},{1,4},{2,2},{3,6},{4,1},{5,5},{6,3},{7,7},{8,8},{9,12},{10,1... | collective-permute-start | bytes 1806344 | tf_op jit(solution)/shard_map/ppermute | solution.py:35
  21.3 31.2 %collective-permute-start.6 = (bf16[784,384]{1,0:T(8,128)(2,1)}, bf16[784,384]{1,0:T(8,128)(2,1)S(1)}, u32[]{:S(2)}, u32[]{:S(2)}) collective-permute-start(bf16[784,384]{1,0:T(8,128)(2,1)} %pad_maximum_fusion), channel_id=1, source_target_pairs={{0,4},{1,0},{2,6},{3,2},{4,5},{5,1},{6,7},{7,3},{8,12},{9,8},{10,1... | collective-permute-start | bytes 1806344 | tf_op jit(solution)/shard_map/ppermute | solution.py:35
  21.4 31.2 %collective-permute-start.7 = (bf16[784,384]{1,0:T(8,128)(2,1)}, bf16[784,384]{1,0:T(8,128)(2,1)S(1)}, u32[]{:S(2)}, u32[]{:S(2)}) collective-permute-start(bf16[784,384]{1,0:T(8,128)(2,1)} %pad_maximum_fusion), channel_id=1, source_target_pairs={{0,2},{1,6},{2,0},{3,4},{4,3},{5,7},{6,1},{7,5},{8,10},{9,14},{10,... | collective-permute-start | bytes 1806344 | tf_op jit(solution)/shard_map/ppermute | solution.py:35
  23.4 10.3 %copy-start.16 = (bf16[256,384]{1,0:T(8,128)(2,1)}, bf16[256,384]{1,0:T(8,128)(2,1)S(1)}, u32[]{:S(2)}) copy-start(bf16[256,384]{1,0:T(8,128)(2,1)S(1)} %collective-permute-done.11) | copy-start | bytes 589828
  23.4 29.1 %collective-permute-start.8 = (bf16[784,384]{1,0:T(8,128)(2,1)}, bf16[784,384]{1,0:T(8,128)(2,1)}, u32[]{:S(2)}, u32[]{:S(2)}) collective-permute-start(bf16[784,384]{1,0:T(8,128)(2,1)} %pad_maximum_fusion), channel_id=1, source_target_pairs={{0,6},{1,2},{2,4},{3,0},{4,7},{5,3},{6,5},{7,1},{8,14},{9,10},{10,... | collective-permute-start | bytes 1806344 | tf_op jit(solution)/shard_map/ppermute | solution.py:35
  33.8 42.8 %copy-start = (bf16[768,384]{1,0:T(8,128)(2,1)}, bf16[768,384]{1,0:T(8,128)(2,1)S(1)}, u32[]{:S(2)}) copy-start(bf16[768,384]{1,0:T(8,128)(2,1)S(1)} %collective-permute-done.3.refs_7_.refs_6_.refs_8_.refs_1_) | copy-start | bytes 1769476
  33.8 13.9 %collective-permute-start.4 = (bf16[768,384]{1,0:T(8,128)(2,1)}, bf16[768,384]{1,0:T(8,128)(2,1)S(1)}, u32[]{:S(2)}, u32[]{:S(2)}) collective-permute-start(bf16[768,384]{1,0:T(8,128)(2,1)} %copy-done.5), channel_id=1, source_target_pairs={{0,24},{1,25},{2,26},{3,27},{4,28},{5,29},{6,30},{7,31},{8,0},{9,1... | collective-permute-start | bytes 1769480 | tf_op jit(solution)/shard_map/ppermute | solution.py:35
  33.8 2.3 %copy-start.17 = (bf16[256,384]{1,0:T(8,128)(2,1)S(1)}, bf16[256,384]{1,0:T(8,128)(2,1)}, u32[]{:S(2)}) copy-start(bf16[256,384]{1,0:T(8,128)(2,1)} %copy-done.16) | copy-start | bytes 589828
  35.1 17.7 %copy-start.6 = (bf16[768,384]{1,0:T(8,128)(2,1)S(1)}, bf16[768,384]{1,0:T(8,128)(2,1)}, u32[]{:S(2)}) copy-start(bf16[768,384]{1,0:T(8,128)(2,1)} %copy-done.5) | copy-start | bytes 1769476
  47.7 28.9 %copy-start.1 = (bf16[768,384]{1,0:T(8,128)(2,1)}, bf16[768,384]{1,0:T(8,128)(2,1)S(1)}, u32[]{:S(2)}) copy-start(bf16[768,384]{1,0:T(8,128)(2,1)S(1)} %collective-permute-done.4.refs_8_.refs_7_.refs_9_.refs_2_) | copy-start | bytes 1769476
  47.7 22.0 %collective-permute-start.12 = (bf16[1024,384]{1,0:T(8,128)(2,1)S(1)}, bf16[1024,384]{1,0:T(8,128)(2,1)S(1)}, u32[]{:S(2)}, u32[]{:S(2)}) collective-permute-start(bf16[1024,384]{1,0:T(8,128)(2,1)S(1)} %constant_dynamic-update-slice_fusion), channel_id=1, source_target_pairs={{0,0},{1,4},{2,2},{3,6},{4,1},{5,5},{6,3},{7,7},{8,8},{9,12},{10,1... | collective-permute-start | bytes 2359304 | tf_op jit(solution)/shard_map/ppermute | solution.py:35
  49.9 26.7 %copy-start.2 = (bf16[784,384]{1,0:T(8,128)(2,1)}, bf16[784,384]{1,0:T(8,128)(2,1)S(1)}, u32[]{:S(2)}) copy-start(bf16[784,384]{1,0:T(8,128)(2,1)S(1)} %collective-permute-done.5.refs_0_.refs_1_.refs_3_) | copy-start | bytes 1806340
  49.9 19.8 %collective-permute-start.13 = (bf16[1024,384]{1,0:T(8,128)(2,1)S(1)}, bf16[1024,384]{1,0:T(8,128)(2,1)S(1)}, u32[]{:S(2)}, u32[]{:S(2)}) collective-permute-start(bf16[1024,384]{1,0:T(8,128)(2,1)S(1)} %constant_dynamic-update-slice_fusion), channel_id=1, source_target_pairs={{0,2},{1,6},{2,0},{3,4},{4,3},{5,7},{6,1},{7,5},{8,10},{9,14},{10,... | collective-permute-start | bytes 2359304 | tf_op jit(solution)/shard_map/ppermute | solution.py:35
  52.5 24.1 %copy-start.3 = (bf16[784,384]{1,0:T(8,128)(2,1)}, bf16[784,384]{1,0:T(8,128)(2,1)S(1)}, u32[]{:S(2)}) copy-start(bf16[784,384]{1,0:T(8,128)(2,1)S(1)} %collective-permute-done.6.refs_1_.refs_2_.refs_4_) | copy-start | bytes 1806340
  52.6 24.1 %copy-start.4 = (bf16[784,384]{1,0:T(8,128)(2,1)}, bf16[784,384]{1,0:T(8,128)(2,1)S(1)}, u32[]{:S(2)}) copy-start(bf16[784,384]{1,0:T(8,128)(2,1)S(1)} %collective-permute-done.7.refs_2_.refs_3_.refs_5_) | copy-start | bytes 1806340
  52.7 17.0 %collective-permute-start.9 = (bf16[768,384]{1,0:T(8,128)(2,1)S(1)}, bf16[768,384]{1,0:T(8,128)(2,1)S(1)}, u32[]{:S(2)}, u32[]{:S(2)}) collective-permute-start(bf16[768,384]{1,0:T(8,128)(2,1)S(1)} %broadcast_select_fusion), channel_id=1, source_target_pairs={{0,8},{1,9},{2,10},{3,11},{4,12},{5,13},{6,14},{7,15},{8,0},{9,1},... | collective-permute-start | bytes 1769480 | tf_op jit(solution)/shard_map/ppermute | solution.py:35
  52.8 18.0 %collective-permute-start.14 = (bf16[768,384]{1,0:T(8,128)(2,1)S(1)}, bf16[768,384]{1,0:T(8,128)(2,1)S(1)}, u32[]{:S(2)}, u32[]{:S(2)}) collective-permute-start(bf16[768,384]{1,0:T(8,128)(2,1)S(1)} %copy-done.6), channel_id=1, source_target_pairs={{0,1},{1,0},{2,3},{3,2},{4,5},{5,4},{6,7},{7,6},{8,9},{9,8},{10,11... | collective-permute-start | bytes 1769480 | tf_op jit(solution)/shard_map/ppermute | solution.py:35
  52.8 18.0 %collective-permute-start.15 = (bf16[768,384]{1,0:T(8,128)(2,1)S(1)}, bf16[768,384]{1,0:T(8,128)(2,1)S(1)}, u32[]{:S(2)}, u32[]{:S(2)}) collective-permute-start(bf16[768,384]{1,0:T(8,128)(2,1)S(1)} %collective-permute-done.3.refs_7_.refs_6_.refs_8_.refs_1_), channel_id=1, source_target_pairs={{0,1},{1,0},{2,3},{3,2},{4,5},{5,4},{6,7},{7,6},{8,9},{9,8},{10,11... | collective-permute-start | bytes 1769480 | tf_op jit(solution)/shard_map/ppermute | solution.py:35
  69.7 2.0 %collective-permute-start.16 = (bf16[768,384]{1,0:T(8,128)(2,1)S(1)}, bf16[768,384]{1,0:T(8,128)(2,1)S(1)}, u32[]{:S(2)}, u32[]{:S(2)}) collective-permute-start(bf16[768,384]{1,0:T(8,128)(2,1)S(1)} %collective-permute-done.4.refs_8_.refs_7_.refs_9_.refs_2_), channel_id=1, source_target_pairs={{0,1},{1,0},{2,3},{3,2},{4,5},{5,4},{6,7},{7,6},{8,9},{9,8},{10,11... | collective-permute-start | bytes 1769480 | tf_op jit(solution)/shard_map/ppermute | solution.py:35
  69.7 6.9 %copy-start.7 = (bf16[768,384]{1,0:T(8,128)(2,1)}, bf16[768,384]{1,0:T(8,128)(2,1)S(1)}, u32[]{:S(2)}) copy-start(bf16[768,384]{1,0:T(8,128)(2,1)S(1)} %collective-permute-done.9.refs_9_.refs_8_.refs_10_.refs_3_) | copy-start | bytes 1769476
  69.7 2.8 %collective-permute-start.17 = (bf16[768,384]{1,0:T(8,128)(2,1)S(1)}, bf16[768,384]{1,0:T(8,128)(2,1)S(1)}, u32[]{:S(2)}, u32[]{:S(2)}) collective-permute-start(bf16[768,384]{1,0:T(8,128)(2,1)S(1)} %collective-permute-done.9.refs_9_.refs_8_.refs_10_.refs_3_), channel_id=1, source_target_pairs={{0,1},{1,0},{2,3},{3,2},{4,5},{5,4},{6,7},{7,6},{8,9},{9,8},{10,11... | collective-permute-start | bytes 1769480 | tf_op jit(solution)/shard_map/ppermute | solution.py:35
  70.8 5.8 %copy-start.8 = (bf16[768,384]{1,0:T(8,128)(2,1)}, bf16[768,384]{1,0:T(8,128)(2,1)S(1)}, u32[]{:S(2)}) copy-start(bf16[768,384]{1,0:T(8,128)(2,1)S(1)} %collective-permute-done.14.refs_10_.refs_9_.refs_11_.refs_4_) | copy-start | bytes 1769476
  70.8 5.8 %copy-start.9 = (bf16[768,384]{1,0:T(8,128)(2,1)}, bf16[768,384]{1,0:T(8,128)(2,1)S(1)}, u32[]{:S(2)}) copy-start(bf16[768,384]{1,0:T(8,128)(2,1)S(1)} %collective-permute-done.15.refs_11_.refs_10_.refs_12_.refs_5_) | copy-start | bytes 1769476
  71.7 4.9 %copy-start.10 = (bf16[768,384]{1,0:T(8,128)(2,1)}, bf16[768,384]{1,0:T(8,128)(2,1)S(1)}, u32[]{:S(2)}) copy-start(bf16[768,384]{1,0:T(8,128)(2,1)S(1)} %collective-permute-done.16.refs_12_.refs_11_.refs_13_.refs_6_) | copy-start | bytes 1769476
  72.6 4.1 %copy-start.11 = (bf16[768,384]{1,0:T(8,128)(2,1)}, bf16[768,384]{1,0:T(8,128)(2,1)S(1)}, u32[]{:S(2)}) copy-start(bf16[768,384]{1,0:T(8,128)(2,1)S(1)} %collective-permute-done.17.refs_13_.refs_12_.refs_14_.refs_7_) | copy-start | bytes 1769476
  76.2 3.0 %collective-permute-start.18 = (bf16[512,768]{1,0:T(8,128)(2,1)S(1)}, bf16[512,768]{1,0:T(8,128)(2,1)S(1)}, u32[]{:S(2)}, u32[]{:S(2)}) collective-permute-start(bf16[512,768]{1,0:T(8,128)(2,1)S(1)} %get-tuple-element.59), channel_id=1, source_target_pairs={{0,1},{1,0},{2,3},{3,2},{4,5},{5,4},{6,7},{7,6},{8,9},{9,8},{10,11... | collective-permute-start | bytes 2359304 | tf_op jit(solution)/shard_map/ppermute | solution.py:35
  83.0 3.8 %collective-permute-start.19 = (bf16[512,768]{1,0:T(8,128)(2,1)}, bf16[512,768]{1,0:T(8,128)(2,1)S(1)}, u32[]{:S(2)}, u32[]{:S(2)}) collective-permute-start(bf16[512,768]{1,0:T(8,128)(2,1)} %get-tuple-element.64), channel_id=1, source_target_pairs={{0,1},{1,0},{2,3},{3,2},{4,5},{5,4},{6,7},{7,6},{8,9},{9,8},{10,11... | collective-permute-start | bytes 2359304 | tf_op jit(solution)/shard_map/ppermute | solution.py:35
  87.1 12.3 %collective-permute-start.24 = (bf16[256,768]{1,0:T(8,128)(2,1)S(1)}, bf16[256,768]{1,0:T(8,128)(2,1)S(1)}, u32[]{:S(2)}, u32[]{:S(2)}) collective-permute-start(bf16[256,768]{1,0:T(8,128)(2,1)S(1)} %get-tuple-element.79), channel_id=1, source_target_pairs={{0,8},{1,9},{2,10},{3,11},{4,12},{5,13},{6,14},{7,15},{8,16},{9,17... | collective-permute-start | bytes 1179656 | tf_op jit(solution)/shard_map/ppermute | solution.py:35
  87.2 24.5 %collective-permute-start.20 = (bf16[528,384]{1,0:T(8,128)(2,1)S(1)}, bf16[528,384]{1,0:T(8,128)(2,1)S(1)}, u32[]{:S(2)}, u32[]{:S(2)}) collective-permute-start(bf16[528,384]{1,0:T(8,128)(2,1)S(1)} %get-tuple-element.72), channel_id=1, source_target_pairs={{0,0},{1,4},{2,2},{3,6},{4,1},{5,5},{6,3},{7,7},{8,8},{9,12},{10,1... | collective-permute-start | bytes 1216520 | tf_op jit(solution)/shard_map/ppermute | solution.py:35
  90.6 21.9 %collective-permute-start.21 = (bf16[528,384]{1,0:T(8,128)(2,1)S(1)}, bf16[528,384]{1,0:T(8,128)(2,1)S(1)}, u32[]{:S(2)}, u32[]{:S(2)}) collective-permute-start(bf16[528,384]{1,0:T(8,128)(2,1)S(1)} %get-tuple-element.73), channel_id=1, source_target_pairs={{0,1},{1,5},{2,3},{3,7},{4,0},{5,4},{6,2},{7,6},{8,9},{9,13},{10,1... | collective-permute-start | bytes 1216520 | tf_op jit(solution)/shard_map/ppermute | solution.py:35
  90.6 21.9 %collective-permute-start.22 = (bf16[528,384]{1,0:T(8,128)(2,1)S(1)}, bf16[528,384]{1,0:T(8,128)(2,1)S(1)}, u32[]{:S(2)}, u32[]{:S(2)}) collective-permute-start(bf16[528,384]{1,0:T(8,128)(2,1)S(1)} %get-tuple-element.74), channel_id=1, source_target_pairs={{0,2},{1,6},{2,0},{3,4},{4,3},{5,7},{6,1},{7,5},{8,10},{9,14},{10,... | collective-permute-start | bytes 1216520 | tf_op jit(solution)/shard_map/ppermute | solution.py:35
  92.0 16.4 %collective-permute-start.25 = (bf16[256,768]{1,0:T(8,128)(2,1)S(1)}, bf16[256,768]{1,0:T(8,128)(2,1)S(1)}, u32[]{:S(2)}, u32[]{:S(2)}) collective-permute-start(bf16[256,768]{1,0:T(8,128)(2,1)S(1)} %get-tuple-element.80), channel_id=1, source_target_pairs={{0,24},{1,25},{2,26},{3,27},{4,28},{5,29},{6,30},{7,31},{8,0},{9,1... | collective-permute-start | bytes 1179656 | tf_op jit(solution)/shard_map/ppermute | solution.py:35
  99.4 15.9 %collective-permute-start.23 = (bf16[528,384]{1,0:T(8,128)(2,1)S(1)}, bf16[528,384]{1,0:T(8,128)(2,1)S(1)}, u32[]{:S(2)}, u32[]{:S(2)}) collective-permute-start(bf16[528,384]{1,0:T(8,128)(2,1)S(1)} %get-tuple-element.75), channel_id=1, source_target_pairs={{0,3},{1,7},{2,1},{3,5},{4,2},{5,6},{6,0},{7,4},{8,11},{9,15},{10,... | collective-permute-start | bytes 1216520 | tf_op jit(solution)/shard_map/ppermute | solution.py:35
  108.4 6.9 %copy-start.13 = (bf16[384]{0:T(512)(128)(2,1)S(1)}, bf16[384]{0:T(512)(128)(2,1)}, u32[]{:S(2)}) copy-start(bf16[384]{0:T(512)(128)(2,1)} %gain.1) | copy-start | bytes 2308
  109.4 7.3 %collective-permute-start.29 = (bf16[256,384]{1,0:T(8,128)(2,1)S(1)}, bf16[256,384]{1,0:T(8,128)(2,1)S(1)}, u32[]{:S(2)}, u32[]{:S(2)}) collective-permute-start(bf16[256,384]{1,0:T(8,128)(2,1)S(1)} %get-tuple-element.84), channel_id=1, source_target_pairs={{0,3},{1,7},{2,1},{3,5},{4,2},{5,6},{6,0},{7,4},{8,11},{9,15},{10,... | collective-permute-start | bytes 589832 | tf_op jit(solution)/shard_map/ppermute | solution.py:35
  111.6 10.2 %collective-permute-start.28 = (bf16[256,384]{1,0:T(8,128)(2,1)S(1)}, bf16[256,384]{1,0:T(8,128)(2,1)S(1)}, u32[]{:S(2)}, u32[]{:S(2)}) collective-permute-start(bf16[256,384]{1,0:T(8,128)(2,1)S(1)} %get-tuple-element.83), channel_id=1, source_target_pairs={{0,2},{1,6},{2,0},{3,4},{4,3},{5,7},{6,1},{7,5},{8,10},{9,14},{10,... | collective-permute-start | bytes 589832 | tf_op jit(solution)/shard_map/ppermute | solution.py:35
  112.5 9.3 %collective-permute-start.27 = (bf16[256,384]{1,0:T(8,128)(2,1)S(1)}, bf16[256,384]{1,0:T(8,128)(2,1)S(1)}, u32[]{:S(2)}, u32[]{:S(2)}) collective-permute-start(bf16[256,384]{1,0:T(8,128)(2,1)S(1)} %get-tuple-element.82), channel_id=1, source_target_pairs={{0,1},{1,5},{2,3},{3,7},{4,0},{5,4},{6,2},{7,6},{8,9},{9,13},{10,1... | collective-permute-start | bytes 589832 | tf_op jit(solution)/shard_map/ppermute | solution.py:35
  112.5 10.0 %collective-permute-start.26 = (bf16[256,384]{1,0:T(8,128)(2,1)S(1)}, bf16[256,384]{1,0:T(8,128)(2,1)S(1)}, u32[]{:S(2)}, u32[]{:S(2)}) collective-permute-start(bf16[256,384]{1,0:T(8,128)(2,1)S(1)} %get-tuple-element.81), channel_id=1, source_target_pairs={{0,0},{1,4},{2,2},{3,6},{4,1},{5,5},{6,3},{7,7},{8,8},{9,12},{10,1... | collective-permute-start | bytes 589832 | tf_op jit(solution)/shard_map/ppermute | solution.py:35

commit v8 on v7

--- a/solution.py
+++ b/solution.py
@@ -112,10 +112,17 @@
 
 
 def block(refs, k, start, rows):
-    if len(refs) == 4:
-        return refs[k].at[pl.ds(start, rows)]
     ref = refs[k // 2]
     return ref.at[pl.ds((k % 2) * (ref.shape[0] // 2) + start, rows)]
+
+
+def join_kernel(*refs):
+    parts, (out, sems) = refs[:-2], refs[-2:]
+    pairs, start = [], 0
+    for part in parts:
+        pairs.append((part, out.at[pl.ds(start, part.shape[0])]))
+        start += part.shape[0]
+    run_copies(pairs, sems)
 
 
 def whole_kernel(*refs):
@@ -124,7 +131,7 @@
 
 
 def norm_kernel(token_count, *refs):
-    tokens, (normed, inv_out, rows_in, sems) = refs[:4], refs[4:]
+    tokens, (normed, inv_out, rows_in, sems) = refs[:2], refs[2:]
     width = tokens[0].shape[1]
     run_copies(
         [(block(tokens, k, 0, token_count + EXTRA), rows_in.at[k]) for k in range(4)],
@@ -144,8 +151,8 @@
 
 
 def table_kernel(token_count, *refs):
-    tokens, outers = refs[:4], refs[4:6]
-    pieces, (tables, shared, whole, encs, sems) = refs[6:-5], refs[-5:]
+    tokens, outers = refs[:2], refs[2:4]
+    pieces, (tables, shared, whole, encs, sems) = refs[4:-5], refs[-5:]
     width = tokens[0].shape[1]
     pairs = weight_copies(pieces, whole, 0)
     sources = ((outers, 0), (tokens, 2 * token_count + EXTRA), (outers, OWN_ROWS))
@@ -162,8 +169,8 @@
 
 
 def query_kernel(token_count, *refs):
-    normed, tokens = refs[0], refs[1:5]
-    pieces, (queries, d_attended, whole, rows_in, grads, sems) = refs[5:-6], refs[-6:]
+    normed, tokens = refs[0], refs[1:3]
+    pieces, (queries, d_attended, whole, rows_in, grads, sems) = refs[3:-6], refs[-6:]
     width = tokens[0].shape[1]
     pairs = weight_copies(pieces, whole, 2) + [(normed, rows_in)]
     for k in range(4):
@@ -250,8 +257,8 @@
 
 
 def product_kernel(*refs):
-    attended, d_queries, inv_rms, tokens = refs[0], refs[1], refs[2], refs[3:7]
-    pieces, outs, (whole, rows_in, sems) = refs[7:-7], refs[-7:-3], refs[-3:]
+    attended, d_queries, inv_rms, tokens = refs[0], refs[1], refs[2], refs[3:5]
+    pieces, outs, (whole, rows_in, sems) = refs[5:-7], refs[-7:-3], refs[-3:]
     token_count, width = attended.shape
     term_rows = 2 * token_count + EXTRA
     pairs = weight_copies(pieces, whole, 2)
@@ -335,6 +342,18 @@
     )(*operands)
 
 
+def join(parts):
+    rows = sum(part.shape[0] for part in parts)
+    return call(
+        join_kernel,
+        parts,
+        [ANY] * len(parts),
+        [((rows, parts[0].shape[1]), LOW)],
+        copies=len(parts),
+        out_specs=[ANY],
+    )[0]
+
+
 def shards(hidden_rows, norm_gain, encodings, w_query, w_key, w_value, w_out, neighbours, grad_out):
     seq_count = lax.axis_size("seq")
     z, y, x, c = place()
@@ -349,12 +368,13 @@
     enc_below, enc_above = move(own_enc, ring_up), move(own_enc, ring_down)
     id_row = jnp.pad(neighbours.reshape(1, ids).astype(LOW), ((1, EXTRA - 2), (0, width - ids)))
     extra = jnp.pad(norm_gain[None, :], ((0, EXTRA - 1), (0, 0))) + id_row
-    packed = jnp.concatenate([hidden_rows, extra, grad_out, own_enc], axis=0)
-    weights, enc_below, enc_above, packed = tie(weights, enc_below, enc_above, packed)
-    tokens = [move(packed, spread(k)) for k in range(4)]
-    outer = jnp.concatenate(
-        [enc_below, enc_above, move(enc_below, flip_core), move(enc_above, flip_core)], axis=0
-    )
+    parts = [jnp.concatenate([hidden_rows, extra], axis=0), jnp.concatenate([grad_out, own_enc], axis=0)]
+    packed = join(parts + [move(part, flip_core) for part in parts])
+    weights, enc_below, enc_above = tie(weights, enc_below, enc_above)
+    below_other = move(enc_below, flip_core)
+    packed, below_other = tie(packed, below_other)
+    tokens = [move(packed, spread(0)), move(packed, spread(2))]
+    outer = jnp.concatenate([enc_below, enc_above, below_other, move(enc_above, flip_core)], axis=0)
     if seq_count == 8:
         below, above = move(weights, ring_up), move(weights, ring_down)
         below, above, *tokens = tie(below, above, *tokens)
@@ -362,7 +382,7 @@
     normed, inv_rms = call(
         lambda *refs: norm_kernel(token_count, *refs),
         tokens,
-        [ANY] * 4,
+        [ANY] * 2,
         [((token_count, full_width), LOW), ((token_count, 1), F32)],
         [pltpu.VMEM((4, token_count + EXTRA, width), LOW)],
         4,
@@ -381,7 +401,7 @@
     tables, shared = call(
         lambda *refs: table_kernel(token_count, *refs),
         tokens + outers + kv_pieces,
-        [ANY] * (6 + piece_count),
+        [ANY] * (4 + piece_count),
         [((3 * OWN_ROWS, wide), LOW), ((2 * OWN_ROWS, wide), LOW)],
         [pltpu.VMEM((full_width, wide), LOW), pltpu.VMEM((3 * OWN_ROWS, full_width), LOW)],
         12 + 2 * piece_count,
@@ -390,7 +410,7 @@
     queries, d_attended = call(
         lambda *refs: query_kernel(token_count, *refs),
         [normed] + tokens + qo_pieces,
-        [ANY] * (5 + piece_count),
+        [ANY] * (3 + piece_count),
         [((token_count, width), LOW), ((token_count, width), LOW)],
         [pltpu.VMEM((full_width, wide), LOW)] + [pltpu.VMEM((token_count, full_width), LOW)] * 2,
         5 + 2 * piece_count,
@@ -417,7 +437,7 @@
     terms = call(
         product_kernel,
         [attended, d_queries, inv_rms] + [in_hbm(o) for o in tokens + qo_pieces],
-        [VMEM, VMEM, VMEM] + [ANY] * (4 + piece_count),
+        [VMEM, VMEM, VMEM] + [ANY] * (2 + piece_count),
         [((2 * token_count + EXTRA, width), LOW)] * 4,
         [
             pltpu.VMEM((full_width, wide), LOW),

time: 124 us -> 121 us (0.976)
  waiting for transfers between devices: 57.7 us -> 55 us
  starting transfers between devices: 37.8 us -> 39.9 us
  other arithmetic: 3.94 us -> 2.43 us
    ppermute x30, waiting for transfers between devices: 57.7 us -> 55 us  [move(): return lax.ppermute(value, ('seq', 'mp'), pairs)]
    ppermute x30, starting transfers between devices: 37.8 us -> 39.9 us  [move(): return lax.ppermute(value, ('seq', 'mp'), pairs)]
    pallas_call x8 -> x9, Pallas kernels: 19.6 us -> 19.7 us  [call(): pl.pallas_call(kernel, out_shape=[jax.ShapeDtypeStruct(shape, dtype) for...]
  transfers between devices with their start and end apart: 30 -> 30, of which waited for: 12 -> 14; matrix products, arithmetic and copies ran while one was open for 4% -> 2% of each run, Pallas kernels for 10% -> 10%
where the time goes in v8:
time: 121 us; the launch traced here: 120 us
  waiting for transfers between devices  55 us (45%)
  starting transfers between devices  39.9 us (33%)
  Pallas kernels  19.7 us (16%)
  other arithmetic  2.43 us (2%)
  local copies, waits for them, and re-layouts  2.23 us (2%)
    ppermute x30, waiting for transfers between devices, move(): return lax.ppermute(value, ('seq', 'mp'), pairs)  55 us
    ppermute x30, starting transfers between devices, move(): return lax.ppermute(value, ('seq', 'mp'), pairs)  39.9 us
    pallas_call x9, Pallas kernels, call(): pl.pallas_call(kernel, out_shape=[jax.ShapeDtypeStruct(shape, dtype) for...  19.7 us
  transfers between devices with their start and end apart: 30, of which 14 were waited for; matrix products, arithmetic and copies ran while one was open for 2% of the time, Pallas kernels for 10%

profile of v8, /device:TPU:1, one launch (start us, length us, event | category | flops | bytes accessed | tf_op | source)
XLA Modules:
  0.0 120.3 jit_solution(13252353753433587539)
XLA Ops:
  0.7 1.3 %pad_maximum_fusion = bf16[768,384]{1,0:T(8,128)(2,1)S(1)} fusion(bf16[192,384]{1,0:T(8,128)(2,1)} %bitcast.10, bf16[192,384]{1,0:T(8,128)(2,1)} %param.12, bf16[192,384]{1,0:T(8,128)(2,1)} %param.14, bf16[192,384]{1,0:T(8,128)(2,1)} %param.13), kind=kLoop, calls=%fused_computation.6 | loop fusion | flops 2359296 | bytes 1179648 | tf_op jit(solution)/shard_map/concatenate | solution.py:367
  1.9 4.5 %collective-permute-start = (bf16[768,384]{1,0:T(8,128)(2,1)S(1)}, bf16[768,384]{1,0:T(8,128)(2,1)S(1)}, u32[]{:S(2)}, u32[]{:S(2)}) collective-permute-start(bf16[768,384]{1,0:T(8,128)(2,1)S(1)} %pad_maximum_fusion), channel_id=1, source_target_pairs={{0,0},{1,4},{2,2},{3,6},{4,1},{5,5},{6,3},{7,7},{8,8},{9,12},{10,1... | collective-permute-start | bytes 1769480 | tf_op jit(solution)/shard_map/ppermute | solution.py:35
  6.5 1.3 %collective-permute-start.1 = (bf16[256,384]{1,0:T(8,128)(2,1)S(1)}, bf16[256,384]{1,0:T(8,128)(2,1)S(1)}, u32[]{:S(2)}, u32[]{:S(2)}) collective-permute-start(bf16[256,384]{1,0:T(8,128)(2,1)S(1)} %bitcast.6), channel_id=1, source_target_pairs={{0,8},{1,9},{2,10},{3,11},{4,12},{5,13},{6,14},{7,15},{8,16},{9,17... | collective-permute-start | bytes 589832 | tf_op jit(solution)/shard_map/ppermute | solution.py:35
  7.8 2.1 %collective-permute-start.2 = (bf16[256,384]{1,0:T(8,128)(2,1)S(1)}, bf16[256,384]{1,0:T(8,128)(2,1)S(1)}, u32[]{:S(2)}, u32[]{:S(2)}) collective-permute-start(bf16[256,384]{1,0:T(8,128)(2,1)S(1)} %bitcast.7), channel_id=1, source_target_pairs={{0,24},{1,25},{2,26},{3,27},{4,28},{5,29},{6,30},{7,31},{8,0},{9,1... | collective-permute-start | bytes 589832 | tf_op jit(solution)/shard_map/ppermute | solution.py:35
  10.3 0.6 collective-permute-start.5
  10.9 4.2 %collective-permute-done.1 = bf16[256,384]{1,0:T(8,128)(2,1)S(1)} collective-permute-done((bf16[256,384]{1,0:T(8,128)(2,1)S(1)}, bf16[256,384]{1,0:T(8,128)(2,1)S(1)}, u32[]{:S(2)}, u32[]{:S(2)}) %collective-permute-start.1) | collective-permute-done | bytes 196640 | tf_op jit(solution)/shard_map/ppermute | solution.py:35
  15.1 2.1 %collective-permute-done.2 = bf16[256,384]{1,0:T(8,128)(2,1)S(1)} collective-permute-done((bf16[256,384]{1,0:T(8,128)(2,1)S(1)}, bf16[256,384]{1,0:T(8,128)(2,1)S(1)}, u32[]{:S(2)}, u32[]{:S(2)}) %collective-permute-start.2) | collective-permute-done | bytes 196640 | tf_op jit(solution)/shard_map/ppermute | solution.py:35
  17.2 0.4 collective-permute-start.7
  17.6 1.1 shard_map.112
  18.8 2.2 %collective-permute-start.8 = (bf16[1568,384]{1,0:T(8,128)(2,1)}, bf16[1568,384]{1,0:T(8,128)(2,1)S(1)}, u32[]{:S(2)}, u32[]{:S(2)}) collective-permute-start(bf16[1568,384]{1,0:T(8,128)(2,1)} %shard_map.112), channel_id=1, source_target_pairs={{0,0},{1,4},{2,2},{3,6},{4,1},{5,5},{6,3},{7,7},{8,8},{9,12},{10,1... | collective-permute-start | bytes 3612680 | tf_op jit(solution)/shard_map/ppermute | solution.py:35
  21.0 2.3 %collective-permute-start.9 = (bf16[1568,384]{1,0:T(8,128)(2,1)}, bf16[1568,384]{1,0:T(8,128)(2,1)S(1)}, u32[]{:S(2)}, u32[]{:S(2)}) collective-permute-start(bf16[1568,384]{1,0:T(8,128)(2,1)} %shard_map.112), channel_id=1, source_target_pairs={{0,2},{1,6},{2,0},{3,4},{4,3},{5,7},{6,1},{7,5},{8,10},{9,14},{10,... | collective-permute-start | bytes 3612680 | tf_op jit(solution)/shard_map/ppermute | solution.py:35
  23.3 0.7 collective-permute-start.3
  24.0 2.5 %collective-permute-start.4 = (bf16[768,384]{1,0:T(8,128)(2,1)}, bf16[768,384]{1,0:T(8,128)(2,1)}, u32[]{:S(2)}, u32[]{:S(2)}) collective-permute-start(bf16[768,384]{1,0:T(8,128)(2,1)} %copy-done.3), channel_id=1, source_target_pairs={{0,24},{1,25},{2,26},{3,27},{4,28},{5,29},{6,30},{7,31},{8,0},{9,1... | collective-permute-start | bytes 1769480 | tf_op jit(solution)/shard_map/ppermute | solution.py:35
  26.6 0.9 constant_dynamic-update-slice_fusion.3
  27.6 1.0 constant_dynamic-update-slice_fusion.1
  28.6 3.0 %collective-permute-start.12 = (bf16[1024,384]{1,0:T(8,128)(2,1)S(1)}, bf16[1024,384]{1,0:T(8,128)(2,1)S(1)}, u32[]{:S(2)}, u32[]{:S(2)}) collective-permute-start(bf16[1024,384]{1,0:T(8,128)(2,1)S(1)} %constant_dynamic-update-slice_fusion), channel_id=1, source_target_pairs={{0,0},{1,4},{2,2},{3,6},{4,1},{5,5},{6,3},{7,7},{8,8},{9,12},{10,1... | collective-permute-start | bytes 2359304 | tf_op jit(solution)/shard_map/ppermute | solution.py:35
  31.6 8.7 %collective-permute-done.3.refs_5_.refs_4_.refs_6_.refs_1_ = bf16[768,384]{1,0:T(8,128)(2,1)S(1)} collective-permute-done((bf16[768,384]{1,0:T(8,128)(2,1)}, bf16[768,384]{1,0:T(8,128)(2,1)S(1)}, u32[]{:S(2)}, u32[]{:S(2)}) %collective-permute-start.3) | collective-permute-done | bytes 589856 | tf_op jit(solution)/shard_map/ppermute | solution.py:35
  40.4 1.6 %collective-permute-start.13 = (bf16[1024,384]{1,0:T(8,128)(2,1)S(1)}, bf16[1024,384]{1,0:T(8,128)(2,1)S(1)}, u32[]{:S(2)}, u32[]{:S(2)}) collective-permute-start(bf16[1024,384]{1,0:T(8,128)(2,1)S(1)} %constant_dynamic-update-slice_fusion), channel_id=1, source_target_pairs={{0,2},{1,6},{2,0},{3,4},{4,3},{5,7},{6,1},{7,5},{8,10},{9,14},{10,... | collective-permute-start | bytes 2359304 | tf_op jit(solution)/shard_map/ppermute | solution.py:35
  42.0 10.2 %collective-permute-done.4.refs_6_.refs_5_.refs_7_.refs_2_ = bf16[768,384]{1,0:T(8,128)(2,1)} collective-permute-done((bf16[768,384]{1,0:T(8,128)(2,1)}, bf16[768,384]{1,0:T(8,128)(2,1)}, u32[]{:S(2)}, u32[]{:S(2)}) %collective-permute-start.4) | collective-permute-done | bytes 589856 | tf_op jit(solution)/shard_map/ppermute | solution.py:35
  52.2 1.7 %collective-permute-start.10 = (bf16[768,384]{1,0:T(8,128)(2,1)S(1)}, bf16[768,384]{1,0:T(8,128)(2,1)S(1)}, u32[]{:S(2)}, u32[]{:S(2)}) collective-permute-start(bf16[768,384]{1,0:T(8,128)(2,1)S(1)} %broadcast_select_fusion), channel_id=1, source_target_pairs={{0,8},{1,9},{2,10},{3,11},{4,12},{5,13},{6,14},{7,15},{8,0},{9,1},... | collective-permute-start | bytes 1769480 | tf_op jit(solution)/shard_map/ppermute | solution.py:35
  54.0 0.5 collective-permute-start.14
  54.5 1.5 %shard_map.113 = (bf16[256,1536]{1,0:T(8,128)(2,1)S(1)}, f32[256,1]{1,0:T(8,128)S(1)}) custom-call(bf16[1568,384]{1,0:T(8,128)(2,1)S(1)} %collective-permute-done.8.refs_0_.refs_1_.refs_3_, bf16[1568,384]{1,0:T(8,128)(2,1)S(1)} %collective-permute-done.9.refs_1_.refs_2_.refs_4_), custom_call_target="tpu_custom_call" | custom-call | tf_op jit(solution)/shard_map/pallas_call | solution.py:335
  56.0 10.9 %collective-permute-done.12.refs_2_ = bf16[1024,384]{1,0:T(8,128)(2,1)S(1)} collective-permute-done((bf16[1024,384]{1,0:T(8,128)(2,1)S(1)}, bf16[1024,384]{1,0:T(8,128)(2,1)S(1)}, u32[]{:S(2)}, u32[]{:S(2)}) %collective-permute-start.12) | collective-permute-done | bytes 786464 | tf_op jit(solution)/shard_map/ppermute | solution.py:35
  67.2 1.0 collective-permute-start.17
  68.3 0.8 collective-permute-done.16.refs_10_.refs_9_.refs_11_.refs_6_
  69.1 0.8 collective-permute-done.17.refs_11_.refs_10_.refs_12_.refs_7_
  69.9 3.5 %shard_map.114 = (bf16[768,768]{1,0:T(8,128)(2,1)S(1)}, bf16[512,768]{1,0:T(8,128)(2,1)S(1)}) custom-call(bf16[1568,384]{1,0:T(8,128)(2,1)S(1)} %collective-permute-done.8.refs_0_.refs_1_.refs_3_, bf16[1568,384]{1,0:T(8,128)(2,1)S(1)} %collective-permute-done.9.refs_1_.refs_2_.refs_4_, bf16[1024,384]{1,0:T(8,128)(2,1)S(1)} %collective-permute-done.12.refs_2_, ...), custom_call_target="tpu_custom_call" | custom-call | tf_op jit(solution)/shard_map/pallas_call | solution.py:335
  73.4 0.5 collective-permute-start.18
  74.0 2.3 %shard_map.115 = (bf16[256,384]{1,0:T(8,128)(2,1)S(1)}, bf16[256,384]{1,0:T(8,128)(2,1)S(1)}) custom-call(bf16[256,1536]{1,0:T(8,128)(2,1)S(1)} %get-tuple-element.58.refs_0_, bf16[1568,384]{1,0:T(8,128)(2,1)S(1)} %collective-permute-done.8.refs_0_.refs_1_.refs_3_, bf16[1568,384]{1,0:T(8,128)(2,1)S(1)} %collective-permute-done.9.refs_1_.refs_2_.refs_4_, ...), custom_call_target="tpu_custom_call" | custom-call | tf_op jit(solution)/shard_map/pallas_call | solution.py:335
  76.3 3.8 %shard_map.116 = (bf16[256,384]{1,0:T(8,128)(2,1)S(1)}, bf16[256,384]{1,0:T(8,128)(2,1)S(1)}, f32[256,768]{1,0:T(8,128)S(1)}, bf16[512,768]{1,0:T(8,128)(2,1)S(1)}, bf16[512,768]{1,0:T(8,128)(2,1)}) custom-call(s32[8]{0:T(128)S(1)} %bitcast_convert_fusion.refs_0_, bf16[768,768]{1,0:T(8,128)(2,1)S(1)} %get-tuple-element.56.refs_1_, ...), custom_call_target="tpu_custom_call" | custom-call | tf_op jit(solution)/shard_map/pallas_call | solution.py:335
  80.2 3.5 %shard_map.117 = (bf16[528,384]{1,0:T(8,128)(2,1)S(1)}, bf16[528,384]{1,0:T(8,128)(2,1)S(1)}, bf16[528,384]{1,0:T(8,128)(2,1)S(1)}, bf16[528,384]{1,0:T(8,128)(2,1)S(1)}) custom-call(bf16[256,384]{1,0:T(8,128)(2,1)S(1)} %get-tuple-element.63.refs_0_, bf16[256,384]{1,0:T(8,128)(2,1)S(1)} %get-tuple-element.64.refs_1_, ...), custom_call_target="tpu_custom_call" | custom-call | tf_op jit(solution)/shard_map/pallas_call | solution.py:335
  84.0 1.5 %collective-permute-start.24 = (bf16[256,768]{1,0:T(8,128)(2,1)S(1)}, bf16[256,768]{1,0:T(8,128)(2,1)S(1)}, u32[]{:S(2)}, u32[]{:S(2)}) collective-permute-start(bf16[256,768]{1,0:T(8,128)(2,1)S(1)} %get-tuple-element.77), channel_id=1, source_target_pairs={{0,8},{1,9},{2,10},{3,11},{4,12},{5,13},{6,14},{7,15},{8,16},{9,17... | collective-permute-start | bytes 1179656 | tf_op jit(solution)/shard_map/ppermute | solution.py:35
  85.5 1.9 %collective-permute-start.20 = (bf16[528,384]{1,0:T(8,128)(2,1)S(1)}, bf16[528,384]{1,0:T(8,128)(2,1)S(1)}, u32[]{:S(2)}, u32[]{:S(2)}) collective-permute-start(bf16[528,384]{1,0:T(8,128)(2,1)S(1)} %get-tuple-element.70), channel_id=1, source_target_pairs={{0,0},{1,4},{2,2},{3,6},{4,1},{5,5},{6,3},{7,7},{8,8},{9,12},{10,1... | collective-permute-start | bytes 1216520 | tf_op jit(solution)/shard_map/ppermute | solution.py:35
  87.4 2.3 %collective-permute-start.22 = (bf16[528,384]{1,0:T(8,128)(2,1)S(1)}, bf16[528,384]{1,0:T(8,128)(2,1)S(1)}, u32[]{:S(2)}, u32[]{:S(2)}) collective-permute-start(bf16[528,384]{1,0:T(8,128)(2,1)S(1)} %get-tuple-element.72), channel_id=1, source_target_pairs={{0,2},{1,6},{2,0},{3,4},{4,3},{5,7},{6,1},{7,5},{8,10},{9,14},{10,... | collective-permute-start | bytes 1216520 | tf_op jit(solution)/shard_map/ppermute | solution.py:35
  89.7 2.0 %collective-permute-start.25 = (bf16[256,768]{1,0:T(8,128)(2,1)S(1)}, bf16[256,768]{1,0:T(8,128)(2,1)S(1)}, u32[]{:S(2)}, u32[]{:S(2)}) collective-permute-start(bf16[256,768]{1,0:T(8,128)(2,1)S(1)} %get-tuple-element.78), channel_id=1, source_target_pairs={{0,24},{1,25},{2,26},{3,27},{4,28},{5,29},{6,30},{7,31},{8,0},{9,1... | collective-permute-start | bytes 1179656 | tf_op jit(solution)/shard_map/ppermute | solution.py:35
  91.7 4.5 %collective-permute-done.24.up = bf16[256,768]{1,0:T(8,128)(2,1)S(1)} collective-permute-done((bf16[256,768]{1,0:T(8,128)(2,1)S(1)}, bf16[256,768]{1,0:T(8,128)(2,1)S(1)}, u32[]{:S(2)}, u32[]{:S(2)}) %collective-permute-start.24) | collective-permute-done | bytes 393248 | tf_op jit(solution)/shard_map/ppermute | solution.py:35
  96.1 1.2 %collective-permute-start.23 = (bf16[528,384]{1,0:T(8,128)(2,1)S(1)}, bf16[528,384]{1,0:T(8,128)(2,1)S(1)}, u32[]{:S(2)}, u32[]{:S(2)}) collective-permute-start(bf16[528,384]{1,0:T(8,128)(2,1)S(1)} %get-tuple-element.73), channel_id=1, source_target_pairs={{0,3},{1,7},{2,1},{3,5},{4,2},{5,6},{6,0},{7,4},{8,11},{9,15},{10,... | collective-permute-start | bytes 1216520 | tf_op jit(solution)/shard_map/ppermute | solution.py:35
  97.4 1.8 %shard_map.119.whole = bf16[1536,768]{1,0:T(8,128)(2,1)S(1)} custom-call(bf16[768,384]{1,0:T(8,128)(2,1)} %copy-done.3, bf16[768,384]{1,0:T(8,128)(2,1)} %copy-done.2, bf16[768,384]{1,0:T(8,128)(2,1)} %collective-permute-done.4.refs_6_.refs_5_.refs_7_.refs_2_, bf16[768,384]{1,0:T(8,128)(2,1)} %copy-done.5, bf16[768,384]{1,0:T(8,128)(2,1)} %copy-done.6, ...), custom_call_target="tpu_custom_call" | custom-call | tf_op jit(solution)/shard_map/pallas_call | solution.py:335
  99.2 6.1 %collective-permute-done.25.down = bf16[256,768]{1,0:T(8,128)(2,1)S(1)} collective-permute-done((bf16[256,768]{1,0:T(8,128)(2,1)S(1)}, bf16[256,768]{1,0:T(8,128)(2,1)S(1)}, u32[]{:S(2)}, u32[]{:S(2)}) %collective-permute-start.25) | collective-permute-done | bytes 393248 | tf_op jit(solution)/shard_map/ppermute | solution.py:35
  105.3 1.0 shard_map.120
  106.4 1.3 %collective-permute-start.29 = (bf16[256,384]{1,0:T(8,128)(2,1)S(1)}, bf16[256,384]{1,0:T(8,128)(2,1)S(1)}, u32[]{:S(2)}, u32[]{:S(2)}) collective-permute-start(bf16[256,384]{1,0:T(8,128)(2,1)S(1)} %get-tuple-element.82), channel_id=1, source_target_pairs={{0,3},{1,7},{2,1},{3,5},{4,2},{5,6},{6,0},{7,4},{8,11},{9,15},{10,... | collective-permute-start | bytes 589832 | tf_op jit(solution)/shard_map/ppermute | solution.py:35
  107.6 1.8 %collective-permute-start.28 = (bf16[256,384]{1,0:T(8,128)(2,1)S(1)}, bf16[256,384]{1,0:T(8,128)(2,1)S(1)}, u32[]{:S(2)}, u32[]{:S(2)}) collective-permute-start(bf16[256,384]{1,0:T(8,128)(2,1)S(1)} %get-tuple-element.81), channel_id=1, source_target_pairs={{0,2},{1,6},{2,0},{3,4},{4,3},{5,7},{6,1},{7,5},{8,10},{9,14},{10,... | collective-permute-start | bytes 589832 | tf_op jit(solution)/shard_map/ppermute | solution.py:35
  109.4 2.7 %collective-permute-start.26 = (bf16[256,384]{1,0:T(8,128)(2,1)S(1)}, bf16[256,384]{1,0:T(8,128)(2,1)S(1)}, u32[]{:S(2)}, u32[]{:S(2)}) collective-permute-start(bf16[256,384]{1,0:T(8,128)(2,1)S(1)} %get-tuple-element.79), channel_id=1, source_target_pairs={{0,0},{1,4},{2,2},{3,6},{4,1},{5,5},{6,3},{7,7},{8,8},{9,12},{10,1... | collective-permute-start | bytes 589832 | tf_op jit(solution)/shard_map/ppermute | solution.py:35
  112.1 1.2 shard_map.118
  113.3 0.6 collective-permute-done.29
  113.8 4.1 %collective-permute-done.28 = bf16[256,384]{1,0:T(8,128)(2,1)S(1)} collective-permute-done((bf16[256,384]{1,0:T(8,128)(2,1)S(1)}, bf16[256,384]{1,0:T(8,128)(2,1)S(1)}, u32[]{:S(2)}, u32[]{:S(2)}) %collective-permute-start.28) | collective-permute-done | bytes 196640 | tf_op jit(solution)/shard_map/ppermute | solution.py:35
  118.0 1.5 %collective-permute-done.26 = bf16[256,384]{1,0:T(8,128)(2,1)S(1)} collective-permute-done((bf16[256,384]{1,0:T(8,128)(2,1)S(1)}, bf16[256,384]{1,0:T(8,128)(2,1)S(1)}, u32[]{:S(2)}, u32[]{:S(2)}) %collective-permute-start.26) | collective-permute-done | bytes 196640 | tf_op jit(solution)/shard_map/ppermute | solution.py:35
  119.5 0.8 add_convert_fusion
  (69 shorter events, 1.5 us)
Async XLA Ops:
  0.6 5.9 %copy-start.14 = (bf16[2,128,384]{2,1,0:T(8,128)(2,1)S(1)}, bf16[2,128,384]{2,1,0:T(8,128)(2,1)}, u32[]{:S(2)}) copy-start(bf16[2,128,384]{2,1,0:T(8,128)(2,1)} %param.11) | copy-start | bytes 589828
  0.6 9.3 %copy-start.13 = (bf16[256,384]{1,0:T(8,128)(2,1)S(1)}, bf16[256,384]{1,0:T(8,128)(2,1)}, u32[]{:S(2)}) copy-start(bf16[256,384]{1,0:T(8,128)(2,1)} %param.17) | copy-start | bytes 589828
  0.7 9.4 %copy-start.15 = (s32[4,2]{0,1:T(2,128)S(1)}, s32[4,2]{0,1:T(2,128)}, u32[]{:S(2)}) copy-start(s32[4,2]{0,1:T(2,128)} %param.16) | copy-start | bytes 100
  0.7 9.6 %copy-start.11 = (bf16[384]{0:T(512)(128)(2,1)S(1)}, bf16[384]{0:T(512)(128)(2,1)}, u32[]{:S(2)}) copy-start(bf16[384]{0:T(512)(128)(2,1)} %gain.1) | copy-start | bytes 2308
  0.7 9.6 %copy-start.10 = (bf16[256,384]{1,0:T(8,128)(2,1)S(1)}, bf16[256,384]{1,0:T(8,128)(2,1)}, u32[]{:S(2)}) copy-start(bf16[256,384]{1,0:T(8,128)(2,1)} %hidden.1) | copy-start | bytes 589828
  1.9 15.3 %collective-permute-start = (bf16[768,384]{1,0:T(8,128)(2,1)S(1)}, bf16[768,384]{1,0:T(8,128)(2,1)S(1)}, u32[]{:S(2)}, u32[]{:S(2)}) collective-permute-start(bf16[768,384]{1,0:T(8,128)(2,1)S(1)} %pad_maximum_fusion), channel_id=1, source_target_pairs={{0,0},{1,4},{2,2},{3,6},{4,1},{5,5},{6,3},{7,7},{8,8},{9,12},{10,1... | collective-permute-start | bytes 1769480 | tf_op jit(solution)/shard_map/ppermute | solution.py:35
  6.5 8.6 %collective-permute-start.1 = (bf16[256,384]{1,0:T(8,128)(2,1)S(1)}, bf16[256,384]{1,0:T(8,128)(2,1)S(1)}, u32[]{:S(2)}, u32[]{:S(2)}) collective-permute-start(bf16[256,384]{1,0:T(8,128)(2,1)S(1)} %bitcast.6), channel_id=1, source_target_pairs={{0,8},{1,9},{2,10},{3,11},{4,12},{5,13},{6,14},{7,15},{8,16},{9,17... | collective-permute-start | bytes 589832 | tf_op jit(solution)/shard_map/ppermute | solution.py:35
  7.8 9.3 %collective-permute-start.2 = (bf16[256,384]{1,0:T(8,128)(2,1)S(1)}, bf16[256,384]{1,0:T(8,128)(2,1)S(1)}, u32[]{:S(2)}, u32[]{:S(2)}) collective-permute-start(bf16[256,384]{1,0:T(8,128)(2,1)S(1)} %bitcast.7), channel_id=1, source_target_pairs={{0,24},{1,25},{2,26},{3,27},{4,28},{5,29},{6,30},{7,31},{8,0},{9,1... | collective-permute-start | bytes 589832 | tf_op jit(solution)/shard_map/ppermute | solution.py:35
  10.0 7.6 %collective-permute-start.6 = (bf16[512,384]{1,0:T(8,128)(2,1)S(1)}, bf16[512,384]{1,0:T(8,128)(2,1)S(1)}, u32[]{:S(2)}, u32[]{:S(2)}) collective-permute-start(bf16[512,384]{1,0:T(8,128)(2,1)S(1)} %pad_maximum_fusion.1.refs_1_), channel_id=1, source_target_pairs={{0,1},{1,0},{2,3},{3,2},{4,5},{5,4},{6,7},{7,6},{8,9},{9,8},{10,11... | collective-permute-start | bytes 1179656 | tf_op jit(solution)/shard_map/ppermute | solution.py:35
  10.3 7.3 %collective-permute-start.5 = (bf16[272,384]{1,0:T(8,128)(2,1)S(1)}, bf16[272,384]{1,0:T(8,128)(2,1)S(1)}, u32[]{:S(2)}, u32[]{:S(2)}) collective-permute-start(bf16[272,384]{1,0:T(8,128)(2,1)S(1)} %pad_maximum_fusion.2.refs_0_), channel_id=1, source_target_pairs={{0,1},{1,0},{2,3},{3,2},{4,5},{5,4},{6,7},{7,6},{8,9},{9,8},{10,11... | collective-permute-start | bytes 626696 | tf_op jit(solution)/shard_map/ppermute | solution.py:35
  15.1 3.7 %copy-start.12 = (bf16[256,384]{1,0:T(8,128)(2,1)}, bf16[256,384]{1,0:T(8,128)(2,1)S(1)}, u32[]{:S(2)}) copy-start(bf16[256,384]{1,0:T(8,128)(2,1)S(1)} %collective-permute-done.1) | copy-start | bytes 589828
  17.2 1.5 %copy-start.3 = (bf16[768,384]{1,0:T(8,128)(2,1)}, bf16[768,384]{1,0:T(8,128)(2,1)S(1)}, u32[]{:S(2)}) copy-start(bf16[768,384]{1,0:T(8,128)(2,1)S(1)} %collective-permute-done.refs_4_.refs_3_.refs_5_.refs_0_) | copy-start | bytes 1769476
  17.2 1.6 %collective-permute-start.7 = (bf16[256,384]{1,0:T(8,128)(2,1)S(1)}, bf16[256,384]{1,0:T(8,128)(2,1)}, u32[]{:S(2)}, u32[]{:S(2)}) collective-permute-start(bf16[256,384]{1,0:T(8,128)(2,1)S(1)} %collective-permute-done.1), channel_id=1, source_target_pairs={{0,1},{1,0},{2,3},{3,2},{4,5},{5,4},{6,7},{7,6},{8,9},{9,8},{10,11... | collective-permute-start | bytes 589832 | tf_op jit(solution)/shard_map/ppermute | solution.py:35
  18.8 33.3 %collective-permute-start.8 = (bf16[1568,384]{1,0:T(8,128)(2,1)}, bf16[1568,384]{1,0:T(8,128)(2,1)S(1)}, u32[]{:S(2)}, u32[]{:S(2)}) collective-permute-start(bf16[1568,384]{1,0:T(8,128)(2,1)} %shard_map.112), channel_id=1, source_target_pairs={{0,0},{1,4},{2,2},{3,6},{4,1},{5,5},{6,3},{7,7},{8,8},{9,12},{10,1... | collective-permute-start | bytes 3612680 | tf_op jit(solution)/shard_map/ppermute | solution.py:35
  21.0 31.2 %collective-permute-start.9 = (bf16[1568,384]{1,0:T(8,128)(2,1)}, bf16[1568,384]{1,0:T(8,128)(2,1)S(1)}, u32[]{:S(2)}, u32[]{:S(2)}) collective-permute-start(bf16[1568,384]{1,0:T(8,128)(2,1)} %shard_map.112), channel_id=1, source_target_pairs={{0,2},{1,6},{2,0},{3,4},{4,3},{5,7},{6,1},{7,5},{8,10},{9,14},{10,... | collective-permute-start | bytes 3612680 | tf_op jit(solution)/shard_map/ppermute | solution.py:35
  23.3 17.0 %collective-permute-start.3 = (bf16[768,384]{1,0:T(8,128)(2,1)}, bf16[768,384]{1,0:T(8,128)(2,1)S(1)}, u32[]{:S(2)}, u32[]{:S(2)}) collective-permute-start(bf16[768,384]{1,0:T(8,128)(2,1)} %copy-done.3), channel_id=1, source_target_pairs={{0,8},{1,9},{2,10},{3,11},{4,12},{5,13},{6,14},{7,15},{8,16},{9,17... | collective-permute-start | bytes 1769480 | tf_op jit(solution)/shard_map/ppermute | solution.py:35
  24.0 28.1 %collective-permute-start.4 = (bf16[768,384]{1,0:T(8,128)(2,1)}, bf16[768,384]{1,0:T(8,128)(2,1)}, u32[]{:S(2)}, u32[]{:S(2)}) collective-permute-start(bf16[768,384]{1,0:T(8,128)(2,1)} %copy-done.3), channel_id=1, source_target_pairs={{0,24},{1,25},{2,26},{3,27},{4,28},{5,29},{6,30},{7,31},{8,0},{9,1... | collective-permute-start | bytes 1769480 | tf_op jit(solution)/shard_map/ppermute | solution.py:35
  26.6 2.0 %collective-permute-start.11 = (bf16[256,384]{1,0:T(8,128)(2,1)S(1)}, bf16[256,384]{1,0:T(8,128)(2,1)S(1)}, u32[]{:S(2)}, u32[]{:S(2)}) collective-permute-start(bf16[256,384]{1,0:T(8,128)(2,1)S(1)} %collective-permute-done.2), channel_id=1, source_target_pairs={{0,1},{1,0},{2,3},{3,2},{4,5},{5,4},{6,7},{7,6},{8,9},{9,8},{10,11... | collective-permute-start | bytes 589832 | tf_op jit(solution)/shard_map/ppermute | solution.py:35
  28.5 25.4 %copy-start.4 = (bf16[768,384]{1,0:T(8,128)(2,1)S(1)}, bf16[768,384]{1,0:T(8,128)(2,1)}, u32[]{:S(2)}) copy-start(bf16[768,384]{1,0:T(8,128)(2,1)} %copy-done.3) | copy-start | bytes 1769476
  28.6 38.2 %collective-permute-start.12 = (bf16[1024,384]{1,0:T(8,128)(2,1)S(1)}, bf16[1024,384]{1,0:T(8,128)(2,1)S(1)}, u32[]{:S(2)}, u32[]{:S(2)}) collective-permute-start(bf16[1024,384]{1,0:T(8,128)(2,1)S(1)} %constant_dynamic-update-slice_fusion), channel_id=1, source_target_pairs={{0,0},{1,4},{2,2},{3,6},{4,1},{5,5},{6,3},{7,7},{8,8},{9,12},{10,1... | collective-permute-start | bytes 2359304 | tf_op jit(solution)/shard_map/ppermute | solution.py:35
  40.4 33.5 %copy-start.2 = (bf16[768,384]{1,0:T(8,128)(2,1)}, bf16[768,384]{1,0:T(8,128)(2,1)S(1)}, u32[]{:S(2)}) copy-start(bf16[768,384]{1,0:T(8,128)(2,1)S(1)} %collective-permute-done.3.refs_5_.refs_4_.refs_6_.refs_1_) | copy-start | bytes 1769476
  40.4 26.5 %collective-permute-start.13 = (bf16[1024,384]{1,0:T(8,128)(2,1)S(1)}, bf16[1024,384]{1,0:T(8,128)(2,1)S(1)}, u32[]{:S(2)}, u32[]{:S(2)}) collective-permute-start(bf16[1024,384]{1,0:T(8,128)(2,1)S(1)} %constant_dynamic-update-slice_fusion), channel_id=1, source_target_pairs={{0,2},{1,6},{2,0},{3,4},{4,3},{5,7},{6,1},{7,5},{8,10},{9,14},{10,... | collective-permute-start | bytes 2359304 | tf_op jit(solution)/shard_map/ppermute | solution.py:35
  52.1 21.8 %copy-start = (bf16[1568,384]{1,0:T(8,128)(2,1)}, bf16[1568,384]{1,0:T(8,128)(2,1)S(1)}, u32[]{:S(2)}) copy-start(bf16[1568,384]{1,0:T(8,128)(2,1)S(1)} %collective-permute-done.8.refs_0_.refs_1_.refs_3_) | copy-start | bytes 3612676
  52.1 21.8 %copy-start.1 = (bf16[1568,384]{1,0:T(8,128)(2,1)}, bf16[1568,384]{1,0:T(8,128)(2,1)S(1)}, u32[]{:S(2)}) copy-start(bf16[1568,384]{1,0:T(8,128)(2,1)S(1)} %collective-permute-done.9.refs_1_.refs_2_.refs_4_) | copy-start | bytes 3612676
  52.2 15.0 %collective-permute-start.10 = (bf16[768,384]{1,0:T(8,128)(2,1)S(1)}, bf16[768,384]{1,0:T(8,128)(2,1)S(1)}, u32[]{:S(2)}, u32[]{:S(2)}) collective-permute-start(bf16[768,384]{1,0:T(8,128)(2,1)S(1)} %broadcast_select_fusion), channel_id=1, source_target_pairs={{0,8},{1,9},{2,10},{3,11},{4,12},{5,13},{6,14},{7,15},{8,0},{9,1},... | collective-permute-start | bytes 1769480 | tf_op jit(solution)/shard_map/ppermute | solution.py:35
  54.0 14.3 %collective-permute-start.14 = (bf16[768,384]{1,0:T(8,128)(2,1)S(1)}, bf16[768,384]{1,0:T(8,128)(2,1)S(1)}, u32[]{:S(2)}, u32[]{:S(2)}) collective-permute-start(bf16[768,384]{1,0:T(8,128)(2,1)S(1)} %copy-done.4), channel_id=1, source_target_pairs={{0,1},{1,0},{2,3},{3,2},{4,5},{5,4},{6,7},{7,6},{8,9},{9,8},{10,11... | collective-permute-start | bytes 1769480 | tf_op jit(solution)/shard_map/ppermute | solution.py:35
  54.5 13.8 %collective-permute-start.15 = (bf16[768,384]{1,0:T(8,128)(2,1)S(1)}, bf16[768,384]{1,0:T(8,128)(2,1)S(1)}, u32[]{:S(2)}, u32[]{:S(2)}) collective-permute-start(bf16[768,384]{1,0:T(8,128)(2,1)S(1)} %collective-permute-done.3.refs_5_.refs_4_.refs_6_.refs_1_), channel_id=1, source_target_pairs={{0,1},{1,0},{2,3},{3,2},{4,5},{5,4},{6,7},{7,6},{8,9},{9,8},{10,11... | collective-permute-start | bytes 1769480 | tf_op jit(solution)/shard_map/ppermute | solution.py:35
  66.8 2.2 %collective-permute-start.16 = (bf16[768,384]{1,0:T(8,128)(2,1)}, bf16[768,384]{1,0:T(8,128)(2,1)S(1)}, u32[]{:S(2)}, u32[]{:S(2)}) collective-permute-start(bf16[768,384]{1,0:T(8,128)(2,1)} %collective-permute-done.4.refs_6_.refs_5_.refs_7_.refs_2_), channel_id=1, source_target_pairs={{0,1},{1,0},{2,3},{3,2},{4,5},{5,4},{6,7},{7,6},{8,9},{9,8},{10,11... | collective-permute-start | bytes 1769480 | tf_op jit(solution)/shard_map/ppermute | solution.py:35
  67.2 6.7 %copy-start.5 = (bf16[768,384]{1,0:T(8,128)(2,1)}, bf16[768,384]{1,0:T(8,128)(2,1)S(1)}, u32[]{:S(2)}) copy-start(bf16[768,384]{1,0:T(8,128)(2,1)S(1)} %collective-permute-done.10.refs_7_.refs_6_.refs_8_.refs_3_) | copy-start | bytes 1769476
  67.2 2.6 %collective-permute-start.17 = (bf16[768,384]{1,0:T(8,128)(2,1)S(1)}, bf16[768,384]{1,0:T(8,128)(2,1)S(1)}, u32[]{:S(2)}, u32[]{:S(2)}) collective-permute-start(bf16[768,384]{1,0:T(8,128)(2,1)S(1)} %collective-permute-done.10.refs_7_.refs_6_.refs_8_.refs_3_), channel_id=1, source_target_pairs={{0,1},{1,0},{2,3},{3,2},{4,5},{5,4},{6,7},{7,6},{8,9},{9,8},{10,11... | collective-permute-start | bytes 1769480 | tf_op jit(solution)/shard_map/ppermute | solution.py:35
  68.2 5.7 %copy-start.6 = (bf16[768,384]{1,0:T(8,128)(2,1)}, bf16[768,384]{1,0:T(8,128)(2,1)S(1)}, u32[]{:S(2)}) copy-start(bf16[768,384]{1,0:T(8,128)(2,1)S(1)} %collective-permute-done.14.refs_8_.refs_7_.refs_9_.refs_4_) | copy-start | bytes 1769476
  68.2 5.7 %copy-start.7 = (bf16[768,384]{1,0:T(8,128)(2,1)}, bf16[768,384]{1,0:T(8,128)(2,1)S(1)}, u32[]{:S(2)}) copy-start(bf16[768,384]{1,0:T(8,128)(2,1)S(1)} %collective-permute-done.15.refs_9_.refs_8_.refs_10_.refs_5_) | copy-start | bytes 1769476
  69.0 4.9 %copy-start.8 = (bf16[768,384]{1,0:T(8,128)(2,1)}, bf16[768,384]{1,0:T(8,128)(2,1)S(1)}, u32[]{:S(2)}) copy-start(bf16[768,384]{1,0:T(8,128)(2,1)S(1)} %collective-permute-done.16.refs_10_.refs_9_.refs_11_.refs_6_) | copy-start | bytes 1769476
  69.9 4.1 %copy-start.9 = (bf16[768,384]{1,0:T(8,128)(2,1)}, bf16[768,384]{1,0:T(8,128)(2,1)S(1)}, u32[]{:S(2)}) copy-start(bf16[768,384]{1,0:T(8,128)(2,1)S(1)} %collective-permute-done.17.refs_11_.refs_10_.refs_12_.refs_7_) | copy-start | bytes 1769476
  73.4 2.8 %collective-permute-start.18 = (bf16[512,768]{1,0:T(8,128)(2,1)S(1)}, bf16[512,768]{1,0:T(8,128)(2,1)S(1)}, u32[]{:S(2)}, u32[]{:S(2)}) collective-permute-start(bf16[512,768]{1,0:T(8,128)(2,1)S(1)} %get-tuple-element.57), channel_id=1, source_target_pairs={{0,1},{1,0},{2,3},{3,2},{4,5},{5,4},{6,7},{7,6},{8,9},{9,8},{10,11... | collective-permute-start | bytes 2359304 | tf_op jit(solution)/shard_map/ppermute | solution.py:35
  80.1 3.7 %collective-permute-start.19 = (bf16[512,768]{1,0:T(8,128)(2,1)}, bf16[512,768]{1,0:T(8,128)(2,1)S(1)}, u32[]{:S(2)}, u32[]{:S(2)}) collective-permute-start(bf16[512,768]{1,0:T(8,128)(2,1)} %get-tuple-element.62), channel_id=1, source_target_pairs={{0,1},{1,0},{2,3},{3,2},{4,5},{5,4},{6,7},{7,6},{8,9},{9,8},{10,11... | collective-permute-start | bytes 2359304 | tf_op jit(solution)/shard_map/ppermute | solution.py:35
  84.0 12.2 %collective-permute-start.24 = (bf16[256,768]{1,0:T(8,128)(2,1)S(1)}, bf16[256,768]{1,0:T(8,128)(2,1)S(1)}, u32[]{:S(2)}, u32[]{:S(2)}) collective-permute-start(bf16[256,768]{1,0:T(8,128)(2,1)S(1)} %get-tuple-element.77), channel_id=1, source_target_pairs={{0,8},{1,9},{2,10},{3,11},{4,12},{5,13},{6,14},{7,15},{8,16},{9,17... | collective-permute-start | bytes 1179656 | tf_op jit(solution)/shard_map/ppermute | solution.py:35
  85.5 22.2 %collective-permute-start.20 = (bf16[528,384]{1,0:T(8,128)(2,1)S(1)}, bf16[528,384]{1,0:T(8,128)(2,1)S(1)}, u32[]{:S(2)}, u32[]{:S(2)}) collective-permute-start(bf16[528,384]{1,0:T(8,128)(2,1)S(1)} %get-tuple-element.70), channel_id=1, source_target_pairs={{0,0},{1,4},{2,2},{3,6},{4,1},{5,5},{6,3},{7,7},{8,8},{9,12},{10,1... | collective-permute-start | bytes 1216520 | tf_op jit(solution)/shard_map/ppermute | solution.py:35
  87.4 22.0 %collective-permute-start.21 = (bf16[528,384]{1,0:T(8,128)(2,1)S(1)}, bf16[528,384]{1,0:T(8,128)(2,1)S(1)}, u32[]{:S(2)}, u32[]{:S(2)}) collective-permute-start(bf16[528,384]{1,0:T(8,128)(2,1)S(1)} %get-tuple-element.71), channel_id=1, source_target_pairs={{0,1},{1,5},{2,3},{3,7},{4,0},{5,4},{6,2},{7,6},{8,9},{9,13},{10,1... | collective-permute-start | bytes 1216520 | tf_op jit(solution)/shard_map/ppermute | solution.py:35
  87.4 22.0 %collective-permute-start.22 = (bf16[528,384]{1,0:T(8,128)(2,1)S(1)}, bf16[528,384]{1,0:T(8,128)(2,1)S(1)}, u32[]{:S(2)}, u32[]{:S(2)}) collective-permute-start(bf16[528,384]{1,0:T(8,128)(2,1)S(1)} %get-tuple-element.72), channel_id=1, source_target_pairs={{0,2},{1,6},{2,0},{3,4},{4,3},{5,7},{6,1},{7,5},{8,10},{9,14},{10,... | collective-permute-start | bytes 1216520 | tf_op jit(solution)/shard_map/ppermute | solution.py:35
  89.7 15.7 %collective-permute-start.25 = (bf16[256,768]{1,0:T(8,128)(2,1)S(1)}, bf16[256,768]{1,0:T(8,128)(2,1)S(1)}, u32[]{:S(2)}, u32[]{:S(2)}) collective-permute-start(bf16[256,768]{1,0:T(8,128)(2,1)S(1)} %get-tuple-element.78), channel_id=1, source_target_pairs={{0,24},{1,25},{2,26},{3,27},{4,28},{5,29},{6,30},{7,31},{8,0},{9,1... | collective-permute-start | bytes 1179656 | tf_op jit(solution)/shard_map/ppermute | solution.py:35
  96.1 16.0 %collective-permute-start.23 = (bf16[528,384]{1,0:T(8,128)(2,1)S(1)}, bf16[528,384]{1,0:T(8,128)(2,1)S(1)}, u32[]{:S(2)}, u32[]{:S(2)}) collective-permute-start(bf16[528,384]{1,0:T(8,128)(2,1)S(1)} %get-tuple-element.73), channel_id=1, source_target_pairs={{0,3},{1,7},{2,1},{3,5},{4,2},{5,6},{6,0},{7,4},{8,11},{9,15},{10,... | collective-permute-start | bytes 1216520 | tf_op jit(solution)/shard_map/ppermute | solution.py:35
  106.4 7.5 %collective-permute-start.29 = (bf16[256,384]{1,0:T(8,128)(2,1)S(1)}, bf16[256,384]{1,0:T(8,128)(2,1)S(1)}, u32[]{:S(2)}, u32[]{:S(2)}) collective-permute-start(bf16[256,384]{1,0:T(8,128)(2,1)S(1)} %get-tuple-element.82), channel_id=1, source_target_pairs={{0,3},{1,7},{2,1},{3,5},{4,2},{5,6},{6,0},{7,4},{8,11},{9,15},{10,... | collective-permute-start | bytes 589832 | tf_op jit(solution)/shard_map/ppermute | solution.py:35
  107.6 10.3 %collective-permute-start.28 = (bf16[256,384]{1,0:T(8,128)(2,1)S(1)}, bf16[256,384]{1,0:T(8,128)(2,1)S(1)}, u32[]{:S(2)}, u32[]{:S(2)}) collective-permute-start(bf16[256,384]{1,0:T(8,128)(2,1)S(1)} %get-tuple-element.81), channel_id=1, source_target_pairs={{0,2},{1,6},{2,0},{3,4},{4,3},{5,7},{6,1},{7,5},{8,10},{9,14},{10,... | collective-permute-start | bytes 589832 | tf_op jit(solution)/shard_map/ppermute | solution.py:35
  109.4 8.6 %collective-permute-start.27 = (bf16[256,384]{1,0:T(8,128)(2,1)S(1)}, bf16[256,384]{1,0:T(8,128)(2,1)S(1)}, u32[]{:S(2)}, u32[]{:S(2)}) collective-permute-start(bf16[256,384]{1,0:T(8,128)(2,1)S(1)} %get-tuple-element.80), channel_id=1, source_target_pairs={{0,1},{1,5},{2,3},{3,7},{4,0},{5,4},{6,2},{7,6},{8,9},{9,13},{10,1... | collective-permute-start | bytes 589832 | tf_op jit(solution)/shard_map/ppermute | solution.py:35
  109.4 10.1 %collective-permute-start.26 = (bf16[256,384]{1,0:T(8,128)(2,1)S(1)}, bf16[256,384]{1,0:T(8,128)(2,1)S(1)}, u32[]{:S(2)}, u32[]{:S(2)}) collective-permute-start(bf16[256,384]{1,0:T(8,128)(2,1)S(1)} %get-tuple-element.79), channel_id=1, source_target_pairs={{0,0},{1,4},{2,2},{3,6},{4,1},{5,5},{6,3},{7,7},{8,8},{9,12},{10,1... | collective-permute-start | bytes 589832 | tf_op jit(solution)/shard_map/ppermute | solution.py:35

commit v9 on v8

--- a/solution.py
+++ b/solution.py
@@ -155,16 +155,16 @@
     pieces, (tables, shared, whole, encs, sems) = refs[4:-5], refs[-5:]
     width = tokens[0].shape[1]
     pairs = weight_copies(pieces, whole, 0)
-    sources = ((outers, 0), (tokens, 2 * token_count + EXTRA), (outers, OWN_ROWS))
-    for i, (pair, start) in enumerate(sources):
-        for k in range(4):
-            target = encs.at[pl.ds(i * OWN_ROWS, OWN_ROWS), pl.ds(k * width, width)]
-            pairs.append((block(pair, k, start, OWN_ROWS), target))
+    for k in range(4):
+        columns = pl.ds(k * width, width)
+        pairs.append((block(outers, k, 0, 2 * OWN_ROWS), encs.at[pl.ds(0, 2 * OWN_ROWS), columns]))
+        own = block(tokens, k, 2 * token_count + EXTRA, OWN_ROWS)
+        pairs.append((own, encs.at[pl.ds(2 * OWN_ROWS, OWN_ROWS), columns]))
     run_copies(pairs, sems)
     tables[...] = jnp.dot(encs[...], whole[...], preferred_element_type=F32).astype(LOW)
-    shared[0:OWN_ROWS, :] = tables[OWN_ROWS : 2 * OWN_ROWS, :]
+    shared[0:OWN_ROWS, :] = tables[2 * OWN_ROWS : 3 * OWN_ROWS, :]
     z, y, x, c = place()
-    start = pl.multiple_of(jnp.where(c == 1, 0, 2 * OWN_ROWS), OWN_ROWS)
+    start = pl.multiple_of(jnp.where(c == 1, 0, OWN_ROWS), OWN_ROWS)
     shared[OWN_ROWS : 2 * OWN_ROWS, :] = tables[pl.ds(start, OWN_ROWS), :]
 
 
@@ -183,15 +183,8 @@
 
 def attention_kernel(seq_count, *refs):
     chosen, tables, shared, queries, d_attended = refs[:5]
-    attended, d_queries, d_own, d_outer, d_shared, window, d_window, logits, slopes, weights, d_scores, sems = refs[5:]
+    attended, d_queries, d_own, d_outer, d_shared, d_window, logits, slopes, weights, d_scores = refs[5:]
     token_count, width = queries.shape
-    sources = [
-        (tables, window.at[pl.ds(0, 3 * OWN_ROWS)]),
-        (shared, window.at[pl.ds(3 * OWN_ROWS, 2 * OWN_ROWS)]),
-    ]
-    copies = [pltpu.make_async_copy(a, b, sems.at[i]) for i, (a, b) in enumerate(sources)]
-    for copy in copies:
-        copy.start()
     d_window[...] = jnp.zeros_like(d_window)
     scale = HD ** (-0.5)
     z, y, x, c = place()
@@ -202,19 +195,28 @@
         for j in range(NBR):
             name = chosen[s * NBR + j]
             away = (name // OWN_DEV - t + 2 + seq_count) % seq_count
-            odd = 3 + jnp.where(away == 1, 1 - c, c)
-            index = jnp.where(away % 2 == 0, away // 2, odd)
-            starts.append(pl.multiple_of(index * OWN_ROWS + (name % OWN_DEV) * RET, RET))
+            here = away % 2 == 0
+            local = (name % OWN_DEV) * RET
+            place_here = jnp.where(away == 4, 1, away)
+            in_tables = pl.multiple_of(jnp.where(here, place_here, 0) * OWN_ROWS + local, RET)
+            other = jnp.where(away == 1, 1 - c, c)
+            in_shared = pl.multiple_of(jnp.where(here, 0, other) * OWN_ROWS + local, RET)
+            row = pl.multiple_of(jnp.where(here, place_here, 3 + other) * OWN_ROWS + local, RET)
+            starts.append((here, in_tables, in_shared, row))
         for h in range(width // HD):
             rows = slice(len(items) * STRETCH, (len(items) + 1) * STRETCH)
             tokens = slice(s * STRETCH, (s + 1) * STRETCH)
             items.append((rows, tokens, slice(h * HD, (h + 1) * HD), slice(width + h * HD, width + (h + 1) * HD), starts))
 
     def picked(starts, columns):
-        return jnp.concatenate([window[pl.ds(a, RET), columns] for a in starts], axis=0)
-
-    for copy in copies:
-        copy.wait()
+        return jnp.concatenate(
+            [
+                jnp.where(here, tables[pl.ds(a, RET), columns], shared[pl.ds(b, RET), columns])
+                for here, a, b, _ in starts
+            ],
+            axis=0,
+        )
+
     for rows, tokens, left, right, starts in items:
         logits[rows, :] = lax.dot_general(
             queries[tokens, left], picked(starts, left), ACROSS, preferred_element_type=F32
@@ -230,25 +232,24 @@
     weights[...] = soft.astype(LOW)
     d_scores[...] = (soft * (d_weights - inner) * scale).astype(LOW)
     for rows, tokens, left, right, starts in items:
+        d_keys = lax.dot_general(
+            d_scores[rows, :], queries[tokens, left], DOWN, preferred_element_type=F32
+        )
+        d_values = lax.dot_general(
+            weights[rows, :], d_attended[tokens, left], DOWN, preferred_element_type=F32
+        )
+        for j, (_, _, _, a) in enumerate(starts):
+            d_window[pl.ds(a, RET), left] += d_keys[j * RET : (j + 1) * RET, :]
+            d_window[pl.ds(a, RET), right] += d_values[j * RET : (j + 1) * RET, :]
+    for rows, tokens, left, right, starts in items:
         attended[tokens, left] = jnp.dot(
             weights[rows, :], picked(starts, right), preferred_element_type=F32
         ).astype(LOW)
         d_queries[tokens, left] = jnp.dot(
             d_scores[rows, :], picked(starts, left), preferred_element_type=F32
         ).astype(LOW)
-    for rows, tokens, left, right, starts in items:
-        d_keys = lax.dot_general(
-            d_scores[rows, :], queries[tokens, left], DOWN, preferred_element_type=F32
-        )
-        d_values = lax.dot_general(
-            weights[rows, :], d_attended[tokens, left], DOWN, preferred_element_type=F32
-        )
-        for j, a in enumerate(starts):
-            d_window[pl.ds(a, RET), left] += d_keys[j * RET : (j + 1) * RET, :]
-            d_window[pl.ds(a, RET), right] += d_values[j * RET : (j + 1) * RET, :]
-    d_own[...] = d_window[OWN_ROWS : 2 * OWN_ROWS, :]
-    d_outer[0:OWN_ROWS, :] = d_window[0:OWN_ROWS, :].astype(LOW)
-    d_outer[OWN_ROWS : 2 * OWN_ROWS, :] = d_window[2 * OWN_ROWS : 3 * OWN_ROWS, :].astype(LOW)
+    d_own[...] = d_window[2 * OWN_ROWS : 3 * OWN_ROWS, :]
+    d_outer[...] = d_window[0 : 2 * OWN_ROWS, :].astype(LOW)
     d_shared[...] = d_window[3 * OWN_ROWS : 5 * OWN_ROWS, :].astype(LOW)
 
 
@@ -404,7 +405,7 @@
         [ANY] * (4 + piece_count),
         [((3 * OWN_ROWS, wide), LOW), ((2 * OWN_ROWS, wide), LOW)],
         [pltpu.VMEM((full_width, wide), LOW), pltpu.VMEM((3 * OWN_ROWS, full_width), LOW)],
-        12 + 2 * piece_count,
+        8 + 2 * piece_count,
     )
     shared = move(shared, flip_core)
     queries, d_attended = call(
@@ -418,7 +419,7 @@
     attended, d_queries, d_own, d_outer, d_shared = call(
         lambda *refs: attention_kernel(seq_count, *refs),
         [chosen, tables, shared, queries, d_attended],
-        [SMEM, ANY, ANY, VMEM, VMEM],
+        [SMEM, VMEM, VMEM, VMEM, VMEM],
         [
             ((token_count, width), LOW),
             ((token_count, width), LOW),
@@ -426,9 +427,8 @@
             ((2 * OWN_ROWS, wide), LOW),
             ((2 * OWN_ROWS, wide), LOW),
         ],
-        [pltpu.VMEM((5 * OWN_ROWS, wide), LOW), pltpu.VMEM((5 * OWN_ROWS, wide), F32)]
+        [pltpu.VMEM((5 * OWN_ROWS, wide), F32)]
         + [pltpu.VMEM((token_count * width // HD, NBR * RET), dtype) for dtype in (F32, F32, LOW, LOW)],
-        2,
     )
     from_core = move(d_shared, flip_core)
     shared_grad = from_core[OWN_ROWS:].astype(F32)

time: 121 us -> 121 us (level)
  no operation moved by 1% of the time
where the time goes in v9:
time: 121 us; the launch traced here: 120 us
  waiting for transfers between devices  55.1 us (46%)
  starting transfers between devices  39.8 us (33%)
  Pallas kernels  19.5 us (16%)
  other arithmetic  2.43 us (2%)
  local copies, waits for them, and re-layouts  2.23 us (2%)
    ppermute x30, waiting for transfers between devices, move(): return lax.ppermute(value, ('seq', 'mp'), pairs)  55.1 us
    ppermute x30, starting transfers between devices, move(): return lax.ppermute(value, ('seq', 'mp'), pairs)  39.8 us
    pallas_call x9, Pallas kernels, call(): pl.pallas_call(kernel, out_shape=[jax.ShapeDtypeStruct(shape, dtype) for...  19.5 us
  transfers between devices with their start and end apart: 30, of which 14 were waited for; matrix products, arithmetic and copies ran while one was open for 2% of the time, Pallas kernels for 10%

profile of v9, /device:TPU:1, one launch (start us, length us, event | category | flops | bytes accessed | tf_op | source)
XLA Modules:
  0.0 120.1 jit_solution(8663250398896048462)
XLA Ops:
  0.7 1.3 %pad_maximum_fusion = bf16[768,384]{1,0:T(8,128)(2,1)S(1)} fusion(bf16[192,384]{1,0:T(8,128)(2,1)} %bitcast.10, bf16[192,384]{1,0:T(8,128)(2,1)} %param.12, bf16[192,384]{1,0:T(8,128)(2,1)} %param.14, bf16[192,384]{1,0:T(8,128)(2,1)} %param.13), kind=kLoop, calls=%fused_computation.6 | loop fusion | flops 2359296 | bytes 1179648 | tf_op jit(solution)/shard_map/concatenate | solution.py:368
  1.9 4.5 %collective-permute-start = (bf16[768,384]{1,0:T(8,128)(2,1)S(1)}, bf16[768,384]{1,0:T(8,128)(2,1)S(1)}, u32[]{:S(2)}, u32[]{:S(2)}) collective-permute-start(bf16[768,384]{1,0:T(8,128)(2,1)S(1)} %pad_maximum_fusion), channel_id=1, source_target_pairs={{0,0},{1,4},{2,2},{3,6},{4,1},{5,5},{6,3},{7,7},{8,8},{9,12},{10,1... | collective-permute-start | bytes 1769480 | tf_op jit(solution)/shard_map/ppermute | solution.py:35
  6.5 1.3 %collective-permute-start.1 = (bf16[256,384]{1,0:T(8,128)(2,1)S(1)}, bf16[256,384]{1,0:T(8,128)(2,1)S(1)}, u32[]{:S(2)}, u32[]{:S(2)}) collective-permute-start(bf16[256,384]{1,0:T(8,128)(2,1)S(1)} %bitcast.6), channel_id=1, source_target_pairs={{0,8},{1,9},{2,10},{3,11},{4,12},{5,13},{6,14},{7,15},{8,16},{9,17... | collective-permute-start | bytes 589832 | tf_op jit(solution)/shard_map/ppermute | solution.py:35
  7.8 2.1 %collective-permute-start.2 = (bf16[256,384]{1,0:T(8,128)(2,1)S(1)}, bf16[256,384]{1,0:T(8,128)(2,1)S(1)}, u32[]{:S(2)}, u32[]{:S(2)}) collective-permute-start(bf16[256,384]{1,0:T(8,128)(2,1)S(1)} %bitcast.7), channel_id=1, source_target_pairs={{0,24},{1,25},{2,26},{3,27},{4,28},{5,29},{6,30},{7,31},{8,0},{9,1... | collective-permute-start | bytes 589832 | tf_op jit(solution)/shard_map/ppermute | solution.py:35
  10.3 0.6 collective-permute-start.5
  10.9 4.2 %collective-permute-done.1 = bf16[256,384]{1,0:T(8,128)(2,1)S(1)} collective-permute-done((bf16[256,384]{1,0:T(8,128)(2,1)S(1)}, bf16[256,384]{1,0:T(8,128)(2,1)S(1)}, u32[]{:S(2)}, u32[]{:S(2)}) %collective-permute-start.1) | collective-permute-done | bytes 196640 | tf_op jit(solution)/shard_map/ppermute | solution.py:35
  15.1 2.1 %collective-permute-done.2 = bf16[256,384]{1,0:T(8,128)(2,1)S(1)} collective-permute-done((bf16[256,384]{1,0:T(8,128)(2,1)S(1)}, bf16[256,384]{1,0:T(8,128)(2,1)S(1)}, u32[]{:S(2)}, u32[]{:S(2)}) %collective-permute-start.2) | collective-permute-done | bytes 196640 | tf_op jit(solution)/shard_map/ppermute | solution.py:35
  17.2 0.4 collective-permute-start.7
  17.6 1.1 shard_map.112
  18.8 2.2 %collective-permute-start.8 = (bf16[1568,384]{1,0:T(8,128)(2,1)}, bf16[1568,384]{1,0:T(8,128)(2,1)S(1)}, u32[]{:S(2)}, u32[]{:S(2)}) collective-permute-start(bf16[1568,384]{1,0:T(8,128)(2,1)} %shard_map.112), channel_id=1, source_target_pairs={{0,0},{1,4},{2,2},{3,6},{4,1},{5,5},{6,3},{7,7},{8,8},{9,12},{10,1... | collective-permute-start | bytes 3612680 | tf_op jit(solution)/shard_map/ppermute | solution.py:35
  21.0 2.3 %collective-permute-start.9 = (bf16[1568,384]{1,0:T(8,128)(2,1)}, bf16[1568,384]{1,0:T(8,128)(2,1)S(1)}, u32[]{:S(2)}, u32[]{:S(2)}) collective-permute-start(bf16[1568,384]{1,0:T(8,128)(2,1)} %shard_map.112), channel_id=1, source_target_pairs={{0,2},{1,6},{2,0},{3,4},{4,3},{5,7},{6,1},{7,5},{8,10},{9,14},{10,... | collective-permute-start | bytes 3612680 | tf_op jit(solution)/shard_map/ppermute | solution.py:35
  23.3 0.7 collective-permute-start.3
  24.0 2.5 %collective-permute-start.4 = (bf16[768,384]{1,0:T(8,128)(2,1)}, bf16[768,384]{1,0:T(8,128)(2,1)}, u32[]{:S(2)}, u32[]{:S(2)}) collective-permute-start(bf16[768,384]{1,0:T(8,128)(2,1)} %copy-done.3), channel_id=1, source_target_pairs={{0,24},{1,25},{2,26},{3,27},{4,28},{5,29},{6,30},{7,31},{8,0},{9,1... | collective-permute-start | bytes 1769480 | tf_op jit(solution)/shard_map/ppermute | solution.py:35
  26.6 0.9 constant_dynamic-update-slice_fusion.3
  27.6 1.0 constant_dynamic-update-slice_fusion.1
  28.6 3.0 %collective-permute-start.12 = (bf16[1024,384]{1,0:T(8,128)(2,1)S(1)}, bf16[1024,384]{1,0:T(8,128)(2,1)S(1)}, u32[]{:S(2)}, u32[]{:S(2)}) collective-permute-start(bf16[1024,384]{1,0:T(8,128)(2,1)S(1)} %constant_dynamic-update-slice_fusion), channel_id=1, source_target_pairs={{0,0},{1,4},{2,2},{3,6},{4,1},{5,5},{6,3},{7,7},{8,8},{9,12},{10,1... | collective-permute-start | bytes 2359304 | tf_op jit(solution)/shard_map/ppermute | solution.py:35
  31.6 8.7 %collective-permute-done.3.refs_5_.refs_4_.refs_6_.refs_1_ = bf16[768,384]{1,0:T(8,128)(2,1)S(1)} collective-permute-done((bf16[768,384]{1,0:T(8,128)(2,1)}, bf16[768,384]{1,0:T(8,128)(2,1)S(1)}, u32[]{:S(2)}, u32[]{:S(2)}) %collective-permute-start.3) | collective-permute-done | bytes 589856 | tf_op jit(solution)/shard_map/ppermute | solution.py:35
  40.4 1.6 %collective-permute-start.13 = (bf16[1024,384]{1,0:T(8,128)(2,1)S(1)}, bf16[1024,384]{1,0:T(8,128)(2,1)S(1)}, u32[]{:S(2)}, u32[]{:S(2)}) collective-permute-start(bf16[1024,384]{1,0:T(8,128)(2,1)S(1)} %constant_dynamic-update-slice_fusion), channel_id=1, source_target_pairs={{0,2},{1,6},{2,0},{3,4},{4,3},{5,7},{6,1},{7,5},{8,10},{9,14},{10,... | collective-permute-start | bytes 2359304 | tf_op jit(solution)/shard_map/ppermute | solution.py:35
  42.0 10.2 %collective-permute-done.4.refs_6_.refs_5_.refs_7_.refs_2_ = bf16[768,384]{1,0:T(8,128)(2,1)} collective-permute-done((bf16[768,384]{1,0:T(8,128)(2,1)}, bf16[768,384]{1,0:T(8,128)(2,1)}, u32[]{:S(2)}, u32[]{:S(2)}) %collective-permute-start.4) | collective-permute-done | bytes 589856 | tf_op jit(solution)/shard_map/ppermute | solution.py:35
  52.2 1.7 %collective-permute-start.10 = (bf16[768,384]{1,0:T(8,128)(2,1)S(1)}, bf16[768,384]{1,0:T(8,128)(2,1)S(1)}, u32[]{:S(2)}, u32[]{:S(2)}) collective-permute-start(bf16[768,384]{1,0:T(8,128)(2,1)S(1)} %broadcast_select_fusion), channel_id=1, source_target_pairs={{0,8},{1,9},{2,10},{3,11},{4,12},{5,13},{6,14},{7,15},{8,0},{9,1},... | collective-permute-start | bytes 1769480 | tf_op jit(solution)/shard_map/ppermute | solution.py:35
  54.0 0.5 collective-permute-start.14
  54.5 1.5 %shard_map.113 = (bf16[256,1536]{1,0:T(8,128)(2,1)S(1)}, f32[256,1]{1,0:T(8,128)S(1)}) custom-call(bf16[1568,384]{1,0:T(8,128)(2,1)S(1)} %collective-permute-done.8.refs_0_.refs_1_.refs_3_, bf16[1568,384]{1,0:T(8,128)(2,1)S(1)} %collective-permute-done.9.refs_1_.refs_2_.refs_4_), custom_call_target="tpu_custom_call" | custom-call | tf_op jit(solution)/shard_map/pallas_call | solution.py:336
  56.0 10.9 %collective-permute-done.12.refs_2_ = bf16[1024,384]{1,0:T(8,128)(2,1)S(1)} collective-permute-done((bf16[1024,384]{1,0:T(8,128)(2,1)S(1)}, bf16[1024,384]{1,0:T(8,128)(2,1)S(1)}, u32[]{:S(2)}, u32[]{:S(2)}) %collective-permute-start.12) | collective-permute-done | bytes 786464 | tf_op jit(solution)/shard_map/ppermute | solution.py:35
  67.2 1.0 collective-permute-start.17
  68.3 0.8 collective-permute-done.16.refs_10_.refs_9_.refs_11_.refs_6_
  69.1 0.8 collective-permute-done.17.refs_11_.refs_10_.refs_12_.refs_7_
  69.9 3.5 %shard_map.114 = (bf16[768,768]{1,0:T(8,128)(2,1)S(1)}, bf16[512,768]{1,0:T(8,128)(2,1)S(1)}) custom-call(bf16[1568,384]{1,0:T(8,128)(2,1)S(1)} %collective-permute-done.8.refs_0_.refs_1_.refs_3_, bf16[1568,384]{1,0:T(8,128)(2,1)S(1)} %collective-permute-done.9.refs_1_.refs_2_.refs_4_, bf16[1024,384]{1,0:T(8,128)(2,1)S(1)} %collective-permute-done.12.refs_2_, ...), custom_call_target="tpu_custom_call" | custom-call | tf_op jit(solution)/shard_map/pallas_call | solution.py:336
  73.4 0.5 collective-permute-start.18
  73.9 2.3 %shard_map.115 = (bf16[256,384]{1,0:T(8,128)(2,1)S(1)}, bf16[256,384]{1,0:T(8,128)(2,1)S(1)}) custom-call(bf16[256,1536]{1,0:T(8,128)(2,1)S(1)} %get-tuple-element.58.refs_0_, bf16[1568,384]{1,0:T(8,128)(2,1)S(1)} %collective-permute-done.8.refs_0_.refs_1_.refs_3_, bf16[1568,384]{1,0:T(8,128)(2,1)S(1)} %collective-permute-done.9.refs_1_.refs_2_.refs_4_, ...), custom_call_target="tpu_custom_call" | custom-call | tf_op jit(solution)/shard_map/pallas_call | solution.py:336
  76.2 3.7 %shard_map.116 = (bf16[256,384]{1,0:T(8,128)(2,1)S(1)}, bf16[256,384]{1,0:T(8,128)(2,1)S(1)}, f32[256,768]{1,0:T(8,128)S(1)}, bf16[512,768]{1,0:T(8,128)(2,1)S(1)}, bf16[512,768]{1,0:T(8,128)(2,1)}) custom-call(s32[8]{0:T(128)S(1)} %bitcast_convert_fusion.refs_0_, bf16[768,768]{1,0:T(8,128)(2,1)S(1)} %get-tuple-element.56.refs_1_, ...), custom_call_target="tpu_custom_call" | custom-call | tf_op jit(solution)/shard_map/pallas_call | solution.py:336
  80.0 3.5 %shard_map.117 = (bf16[528,384]{1,0:T(8,128)(2,1)S(1)}, bf16[528,384]{1,0:T(8,128)(2,1)S(1)}, bf16[528,384]{1,0:T(8,128)(2,1)S(1)}, bf16[528,384]{1,0:T(8,128)(2,1)S(1)}) custom-call(bf16[256,384]{1,0:T(8,128)(2,1)S(1)} %get-tuple-element.63.refs_0_, bf16[256,384]{1,0:T(8,128)(2,1)S(1)} %get-tuple-element.64.refs_1_, ...), custom_call_target="tpu_custom_call" | custom-call | tf_op jit(solution)/shard_map/pallas_call | solution.py:336
  83.8 1.5 %collective-permute-start.24 = (bf16[256,768]{1,0:T(8,128)(2,1)S(1)}, bf16[256,768]{1,0:T(8,128)(2,1)S(1)}, u32[]{:S(2)}, u32[]{:S(2)}) collective-permute-start(bf16[256,768]{1,0:T(8,128)(2,1)S(1)} %get-tuple-element.77), channel_id=1, source_target_pairs={{0,8},{1,9},{2,10},{3,11},{4,12},{5,13},{6,14},{7,15},{8,16},{9,17... | collective-permute-start | bytes 1179656 | tf_op jit(solution)/shard_map/ppermute | solution.py:35
  85.3 1.9 %collective-permute-start.20 = (bf16[528,384]{1,0:T(8,128)(2,1)S(1)}, bf16[528,384]{1,0:T(8,128)(2,1)S(1)}, u32[]{:S(2)}, u32[]{:S(2)}) collective-permute-start(bf16[528,384]{1,0:T(8,128)(2,1)S(1)} %get-tuple-element.70), channel_id=1, source_target_pairs={{0,0},{1,4},{2,2},{3,6},{4,1},{5,5},{6,3},{7,7},{8,8},{9,12},{10,1... | collective-permute-start | bytes 1216520 | tf_op jit(solution)/shard_map/ppermute | solution.py:35
  87.2 2.3 %collective-permute-start.22 = (bf16[528,384]{1,0:T(8,128)(2,1)S(1)}, bf16[528,384]{1,0:T(8,128)(2,1)S(1)}, u32[]{:S(2)}, u32[]{:S(2)}) collective-permute-start(bf16[528,384]{1,0:T(8,128)(2,1)S(1)} %get-tuple-element.72), channel_id=1, source_target_pairs={{0,2},{1,6},{2,0},{3,4},{4,3},{5,7},{6,1},{7,5},{8,10},{9,14},{10,... | collective-permute-start | bytes 1216520 | tf_op jit(solution)/shard_map/ppermute | solution.py:35
  89.5 2.0 %collective-permute-start.25 = (bf16[256,768]{1,0:T(8,128)(2,1)S(1)}, bf16[256,768]{1,0:T(8,128)(2,1)S(1)}, u32[]{:S(2)}, u32[]{:S(2)}) collective-permute-start(bf16[256,768]{1,0:T(8,128)(2,1)S(1)} %get-tuple-element.78), channel_id=1, source_target_pairs={{0,24},{1,25},{2,26},{3,27},{4,28},{5,29},{6,30},{7,31},{8,0},{9,1... | collective-permute-start | bytes 1179656 | tf_op jit(solution)/shard_map/ppermute | solution.py:35
  91.5 4.5 %collective-permute-done.24.up = bf16[256,768]{1,0:T(8,128)(2,1)S(1)} collective-permute-done((bf16[256,768]{1,0:T(8,128)(2,1)S(1)}, bf16[256,768]{1,0:T(8,128)(2,1)S(1)}, u32[]{:S(2)}, u32[]{:S(2)}) %collective-permute-start.24) | collective-permute-done | bytes 393248 | tf_op jit(solution)/shard_map/ppermute | solution.py:35
  96.0 1.2 collective-permute-start.23
  97.2 1.8 %shard_map.119.whole = bf16[1536,768]{1,0:T(8,128)(2,1)S(1)} custom-call(bf16[768,384]{1,0:T(8,128)(2,1)} %copy-done.3, bf16[768,384]{1,0:T(8,128)(2,1)} %copy-done.2, bf16[768,384]{1,0:T(8,128)(2,1)} %collective-permute-done.4.refs_6_.refs_5_.refs_7_.refs_2_, bf16[768,384]{1,0:T(8,128)(2,1)} %copy-done.5, bf16[768,384]{1,0:T(8,128)(2,1)} %copy-done.6, ...), custom_call_target="tpu_custom_call" | custom-call | tf_op jit(solution)/shard_map/pallas_call | solution.py:336
  99.0 6.1 %collective-permute-done.25.down = bf16[256,768]{1,0:T(8,128)(2,1)S(1)} collective-permute-done((bf16[256,768]{1,0:T(8,128)(2,1)S(1)}, bf16[256,768]{1,0:T(8,128)(2,1)S(1)}, u32[]{:S(2)}, u32[]{:S(2)}) %collective-permute-start.25) | collective-permute-done | bytes 393248 | tf_op jit(solution)/shard_map/ppermute | solution.py:35
  105.1 1.0 shard_map.120
  106.2 1.3 %collective-permute-start.29 = (bf16[256,384]{1,0:T(8,128)(2,1)S(1)}, bf16[256,384]{1,0:T(8,128)(2,1)S(1)}, u32[]{:S(2)}, u32[]{:S(2)}) collective-permute-start(bf16[256,384]{1,0:T(8,128)(2,1)S(1)} %get-tuple-element.82), channel_id=1, source_target_pairs={{0,3},{1,7},{2,1},{3,5},{4,2},{5,6},{6,0},{7,4},{8,11},{9,15},{10,... | collective-permute-start | bytes 589832 | tf_op jit(solution)/shard_map/ppermute | solution.py:35
  107.4 1.8 %collective-permute-start.28 = (bf16[256,384]{1,0:T(8,128)(2,1)S(1)}, bf16[256,384]{1,0:T(8,128)(2,1)S(1)}, u32[]{:S(2)}, u32[]{:S(2)}) collective-permute-start(bf16[256,384]{1,0:T(8,128)(2,1)S(1)} %get-tuple-element.81), channel_id=1, source_target_pairs={{0,2},{1,6},{2,0},{3,4},{4,3},{5,7},{6,1},{7,5},{8,10},{9,14},{10,... | collective-permute-start | bytes 589832 | tf_op jit(solution)/shard_map/ppermute | solution.py:35
  109.2 2.7 %collective-permute-start.26 = (bf16[256,384]{1,0:T(8,128)(2,1)S(1)}, bf16[256,384]{1,0:T(8,128)(2,1)S(1)}, u32[]{:S(2)}, u32[]{:S(2)}) collective-permute-start(bf16[256,384]{1,0:T(8,128)(2,1)S(1)} %get-tuple-element.79), channel_id=1, source_target_pairs={{0,0},{1,4},{2,2},{3,6},{4,1},{5,5},{6,3},{7,7},{8,8},{9,12},{10,1... | collective-permute-start | bytes 589832 | tf_op jit(solution)/shard_map/ppermute | solution.py:35
  111.9 1.2 shard_map.118
  113.1 0.6 collective-permute-done.29
  113.6 4.1 %collective-permute-done.28 = bf16[256,384]{1,0:T(8,128)(2,1)S(1)} collective-permute-done((bf16[256,384]{1,0:T(8,128)(2,1)S(1)}, bf16[256,384]{1,0:T(8,128)(2,1)S(1)}, u32[]{:S(2)}, u32[]{:S(2)}) %collective-permute-start.28) | collective-permute-done | bytes 196640 | tf_op jit(solution)/shard_map/ppermute | solution.py:35
  117.7 1.5 %collective-permute-done.26 = bf16[256,384]{1,0:T(8,128)(2,1)S(1)} collective-permute-done((bf16[256,384]{1,0:T(8,128)(2,1)S(1)}, bf16[256,384]{1,0:T(8,128)(2,1)S(1)}, u32[]{:S(2)}, u32[]{:S(2)}) %collective-permute-start.26) | collective-permute-done | bytes 196640 | tf_op jit(solution)/shard_map/ppermute | solution.py:35
  119.3 0.8 add_convert_fusion
  (69 shorter events, 1.5 us)
Async XLA Ops:
  0.6 5.9 %copy-start.14 = (bf16[2,128,384]{2,1,0:T(8,128)(2,1)S(1)}, bf16[2,128,384]{2,1,0:T(8,128)(2,1)}, u32[]{:S(2)}) copy-start(bf16[2,128,384]{2,1,0:T(8,128)(2,1)} %param.11) | copy-start | bytes 589828
  0.6 9.3 %copy-start.13 = (bf16[256,384]{1,0:T(8,128)(2,1)S(1)}, bf16[256,384]{1,0:T(8,128)(2,1)}, u32[]{:S(2)}) copy-start(bf16[256,384]{1,0:T(8,128)(2,1)} %param.17) | copy-start | bytes 589828
  0.7 9.4 %copy-start.15 = (s32[4,2]{0,1:T(2,128)S(1)}, s32[4,2]{0,1:T(2,128)}, u32[]{:S(2)}) copy-start(s32[4,2]{0,1:T(2,128)} %param.16) | copy-start | bytes 100
  0.7 9.6 %copy-start.11 = (bf16[384]{0:T(512)(128)(2,1)S(1)}, bf16[384]{0:T(512)(128)(2,1)}, u32[]{:S(2)}) copy-start(bf16[384]{0:T(512)(128)(2,1)} %gain.1) | copy-start | bytes 2308
  0.7 9.6 %copy-start.10 = (bf16[256,384]{1,0:T(8,128)(2,1)S(1)}, bf16[256,384]{1,0:T(8,128)(2,1)}, u32[]{:S(2)}) copy-start(bf16[256,384]{1,0:T(8,128)(2,1)} %hidden.1) | copy-start | bytes 589828
  1.9 15.3 %collective-permute-start = (bf16[768,384]{1,0:T(8,128)(2,1)S(1)}, bf16[768,384]{1,0:T(8,128)(2,1)S(1)}, u32[]{:S(2)}, u32[]{:S(2)}) collective-permute-start(bf16[768,384]{1,0:T(8,128)(2,1)S(1)} %pad_maximum_fusion), channel_id=1, source_target_pairs={{0,0},{1,4},{2,2},{3,6},{4,1},{5,5},{6,3},{7,7},{8,8},{9,12},{10,1... | collective-permute-start | bytes 1769480 | tf_op jit(solution)/shard_map/ppermute | solution.py:35
  6.5 8.6 %collective-permute-start.1 = (bf16[256,384]{1,0:T(8,128)(2,1)S(1)}, bf16[256,384]{1,0:T(8,128)(2,1)S(1)}, u32[]{:S(2)}, u32[]{:S(2)}) collective-permute-start(bf16[256,384]{1,0:T(8,128)(2,1)S(1)} %bitcast.6), channel_id=1, source_target_pairs={{0,8},{1,9},{2,10},{3,11},{4,12},{5,13},{6,14},{7,15},{8,16},{9,17... | collective-permute-start | bytes 589832 | tf_op jit(solution)/shard_map/ppermute | solution.py:35
  7.8 9.3 %collective-permute-start.2 = (bf16[256,384]{1,0:T(8,128)(2,1)S(1)}, bf16[256,384]{1,0:T(8,128)(2,1)S(1)}, u32[]{:S(2)}, u32[]{:S(2)}) collective-permute-start(bf16[256,384]{1,0:T(8,128)(2,1)S(1)} %bitcast.7), channel_id=1, source_target_pairs={{0,24},{1,25},{2,26},{3,27},{4,28},{5,29},{6,30},{7,31},{8,0},{9,1... | collective-permute-start | bytes 589832 | tf_op jit(solution)/shard_map/ppermute | solution.py:35
  10.0 7.6 %collective-permute-start.6 = (bf16[512,384]{1,0:T(8,128)(2,1)S(1)}, bf16[512,384]{1,0:T(8,128)(2,1)S(1)}, u32[]{:S(2)}, u32[]{:S(2)}) collective-permute-start(bf16[512,384]{1,0:T(8,128)(2,1)S(1)} %pad_maximum_fusion.1.refs_1_), channel_id=1, source_target_pairs={{0,1},{1,0},{2,3},{3,2},{4,5},{5,4},{6,7},{7,6},{8,9},{9,8},{10,11... | collective-permute-start | bytes 1179656 | tf_op jit(solution)/shard_map/ppermute | solution.py:35
  10.3 7.3 %collective-permute-start.5 = (bf16[272,384]{1,0:T(8,128)(2,1)S(1)}, bf16[272,384]{1,0:T(8,128)(2,1)S(1)}, u32[]{:S(2)}, u32[]{:S(2)}) collective-permute-start(bf16[272,384]{1,0:T(8,128)(2,1)S(1)} %pad_maximum_fusion.2.refs_0_), channel_id=1, source_target_pairs={{0,1},{1,0},{2,3},{3,2},{4,5},{5,4},{6,7},{7,6},{8,9},{9,8},{10,11... | collective-permute-start | bytes 626696 | tf_op jit(solution)/shard_map/ppermute | solution.py:35
  15.1 3.7 %copy-start.12 = (bf16[256,384]{1,0:T(8,128)(2,1)}, bf16[256,384]{1,0:T(8,128)(2,1)S(1)}, u32[]{:S(2)}) copy-start(bf16[256,384]{1,0:T(8,128)(2,1)S(1)} %collective-permute-done.1) | copy-start | bytes 589828
  17.2 1.5 %copy-start.3 = (bf16[768,384]{1,0:T(8,128)(2,1)}, bf16[768,384]{1,0:T(8,128)(2,1)S(1)}, u32[]{:S(2)}) copy-start(bf16[768,384]{1,0:T(8,128)(2,1)S(1)} %collective-permute-done.refs_4_.refs_3_.refs_5_.refs_0_) | copy-start | bytes 1769476
  17.2 1.6 %collective-permute-start.7 = (bf16[256,384]{1,0:T(8,128)(2,1)S(1)}, bf16[256,384]{1,0:T(8,128)(2,1)}, u32[]{:S(2)}, u32[]{:S(2)}) collective-permute-start(bf16[256,384]{1,0:T(8,128)(2,1)S(1)} %collective-permute-done.1), channel_id=1, source_target_pairs={{0,1},{1,0},{2,3},{3,2},{4,5},{5,4},{6,7},{7,6},{8,9},{9,8},{10,11... | collective-permute-start | bytes 589832 | tf_op jit(solution)/shard_map/ppermute | solution.py:35
  18.8 33.3 %collective-permute-start.8 = (bf16[1568,384]{1,0:T(8,128)(2,1)}, bf16[1568,384]{1,0:T(8,128)(2,1)S(1)}, u32[]{:S(2)}, u32[]{:S(2)}) collective-permute-start(bf16[1568,384]{1,0:T(8,128)(2,1)} %shard_map.112), channel_id=1, source_target_pairs={{0,0},{1,4},{2,2},{3,6},{4,1},{5,5},{6,3},{7,7},{8,8},{9,12},{10,1... | collective-permute-start | bytes 3612680 | tf_op jit(solution)/shard_map/ppermute | solution.py:35
  21.0 31.2 %collective-permute-start.9 = (bf16[1568,384]{1,0:T(8,128)(2,1)}, bf16[1568,384]{1,0:T(8,128)(2,1)S(1)}, u32[]{:S(2)}, u32[]{:S(2)}) collective-permute-start(bf16[1568,384]{1,0:T(8,128)(2,1)} %shard_map.112), channel_id=1, source_target_pairs={{0,2},{1,6},{2,0},{3,4},{4,3},{5,7},{6,1},{7,5},{8,10},{9,14},{10,... | collective-permute-start | bytes 3612680 | tf_op jit(solution)/shard_map/ppermute | solution.py:35
  23.3 17.0 %collective-permute-start.3 = (bf16[768,384]{1,0:T(8,128)(2,1)}, bf16[768,384]{1,0:T(8,128)(2,1)S(1)}, u32[]{:S(2)}, u32[]{:S(2)}) collective-permute-start(bf16[768,384]{1,0:T(8,128)(2,1)} %copy-done.3), channel_id=1, source_target_pairs={{0,8},{1,9},{2,10},{3,11},{4,12},{5,13},{6,14},{7,15},{8,16},{9,17... | collective-permute-start | bytes 1769480 | tf_op jit(solution)/shard_map/ppermute | solution.py:35
  24.0 28.1 %collective-permute-start.4 = (bf16[768,384]{1,0:T(8,128)(2,1)}, bf16[768,384]{1,0:T(8,128)(2,1)}, u32[]{:S(2)}, u32[]{:S(2)}) collective-permute-start(bf16[768,384]{1,0:T(8,128)(2,1)} %copy-done.3), channel_id=1, source_target_pairs={{0,24},{1,25},{2,26},{3,27},{4,28},{5,29},{6,30},{7,31},{8,0},{9,1... | collective-permute-start | bytes 1769480 | tf_op jit(solution)/shard_map/ppermute | solution.py:35
  26.6 2.0 %collective-permute-start.11 = (bf16[256,384]{1,0:T(8,128)(2,1)S(1)}, bf16[256,384]{1,0:T(8,128)(2,1)S(1)}, u32[]{:S(2)}, u32[]{:S(2)}) collective-permute-start(bf16[256,384]{1,0:T(8,128)(2,1)S(1)} %collective-permute-done.2), channel_id=1, source_target_pairs={{0,1},{1,0},{2,3},{3,2},{4,5},{5,4},{6,7},{7,6},{8,9},{9,8},{10,11... | collective-permute-start | bytes 589832 | tf_op jit(solution)/shard_map/ppermute | solution.py:35
  28.5 25.4 %copy-start.4 = (bf16[768,384]{1,0:T(8,128)(2,1)S(1)}, bf16[768,384]{1,0:T(8,128)(2,1)}, u32[]{:S(2)}) copy-start(bf16[768,384]{1,0:T(8,128)(2,1)} %copy-done.3) | copy-start | bytes 1769476
  28.6 38.2 %collective-permute-start.12 = (bf16[1024,384]{1,0:T(8,128)(2,1)S(1)}, bf16[1024,384]{1,0:T(8,128)(2,1)S(1)}, u32[]{:S(2)}, u32[]{:S(2)}) collective-permute-start(bf16[1024,384]{1,0:T(8,128)(2,1)S(1)} %constant_dynamic-update-slice_fusion), channel_id=1, source_target_pairs={{0,0},{1,4},{2,2},{3,6},{4,1},{5,5},{6,3},{7,7},{8,8},{9,12},{10,1... | collective-permute-start | bytes 2359304 | tf_op jit(solution)/shard_map/ppermute | solution.py:35
  40.4 33.5 %copy-start.2 = (bf16[768,384]{1,0:T(8,128)(2,1)}, bf16[768,384]{1,0:T(8,128)(2,1)S(1)}, u32[]{:S(2)}) copy-start(bf16[768,384]{1,0:T(8,128)(2,1)S(1)} %collective-permute-done.3.refs_5_.refs_4_.refs_6_.refs_1_) | copy-start | bytes 1769476
  40.4 26.5 %collective-permute-start.13 = (bf16[1024,384]{1,0:T(8,128)(2,1)S(1)}, bf16[1024,384]{1,0:T(8,128)(2,1)S(1)}, u32[]{:S(2)}, u32[]{:S(2)}) collective-permute-start(bf16[1024,384]{1,0:T(8,128)(2,1)S(1)} %constant_dynamic-update-slice_fusion), channel_id=1, source_target_pairs={{0,2},{1,6},{2,0},{3,4},{4,3},{5,7},{6,1},{7,5},{8,10},{9,14},{10,... | collective-permute-start | bytes 2359304 | tf_op jit(solution)/shard_map/ppermute | solution.py:35
  52.1 21.7 %copy-start = (bf16[1568,384]{1,0:T(8,128)(2,1)}, bf16[1568,384]{1,0:T(8,128)(2,1)S(1)}, u32[]{:S(2)}) copy-start(bf16[1568,384]{1,0:T(8,128)(2,1)S(1)} %collective-permute-done.8.refs_0_.refs_1_.refs_3_) | copy-start | bytes 3612676
  52.1 21.7 %copy-start.1 = (bf16[1568,384]{1,0:T(8,128)(2,1)}, bf16[1568,384]{1,0:T(8,128)(2,1)S(1)}, u32[]{:S(2)}) copy-start(bf16[1568,384]{1,0:T(8,128)(2,1)S(1)} %collective-permute-done.9.refs_1_.refs_2_.refs_4_) | copy-start | bytes 3612676
  52.2 15.0 %collective-permute-start.10 = (bf16[768,384]{1,0:T(8,128)(2,1)S(1)}, bf16[768,384]{1,0:T(8,128)(2,1)S(1)}, u32[]{:S(2)}, u32[]{:S(2)}) collective-permute-start(bf16[768,384]{1,0:T(8,128)(2,1)S(1)} %broadcast_select_fusion), channel_id=1, source_target_pairs={{0,8},{1,9},{2,10},{3,11},{4,12},{5,13},{6,14},{7,15},{8,0},{9,1},... | collective-permute-start | bytes 1769480 | tf_op jit(solution)/shard_map/ppermute | solution.py:35
  54.0 14.3 %collective-permute-start.14 = (bf16[768,384]{1,0:T(8,128)(2,1)S(1)}, bf16[768,384]{1,0:T(8,128)(2,1)S(1)}, u32[]{:S(2)}, u32[]{:S(2)}) collective-permute-start(bf16[768,384]{1,0:T(8,128)(2,1)S(1)} %copy-done.4), channel_id=1, source_target_pairs={{0,1},{1,0},{2,3},{3,2},{4,5},{5,4},{6,7},{7,6},{8,9},{9,8},{10,11... | collective-permute-start | bytes 1769480 | tf_op jit(solution)/shard_map/ppermute | solution.py:35
  54.5 13.8 %collective-permute-start.15 = (bf16[768,384]{1,0:T(8,128)(2,1)S(1)}, bf16[768,384]{1,0:T(8,128)(2,1)S(1)}, u32[]{:S(2)}, u32[]{:S(2)}) collective-permute-start(bf16[768,384]{1,0:T(8,128)(2,1)S(1)} %collective-permute-done.3.refs_5_.refs_4_.refs_6_.refs_1_), channel_id=1, source_target_pairs={{0,1},{1,0},{2,3},{3,2},{4,5},{5,4},{6,7},{7,6},{8,9},{9,8},{10,11... | collective-permute-start | bytes 1769480 | tf_op jit(solution)/shard_map/ppermute | solution.py:35
  66.8 2.2 %collective-permute-start.16 = (bf16[768,384]{1,0:T(8,128)(2,1)}, bf16[768,384]{1,0:T(8,128)(2,1)S(1)}, u32[]{:S(2)}, u32[]{:S(2)}) collective-permute-start(bf16[768,384]{1,0:T(8,128)(2,1)} %collective-permute-done.4.refs_6_.refs_5_.refs_7_.refs_2_), channel_id=1, source_target_pairs={{0,1},{1,0},{2,3},{3,2},{4,5},{5,4},{6,7},{7,6},{8,9},{9,8},{10,11... | collective-permute-start | bytes 1769480 | tf_op jit(solution)/shard_map/ppermute | solution.py:35
  67.2 6.6 %copy-start.5 = (bf16[768,384]{1,0:T(8,128)(2,1)}, bf16[768,384]{1,0:T(8,128)(2,1)S(1)}, u32[]{:S(2)}) copy-start(bf16[768,384]{1,0:T(8,128)(2,1)S(1)} %collective-permute-done.10.refs_7_.refs_6_.refs_8_.refs_3_) | copy-start | bytes 1769476
  67.2 2.6 %collective-permute-start.17 = (bf16[768,384]{1,0:T(8,128)(2,1)S(1)}, bf16[768,384]{1,0:T(8,128)(2,1)S(1)}, u32[]{:S(2)}, u32[]{:S(2)}) collective-permute-start(bf16[768,384]{1,0:T(8,128)(2,1)S(1)} %collective-permute-done.10.refs_7_.refs_6_.refs_8_.refs_3_), channel_id=1, source_target_pairs={{0,1},{1,0},{2,3},{3,2},{4,5},{5,4},{6,7},{7,6},{8,9},{9,8},{10,11... | collective-permute-start | bytes 1769480 | tf_op jit(solution)/shard_map/ppermute | solution.py:35
  68.2 5.6 %copy-start.6 = (bf16[768,384]{1,0:T(8,128)(2,1)}, bf16[768,384]{1,0:T(8,128)(2,1)S(1)}, u32[]{:S(2)}) copy-start(bf16[768,384]{1,0:T(8,128)(2,1)S(1)} %collective-permute-done.14.refs_8_.refs_7_.refs_9_.refs_4_) | copy-start | bytes 1769476
  68.2 5.6 %copy-start.7 = (bf16[768,384]{1,0:T(8,128)(2,1)}, bf16[768,384]{1,0:T(8,128)(2,1)S(1)}, u32[]{:S(2)}) copy-start(bf16[768,384]{1,0:T(8,128)(2,1)S(1)} %collective-permute-done.15.refs_9_.refs_8_.refs_10_.refs_5_) | copy-start | bytes 1769476
  69.0 4.8 %copy-start.8 = (bf16[768,384]{1,0:T(8,128)(2,1)}, bf16[768,384]{1,0:T(8,128)(2,1)S(1)}, u32[]{:S(2)}) copy-start(bf16[768,384]{1,0:T(8,128)(2,1)S(1)} %collective-permute-done.16.refs_10_.refs_9_.refs_11_.refs_6_) | copy-start | bytes 1769476
  69.9 4.0 %copy-start.9 = (bf16[768,384]{1,0:T(8,128)(2,1)}, bf16[768,384]{1,0:T(8,128)(2,1)S(1)}, u32[]{:S(2)}) copy-start(bf16[768,384]{1,0:T(8,128)(2,1)S(1)} %collective-permute-done.17.refs_11_.refs_10_.refs_12_.refs_7_) | copy-start | bytes 1769476
  73.4 2.8 %collective-permute-start.18 = (bf16[512,768]{1,0:T(8,128)(2,1)S(1)}, bf16[512,768]{1,0:T(8,128)(2,1)S(1)}, u32[]{:S(2)}, u32[]{:S(2)}) collective-permute-start(bf16[512,768]{1,0:T(8,128)(2,1)S(1)} %get-tuple-element.57), channel_id=1, source_target_pairs={{0,1},{1,0},{2,3},{3,2},{4,5},{5,4},{6,7},{7,6},{8,9},{9,8},{10,11... | collective-permute-start | bytes 2359304 | tf_op jit(solution)/shard_map/ppermute | solution.py:35
  79.9 3.6 %collective-permute-start.19 = (bf16[512,768]{1,0:T(8,128)(2,1)}, bf16[512,768]{1,0:T(8,128)(2,1)S(1)}, u32[]{:S(2)}, u32[]{:S(2)}) collective-permute-start(bf16[512,768]{1,0:T(8,128)(2,1)} %get-tuple-element.62), channel_id=1, source_target_pairs={{0,1},{1,0},{2,3},{3,2},{4,5},{5,4},{6,7},{7,6},{8,9},{9,8},{10,11... | collective-permute-start | bytes 2359304 | tf_op jit(solution)/shard_map/ppermute | solution.py:35
  83.8 12.2 %collective-permute-start.24 = (bf16[256,768]{1,0:T(8,128)(2,1)S(1)}, bf16[256,768]{1,0:T(8,128)(2,1)S(1)}, u32[]{:S(2)}, u32[]{:S(2)}) collective-permute-start(bf16[256,768]{1,0:T(8,128)(2,1)S(1)} %get-tuple-element.77), channel_id=1, source_target_pairs={{0,8},{1,9},{2,10},{3,11},{4,12},{5,13},{6,14},{7,15},{8,16},{9,17... | collective-permute-start | bytes 1179656 | tf_op jit(solution)/shard_map/ppermute | solution.py:35
  85.3 22.2 %collective-permute-start.20 = (bf16[528,384]{1,0:T(8,128)(2,1)S(1)}, bf16[528,384]{1,0:T(8,128)(2,1)S(1)}, u32[]{:S(2)}, u32[]{:S(2)}) collective-permute-start(bf16[528,384]{1,0:T(8,128)(2,1)S(1)} %get-tuple-element.70), channel_id=1, source_target_pairs={{0,0},{1,4},{2,2},{3,6},{4,1},{5,5},{6,3},{7,7},{8,8},{9,12},{10,1... | collective-permute-start | bytes 1216520 | tf_op jit(solution)/shard_map/ppermute | solution.py:35
  87.2 22.0 %collective-permute-start.21 = (bf16[528,384]{1,0:T(8,128)(2,1)S(1)}, bf16[528,384]{1,0:T(8,128)(2,1)S(1)}, u32[]{:S(2)}, u32[]{:S(2)}) collective-permute-start(bf16[528,384]{1,0:T(8,128)(2,1)S(1)} %get-tuple-element.71), channel_id=1, source_target_pairs={{0,1},{1,5},{2,3},{3,7},{4,0},{5,4},{6,2},{7,6},{8,9},{9,13},{10,1... | collective-permute-start | bytes 1216520 | tf_op jit(solution)/shard_map/ppermute | solution.py:35
  87.2 22.0 %collective-permute-start.22 = (bf16[528,384]{1,0:T(8,128)(2,1)S(1)}, bf16[528,384]{1,0:T(8,128)(2,1)S(1)}, u32[]{:S(2)}, u32[]{:S(2)}) collective-permute-start(bf16[528,384]{1,0:T(8,128)(2,1)S(1)} %get-tuple-element.72), channel_id=1, source_target_pairs={{0,2},{1,6},{2,0},{3,4},{4,3},{5,7},{6,1},{7,5},{8,10},{9,14},{10,... | collective-permute-start | bytes 1216520 | tf_op jit(solution)/shard_map/ppermute | solution.py:35
  89.5 15.7 %collective-permute-start.25 = (bf16[256,768]{1,0:T(8,128)(2,1)S(1)}, bf16[256,768]{1,0:T(8,128)(2,1)S(1)}, u32[]{:S(2)}, u32[]{:S(2)}) collective-permute-start(bf16[256,768]{1,0:T(8,128)(2,1)S(1)} %get-tuple-element.78), channel_id=1, source_target_pairs={{0,24},{1,25},{2,26},{3,27},{4,28},{5,29},{6,30},{7,31},{8,0},{9,1... | collective-permute-start | bytes 1179656 | tf_op jit(solution)/shard_map/ppermute | solution.py:35
  96.0 15.9 %collective-permute-start.23 = (bf16[528,384]{1,0:T(8,128)(2,1)S(1)}, bf16[528,384]{1,0:T(8,128)(2,1)S(1)}, u32[]{:S(2)}, u32[]{:S(2)}) collective-permute-start(bf16[528,384]{1,0:T(8,128)(2,1)S(1)} %get-tuple-element.73), channel_id=1, source_target_pairs={{0,3},{1,7},{2,1},{3,5},{4,2},{5,6},{6,0},{7,4},{8,11},{9,15},{10,... | collective-permute-start | bytes 1216520 | tf_op jit(solution)/shard_map/ppermute | solution.py:35
  106.2 7.5 %collective-permute-start.29 = (bf16[256,384]{1,0:T(8,128)(2,1)S(1)}, bf16[256,384]{1,0:T(8,128)(2,1)S(1)}, u32[]{:S(2)}, u32[]{:S(2)}) collective-permute-start(bf16[256,384]{1,0:T(8,128)(2,1)S(1)} %get-tuple-element.82), channel_id=1, source_target_pairs={{0,3},{1,7},{2,1},{3,5},{4,2},{5,6},{6,0},{7,4},{8,11},{9,15},{10,... | collective-permute-start | bytes 589832 | tf_op jit(solution)/shard_map/ppermute | solution.py:35
  107.4 10.3 %collective-permute-start.28 = (bf16[256,384]{1,0:T(8,128)(2,1)S(1)}, bf16[256,384]{1,0:T(8,128)(2,1)S(1)}, u32[]{:S(2)}, u32[]{:S(2)}) collective-permute-start(bf16[256,384]{1,0:T(8,128)(2,1)S(1)} %get-tuple-element.81), channel_id=1, source_target_pairs={{0,2},{1,6},{2,0},{3,4},{4,3},{5,7},{6,1},{7,5},{8,10},{9,14},{10,... | collective-permute-start | bytes 589832 | tf_op jit(solution)/shard_map/ppermute | solution.py:35
  109.2 8.6 %collective-permute-start.27 = (bf16[256,384]{1,0:T(8,128)(2,1)S(1)}, bf16[256,384]{1,0:T(8,128)(2,1)S(1)}, u32[]{:S(2)}, u32[]{:S(2)}) collective-permute-start(bf16[256,384]{1,0:T(8,128)(2,1)S(1)} %get-tuple-element.80), channel_id=1, source_target_pairs={{0,1},{1,5},{2,3},{3,7},{4,0},{5,4},{6,2},{7,6},{8,9},{9,13},{10,1... | collective-permute-start | bytes 589832 | tf_op jit(solution)/shard_map/ppermute | solution.py:35
  109.2 10.1 %collective-permute-start.26 = (bf16[256,384]{1,0:T(8,128)(2,1)S(1)}, bf16[256,384]{1,0:T(8,128)(2,1)S(1)}, u32[]{:S(2)}, u32[]{:S(2)}) collective-permute-start(bf16[256,384]{1,0:T(8,128)(2,1)S(1)} %get-tuple-element.79), channel_id=1, source_target_pairs={{0,0},{1,4},{2,2},{3,6},{4,1},{5,5},{6,3},{7,7},{8,8},{9,12},{10,1... | collective-permute-start | bytes 589832 | tf_op jit(solution)/shard_map/ppermute | solution.py:35

commit v10 on v9

--- a/solution.py
+++ b/solution.py
@@ -258,14 +258,11 @@
 
 
 def product_kernel(*refs):
-    attended, d_queries, inv_rms, tokens = refs[0], refs[1], refs[2], refs[3:5]
-    pieces, outs, (whole, rows_in, sems) = refs[5:-7], refs[-7:-3], refs[-3:]
+    attended, d_queries, inv_rms, normed = refs[:4]
+    pieces, outs, (whole, rows_in, sems) = refs[4:-7], refs[-7:-3], refs[-3:]
     token_count, width = attended.shape
     term_rows = 2 * token_count + EXTRA
-    pairs = weight_copies(pieces, whole, 2)
-    for k in range(4):
-        pairs.append((block(tokens, k, 0, token_count + EXTRA), rows_in.at[k]))
-    run_copies(pairs, sems)
+    run_copies(weight_copies(pieces, whole, 2) + [(normed, rows_in)], sems)
     total = None
     for k in range(4):
         columns = slice(k * width, (k + 1) * width)
@@ -276,12 +273,10 @@
             d_queries[...], whole[columns, 0:width], ACROSS, preferred_element_type=F32
         ).astype(LOW)
         outs[k][token_count : 2 * token_count, :] = back
-        rows = rows_in[k, 0:token_count, :].astype(F32)
-        gain = rows_in[k, token_count : token_count + 1, :].astype(F32)
-        part = jnp.sum(rows * gain * back.astype(F32), axis=1, keepdims=True)
+        part = jnp.sum(rows_in[:, columns].astype(F32) * back.astype(F32), axis=1, keepdims=True)
         total = part if total is None else total + part
     lines = []
-    for column in (total, inv_rms[...]):
+    for column in (total / inv_rms[...], inv_rms[...]):
         line = as_row(column)
         high = line.astype(LOW).astype(F32)
         lines += [high, line - high]
@@ -436,14 +431,14 @@
     to_above = (d_outer[OWN_ROWS:] + jnp.where(c == 0, shared_grad, 0.0)).astype(LOW)
     terms = call(
         product_kernel,
-        [attended, d_queries, inv_rms] + [in_hbm(o) for o in tokens + qo_pieces],
-        [VMEM, VMEM, VMEM] + [ANY] * (2 + piece_count),
+        [attended, d_queries, inv_rms] + [in_hbm(o) for o in [normed] + qo_pieces],
+        [VMEM, VMEM, VMEM] + [ANY] * (1 + piece_count),
         [((2 * token_count + EXTRA, width), LOW)] * 4,
         [
             pltpu.VMEM((full_width, wide), LOW),
-            pltpu.VMEM((4, token_count + EXTRA, width), LOW),
+            pltpu.VMEM((token_count, full_width), LOW),
         ],
-        4 + 2 * piece_count,
+        1 + 2 * piece_count,
     )
     to_below, to_above, *terms = tie(to_below, to_above, *terms)
     up, down = move(to_above, ring_up), move(to_below, ring_down)

time: 121 us -> 121 us (level)
  starting transfers between devices: 39.8 us -> 38.1 us
  Pallas kernels: 19.5 us -> 20.9 us
    ppermute x30, starting transfers between devices: 39.8 us -> 38.1 us  [move(): return lax.ppermute(value, ('seq', 'mp'), pairs)]
    pallas_call x9, Pallas kernels: 19.5 us -> 20.9 us  [call(): pl.pallas_call(kernel, out_shape=[jax.ShapeDtypeStruct(shape, dtype) for...]
  transfers between devices with their start and end apart: 30 -> 30, of which waited for: 14 -> 13; matrix products, arithmetic and copies ran while one was open for 2% -> 2% of each run, Pallas kernels for 10% -> 11%
where the time goes in v10:
time: 121 us
  waiting for transfers between devices  56 us (46%)
  starting transfers between devices  38.1 us (31%)
  Pallas kernels  20.9 us (17%)
  other arithmetic  2.4 us (2%)
  local copies, waits for them, and re-layouts  2.23 us (2%)
    ppermute x30, waiting for transfers between devices, move(): return lax.ppermute(value, ('seq', 'mp'), pairs)  56 us
    ppermute x30, starting transfers between devices, move(): return lax.ppermute(value, ('seq', 'mp'), pairs)  38.1 us
    pallas_call x9, Pallas kernels, call(): pl.pallas_call(kernel, out_shape=[jax.ShapeDtypeStruct(shape, dtype) for...  20.9 us
  transfers between devices with their start and end apart: 30, of which 13 were waited for; matrix products, arithmetic and copies ran while one was open for 2% of the time, Pallas kernels for 11%

profile of v10, /device:TPU:1, one launch (start us, length us, event | category | flops | bytes accessed | tf_op | source)
XLA Modules:
  0.0 120.6 jit_solution(17618330354513020096)
XLA Ops:
  0.7 1.3 %pad_maximum_fusion = bf16[768,384]{1,0:T(8,128)(2,1)S(1)} fusion(bf16[192,384]{1,0:T(8,128)(2,1)} %bitcast.10, bf16[192,384]{1,0:T(8,128)(2,1)} %param.12, bf16[192,384]{1,0:T(8,128)(2,1)} %param.14, bf16[192,384]{1,0:T(8,128)(2,1)} %param.13), kind=kLoop, calls=%fused_computation.6 | loop fusion | flops 2359296 | bytes 1179648 | tf_op jit(solution)/shard_map/concatenate | solution.py:363
  1.9 4.5 %collective-permute-start = (bf16[768,384]{1,0:T(8,128)(2,1)S(1)}, bf16[768,384]{1,0:T(8,128)(2,1)S(1)}, u32[]{:S(2)}, u32[]{:S(2)}) collective-permute-start(bf16[768,384]{1,0:T(8,128)(2,1)S(1)} %pad_maximum_fusion), channel_id=1, source_target_pairs={{0,0},{1,4},{2,2},{3,6},{4,1},{5,5},{6,3},{7,7},{8,8},{9,12},{10,1... | collective-permute-start | bytes 1769480 | tf_op jit(solution)/shard_map/ppermute | solution.py:35
  6.5 1.3 %collective-permute-start.1 = (bf16[256,384]{1,0:T(8,128)(2,1)S(1)}, bf16[256,384]{1,0:T(8,128)(2,1)S(1)}, u32[]{:S(2)}, u32[]{:S(2)}) collective-permute-start(bf16[256,384]{1,0:T(8,128)(2,1)S(1)} %bitcast.6), channel_id=1, source_target_pairs={{0,8},{1,9},{2,10},{3,11},{4,12},{5,13},{6,14},{7,15},{8,16},{9,17... | collective-permute-start | bytes 589832 | tf_op jit(solution)/shard_map/ppermute | solution.py:35
  7.8 2.1 %collective-permute-start.2 = (bf16[256,384]{1,0:T(8,128)(2,1)S(1)}, bf16[256,384]{1,0:T(8,128)(2,1)S(1)}, u32[]{:S(2)}, u32[]{:S(2)}) collective-permute-start(bf16[256,384]{1,0:T(8,128)(2,1)S(1)} %bitcast.7), channel_id=1, source_target_pairs={{0,24},{1,25},{2,26},{3,27},{4,28},{5,29},{6,30},{7,31},{8,0},{9,1... | collective-permute-start | bytes 589832 | tf_op jit(solution)/shard_map/ppermute | solution.py:35
  10.3 0.6 collective-permute-start.5
  10.9 4.2 %collective-permute-done.1 = bf16[256,384]{1,0:T(8,128)(2,1)S(1)} collective-permute-done((bf16[256,384]{1,0:T(8,128)(2,1)S(1)}, bf16[256,384]{1,0:T(8,128)(2,1)S(1)}, u32[]{:S(2)}, u32[]{:S(2)}) %collective-permute-start.1) | collective-permute-done | bytes 196640 | tf_op jit(solution)/shard_map/ppermute | solution.py:35
  15.1 2.1 %collective-permute-done.2 = bf16[256,384]{1,0:T(8,128)(2,1)S(1)} collective-permute-done((bf16[256,384]{1,0:T(8,128)(2,1)S(1)}, bf16[256,384]{1,0:T(8,128)(2,1)S(1)}, u32[]{:S(2)}, u32[]{:S(2)}) %collective-permute-start.2) | collective-permute-done | bytes 196640 | tf_op jit(solution)/shard_map/ppermute | solution.py:35
  17.2 0.4 collective-permute-start.7
  17.6 1.1 shard_map.112
  18.8 2.2 %collective-permute-start.8 = (bf16[1568,384]{1,0:T(8,128)(2,1)}, bf16[1568,384]{1,0:T(8,128)(2,1)S(1)}, u32[]{:S(2)}, u32[]{:S(2)}) collective-permute-start(bf16[1568,384]{1,0:T(8,128)(2,1)} %shard_map.112), channel_id=1, source_target_pairs={{0,0},{1,4},{2,2},{3,6},{4,1},{5,5},{6,3},{7,7},{8,8},{9,12},{10,1... | collective-permute-start | bytes 3612680 | tf_op jit(solution)/shard_map/ppermute | solution.py:35
  21.0 2.3 %collective-permute-start.9 = (bf16[1568,384]{1,0:T(8,128)(2,1)}, bf16[1568,384]{1,0:T(8,128)(2,1)}, u32[]{:S(2)}, u32[]{:S(2)}) collective-permute-start(bf16[1568,384]{1,0:T(8,128)(2,1)} %shard_map.112), channel_id=1, source_target_pairs={{0,2},{1,6},{2,0},{3,4},{4,3},{5,7},{6,1},{7,5},{8,10},{9,14},{10,... | collective-permute-start | bytes 3612680 | tf_op jit(solution)/shard_map/ppermute | solution.py:35
  23.3 0.7 collective-permute-start.3
  24.0 2.5 %collective-permute-start.4 = (bf16[768,384]{1,0:T(8,128)(2,1)S(1)}, bf16[768,384]{1,0:T(8,128)(2,1)S(1)}, u32[]{:S(2)}, u32[]{:S(2)}) collective-permute-start(bf16[768,384]{1,0:T(8,128)(2,1)S(1)} %collective-permute-done.refs_4_.refs_3_.refs_0_), channel_id=1, source_target_pairs={{0,24},{1,25},{2,26},{3,27},{4,28},{5,29},{6,30},{7,31},{8,0},{9,1... | collective-permute-start | bytes 1769480 | tf_op jit(solution)/shard_map/ppermute | solution.py:35
  26.6 0.9 constant_dynamic-update-slice_fusion.3
  27.6 1.0 constant_dynamic-update-slice_fusion.1
  28.6 2.9 %collective-permute-start.12 = (bf16[1024,384]{1,0:T(8,128)(2,1)S(1)}, bf16[1024,384]{1,0:T(8,128)(2,1)S(1)}, u32[]{:S(2)}, u32[]{:S(2)}) collective-permute-start(bf16[1024,384]{1,0:T(8,128)(2,1)S(1)} %constant_dynamic-update-slice_fusion), channel_id=1, source_target_pairs={{0,0},{1,4},{2,2},{3,6},{4,1},{5,5},{6,3},{7,7},{8,8},{9,12},{10,1... | collective-permute-start | bytes 2359304 | tf_op jit(solution)/shard_map/ppermute | solution.py:35
  31.5 8.7 %collective-permute-done.3.refs_5_.refs_4_.refs_1_ = bf16[768,384]{1,0:T(8,128)(2,1)S(1)} collective-permute-done((bf16[768,384]{1,0:T(8,128)(2,1)S(1)}, bf16[768,384]{1,0:T(8,128)(2,1)S(1)}, u32[]{:S(2)}, u32[]{:S(2)}) %collective-permute-start.3) | collective-permute-done | bytes 589856 | tf_op jit(solution)/shard_map/ppermute | solution.py:35
  40.1 1.6 %collective-permute-start.13 = (bf16[1024,384]{1,0:T(8,128)(2,1)S(1)}, bf16[1024,384]{1,0:T(8,128)(2,1)S(1)}, u32[]{:S(2)}, u32[]{:S(2)}) collective-permute-start(bf16[1024,384]{1,0:T(8,128)(2,1)S(1)} %constant_dynamic-update-slice_fusion), channel_id=1, source_target_pairs={{0,2},{1,6},{2,0},{3,4},{4,3},{5,7},{6,1},{7,5},{8,10},{9,14},{10,... | collective-permute-start | bytes 2359304 | tf_op jit(solution)/shard_map/ppermute | solution.py:35
  41.8 10.2 %collective-permute-done.4.refs_6_.refs_5_.refs_2_ = bf16[768,384]{1,0:T(8,128)(2,1)S(1)} collective-permute-done((bf16[768,384]{1,0:T(8,128)(2,1)S(1)}, bf16[768,384]{1,0:T(8,128)(2,1)S(1)}, u32[]{:S(2)}, u32[]{:S(2)}) %collective-permute-start.4) | collective-permute-done | bytes 589856 | tf_op jit(solution)/shard_map/ppermute | solution.py:35
  52.2 0.4 collective-permute-start.14
  52.7 2.0 %shard_map.113 = (bf16[256,1536]{1,0:T(8,128)(2,1)S(1)}, f32[256,1]{1,0:T(8,128)S(1)}) custom-call(bf16[1568,384]{1,0:T(8,128)(2,1)S(1)} %collective-permute-done.8.refs_0_.refs_1_, bf16[1568,384]{1,0:T(8,128)(2,1)} %collective-permute-done.9.refs_1_.refs_2_), custom_call_target="tpu_custom_call" | custom-call | tf_op jit(solution)/shard_map/pallas_call | solution.py:331
  54.7 12.1 %collective-permute-done.12.refs_2_ = bf16[1024,384]{1,0:T(8,128)(2,1)S(1)} collective-permute-done((bf16[1024,384]{1,0:T(8,128)(2,1)S(1)}, bf16[1024,384]{1,0:T(8,128)(2,1)S(1)}, u32[]{:S(2)}, u32[]{:S(2)}) %collective-permute-start.12) | collective-permute-done | bytes 786464 | tf_op jit(solution)/shard_map/ppermute | solution.py:35
  66.9 1.0 collective-permute-start.17
  67.8 1.0 collective-permute-done.16.refs_10_.refs_9_.refs_6_
  68.8 0.8 collective-permute-done.17.refs_11_.refs_10_.refs_7_
  69.7 3.7 %shard_map.114 = (bf16[768,768]{1,0:T(8,128)(2,1)S(1)}, bf16[512,768]{1,0:T(8,128)(2,1)S(1)}) custom-call(bf16[1568,384]{1,0:T(8,128)(2,1)S(1)} %collective-permute-done.8.refs_0_.refs_1_, bf16[1568,384]{1,0:T(8,128)(2,1)} %collective-permute-done.9.refs_1_.refs_2_, bf16[1024,384]{1,0:T(8,128)(2,1)S(1)} %collective-permute-done.12.refs_2_, ...), custom_call_target="tpu_custom_call" | custom-call | tf_op jit(solution)/shard_map/pallas_call | solution.py:331
  73.4 0.2 collective-permute-start.18
  73.7 2.6 %shard_map.115 = (bf16[256,384]{1,0:T(8,128)(2,1)S(1)}, bf16[256,384]{1,0:T(8,128)(2,1)S(1)}) custom-call(bf16[256,1536]{1,0:T(8,128)(2,1)S(1)} %get-tuple-element.58.refs_0_.refs_3_, bf16[1568,384]{1,0:T(8,128)(2,1)S(1)} %collective-permute-done.8.refs_0_.refs_1_, bf16[1568,384]{1,0:T(8,128)(2,1)} %collective-permute-done.9.refs_1_.refs_2_, ...), custom_call_target="tpu_custom_call" | custom-call | tf_op jit(solution)/shard_map/pallas_call | solution.py:331
  76.3 3.9 %shard_map.116 = (bf16[256,384]{1,0:T(8,128)(2,1)S(1)}, bf16[256,384]{1,0:T(8,128)(2,1)S(1)}, f32[256,768]{1,0:T(8,128)S(1)}, bf16[512,768]{1,0:T(8,128)(2,1)S(1)}, bf16[512,768]{1,0:T(8,128)(2,1)}) custom-call(s32[8]{0:T(128)S(1)} %bitcast_convert_fusion.refs_0_, bf16[768,768]{1,0:T(8,128)(2,1)S(1)} %get-tuple-element.56.refs_1_, ...), custom_call_target="tpu_custom_call" | custom-call | tf_op jit(solution)/shard_map/pallas_call | solution.py:331
  80.2 0.4 collective-permute-start.19
  80.6 3.6 %shard_map.117 = (bf16[528,384]{1,0:T(8,128)(2,1)S(1)}, bf16[528,384]{1,0:T(8,128)(2,1)S(1)}, bf16[528,384]{1,0:T(8,128)(2,1)S(1)}, bf16[528,384]{1,0:T(8,128)(2,1)S(1)}) custom-call(bf16[256,384]{1,0:T(8,128)(2,1)S(1)} %get-tuple-element.63.refs_0_, bf16[256,384]{1,0:T(8,128)(2,1)S(1)} %get-tuple-element.64.refs_1_, ...), custom_call_target="tpu_custom_call" | custom-call | tf_op jit(solution)/shard_map/pallas_call | solution.py:331
  84.4 0.3 collective-permute-start.24
  84.7 3.1 %collective-permute-start.20 = (bf16[528,384]{1,0:T(8,128)(2,1)S(1)}, bf16[528,384]{1,0:T(8,128)(2,1)S(1)}, u32[]{:S(2)}, u32[]{:S(2)}) collective-permute-start(bf16[528,384]{1,0:T(8,128)(2,1)S(1)} %get-tuple-element.70), channel_id=1, source_target_pairs={{0,0},{1,4},{2,2},{3,6},{4,1},{5,5},{6,3},{7,7},{8,8},{9,12},{10,1... | collective-permute-start | bytes 1216520 | tf_op jit(solution)/shard_map/ppermute | solution.py:35
  87.9 1.6 %collective-permute-start.22 = (bf16[528,384]{1,0:T(8,128)(2,1)S(1)}, bf16[528,384]{1,0:T(8,128)(2,1)S(1)}, u32[]{:S(2)}, u32[]{:S(2)}) collective-permute-start(bf16[528,384]{1,0:T(8,128)(2,1)S(1)} %get-tuple-element.72), channel_id=1, source_target_pairs={{0,2},{1,6},{2,0},{3,4},{4,3},{5,7},{6,1},{7,5},{8,10},{9,14},{10,... | collective-permute-start | bytes 1216520 | tf_op jit(solution)/shard_map/ppermute | solution.py:35
  89.4 2.7 %collective-permute-start.25 = (bf16[256,768]{1,0:T(8,128)(2,1)S(1)}, bf16[256,768]{1,0:T(8,128)(2,1)S(1)}, u32[]{:S(2)}, u32[]{:S(2)}) collective-permute-start(bf16[256,768]{1,0:T(8,128)(2,1)S(1)} %get-tuple-element.78), channel_id=1, source_target_pairs={{0,24},{1,25},{2,26},{3,27},{4,28},{5,29},{6,30},{7,31},{8,0},{9,1... | collective-permute-start | bytes 1179656 | tf_op jit(solution)/shard_map/ppermute | solution.py:35
  92.2 4.7 %collective-permute-done.24.up = bf16[256,768]{1,0:T(8,128)(2,1)S(1)} collective-permute-done((bf16[256,768]{1,0:T(8,128)(2,1)S(1)}, bf16[256,768]{1,0:T(8,128)(2,1)S(1)}, u32[]{:S(2)}, u32[]{:S(2)}) %collective-permute-start.24) | collective-permute-done | bytes 393248 | tf_op jit(solution)/shard_map/ppermute | solution.py:35
  96.9 1.1 collective-permute-start.23
  98.0 1.8 %shard_map.119.whole = bf16[1536,768]{1,0:T(8,128)(2,1)S(1)} custom-call(bf16[768,384]{1,0:T(8,128)(2,1)} %copy-done.2, bf16[768,384]{1,0:T(8,128)(2,1)} %copy-done, bf16[768,384]{1,0:T(8,128)(2,1)} %copy-done.1, bf16[768,384]{1,0:T(8,128)(2,1)} %copy-done.3, bf16[768,384]{1,0:T(8,128)(2,1)} %copy-done.4, bf16[768,384]{1,0:T(8,128)(2,1)} %copy-done.5, ...), custom_call_target="tpu_custom_call" | custom-call | tf_op jit(solution)/shard_map/pallas_call | solution.py:331
  99.8 5.9 %collective-permute-done.25.down = bf16[256,768]{1,0:T(8,128)(2,1)S(1)} collective-permute-done((bf16[256,768]{1,0:T(8,128)(2,1)S(1)}, bf16[256,768]{1,0:T(8,128)(2,1)S(1)}, u32[]{:S(2)}, u32[]{:S(2)}) %collective-permute-start.25) | collective-permute-done | bytes 393248 | tf_op jit(solution)/shard_map/ppermute | solution.py:35
  105.7 1.0 shard_map.120
  106.7 1.4 %collective-permute-start.29 = (bf16[256,384]{1,0:T(8,128)(2,1)S(1)}, bf16[256,384]{1,0:T(8,128)(2,1)S(1)}, u32[]{:S(2)}, u32[]{:S(2)}) collective-permute-start(bf16[256,384]{1,0:T(8,128)(2,1)S(1)} %get-tuple-element.82), channel_id=1, source_target_pairs={{0,3},{1,7},{2,1},{3,5},{4,2},{5,6},{6,0},{7,4},{8,11},{9,15},{10,... | collective-permute-start | bytes 589832 | tf_op jit(solution)/shard_map/ppermute | solution.py:35
  108.1 1.7 %collective-permute-start.28 = (bf16[256,384]{1,0:T(8,128)(2,1)S(1)}, bf16[256,384]{1,0:T(8,128)(2,1)S(1)}, u32[]{:S(2)}, u32[]{:S(2)}) collective-permute-start(bf16[256,384]{1,0:T(8,128)(2,1)S(1)} %get-tuple-element.81), channel_id=1, source_target_pairs={{0,2},{1,6},{2,0},{3,4},{4,3},{5,7},{6,1},{7,5},{8,10},{9,14},{10,... | collective-permute-start | bytes 589832 | tf_op jit(solution)/shard_map/ppermute | solution.py:35
  109.8 2.6 %collective-permute-start.26 = (bf16[256,384]{1,0:T(8,128)(2,1)S(1)}, bf16[256,384]{1,0:T(8,128)(2,1)S(1)}, u32[]{:S(2)}, u32[]{:S(2)}) collective-permute-start(bf16[256,384]{1,0:T(8,128)(2,1)S(1)} %get-tuple-element.79), channel_id=1, source_target_pairs={{0,0},{1,4},{2,2},{3,6},{4,1},{5,5},{6,3},{7,7},{8,8},{9,12},{10,1... | collective-permute-start | bytes 589832 | tf_op jit(solution)/shard_map/ppermute | solution.py:35
  112.5 1.2 shard_map.118
  113.6 0.6 collective-permute-done.29
  114.3 4.3 %collective-permute-done.28 = bf16[256,384]{1,0:T(8,128)(2,1)S(1)} collective-permute-done((bf16[256,384]{1,0:T(8,128)(2,1)S(1)}, bf16[256,384]{1,0:T(8,128)(2,1)S(1)}, u32[]{:S(2)}, u32[]{:S(2)}) %collective-permute-start.28) | collective-permute-done | bytes 196640 | tf_op jit(solution)/shard_map/ppermute | solution.py:35
  118.6 1.3 %collective-permute-done.26 = bf16[256,384]{1,0:T(8,128)(2,1)S(1)} collective-permute-done((bf16[256,384]{1,0:T(8,128)(2,1)S(1)}, bf16[256,384]{1,0:T(8,128)(2,1)S(1)}, u32[]{:S(2)}, u32[]{:S(2)}) %collective-permute-start.26) | collective-permute-done | bytes 196640 | tf_op jit(solution)/shard_map/ppermute | solution.py:35
  119.9 0.8 add_convert_fusion
  (67 shorter events, 1.2 us)
Async XLA Ops:
  0.6 5.9 %copy-start.13 = (bf16[2,128,384]{2,1,0:T(8,128)(2,1)S(1)}, bf16[2,128,384]{2,1,0:T(8,128)(2,1)}, u32[]{:S(2)}) copy-start(bf16[2,128,384]{2,1,0:T(8,128)(2,1)} %param.11) | copy-start | bytes 589828
  0.6 9.3 %copy-start.12 = (bf16[256,384]{1,0:T(8,128)(2,1)S(1)}, bf16[256,384]{1,0:T(8,128)(2,1)}, u32[]{:S(2)}) copy-start(bf16[256,384]{1,0:T(8,128)(2,1)} %param.17) | copy-start | bytes 589828
  0.7 9.4 %copy-start.14 = (s32[4,2]{0,1:T(2,128)S(1)}, s32[4,2]{0,1:T(2,128)}, u32[]{:S(2)}) copy-start(s32[4,2]{0,1:T(2,128)} %param.16) | copy-start | bytes 100
  0.7 9.6 %copy-start.10 = (bf16[384]{0:T(512)(128)(2,1)S(1)}, bf16[384]{0:T(512)(128)(2,1)}, u32[]{:S(2)}) copy-start(bf16[384]{0:T(512)(128)(2,1)} %gain.1) | copy-start | bytes 2308
  0.7 9.6 %copy-start.9 = (bf16[256,384]{1,0:T(8,128)(2,1)S(1)}, bf16[256,384]{1,0:T(8,128)(2,1)}, u32[]{:S(2)}) copy-start(bf16[256,384]{1,0:T(8,128)(2,1)} %hidden.1) | copy-start | bytes 589828
  1.9 15.3 %collective-permute-start = (bf16[768,384]{1,0:T(8,128)(2,1)S(1)}, bf16[768,384]{1,0:T(8,128)(2,1)S(1)}, u32[]{:S(2)}, u32[]{:S(2)}) collective-permute-start(bf16[768,384]{1,0:T(8,128)(2,1)S(1)} %pad_maximum_fusion), channel_id=1, source_target_pairs={{0,0},{1,4},{2,2},{3,6},{4,1},{5,5},{6,3},{7,7},{8,8},{9,12},{10,1... | collective-permute-start | bytes 1769480 | tf_op jit(solution)/shard_map/ppermute | solution.py:35
  6.5 8.6 %collective-permute-start.1 = (bf16[256,384]{1,0:T(8,128)(2,1)S(1)}, bf16[256,384]{1,0:T(8,128)(2,1)S(1)}, u32[]{:S(2)}, u32[]{:S(2)}) collective-permute-start(bf16[256,384]{1,0:T(8,128)(2,1)S(1)} %bitcast.6), channel_id=1, source_target_pairs={{0,8},{1,9},{2,10},{3,11},{4,12},{5,13},{6,14},{7,15},{8,16},{9,17... | collective-permute-start | bytes 589832 | tf_op jit(solution)/shard_map/ppermute | solution.py:35
  7.8 9.3 %collective-permute-start.2 = (bf16[256,384]{1,0:T(8,128)(2,1)S(1)}, bf16[256,384]{1,0:T(8,128)(2,1)S(1)}, u32[]{:S(2)}, u32[]{:S(2)}) collective-permute-start(bf16[256,384]{1,0:T(8,128)(2,1)S(1)} %bitcast.7), channel_id=1, source_target_pairs={{0,24},{1,25},{2,26},{3,27},{4,28},{5,29},{6,30},{7,31},{8,0},{9,1... | collective-permute-start | bytes 589832 | tf_op jit(solution)/shard_map/ppermute | solution.py:35
  10.0 7.6 %collective-permute-start.6 = (bf16[512,384]{1,0:T(8,128)(2,1)S(1)}, bf16[512,384]{1,0:T(8,128)(2,1)S(1)}, u32[]{:S(2)}, u32[]{:S(2)}) collective-permute-start(bf16[512,384]{1,0:T(8,128)(2,1)S(1)} %pad_maximum_fusion.1.refs_1_), channel_id=1, source_target_pairs={{0,1},{1,0},{2,3},{3,2},{4,5},{5,4},{6,7},{7,6},{8,9},{9,8},{10,11... | collective-permute-start | bytes 1179656 | tf_op jit(solution)/shard_map/ppermute | solution.py:35
  10.3 7.3 %collective-permute-start.5 = (bf16[272,384]{1,0:T(8,128)(2,1)S(1)}, bf16[272,384]{1,0:T(8,128)(2,1)S(1)}, u32[]{:S(2)}, u32[]{:S(2)}) collective-permute-start(bf16[272,384]{1,0:T(8,128)(2,1)S(1)} %pad_maximum_fusion.2.refs_0_), channel_id=1, source_target_pairs={{0,1},{1,0},{2,3},{3,2},{4,5},{5,4},{6,7},{7,6},{8,9},{9,8},{10,11... | collective-permute-start | bytes 626696 | tf_op jit(solution)/shard_map/ppermute | solution.py:35
  15.1 3.6 %copy-start.11 = (bf16[256,384]{1,0:T(8,128)(2,1)}, bf16[256,384]{1,0:T(8,128)(2,1)S(1)}, u32[]{:S(2)}) copy-start(bf16[256,384]{1,0:T(8,128)(2,1)S(1)} %collective-permute-done.1) | copy-start | bytes 589828
  17.2 56.4 %copy-start.2 = (bf16[768,384]{1,0:T(8,128)(2,1)}, bf16[768,384]{1,0:T(8,128)(2,1)S(1)}, u32[]{:S(2)}) copy-start(bf16[768,384]{1,0:T(8,128)(2,1)S(1)} %collective-permute-done.refs_4_.refs_3_.refs_0_) | copy-start | bytes 1769476
  17.2 1.6 %collective-permute-start.7 = (bf16[256,384]{1,0:T(8,128)(2,1)S(1)}, bf16[256,384]{1,0:T(8,128)(2,1)}, u32[]{:S(2)}, u32[]{:S(2)}) collective-permute-start(bf16[256,384]{1,0:T(8,128)(2,1)S(1)} %collective-permute-done.1), channel_id=1, source_target_pairs={{0,1},{1,0},{2,3},{3,2},{4,5},{5,4},{6,7},{7,6},{8,9},{9,8},{10,11... | collective-permute-start | bytes 589832 | tf_op jit(solution)/shard_map/ppermute | solution.py:35
  18.8 33.1 %collective-permute-start.8 = (bf16[1568,384]{1,0:T(8,128)(2,1)}, bf16[1568,384]{1,0:T(8,128)(2,1)S(1)}, u32[]{:S(2)}, u32[]{:S(2)}) collective-permute-start(bf16[1568,384]{1,0:T(8,128)(2,1)} %shard_map.112), channel_id=1, source_target_pairs={{0,0},{1,4},{2,2},{3,6},{4,1},{5,5},{6,3},{7,7},{8,8},{9,12},{10,1... | collective-permute-start | bytes 3612680 | tf_op jit(solution)/shard_map/ppermute | solution.py:35
  21.0 30.9 %collective-permute-start.9 = (bf16[1568,384]{1,0:T(8,128)(2,1)}, bf16[1568,384]{1,0:T(8,128)(2,1)}, u32[]{:S(2)}, u32[]{:S(2)}) collective-permute-start(bf16[1568,384]{1,0:T(8,128)(2,1)} %shard_map.112), channel_id=1, source_target_pairs={{0,2},{1,6},{2,0},{3,4},{4,3},{5,7},{6,1},{7,5},{8,10},{9,14},{10,... | collective-permute-start | bytes 3612680 | tf_op jit(solution)/shard_map/ppermute | solution.py:35
  23.3 16.8 %collective-permute-start.3 = (bf16[768,384]{1,0:T(8,128)(2,1)S(1)}, bf16[768,384]{1,0:T(8,128)(2,1)S(1)}, u32[]{:S(2)}, u32[]{:S(2)}) collective-permute-start(bf16[768,384]{1,0:T(8,128)(2,1)S(1)} %collective-permute-done.refs_4_.refs_3_.refs_0_), channel_id=1, source_target_pairs={{0,8},{1,9},{2,10},{3,11},{4,12},{5,13},{6,14},{7,15},{8,16},{9,17... | collective-permute-start | bytes 1769480 | tf_op jit(solution)/shard_map/ppermute | solution.py:35
  24.0 27.9 %collective-permute-start.4 = (bf16[768,384]{1,0:T(8,128)(2,1)S(1)}, bf16[768,384]{1,0:T(8,128)(2,1)S(1)}, u32[]{:S(2)}, u32[]{:S(2)}) collective-permute-start(bf16[768,384]{1,0:T(8,128)(2,1)S(1)} %collective-permute-done.refs_4_.refs_3_.refs_0_), channel_id=1, source_target_pairs={{0,24},{1,25},{2,26},{3,27},{4,28},{5,29},{6,30},{7,31},{8,0},{9,1... | collective-permute-start | bytes 1769480 | tf_op jit(solution)/shard_map/ppermute | solution.py:35
  26.6 2.0 %collective-permute-start.11 = (bf16[256,384]{1,0:T(8,128)(2,1)S(1)}, bf16[256,384]{1,0:T(8,128)(2,1)S(1)}, u32[]{:S(2)}, u32[]{:S(2)}) collective-permute-start(bf16[256,384]{1,0:T(8,128)(2,1)S(1)} %collective-permute-done.2), channel_id=1, source_target_pairs={{0,1},{1,0},{2,3},{3,2},{4,5},{5,4},{6,7},{7,6},{8,9},{9,8},{10,11... | collective-permute-start | bytes 589832 | tf_op jit(solution)/shard_map/ppermute | solution.py:35
  28.6 38.2 %collective-permute-start.12 = (bf16[1024,384]{1,0:T(8,128)(2,1)S(1)}, bf16[1024,384]{1,0:T(8,128)(2,1)S(1)}, u32[]{:S(2)}, u32[]{:S(2)}) collective-permute-start(bf16[1024,384]{1,0:T(8,128)(2,1)S(1)} %constant_dynamic-update-slice_fusion), channel_id=1, source_target_pairs={{0,0},{1,4},{2,2},{3,6},{4,1},{5,5},{6,3},{7,7},{8,8},{9,12},{10,1... | collective-permute-start | bytes 2359304 | tf_op jit(solution)/shard_map/ppermute | solution.py:35
  40.1 33.5 %copy-start = (bf16[768,384]{1,0:T(8,128)(2,1)}, bf16[768,384]{1,0:T(8,128)(2,1)S(1)}, u32[]{:S(2)}) copy-start(bf16[768,384]{1,0:T(8,128)(2,1)S(1)} %collective-permute-done.3.refs_5_.refs_4_.refs_1_) | copy-start | bytes 1769476
  40.1 26.7 %collective-permute-start.13 = (bf16[1024,384]{1,0:T(8,128)(2,1)S(1)}, bf16[1024,384]{1,0:T(8,128)(2,1)S(1)}, u32[]{:S(2)}, u32[]{:S(2)}) collective-permute-start(bf16[1024,384]{1,0:T(8,128)(2,1)S(1)} %constant_dynamic-update-slice_fusion), channel_id=1, source_target_pairs={{0,2},{1,6},{2,0},{3,4},{4,3},{5,7},{6,1},{7,5},{8,10},{9,14},{10,... | collective-permute-start | bytes 2359304 | tf_op jit(solution)/shard_map/ppermute | solution.py:35
  51.9 21.7 %copy-start.1 = (bf16[768,384]{1,0:T(8,128)(2,1)}, bf16[768,384]{1,0:T(8,128)(2,1)S(1)}, u32[]{:S(2)}) copy-start(bf16[768,384]{1,0:T(8,128)(2,1)S(1)} %collective-permute-done.4.refs_6_.refs_5_.refs_2_) | copy-start | bytes 1769476
  52.0 14.8 %collective-permute-start.10 = (bf16[768,384]{1,0:T(8,128)(2,1)S(1)}, bf16[768,384]{1,0:T(8,128)(2,1)S(1)}, u32[]{:S(2)}, u32[]{:S(2)}) collective-permute-start(bf16[768,384]{1,0:T(8,128)(2,1)S(1)} %broadcast_select_fusion), channel_id=1, source_target_pairs={{0,8},{1,9},{2,10},{3,11},{4,12},{5,13},{6,14},{7,15},{8,0},{9,1},... | collective-permute-start | bytes 1769480 | tf_op jit(solution)/shard_map/ppermute | solution.py:35
  52.2 15.6 %collective-permute-start.14 = (bf16[768,384]{1,0:T(8,128)(2,1)S(1)}, bf16[768,384]{1,0:T(8,128)(2,1)S(1)}, u32[]{:S(2)}, u32[]{:S(2)}) collective-permute-start(bf16[768,384]{1,0:T(8,128)(2,1)S(1)} %collective-permute-done.refs_4_.refs_3_.refs_0_), channel_id=1, source_target_pairs={{0,1},{1,0},{2,3},{3,2},{4,5},{5,4},{6,7},{7,6},{8,9},{9,8},{10,11... | collective-permute-start | bytes 1769480 | tf_op jit(solution)/shard_map/ppermute | solution.py:35
  52.6 15.2 %collective-permute-start.15 = (bf16[768,384]{1,0:T(8,128)(2,1)S(1)}, bf16[768,384]{1,0:T(8,128)(2,1)S(1)}, u32[]{:S(2)}, u32[]{:S(2)}) collective-permute-start(bf16[768,384]{1,0:T(8,128)(2,1)S(1)} %collective-permute-done.3.refs_5_.refs_4_.refs_1_), channel_id=1, source_target_pairs={{0,1},{1,0},{2,3},{3,2},{4,5},{5,4},{6,7},{7,6},{8,9},{9,8},{10,11... | collective-permute-start | bytes 1769480 | tf_op jit(solution)/shard_map/ppermute | solution.py:35
  54.7 19.0 %copy-start.8 = (bf16[256,1536]{1,0:T(8,128)(2,1)}, bf16[256,1536]{1,0:T(8,128)(2,1)S(1)}, u32[]{:S(2)}) copy-start(bf16[256,1536]{1,0:T(8,128)(2,1)S(1)} %get-tuple-element.58.refs_0_.refs_3_) | copy-start | bytes 2359300
  66.8 2.0 %collective-permute-start.16 = (bf16[768,384]{1,0:T(8,128)(2,1)S(1)}, bf16[768,384]{1,0:T(8,128)(2,1)S(1)}, u32[]{:S(2)}, u32[]{:S(2)}) collective-permute-start(bf16[768,384]{1,0:T(8,128)(2,1)S(1)} %collective-permute-done.4.refs_6_.refs_5_.refs_2_), channel_id=1, source_target_pairs={{0,1},{1,0},{2,3},{3,2},{4,5},{5,4},{6,7},{7,6},{8,9},{9,8},{10,11... | collective-permute-start | bytes 1769480 | tf_op jit(solution)/shard_map/ppermute | solution.py:35
  66.8 6.8 %copy-start.3 = (bf16[768,384]{1,0:T(8,128)(2,1)}, bf16[768,384]{1,0:T(8,128)(2,1)S(1)}, u32[]{:S(2)}) copy-start(bf16[768,384]{1,0:T(8,128)(2,1)S(1)} %collective-permute-done.10.refs_7_.refs_6_.refs_3_) | copy-start | bytes 1769476
  66.9 2.8 %collective-permute-start.17 = (bf16[768,384]{1,0:T(8,128)(2,1)S(1)}, bf16[768,384]{1,0:T(8,128)(2,1)S(1)}, u32[]{:S(2)}, u32[]{:S(2)}) collective-permute-start(bf16[768,384]{1,0:T(8,128)(2,1)S(1)} %collective-permute-done.10.refs_7_.refs_6_.refs_3_), channel_id=1, source_target_pairs={{0,1},{1,0},{2,3},{3,2},{4,5},{5,4},{6,7},{7,6},{8,9},{9,8},{10,11... | collective-permute-start | bytes 1769480 | tf_op jit(solution)/shard_map/ppermute | solution.py:35
  67.8 5.9 %copy-start.4 = (bf16[768,384]{1,0:T(8,128)(2,1)}, bf16[768,384]{1,0:T(8,128)(2,1)S(1)}, u32[]{:S(2)}) copy-start(bf16[768,384]{1,0:T(8,128)(2,1)S(1)} %collective-permute-done.14.refs_8_.refs_7_.refs_4_) | copy-start | bytes 1769476
  67.8 5.9 %copy-start.5 = (bf16[768,384]{1,0:T(8,128)(2,1)}, bf16[768,384]{1,0:T(8,128)(2,1)S(1)}, u32[]{:S(2)}) copy-start(bf16[768,384]{1,0:T(8,128)(2,1)S(1)} %collective-permute-done.15.refs_9_.refs_8_.refs_5_) | copy-start | bytes 1769476
  68.8 4.9 %copy-start.6 = (bf16[768,384]{1,0:T(8,128)(2,1)}, bf16[768,384]{1,0:T(8,128)(2,1)S(1)}, u32[]{:S(2)}) copy-start(bf16[768,384]{1,0:T(8,128)(2,1)S(1)} %collective-permute-done.16.refs_10_.refs_9_.refs_6_) | copy-start | bytes 1769476
  69.7 4.0 %copy-start.7 = (bf16[768,384]{1,0:T(8,128)(2,1)}, bf16[768,384]{1,0:T(8,128)(2,1)S(1)}, u32[]{:S(2)}) copy-start(bf16[768,384]{1,0:T(8,128)(2,1)S(1)} %collective-permute-done.17.refs_11_.refs_10_.refs_7_) | copy-start | bytes 1769476
  73.4 2.9 %collective-permute-start.18 = (bf16[512,768]{1,0:T(8,128)(2,1)S(1)}, bf16[512,768]{1,0:T(8,128)(2,1)S(1)}, u32[]{:S(2)}, u32[]{:S(2)}) collective-permute-start(bf16[512,768]{1,0:T(8,128)(2,1)S(1)} %get-tuple-element.57), channel_id=1, source_target_pairs={{0,1},{1,0},{2,3},{3,2},{4,5},{5,4},{6,7},{7,6},{8,9},{9,8},{10,11... | collective-permute-start | bytes 2359304 | tf_op jit(solution)/shard_map/ppermute | solution.py:35
  80.2 4.0 %collective-permute-start.19 = (bf16[512,768]{1,0:T(8,128)(2,1)}, bf16[512,768]{1,0:T(8,128)(2,1)S(1)}, u32[]{:S(2)}, u32[]{:S(2)}) collective-permute-start(bf16[512,768]{1,0:T(8,128)(2,1)} %get-tuple-element.62), channel_id=1, source_target_pairs={{0,1},{1,0},{2,3},{3,2},{4,5},{5,4},{6,7},{7,6},{8,9},{9,8},{10,11... | collective-permute-start | bytes 2359304 | tf_op jit(solution)/shard_map/ppermute | solution.py:35
  84.4 12.5 %collective-permute-start.24 = (bf16[256,768]{1,0:T(8,128)(2,1)S(1)}, bf16[256,768]{1,0:T(8,128)(2,1)S(1)}, u32[]{:S(2)}, u32[]{:S(2)}) collective-permute-start(bf16[256,768]{1,0:T(8,128)(2,1)S(1)} %get-tuple-element.77), channel_id=1, source_target_pairs={{0,8},{1,9},{2,10},{3,11},{4,12},{5,13},{6,14},{7,15},{8,16},{9,17... | collective-permute-start | bytes 1179656 | tf_op jit(solution)/shard_map/ppermute | solution.py:35
  84.7 23.4 %collective-permute-start.20 = (bf16[528,384]{1,0:T(8,128)(2,1)S(1)}, bf16[528,384]{1,0:T(8,128)(2,1)S(1)}, u32[]{:S(2)}, u32[]{:S(2)}) collective-permute-start(bf16[528,384]{1,0:T(8,128)(2,1)S(1)} %get-tuple-element.70), channel_id=1, source_target_pairs={{0,0},{1,4},{2,2},{3,6},{4,1},{5,5},{6,3},{7,7},{8,8},{9,12},{10,1... | collective-permute-start | bytes 1216520 | tf_op jit(solution)/shard_map/ppermute | solution.py:35
  87.9 22.0 %collective-permute-start.21 = (bf16[528,384]{1,0:T(8,128)(2,1)S(1)}, bf16[528,384]{1,0:T(8,128)(2,1)S(1)}, u32[]{:S(2)}, u32[]{:S(2)}) collective-permute-start(bf16[528,384]{1,0:T(8,128)(2,1)S(1)} %get-tuple-element.71), channel_id=1, source_target_pairs={{0,1},{1,5},{2,3},{3,7},{4,0},{5,4},{6,2},{7,6},{8,9},{9,13},{10,1... | collective-permute-start | bytes 1216520 | tf_op jit(solution)/shard_map/ppermute | solution.py:35
  87.9 22.0 %collective-permute-start.22 = (bf16[528,384]{1,0:T(8,128)(2,1)S(1)}, bf16[528,384]{1,0:T(8,128)(2,1)S(1)}, u32[]{:S(2)}, u32[]{:S(2)}) collective-permute-start(bf16[528,384]{1,0:T(8,128)(2,1)S(1)} %get-tuple-element.72), channel_id=1, source_target_pairs={{0,2},{1,6},{2,0},{3,4},{4,3},{5,7},{6,1},{7,5},{8,10},{9,14},{10,... | collective-permute-start | bytes 1216520 | tf_op jit(solution)/shard_map/ppermute | solution.py:35
  89.4 16.3 %collective-permute-start.25 = (bf16[256,768]{1,0:T(8,128)(2,1)S(1)}, bf16[256,768]{1,0:T(8,128)(2,1)S(1)}, u32[]{:S(2)}, u32[]{:S(2)}) collective-permute-start(bf16[256,768]{1,0:T(8,128)(2,1)S(1)} %get-tuple-element.78), channel_id=1, source_target_pairs={{0,24},{1,25},{2,26},{3,27},{4,28},{5,29},{6,30},{7,31},{8,0},{9,1... | collective-permute-start | bytes 1179656 | tf_op jit(solution)/shard_map/ppermute | solution.py:35
  96.9 15.6 %collective-permute-start.23 = (bf16[528,384]{1,0:T(8,128)(2,1)S(1)}, bf16[528,384]{1,0:T(8,128)(2,1)S(1)}, u32[]{:S(2)}, u32[]{:S(2)}) collective-permute-start(bf16[528,384]{1,0:T(8,128)(2,1)S(1)} %get-tuple-element.73), channel_id=1, source_target_pairs={{0,3},{1,7},{2,1},{3,5},{4,2},{5,6},{6,0},{7,4},{8,11},{9,15},{10,... | collective-permute-start | bytes 1216520 | tf_op jit(solution)/shard_map/ppermute | solution.py:35
  106.7 7.6 %collective-permute-start.29 = (bf16[256,384]{1,0:T(8,128)(2,1)S(1)}, bf16[256,384]{1,0:T(8,128)(2,1)S(1)}, u32[]{:S(2)}, u32[]{:S(2)}) collective-permute-start(bf16[256,384]{1,0:T(8,128)(2,1)S(1)} %get-tuple-element.82), channel_id=1, source_target_pairs={{0,3},{1,7},{2,1},{3,5},{4,2},{5,6},{6,0},{7,4},{8,11},{9,15},{10,... | collective-permute-start | bytes 589832 | tf_op jit(solution)/shard_map/ppermute | solution.py:35
  108.1 10.4 %collective-permute-start.28 = (bf16[256,384]{1,0:T(8,128)(2,1)S(1)}, bf16[256,384]{1,0:T(8,128)(2,1)S(1)}, u32[]{:S(2)}, u32[]{:S(2)}) collective-permute-start(bf16[256,384]{1,0:T(8,128)(2,1)S(1)} %get-tuple-element.81), channel_id=1, source_target_pairs={{0,2},{1,6},{2,0},{3,4},{4,3},{5,7},{6,1},{7,5},{8,10},{9,14},{10,... | collective-permute-start | bytes 589832 | tf_op jit(solution)/shard_map/ppermute | solution.py:35
  109.8 8.7 %collective-permute-start.27 = (bf16[256,384]{1,0:T(8,128)(2,1)S(1)}, bf16[256,384]{1,0:T(8,128)(2,1)S(1)}, u32[]{:S(2)}, u32[]{:S(2)}) collective-permute-start(bf16[256,384]{1,0:T(8,128)(2,1)S(1)} %get-tuple-element.80), channel_id=1, source_target_pairs={{0,1},{1,5},{2,3},{3,7},{4,0},{5,4},{6,2},{7,6},{8,9},{9,13},{10,1... | collective-permute-start | bytes 589832 | tf_op jit(solution)/shard_map/ppermute | solution.py:35
  109.8 10.0 %collective-permute-start.26 = (bf16[256,384]{1,0:T(8,128)(2,1)S(1)}, bf16[256,384]{1,0:T(8,128)(2,1)S(1)}, u32[]{:S(2)}, u32[]{:S(2)}) collective-permute-start(bf16[256,384]{1,0:T(8,128)(2,1)S(1)} %get-tuple-element.79), channel_id=1, source_target_pairs={{0,0},{1,4},{2,2},{3,6},{4,1},{5,5},{6,3},{7,7},{8,8},{9,12},{10,1... | collective-permute-start | bytes 589832 | tf_op jit(solution)/shard_map/ppermute | solution.py:35
